TPU v7x, 32 devices: a whole 2x2x4 slice. The times are simulated.
32 devices in a mesh: ctx: 4 (over z), fsdp: 8 (over y, x, core).
Axes of the slice: x: 2, y: 2, z: 4, core: 2. Of those that a mesh axis runs over, the one named last changes fastest.
Arguments:
- tokens: bfloat16 [4096, 2048], P(('ctx', 'fsdp')), may hold values from -6 to 6
- pair_index: int32 [4], replicated, may hold values from 0 to 3, each once
- gain_attn: bfloat16 [2048], P(('ctx', 'fsdp')), may hold values from 0.5 to 1.5
- w_query: bfloat16 [2048, 2048], P(('ctx', 'fsdp')), may hold values from -0.125 to 0.125
- w_key: bfloat16 [2048, 2048], P(('ctx', 'fsdp')), may hold values from -0.125 to 0.125
- w_value: bfloat16 [2048, 2048], P(('ctx', 'fsdp')), may hold values from -0.125 to 0.125
- w_out: bfloat16 [2048, 2048], P(('ctx', 'fsdp')), may hold values from -0.5 to 0.5
- gain_ffn: bfloat16 [2048], P(('ctx', 'fsdp')), may hold values from 0.5 to 1.5
- w_gate: bfloat16 [8192, 2048], P(('ctx', 'fsdp')), may hold values from -0.125 to 0.125
- w_up: bfloat16 [8192, 2048], P(('ctx', 'fsdp')), may hold values from -0.125 to 0.125
- w_down: bfloat16 [8192, 2048], P(('ctx', 'fsdp')), may hold values from -0.0625 to 0.0625
- cotangent: bfloat16 [4096, 2048], P(('ctx', 'fsdp')), may hold values from -6 to 6
Outputs:
- block_out: bfloat16 [4096, 2048], P(('ctx', 'fsdp'))
- input_grad: float32 [4096, 2048], P(('ctx', 'fsdp'))
- gain_attn_grad: float32 [2048], P(('ctx', 'fsdp'))
- query_grad: float32 [2048, 2048], P(('ctx', 'fsdp'))
- key_grad: float32 [2048, 2048], P(('ctx', 'fsdp'))
- value_grad: float32 [2048, 2048], P(('ctx', 'fsdp'))
- out_grad: float32 [2048, 2048], P(('ctx', 'fsdp'))
- gain_ffn_grad: float32 [2048], P(('ctx', 'fsdp'))
- gate_grad: float32 [8192, 2048], P(('ctx', 'fsdp'))
- up_grad: float32 [8192, 2048], P(('ctx', 'fsdp'))
- down_grad: float32 [8192, 2048], P(('ctx', 'fsdp'))
Inputs may be any that keep to these rules, and one draw needn't show every extreme that they name: Ctx group c holds sequence blocks pair_index[c] and 7 - pair_index[c] of 512 tokens each, rows of the lower block first; every value occurs once.
All inputs are finite; a program needn't handle non-finite values.
Results may differ from a plain program's by a relative error of at most 0.019.
Values may be sent and summed in bfloat16 or wider, within the bound.
No kernel may reach another device: no remote copies, remote signals or barrier semaphores. Data moves between devices by JAX's collectives and lax.ppermute only.
A program may use at most 256 MiB of HBM per device.

v0:
```python
import math

import jax
import jax.numpy as jnp
from jax import lax
from jax.sharding import PartitionSpec as P

HD = 64


EPS = 1e-05
THETA = 130000.0


def place_of(rows, pair_index, n_groups, blk):
    group = rows // (2 * blk)
    within = rows % (2 * blk)
    match = group[:, None] == jnp.arange(n_groups, dtype=jnp.int32)[None, :]
    pair = jnp.sum(jnp.where(match, pair_index[None, :], 0), axis=1)
    block = jnp.where(within < blk, pair, 2 * n_groups - 1 - pair)
    return block * blk + within % blk


def tables(places, head_dim):
    freq = jnp.exp(
        jnp.arange(head_dim // 2, dtype=jnp.float32) * (-2.0 * math.log(THETA) / head_dim)
    )
    angle = places.astype(jnp.float32)[:, None] * freq[None, :]
    return (jnp.cos(angle), jnp.sin(angle))


def rotate(flat, cosine, sine, head_dim):
    rows = flat.shape[0]
    split = flat.reshape(rows, -1, head_dim)
    half = head_dim // 2
    first = split[..., :half]
    second = split[..., half:]
    cos_b = cosine[:, None, :]
    sin_b = sine[:, None, :]
    out = jnp.concatenate([first * cos_b - second * sin_b, second * cos_b + first * sin_b], axis=-1)
    return out.reshape(rows, -1)


def silu_parts(gate):
    sig = jax.nn.sigmoid(gate)
    return (gate * sig, sig * (1.0 + gate * (1.0 - sig)))


def rows_by(left, right):
    return jnp.einsum("td,fd->tf", left, right, preferred_element_type=jnp.float32)


def outer_sum(left, right):
    return jnp.einsum("tf,td->fd", left, right, preferred_element_type=jnp.float32)


def per_device(
    tokens,
    pair_index,
    gain_attn,
    w_query,
    w_key,
    w_value,
    w_out,
    gain_ffn,
    w_gate,
    w_up,
    w_down,
    cotangent,
):
    f32 = jnp.float32
    bf16 = jnp.bfloat16
    n_ctx = lax.axis_size("ctx")
    n_fsdp = lax.axis_size("fsdp")
    tok = tokens.shape[0]
    group_rows = tok * n_fsdp
    blk = group_rows // 2
    total = group_rows * n_ctx
    ctx_index = lax.axis_index("ctx")
    fsdp_index = lax.axis_index("fsdp")
    local_rows = (ctx_index * n_fsdp + fsdp_index) * tok + jnp.arange(tok, dtype=jnp.int32)
    local_places = place_of(local_rows, pair_index, n_ctx, blk)
    group_places = place_of(
        ctx_index * group_rows + jnp.arange(group_rows, dtype=jnp.int32), pair_index, n_ctx, blk
    )
    key_places = place_of(jnp.arange(total, dtype=jnp.int32), pair_index, n_ctx, blk)
    group_cos, group_sin = tables(group_places, HD)
    query_full, key_full, value_full, out_full, gain_one, gain_two = (
        lax.all_gather(w_query, ("ctx", "fsdp"), axis=0, tiled=True),
        lax.all_gather(w_key, ("ctx", "fsdp"), axis=0, tiled=True),
        lax.all_gather(w_value, ("ctx", "fsdp"), axis=0, tiled=True),
        lax.all_gather(w_out, ("ctx", "fsdp"), axis=0, tiled=True),
        lax.all_gather(gain_attn, ("ctx", "fsdp"), axis=0, tiled=True),
        lax.all_gather(gain_ffn, ("ctx", "fsdp"), axis=0, tiled=True),
    )
    gain_one = gain_one.astype(f32)
    gain_two = gain_two.astype(f32)
    x32 = tokens.astype(f32)
    scale_one = lax.rsqrt(jnp.mean(x32 * x32, axis=-1, keepdims=True) + EPS)
    normed_one = (x32 * scale_one * gain_one).astype(bf16)
    cosine, sine = tables(local_places, HD)
    query = rotate(
        jnp.dot(normed_one, query_full, preferred_element_type=f32), cosine, sine, HD
    ).astype(bf16)
    key = rotate(
        jnp.dot(normed_one, key_full, preferred_element_type=f32), cosine, sine, HD
    ).astype(bf16)
    value = jnp.dot(normed_one, value_full, preferred_element_type=f32).astype(bf16)
    query_heads, key_heads, value_heads = (
        lax.all_to_all(query, "fsdp", split_axis=1, concat_axis=0, tiled=True),
        lax.all_to_all(key, "fsdp", split_axis=1, concat_axis=0, tiled=True),
        lax.all_to_all(value, "fsdp", split_axis=1, concat_axis=0, tiled=True),
    )
    key_all, value_all = (
        lax.all_gather(key_heads, "ctx", axis=0, tiled=True),
        lax.all_gather(value_heads, "ctx", axis=0, tiled=True),
    )
    local_width = query_heads.shape[1]
    heads_here = local_width // HD
    scale = HD ** (-0.5)
    query_parts = query_heads.reshape(2, blk, heads_here, HD)
    query_place_tiles = group_places.reshape(2, blk)
    key_tiles = key_all.reshape(2 * n_ctx, blk, heads_here, HD)
    value_tiles = value_all.reshape(2 * n_ctx, blk, heads_here, HD)
    key_place_tiles = key_places.reshape(2 * n_ctx, blk)

    def tile_scores(slot, keys, k_place):
        raw = (
            jnp.einsum("qhd,khd->hqk", query_parts[slot], keys, preferred_element_type=f32) * scale
        )
        keep = k_place[None, None, :] <= query_place_tiles[slot][None, :, None]
        return jnp.where(keep, raw, -1e30)

    def is_live(slot, k_place):
        return jnp.min(k_place) <= jnp.max(query_place_tiles[slot])

    def first_pass(carry, tile):
        keys, k_place = tile
        highs, totals = carry
        new_highs = []
        new_totals = []
        for slot in range(2):

            def first_update(high, summed):
                masked = tile_scores(slot, keys, k_place)
                fresh = jnp.maximum(high, jnp.max(masked, axis=-1))
                summed = summed * jnp.exp(high - fresh) + jnp.sum(
                    jnp.exp(masked - fresh[..., None]), axis=-1
                )
                return (fresh, summed)

            def first_leave(high, summed):
                return (high, summed)

            high, summed = lax.cond(
                is_live(slot, k_place), first_update, first_leave, highs[slot], totals[slot]
            )
            new_highs.append(high)
            new_totals.append(summed)
        return ((jnp.stack(new_highs), jnp.stack(new_totals)), None)

    start_high = jnp.full((2, heads_here, blk), -1e30, f32)
    start_total = jnp.zeros((2, heads_here, blk), f32)
    (highs, totals), unused = lax.scan(
        first_pass, (start_high, start_total), (key_tiles, key_place_tiles)
    )
    log_total = highs + jnp.log(totals)

    def second_pass(carry, tile):
        keys, values, k_place = tile
        outs = []
        for slot in range(2):

            def second_update(acc):
                masked = tile_scores(slot, keys, k_place)
                prob_low = jnp.exp(masked - log_total[slot][..., None]).astype(bf16)
                return acc + jnp.einsum(
                    "hqk,khd->qhd", prob_low, values, preferred_element_type=f32
                )

            def second_leave(acc):
                return acc

            outs.append(lax.cond(is_live(slot, k_place), second_update, second_leave, carry[slot]))
        return (jnp.stack(outs), None)

    acc_start = jnp.zeros((2, blk, heads_here, HD), f32)
    attn_acc, unused = lax.scan(second_pass, acc_start, (key_tiles, value_tiles, key_place_tiles))
    attn32 = attn_acc.reshape(group_rows, local_width)
    attn_tokens = lax.all_to_all(
        attn32.astype(bf16), "fsdp", split_axis=0, concat_axis=1, tiled=True
    )
    mid = x32 + jnp.dot(attn_tokens, out_full, preferred_element_type=f32)
    scale_two = lax.rsqrt(jnp.mean(mid * mid, axis=-1, keepdims=True) + EPS)
    normed_two = (mid * scale_two * gain_two).astype(bf16)
    dy = cotangent.astype(f32)
    dy_low = dy.astype(bf16)
    gate_local, up_local, down_local = (
        lax.all_gather(w_gate, "ctx", axis=0, tiled=True),
        lax.all_gather(w_up, "ctx", axis=0, tiled=True),
        lax.all_gather(w_down, "ctx", axis=0, tiled=True),
    )
    rows_all = lax.all_gather(normed_two, "fsdp", axis=0, tiled=True)
    gate_all = rows_by(rows_all, gate_local)
    up_all = rows_by(rows_all, up_local)
    silu_all, unused_slope = silu_parts(gate_all)
    hidden_all = (silu_all * up_all).astype(bf16)
    branch = lax.psum_scatter(
        jnp.dot(hidden_all, down_local, preferred_element_type=f32).astype(jnp.bfloat16),
        "fsdp",
        scatter_dimension=0,
        tiled=True,
    ).astype(jnp.float32)
    block_out = (mid + branch).astype(bf16)
    grad_rows_all = lax.all_gather(dy_low, "fsdp", axis=0, tiled=True)
    dhidden = rows_by(grad_rows_all, down_local)
    silu_val, slope = silu_parts(gate_all)
    dgate = (dhidden * up_all * slope).astype(bf16)
    dup = (dhidden * silu_val).astype(bf16)
    gate_term = outer_sum(dgate, rows_all)
    up_term = outer_sum(dup, rows_all)
    down_term = outer_sum(hidden_all, grad_rows_all)
    gate_grad, up_grad, down_grad = (
        lax.psum_scatter(
            gate_term.astype(jnp.bfloat16), "ctx", scatter_dimension=0, tiled=True
        ).astype(jnp.float32),
        lax.psum_scatter(
            up_term.astype(jnp.bfloat16), "ctx", scatter_dimension=0, tiled=True
        ).astype(jnp.float32),
        lax.psum_scatter(
            down_term.astype(jnp.bfloat16), "ctx", scatter_dimension=0, tiled=True
        ).astype(jnp.float32),
    )
    dnormed_two = lax.psum_scatter(
        (
            jnp.dot(dgate, gate_local, preferred_element_type=f32)
            + jnp.dot(dup, up_local, preferred_element_type=f32)
        ).astype(jnp.bfloat16),
        "fsdp",
        scatter_dimension=0,
        tiled=True,
    ).astype(jnp.float32)
    gain_two_term = jnp.sum(dnormed_two * mid * scale_two, axis=0)
    scaled_two = gain_two * dnormed_two
    dmid = (
        dy
        + scale_two * scaled_two
        - mid * scale_two**3 * jnp.mean(scaled_two * mid, axis=-1, keepdims=True)
    )
    dmid_low = dmid.astype(bf16)
    out_term = jnp.einsum("td,te->de", attn_tokens, dmid_low, preferred_element_type=f32)
    dattn = jnp.einsum("te,de->td", dmid_low, out_full, preferred_element_type=f32).astype(bf16)
    dattn_heads = lax.all_to_all(dattn, "fsdp", split_axis=1, concat_axis=0, tiled=True)
    delta = jnp.sum((dattn_heads.astype(f32) * attn32).reshape(group_rows, heads_here, HD), axis=-1)
    delta_tiles = delta.reshape(2, blk, heads_here).transpose(0, 2, 1)
    grad_parts = dattn_heads.reshape(2, blk, heads_here, HD)

    def back_pass(carry, tile):
        keys, values, k_place = tile
        key_acc = jnp.zeros((blk, heads_here, HD), f32)
        value_acc = jnp.zeros((blk, heads_here, HD), f32)
        new_query = []
        for slot in range(2):

            def back_update(q_acc, k_acc, v_acc):
                masked = tile_scores(slot, keys, k_place)
                prob = jnp.exp(masked - log_total[slot][..., None])
                prob_low = prob.astype(bf16)
                dprob = jnp.einsum(
                    "qhd,khd->hqk", grad_parts[slot], values, preferred_element_type=f32
                )
                dscore = (prob * (dprob - delta_tiles[slot][..., None])).astype(bf16)
                q_acc = (
                    q_acc
                    + jnp.einsum("hqk,khd->qhd", dscore, keys, preferred_element_type=f32) * scale
                )
                k_acc = (
                    k_acc
                    + jnp.einsum(
                        "hqk,qhd->khd", dscore, query_parts[slot], preferred_element_type=f32
                    )
                    * scale
                )
                v_acc = v_acc + jnp.einsum(
                    "hqk,qhd->khd", prob_low, grad_parts[slot], preferred_element_type=f32
                )
                return (q_acc, k_acc, v_acc)

            def back_leave(q_acc, k_acc, v_acc):
                return (q_acc, k_acc, v_acc)

            q_acc, key_acc, value_acc = lax.cond(
                is_live(slot, k_place), back_update, back_leave, carry[slot], key_acc, value_acc
            )
            new_query.append(q_acc)
        return (jnp.stack(new_query), (key_acc, value_acc))

    dquery_start = jnp.zeros((2, blk, heads_here, HD), f32)
    dquery_acc, (dkey_tiles, dvalue_tiles) = lax.scan(
        back_pass, dquery_start, (key_tiles, value_tiles, key_place_tiles)
    )
    dkey_all = dkey_tiles.reshape(total, local_width)
    dvalue_all = dvalue_tiles.reshape(total, local_width)
    dkey_own, dvalue_own = (
        lax.psum_scatter(
            dkey_all.astype(jnp.bfloat16), "ctx", scatter_dimension=0, tiled=True
        ).astype(jnp.float32),
        lax.psum_scatter(
            dvalue_all.astype(jnp.bfloat16), "ctx", scatter_dimension=0, tiled=True
        ).astype(jnp.float32),
    )
    dquery_low = rotate(
        dquery_acc.reshape(group_rows, local_width), group_cos, -group_sin, HD
    ).astype(bf16)
    dkey_low = rotate(dkey_own, group_cos, -group_sin, HD).astype(bf16)
    dvalue_low = dvalue_own.astype(bf16)
    dquery_tok, dkey_tok, dvalue_tok = (
        lax.all_to_all(dquery_low, "fsdp", split_axis=0, concat_axis=1, tiled=True),
        lax.all_to_all(dkey_low, "fsdp", split_axis=0, concat_axis=1, tiled=True),
        lax.all_to_all(dvalue_low, "fsdp", split_axis=0, concat_axis=1, tiled=True),
    )
    dnormed_one = (
        jnp.einsum("te,de->td", dquery_tok, query_full, preferred_element_type=f32)
        + jnp.einsum("te,de->td", dkey_tok, key_full, preferred_element_type=f32)
        + jnp.einsum("te,de->td", dvalue_tok, value_full, preferred_element_type=f32)
    )
    query_term = jnp.einsum("td,te->de", normed_one, dquery_tok, preferred_element_type=f32)
    key_term = jnp.einsum("td,te->de", normed_one, dkey_tok, preferred_element_type=f32)
    value_term = jnp.einsum("td,te->de", normed_one, dvalue_tok, preferred_element_type=f32)
    gain_one_term = jnp.sum(dnormed_one * x32 * scale_one, axis=0)
    scaled_one = gain_one * dnormed_one
    input_grad = (
        dmid
        + scale_one * scaled_one
        - x32 * scale_one**3 * jnp.mean(scaled_one * x32, axis=-1, keepdims=True)
    )
    query_grad, key_grad, value_grad, out_grad, gain_attn_grad, gain_ffn_grad = (
        lax.psum_scatter(query_term, ("ctx", "fsdp"), scatter_dimension=0, tiled=True),
        lax.psum_scatter(key_term, ("ctx", "fsdp"), scatter_dimension=0, tiled=True),
        lax.psum_scatter(value_term, ("ctx", "fsdp"), scatter_dimension=0, tiled=True),
        lax.psum_scatter(out_term, ("ctx", "fsdp"), scatter_dimension=0, tiled=True),
        lax.psum_scatter(gain_one_term, ("ctx", "fsdp"), scatter_dimension=0, tiled=True),
        lax.psum_scatter(gain_two_term, ("ctx", "fsdp"), scatter_dimension=0, tiled=True),
    )
    return (
        block_out,
        input_grad,
        gain_attn_grad,
        query_grad,
        key_grad,
        value_grad,
        out_grad,
        gain_ffn_grad,
        gate_grad,
        up_grad,
        down_grad,
    )


def solution(mesh):
    placed = (
        P(("ctx", "fsdp"), None),
        P(),
        P(("ctx", "fsdp")),
        P(("ctx", "fsdp"), None),
        P(("ctx", "fsdp"), None),
        P(("ctx", "fsdp"), None),
        P(("ctx", "fsdp"), None),
        P(("ctx", "fsdp")),
        P(("ctx", "fsdp"), None),
        P(("ctx", "fsdp"), None),
        P(("ctx", "fsdp"), None),
        P(("ctx", "fsdp"), None),
    )
    return jax.shard_map(
        per_device,
        mesh=mesh,
        in_specs=placed,
        out_specs=(
            P(("ctx", "fsdp"), None),
            P(("ctx", "fsdp"), None),
            P(("ctx", "fsdp")),
            P(("ctx", "fsdp"), None),
            P(("ctx", "fsdp"), None),
            P(("ctx", "fsdp"), None),
            P(("ctx", "fsdp"), None),
            P(("ctx", "fsdp")),
            P(("ctx", "fsdp"), None),
            P(("ctx", "fsdp"), None),
            P(("ctx", "fsdp"), None),
        ),
        check_vma=False,
    )
```

profile of v0, /device:TPU:0, one launch (start us, length us, event | category | flops | bytes accessed | tf_op | source)
XLA Modules:
  0.0 2091.9 jit_solution(9848082827933812931)
XLA Ops:
  11.2 43.2 %all-reduce.5 = (bf16[2048]{0:T(1024)(128)(2,1)S(1)}, bf16[2048]{0:T(1024)(128)(2,1)S(1)}) all-reduce(bf16[2048]{0:T(1024)(128)(2,1)S(1)} %dynamic-update-slice, bf16[2048]{0:T(1024)(128)(2,1)S(1)} %dynamic-update-slice.1), channel_id=1, replica_groups=mesh['ctx'=4,'fsdp'=8] {'ctx','fsdp'}, use_global_device_ids=true, to_apply=%add | all-reduce | flops 4096 | bytes 16384
  57.1 34.1 %all-gather.12.cloned.1.call-done = bf16[2048,2048]{1,0:T(8,128)(2,1)} async-done(((bf16[64,2048]{1,0:T(8,128)(2,1)}), bf16[2048,2048]{1,0:T(8,128)(2,1)}) %all-gather.12.cloned.1.call-update) | async-done | bytes 8388624 | tf_op jit(solution)/shard_map/all_gather | solution.py:90
  91.2 7.0 fusion.132
  98.2 71.9 %all-gather.20.cloned.1.call-done = bf16[2048,2048]{1,0:T(8,128)(2,1)} async-done(((bf16[64,2048]{1,0:T(8,128)(2,1)}), bf16[2048,2048]{1,0:T(8,128)(2,1)}) %all-gather.20.cloned.1.call-update) | async-done | bytes 8388624 | tf_op jit(solution)/shard_map/all_gather | solution.py:89
  177.3 13.9 all_to_all.131
  192.4 60.1 %all-gather.16.cloned.1.call-done = bf16[2048,2048]{1,0:T(8,128)(2,1)} async-done(((bf16[64,2048]{1,0:T(8,128)(2,1)}), bf16[2048,2048]{1,0:T(8,128)(2,1)}) %all-gather.16.cloned.1.call-update) | async-done | bytes 8388624 | tf_op jit(solution)/shard_map/all_gather | solution.py:91
  257.2 12.8 all_to_all.132
  277.6 8.9 all-to-all-done.2
  287.2 11.8 all-gather.14.cloned.1.call-done
  299.0 7.1 reshape.584
  306.1 7.0 copy.88
  313.1 92.3 %while.39 = (s32[]{:T(128)}, f32[2,4,512]{2,1,0:T(4,128)S(1)}, f32[2,4,512]{2,1,0:T(4,128)S(1)}, s32[8,512]{1,0:T(8,128)S(1)}, s32[]{:T(128)}, /*index=5*/bf16[8...) while((s32[]{:T(128)}, f32[2,4,512]{2,1,0:T(4,128)S(1)}, ...), condition=%wide.region_16.17_spmd, body=%wide.region_6.16_spmd.sunk | while | flops 283656704 | bytes 20287788 | solution.py:164
  405.4 7.1 reshape.585
  412.5 7.0 copy.89
  419.6 69.9 %while.40 = (s32[]{:T(128)}, f32[2,512,4,64]{1,3,2,0:T(8,128)S(1)}, s32[8,512]{1,0:T(8,128)S(1)}, s32[]{:T(128)}, bf16[8,512,4,64]{1,3,2,0:T(8,128)(2,1)}, /*ind...) while((s32[]{:T(128)}, f32[2,512,4,64]{1,3,2,0:T(8,128)S(1)}, ...), condition=%wide.region_23.24_spmd, body=%wide.region_17.23_spmd.sunk | while | flops 546308608 | bytes 10031381 | solution.py:188
  495.2 9.7 all-to-all-done.3
  513.8 8.5 reduce-scatter.14.cloned.1.call-start
  522.3 23.1 %all-gather.24.cloned.1.call-done = bf16[1024,2048]{1,0:T(8,128)(2,1)} async-done(((bf16[128,2048]{1,0:T(8,128)(2,1)}), bf16[1024,2048]{1,0:T(8,128)(2,1)}) %all-gather.24.cloned.1.call-update) | async-done | bytes 4194320 | tf_op jit(solution)/shard_map/all_gather | solution.py:203
  545.4 9.9 fusion.137
  555.3 72.5 %all-gather.28.cloned.1.call-done = bf16[1024,2048]{1,0:T(8,128)(2,1)} async-done(((bf16[256,2048]{1,0:T(8,128)(2,1)}), bf16[1024,2048]{1,0:T(8,128)(2,1)}) %all-gather.28.cloned.1.call-update) | async-done | bytes 4194320 | tf_op jit(solution)/shard_map/all_gather | solution.py:200
  627.8 10.1 fusion.138
  637.9 70.7 %all-gather.30.cloned.1.call-done = bf16[1024,2048]{1,0:T(8,128)(2,1)} async-done(((bf16[256,2048]{1,0:T(8,128)(2,1)}), bf16[1024,2048]{1,0:T(8,128)(2,1)}) %all-gather.30.cloned.1.call-update) | async-done | bytes 4194320 | tf_op jit(solution)/shard_map/all_gather | solution.py:201
  708.5 37.2 %all-gather.32.cloned.1.call-done = bf16[1024,2048]{1,0:T(8,128)(2,1)} async-done(((bf16[128,2048]{1,0:T(8,128)(2,1)}), bf16[1024,2048]{1,0:T(8,128)(2,1)}) %all-gather.32.cloned.1.call-update) | async-done | bytes 4194320 | tf_op jit(solution)/shard_map/all_gather | solution.py:215
  745.7 13.3 multiply_convert_fusion.2
  765.9 8.3 add_convert_fusion
  774.3 9.4 convolution_convert_fusion.3
  783.7 42.0 %reduce-scatter.14.cloned.1.call-done = bf16[128,2048]{1,0:T(8,128)(2,1)} async-done(((bf16[1024,2048]{1,0:T(8,128)(2,1)}), bf16[128,2048]{1,0:T(8,128)(2,1)}) %reduce-scatter.14.cloned.1.call-update) | async-done | bytes 524304 | tf_op jit(solution)/shard_map/reduce_scatter | solution.py:234
  827.7 53.1 %reduce-scatter.12.cloned.1.call-done = bf16[128,2048]{1,0:T(8,128)(2,1)} async-done(((bf16[1024,2048]{1,0:T(8,128)(2,1)}), bf16[128,2048]{1,0:T(8,128)(2,1)}) %reduce-scatter.12.cloned.1.call-update) | async-done | bytes 524304 | tf_op jit(solution)/shard_map/reduce_scatter | solution.py:208
  894.8 9.6 all-to-all-done.4
  906.8 97.2 %while.41 = (s32[]{:T(128)}, f32[2,512,4,64]{1,3,2,0:T(8,128)S(1)}, bf16[8,512,4,64]{1,3,2,0:T(8,128)(2,1)}, bf16[8,512,4,64]{1,3,2,0:T(8,128)(2,1)}, s32[8,512]...) while((s32[]{:T(128)}, f32[2,512,4,64]{1,3,2,0:T(8,128)S(1)}, ...), condition=%wide.region_35.36_spmd, body=%wide.region_29.35_spmd.sunk | while | flops 1364984320 | bytes 59905492 | solution.py:299
  1014.3 9.5 convolution_convert_fusion.2
  1023.8 9.4 convolution_convert_fusion.1
  1033.5 9.4 convolution_convert_fusion
  1044.3 8.1 fusion.96
  1057.8 12.2 all_to_all.133
  1069.9 8.2 fusion.127
  1078.4 12.4 all_to_all.134
  1090.8 8.2 fusion.125
  1100.3 12.2 all_to_all.135
  1112.4 8.2 fusion.123
  1120.6 55.2 %reduce-scatter.28.cloned.1.call-done = bf16[256,2048]{1,0:T(8,128)(2,1)} async-done(((bf16[1024,2048]{1,0:T(8,128)(2,1)}), bf16[256,2048]{1,0:T(8,128)(2,1)}) %reduce-scatter.28.cloned.1.call-update) | async-done | bytes 1048592 | tf_op jit(solution)/shard_map/reduce_scatter | solution.py:224
  1178.6 76.8 %reduce-scatter.30.cloned.1.call-done = bf16[256,2048]{1,0:T(8,128)(2,1)} async-done(((bf16[1024,2048]{1,0:T(8,128)(2,1)}), bf16[256,2048]{1,0:T(8,128)(2,1)}) %reduce-scatter.30.cloned.1.call-update) | async-done | bytes 1048592 | tf_op jit(solution)/shard_map/reduce_scatter | solution.py:227
  1258.1 76.7 %reduce-scatter.32.cloned.1.call-done = bf16[256,2048]{1,0:T(8,128)(2,1)} async-done(((bf16[1024,2048]{1,0:T(8,128)(2,1)}), bf16[256,2048]{1,0:T(8,128)(2,1)}) %reduce-scatter.32.cloned.1.call-update) | async-done | bytes 1048592 | tf_op jit(solution)/shard_map/reduce_scatter | solution.py:230
  1354.6 44.6 %all-reduce.4 = (f32[2048]{0:T(1024)S(1)}, f32[2048]{0:T(1024)S(1)}) all-reduce(f32[2048]{0:T(1024)S(1)} %get-tuple-element.647, f32[2048]{0:T(1024)S(1)} %copy-done.17), channel_id=6, replica_groups=mesh['ctx'=4,'fsdp'=8] {'ctx','fsdp'}, use_global_device_ids=true, to_apply=%region_40.41.clone | all-reduce | flops 4096 | bytes 32768
  1402.9 119.6 %reduce-scatter.26.cloned.1.call-done = f32[64,2048]{1,0:T(8,128)} async-done(((f32[2048,2048]{1,0:T(8,128)}), f32[64,2048]{1,0:T(8,128)}) %reduce-scatter.26.cloned.1.call-update) | async-done | bytes 524304 | tf_op jit(solution)/shard_map/reduce_scatter | solution.py:341
  1522.5 187.2 %reduce-scatter.20.cloned.1.call-done = f32[64,2048]{1,0:T(8,128)} async-done(((f32[2048,2048]{1,0:T(8,128)}), f32[64,2048]{1,0:T(8,128)}) %reduce-scatter.20.cloned.1.call-update) | async-done | bytes 524304 | tf_op jit(solution)/shard_map/reduce_scatter | solution.py:338
  1709.7 187.5 %reduce-scatter.22.cloned.1.call-done = f32[64,2048]{1,0:T(8,128)} async-done(((f32[2048,2048]{1,0:T(8,128)}), f32[64,2048]{1,0:T(8,128)}) %reduce-scatter.22.cloned.1.call-update) | async-done | bytes 524304 | tf_op jit(solution)/shard_map/reduce_scatter | solution.py:339
  1897.2 187.5 %reduce-scatter.24.cloned.1.call-done = f32[64,2048]{1,0:T(8,128)} async-done(((f32[2048,2048]{1,0:T(8,128)}), f32[64,2048]{1,0:T(8,128)}) %reduce-scatter.24.cloned.1.call-update) | async-done | bytes 524304 | tf_op jit(solution)/shard_map/reduce_scatter | solution.py:340
  (564 shorter events, 423.8 us)
Async XLA Ops:
  7.2 84.0 %all-gather.12.cloned.1.call-start = ((), (), s32[]{:S(2)}) async-start(), calls=%async_computation.19 | async-start | bytes 8650752 | tf_op jit(solution)/shard_map/all_gather | solution.py:90
  7.9 162.2 %all-gather.20.cloned.1.call-start = ((), (), s32[]{:S(2)}) async-start(), calls=%async_computation.23 | async-start | bytes 8650752 | tf_op jit(solution)/shard_map/all_gather | solution.py:89
  8.7 243.8 %all-gather.16.cloned.1.call-start = ((), (), s32[]{:S(2)}) async-start(), calls=%async_computation.21 | async-start | bytes 8650752 | tf_op jit(solution)/shard_map/all_gather | solution.py:91
  9.4 289.6 %all-gather.14.cloned.1.call-start = ((), (), s32[]{:S(2)}) async-start(), calls=%async_computation.20 | async-start | bytes 2621440 | tf_op jit(solution)/shard_map/all_gather | solution.py:115
  54.4 198.1 %copy-start.9 = (f32[2048]{0:T(1024)}, f32[2048]{0:T(1024)S(1)}, u32[]{:S(2)}) copy-start(f32[2048]{0:T(1024)S(1)} %convert_element_type.174) | copy-start | bytes 24580
  54.4 43.8 %copy-start.18 = (f32[32]{0:T(128)}, f32[32]{0:T(128)S(1)}, u32[]{:S(2)}) copy-start(f32[32]{0:T(128)S(1)} %multiply_exponential_fusion) | copy-start | bytes 388
  56.9 195.6 %copy-start.13 = (f32[128]{0:T(128)}, f32[128]{0:T(128)S(1)}, u32[]{:S(2)}) copy-start(f32[128]{0:T(128)S(1)} %get-tuple-element.771) | copy-start | bytes 1540
  91.2 78.9 %copy-start = (bf16[128,2048]{1,0:T(8,128)(2,1)S(1)}, bf16[128,2048]{1,0:T(8,128)(2,1)}, u32[]{:S(2)}) copy-start(bf16[128,2048]{1,0:T(8,128)(2,1)} %param.30) | copy-start | bytes 1572868
  192.3 79.1 %copy-start.20 = (s32[4]{0:T(128)S(1)}, s32[4]{0:T(128)}, u32[]{:S(2)}) copy-start(s32[4]{0:T(128)} %param.31) | copy-start | bytes 52
  192.3 213.1 %all-gather.18.cloned.1.call-start = ((), (), s32[]{:S(2)}) async-start(), calls=%async_computation.22 | async-start | bytes 2621440 | tf_op jit(solution)/shard_map/all_gather | solution.py:116
  270.0 225.1 %all-gather.22.cloned.1.call-start = ((), (), s32[]{:S(2)}) async-start(), calls=%async_computation.24 | async-start | bytes 8650752 | tf_op jit(solution)/shard_map/all_gather | solution.py:92
  270.6 251.7 %all-gather.26.cloned.1.call-start = ((), (), s32[]{:S(2)}) async-start(), calls=%async_computation.26 | async-start | bytes 5242880 | tf_op jit(solution)/shard_map/all_gather | solution.py:199
  273.1 13.4 all-to-all-start.2
  491.3 13.5 all-to-all-start.3
  495.1 50.4 %all-gather.24.cloned.1.call-start = ((), (), s32[]{:S(2)}) async-start(), calls=%async_computation.25 | async-start | bytes 4718592 | tf_op jit(solution)/shard_map/all_gather | solution.py:203
  504.8 4.9 copy-start.6
  511.7 116.1 %all-gather.28.cloned.1.call-start = ((), (), s32[]{:S(2)}) async-start(), calls=%async_computation.27 | async-start | bytes 5242880 | tf_op jit(solution)/shard_map/all_gather | solution.py:200
  512.4 196.1 %all-gather.30.cloned.1.call-start = ((), (), s32[]{:S(2)}) async-start(), calls=%async_computation.28 | async-start | bytes 5242880 | tf_op jit(solution)/shard_map/all_gather | solution.py:201
  513.0 232.7 %all-gather.32.cloned.1.call-start = ((), (), s32[]{:S(2)}) async-start(), calls=%async_computation.30 | async-start | bytes 4718592 | tf_op jit(solution)/shard_map/all_gather | solution.py:215
  513.8 312.0 %reduce-scatter.14.cloned.1.call-start = ((), (), s32[]{:S(2)}) async-start(), calls=%async_computation.31 | async-start | bytes 4718592 | tf_op jit(solution)/shard_map/reduce_scatter | solution.py:234
  745.7 13.3 copy-start.22
  759.0 6.9 copy-start.25
  759.0 6.9 copy-start.24
  759.0 6.9 copy-start.23
  774.2 106.6 %reduce-scatter.12.cloned.1.call-start = ((), (), s32[]{:S(2)}) async-start(), calls=%async_computation.29 | async-start | bytes 4718592 | tf_op jit(solution)/shard_map/reduce_scatter | solution.py:208
  783.7 42.1 %copy-start.5 = (f32[128,2048]{1,0:T(8,128)S(1)}, f32[128,2048]{1,0:T(8,128)}, u32[]{:S(2)}) copy-start(f32[128,2048]{1,0:T(8,128)} %copy-done.4) | copy-start | bytes 3145732
  783.7 97.2 %copy-start.8 = (bf16[128,2048]{1,0:T(8,128)(2,1)S(1)}, bf16[128,2048]{1,0:T(8,128)(2,1)}, u32[]{:S(2)}) copy-start(bf16[128,2048]{1,0:T(8,128)(2,1)} %param.41) | copy-start | bytes 1572868
  883.5 6.7 copy-start.2
  891.2 13.2 all-to-all-start.4
  894.7 160.0 %reduce-scatter.16.cloned.1.call-start = ((), (), s32[]{:S(2)}) async-start(), calls=%async_computation.32 | async-start | bytes 2621440 | tf_op jit(solution)/shard_map/reduce_scatter | solution.py:305
  910.3 1.0 copy-start.11
  1009.0 90.1 %reduce-scatter.18.cloned.1.call-start = ((), (), s32[]{:S(2)}) async-start(), calls=%async_computation.33 | async-start | bytes 2621440 | tf_op jit(solution)/shard_map/reduce_scatter | solution.py:308
  1014.0 161.8 %reduce-scatter.28.cloned.1.call-start = ((), (), s32[]{:S(2)}) async-start(), calls=%async_computation.38 | async-start | bytes 5242880 | tf_op jit(solution)/shard_map/reduce_scatter | solution.py:224
  1023.8 231.6 %reduce-scatter.30.cloned.1.call-start = ((), (), s32[]{:S(2)}) async-start(), calls=%async_computation.39 | async-start | bytes 5242880 | tf_op jit(solution)/shard_map/reduce_scatter | solution.py:227
  1033.2 301.5 %reduce-scatter.32.cloned.1.call-start = ((), (), s32[]{:S(2)}) async-start(), calls=%async_computation.40 | async-start | bytes 5242880 | tf_op jit(solution)/shard_map/reduce_scatter | solution.py:230
  1042.9 1.2 copy-start.3
  1042.9 1.4 copy-start.7
  1043.0 479.5 %reduce-scatter.26.cloned.1.call-start = ((), (), s32[]{:S(2)}) async-start(), calls=%async_computation.37 | async-start | bytes 17301504 | tf_op jit(solution)/shard_map/reduce_scatter | solution.py:341
  1052.4 657.3 %reduce-scatter.20.cloned.1.call-start = ((), (), s32[]{:S(2)}) async-start(), calls=%async_computation.34 | async-start | bytes 17301504 | tf_op jit(solution)/shard_map/reduce_scatter | solution.py:338
  1055.9 14.1 copy-start.1
  1055.9 14.0 copy-start.10
  1055.9 14.0 copy-start.14
  1078.2 819.0 %reduce-scatter.22.cloned.1.call-start = ((), (), s32[]{:S(2)}) async-start(), calls=%async_computation.35 | async-start | bytes 17301504 | tf_op jit(solution)/shard_map/reduce_scatter | solution.py:339
  1099.1 985.6 %reduce-scatter.24.cloned.1.call-start = ((), (), s32[]{:S(2)}) async-start(), calls=%async_computation.36 | async-start | bytes 17301504 | tf_op jit(solution)/shard_map/reduce_scatter | solution.py:340
  1337.6 13.0 slice-start
  1344.0 6.5 slice-start.1
  1350.6 4.0 copy-start.17
  1350.6 49.8 %copy-start.21 = (f32[128]{0:T(128)S(1)}, f32[128]{0:T(128)}, u32[]{:S(2)}) copy-start(f32[128]{0:T(128)} %get-tuple-element.770) | copy-start | bytes 1540
  (12 other events, 11.3 us)
Sparse Core Ops, SparseCore 0:
  10.9 80.2 all-gather.11
  94.0 76.0 all-gather.19
  173.0 79.4 all-gather.15
  254.5 44.4 all-gather.13
  300.4 44.6 all-gather.17
  347.8 76.1 all-gather.21
  425.6 79.3 all-gather.25
  511.8 33.5 all-gather.23
  547.0 80.7 all-gather.27
  629.2 79.2 all-gather.29
  710.4 35.2 all-gather.31
  774.4 51.3 reduce-scatter.13
  829.5 51.3 reduce-scatter.11
  1009.1 42.3 reduce-scatter.15
  1054.3 43.1 reduce-scatter.17
  1099.7 76.0 reduce-scatter.27
  1178.0 77.2 reduce-scatter.29
  1257.5 77.2 reduce-scatter.31
  1337.8 184.6 reduce-scatter.25
  1525.3 184.3 reduce-scatter.19
  1712.7 184.4 reduce-scatter.21
  1900.1 184.4 reduce-scatter.23
where the time goes:
time: 2110 us; the launch traced here: 2090 us
  waiting for transfers between devices  1400 us (66%)
  matrix products  245 us (12%)
  blocking collectives  151 us (7%)
  local copies, waits for them, and re-layouts  114 us (5%)
  other arithmetic  80.6 us (4%)
  loops' own time  64.6 us (3%)
    reduce_scatter x1, waiting for transfers between devices, per_device(): lax.psum_scatter(key_term, ('ctx', 'fsdp'), scatter_dimension=0, tiled=True)  187 us
    reduce_scatter x1, waiting for transfers between devices, per_device(): lax.psum_scatter(value_term, ('ctx', 'fsdp'), scatter_dimension=0, tiled=...  187 us
    reduce_scatter x1, waiting for transfers between devices, per_device(): lax.psum_scatter(query_term, ('ctx', 'fsdp'), scatter_dimension=0, tiled=...  187 us
    reduce_scatter x1, waiting for transfers between devices, per_device(): lax.psum_scatter(out_term, ('ctx', 'fsdp'), scatter_dimension=0, tiled=True)  120 us
    unnamed x2, blocking collectives  87.8 us
    reduce_scatter x1, waiting for transfers between devices, per_device(): lax.psum_scatter(up_term.astype(jnp.bfloat16), 'ctx', scatter_dimension=0...  76.8 us
    reduce_scatter x1, waiting for transfers between devices, per_device(): lax.psum_scatter(down_term.astype(jnp.bfloat16), 'ctx', scatter_dimension...  76.7 us
    all_gather x1, waiting for transfers between devices, per_device(): lax.all_gather(w_up, 'ctx', axis=0, tiled=True)  72.5 us
  transfers between devices with their start and end apart: 25, of which 20 were waited for; matrix products, arithmetic and copies ran while one was open for 15% of the time, Pallas kernels for 0%

commit v1 on v0

--- a/solution.py
+++ b/solution.py
@@ -1,8 +1,13 @@
+import functools
 import math
 
 import jax
 import jax.numpy as jnp
+import numpy as np
 from jax import lax
+from jax.experimental import pallas as pl
+from jax.experimental.pallas import tpu as pltpu
+from jax.sharding import Mesh
 from jax.sharding import PartitionSpec as P
 
 HD = 64
@@ -54,7 +59,7 @@
     return jnp.einsum("tf,td->fd", left, right, preferred_element_type=jnp.float32)
 
 
-def per_device(
+def per_device_any(
     tokens,
     pair_index,
     gain_attn,
@@ -357,37 +362,448 @@
     )
 
 
+BF16 = jnp.bfloat16
+F32 = jnp.float32
+LOG2E = math.log2(math.e)
+VMEM = pl.BlockSpec(memory_space=pltpu.VMEM)
+
+
+def mxu(a, b):
+    return jnp.dot(a, b, preferred_element_type=F32)
+
+
+def causal(blk):
+    row = lax.broadcasted_iota(jnp.int32, (blk, blk), 0)
+    col = lax.broadcasted_iota(jnp.int32, (blk, blk), 1)
+    return row <= col
+
+
+def attn_fwd_kernel(
+    slot_ref, qkv_ref, out_ref, o32_ref, lse_ref, seq_ref, k_scr, m_scr, l_scr, acc_scr, *, blocks, width
+):
+    pieces = qkv_ref.shape[0]
+    blk = pieces * width
+    coef = LOG2E * HD**-0.5
+    for s in range(blocks):
+        at = pl.multiple_of(slot_ref[s] * width, width)
+        for j in range(pieces):
+            lo = s * blk + j * width
+            piece = qkv_ref[j, :, pl.ds(at, width)]
+            seq_ref[:, lo : lo + width] = piece
+            k_scr[lo : lo + width, :] = piece[HD : 2 * HD].T
+
+    def tile(kb, q_t, masked):
+        at = pl.multiple_of(kb * blk, blk)
+        score = mxu(k_scr[pl.ds(at, blk), :], q_t) * coef
+        if masked:
+            score = jnp.where(causal(blk), score, -1e30)
+        old = m_scr[...]
+        new = jnp.maximum(old, jnp.max(score, axis=0, keepdims=True))
+        p = jnp.exp2(score - new)
+        fade = jnp.exp2(old - new)
+        m_scr[...] = new
+        l_scr[...] = l_scr[...] * fade + jnp.sum(p, axis=0, keepdims=True)
+        acc_scr[...] = acc_scr[...] * fade + mxu(seq_ref[2 * HD :, pl.ds(at, blk)], p.astype(BF16))
+
+    for qb in range(blocks):
+        lo = qb * blk
+        q_t = seq_ref[:HD, lo : lo + blk]
+        m_scr[...] = jnp.full_like(m_scr, -1e30)
+        l_scr[...] = jnp.zeros_like(l_scr)
+        acc_scr[...] = jnp.zeros_like(acc_scr)
+        tile(qb, q_t, True)
+        if qb > 0:
+
+            @pl.loop(0, qb)
+            def _(kb):
+                tile(kb, q_t, False)
+
+        o = acc_scr[...] / l_scr[...]
+        o32_ref[:, lo : lo + blk] = o
+        lse_ref[:, lo : lo + blk] = m_scr[...] + jnp.log2(l_scr[...])
+        at = pl.multiple_of(slot_ref[qb] * width, width)
+        low = o.astype(BF16)
+        for j in range(pieces):
+            out_ref[j, :, pl.ds(at, width)] = low[:, j * width : (j + 1) * width]
+
+
+def attn_fwd(slot, qkv, blocks):
+    pieces, _, cols = qkv.shape
+    total = pieces * cols
+    blk = total // blocks
+    return pl.pallas_call(
+        functools.partial(attn_fwd_kernel, blocks=blocks, width=cols // blocks),
+        out_shape=(
+            jax.ShapeDtypeStruct((pieces, HD, cols), BF16),
+            jax.ShapeDtypeStruct((HD, total), F32),
+            jax.ShapeDtypeStruct((1, total), F32),
+            jax.ShapeDtypeStruct((3 * HD, total), BF16),
+        ),
+        in_specs=[pl.BlockSpec(memory_space=pltpu.SMEM), VMEM],
+        out_specs=(VMEM,) * 4,
+        scratch_shapes=[
+            pltpu.VMEM((total, HD), BF16),
+            pltpu.VMEM((1, blk), F32),
+            pltpu.VMEM((1, blk), F32),
+            pltpu.VMEM((HD, blk), F32),
+        ],
+        compiler_params=pltpu.CompilerParams(vmem_limit_bytes=40 << 20),
+        cost_estimate=pl.CostEstimate(
+            flops=8 * total * total * HD, bytes_accessed=8 << 20, transcendentals=total * total // 2
+        ),
+        name="attn_fwd",
+    )(slot, qkv)
+
+
+def attn_bwd_kernel(
+    slot_ref,
+    seq_ref,
+    o32_ref,
+    lse_ref,
+    do_ref,
+    cos_ref,
+    sin_ref,
+    out_ref,
+    q_scr,
+    k_scr,
+    v_scr,
+    do_scr,
+    dot_scr,
+    delta_scr,
+    dq_scr,
+    dk_scr,
+    dv_scr,
+    *,
+    blocks,
+    width,
+):
+    pieces = do_ref.shape[0]
+    blk = pieces * width
+    scale = HD**-0.5
+    coef = LOG2E * scale
+    half = HD // 2
+    for s in range(blocks):
+        at = pl.multiple_of(slot_ref[s] * width, width)
+        for j in range(pieces):
+            lo = s * blk + j * width
+            piece = do_ref[j, :, pl.ds(at, width)]
+            dot_scr[:, lo : lo + width] = piece
+            do_scr[lo : lo + width, :] = piece.T
+            delta_scr[:, lo : lo + width] = jnp.sum(
+                piece.astype(F32) * o32_ref[:, lo : lo + width], axis=0, keepdims=True
+            )
+            q_scr[lo : lo + width, :] = seq_ref[:HD, lo : lo + width].T
+            k_scr[lo : lo + width, :] = seq_ref[HD : 2 * HD, lo : lo + width].T
+            v_scr[lo : lo + width, :] = seq_ref[2 * HD :, lo : lo + width].T
+    dq_scr[...] = jnp.zeros_like(dq_scr)
+
+    def turn_back(v, s):
+        c = cos_ref[:, s * blk : (s + 1) * blk]
+        n = sin_ref[:, s * blk : (s + 1) * blk]
+        a, b = v[:half], v[half:]
+        return jnp.concatenate([a * c + b * n, b * c - a * n], axis=0).astype(BF16)
+
+    def put(v, s, row):
+        at = pl.multiple_of(slot_ref[s] * width, width)
+        for j in range(pieces):
+            out_ref[j, row * HD : (row + 1) * HD, pl.ds(at, width)] = v[:, j * width : (j + 1) * width]
+
+    for kb in range(blocks):
+        lo = kb * blk
+        k = k_scr[lo : lo + blk, :]
+        v = v_scr[lo : lo + blk, :]
+        k_t = seq_ref[HD : 2 * HD, lo : lo + blk]
+
+        def tile(qb, masked):
+            here = pl.ds(pl.multiple_of(qb * blk, blk), blk)
+            p = jnp.exp2(mxu(k, seq_ref[:HD, here]) * coef - lse_ref[:, here])
+            if masked:
+                p = jnp.where(causal(blk), p, 0.0)
+            dp = mxu(v, dot_scr[:, here])
+            ds = (p * (dp - delta_scr[:, here])).astype(BF16)
+            dq_scr[:, here] += mxu(k_t, ds)
+            return mxu(ds, q_scr[here, :]), mxu(p.astype(BF16), do_scr[here, :])
+
+        dk_scr[...], dv_scr[...] = tile(kb, True)
+        if kb < blocks - 1:
+
+            @pl.loop(kb + 1, blocks)
+            def _(qb):
+                dk, dv = tile(qb, False)
+                dk_scr[...] += dk
+                dv_scr[...] += dv
+
+        put(turn_back(dq_scr[:, lo : lo + blk] * scale, kb), kb, 0)
+        put(turn_back((dk_scr[...] * scale).T, kb), kb, 1)
+        put(dv_scr[...].T.astype(BF16), kb, 2)
+
+
+def attn_bwd(slot, seq, o32, lse, do, cos, sin, blocks):
+    pieces, _, cols = do.shape
+    total = pieces * cols
+    blk = total // blocks
+    return pl.pallas_call(
+        functools.partial(attn_bwd_kernel, blocks=blocks, width=cols // blocks),
+        out_shape=jax.ShapeDtypeStruct((pieces, 3 * HD, cols), BF16),
+        in_specs=[pl.BlockSpec(memory_space=pltpu.SMEM)] + [VMEM] * 6,
+        out_specs=VMEM,
+        scratch_shapes=[pltpu.VMEM((total, HD), BF16)] * 4
+        + [
+            pltpu.VMEM((HD, total), BF16),
+            pltpu.VMEM((1, total), F32),
+            pltpu.VMEM((HD, total), F32),
+            pltpu.VMEM((blk, HD), F32),
+            pltpu.VMEM((blk, HD), F32),
+        ],
+        compiler_params=pltpu.CompilerParams(vmem_limit_bytes=48 << 20),
+        cost_estimate=pl.CostEstimate(
+            flops=20 * total * total * HD, bytes_accessed=8 << 20, transcendentals=total * total // 2
+        ),
+        name="attn_bwd",
+    )(slot, seq, o32, lse, do, cos, sin)
+
+
+FAR = ("ctx", "row")
+NEAR = ("col", "core")
+
+
+def swap(v, axis):
+    return lax.ppermute(v, axis, [(0, 1), (1, 0)])
+
+
+def shift(v, by):
+    n = lax.axis_size("ctx")
+    return lax.ppermute(v, "ctx", [(i, (i + by) % n) for i in range(n)])
+
+
+def spread(v):
+    parts = [v]
+    for _ in range(lax.axis_size("ctx") - 1):
+        parts.append(shift(parts[-1], 1))
+    return jnp.concatenate(parts + [swap(p, "row") for p in parts], axis=0)
+
+
+def collect(terms, tok):
+    n = lax.axis_size("ctx")
+    other = terms(1).astype(BF16).reshape(n, tok, -1)
+    crossed = [swap(other[c], "row") for c in reversed(range(n))][::-1]
+    own = terms(0).reshape(n, tok, -1)
+    total = None
+    for c in reversed(range(n)):
+        part = own[c] + crossed[c].astype(F32)
+        if total is not None:
+            part = part + shift(total.astype(BF16), -1).astype(F32)
+        total = part
+    return total
+
+
+def by_side(index, mine, theirs):
+    return jnp.where(index == 0, mine, theirs), jnp.where(index == 0, theirs, mine)
+
+
+def per_device_split(
+    tokens,
+    pair_index,
+    gain_attn,
+    w_query,
+    w_key,
+    w_value,
+    w_out,
+    gain_ffn,
+    w_gate,
+    w_up,
+    w_down,
+    cotangent,
+):
+    n_ctx = lax.axis_size("ctx")
+    near = lax.axis_size("col") * lax.axis_size("core")
+    far = 2 * n_ctx
+    tok, width = tokens.shape
+    own_in = w_query.shape[0]
+    ctx_at, row_at, col_at, core_at = (lax.axis_index(a) for a in ("ctx", "row", "col", "core"))
+    near_at = col_at * lax.axis_size("core") + core_at
+    blk = near * tok
+    rows_here = far * tok
+    group = near * HD
+
+    slots = jnp.arange(far, dtype=jnp.int32)
+    slot_ctx = (ctx_at - slots % n_ctx + n_ctx) % n_ctx
+    slot_row = row_at ^ (slots // n_ctx)
+    pair = jnp.sum(
+        jnp.where(
+            slot_ctx[:, None] == jnp.arange(n_ctx, dtype=jnp.int32)[None, :], pair_index[None, :], 0
+        ),
+        axis=1,
+    )
+    slot_block = jnp.where(slot_row == 0, pair, far - 1 - pair)
+    block_slot = jnp.sum(jnp.where(slot_block[None, :] == slots[:, None], slots[None, :], 0), axis=1)
+    freq = jnp.exp(jnp.arange(HD // 2, dtype=F32) * (-2.0 * math.log(THETA) / HD))
+    places = (
+        slot_block[:, None] * blk + near_at * tok + jnp.arange(tok, dtype=jnp.int32)[None, :]
+    ).reshape(rows_here)
+    angle = freq[:, None] * places.astype(F32)[None, :]
+    cosine, sine = jnp.cos(angle), jnp.sin(angle)
+    seq_angle = freq[:, None] * jnp.arange(far * blk, dtype=jnp.int32).astype(F32)[None, :]
+    seq_cos, seq_sin = jnp.cos(seq_angle), jnp.sin(seq_angle)
+
+    gain_one = gain_attn.astype(F32)[:, None]
+    send = jnp.concatenate(
+        [
+            (w.astype(F32) * gain_one).astype(BF16).reshape(own_in, far, group)
+            for w in (w_query, w_key, w_value)
+        ]
+        + [jnp.broadcast_to(gain_ffn[:, None, None], (own_in, far, 128))],
+        axis=2,
+    ).transpose(1, 0, 2)
+    x32 = tokens.astype(F32)
+    scale_one = lax.rsqrt(jnp.mean(x32 * x32, axis=-1, keepdims=True) + EPS)
+    rows_one = spread((x32 * scale_one).astype(BF16))
+    mine = lax.all_to_all(send, FAR, split_axis=0, concat_axis=0, tiled=True)
+    other = swap(mine, "col")
+    mine_pair = by_side(core_at, mine, swap(mine, "core"))
+    other_pair = by_side(core_at, other, swap(other, "core"))
+    halves = [by_side(col_at, a, b) for a, b in zip(mine_pair, other_pair, strict=True)]
+    w_ext = jnp.stack(
+        [halves[0][0], halves[1][0], halves[0][1], halves[1][1]], axis=1
+    ).reshape(width, 3 * group + 128)
+    w_heads = w_ext[:, : 3 * group]
+    gain_two = w_ext[:, 3 * group].astype(F32)[None, :]
+
+    out_rows = lax.all_gather(w_out, NEAR, axis=0, tiled=True)
+    gate_w, up_w, down_w = (
+        lax.all_gather(w, NEAR, axis=0, tiled=True) for w in (w_gate, w_up, w_down)
+    )
+
+    half = HD // 2
+    flat = jnp.einsum("de,td->et", w_heads, rows_one, preferred_element_type=F32)
+    qkv = flat.reshape(3, near, 2, half, rows_here)
+    first, second = qkv[:2, :, 0], qkv[:2, :, 1]
+    turned = jnp.stack([first * cosine - second * sine, second * cosine + first * sine], axis=2)
+    qkv = jnp.concatenate([turned, qkv[2:]], axis=0).astype(BF16)
+    qkv = qkv.transpose(1, 0, 2, 3, 4).reshape(near, 3 * HD, rows_here)
+    qkv_head = lax.all_to_all(qkv, NEAR, split_axis=0, concat_axis=0, tiled=True)
+    attn_head, o32, lse, seq = attn_fwd(block_slot, qkv_head, far)
+    attn = lax.all_to_all(attn_head, NEAR, split_axis=0, concat_axis=0, tiled=True)
+    attn = attn.reshape(group, rows_here)
+    rows_half = rows_here // 2
+
+    def cut(v, r, axis):
+        return lax.slice_in_dim(v, r * rows_half, (r + 1) * rows_half, axis=axis)
+
+    mid = x32 + collect(
+        lambda r: jnp.einsum("et,ed->td", cut(attn, r, 1), out_rows, preferred_element_type=F32), tok
+    )
+    scale_two = lax.rsqrt(jnp.mean(mid * mid, axis=-1, keepdims=True) + EPS)
+    normed_two = (mid * scale_two * gain_two).astype(BF16)
+    rows_two = spread(normed_two)
+    dy_rows = spread(cotangent)
+    gate = rows_by(rows_two, gate_w)
+    up = rows_by(rows_two, up_w)
+    silu_val, slope = silu_parts(gate)
+    hidden = (silu_val * up).astype(BF16)
+    dhidden = rows_by(dy_rows, down_w)
+    dgate = (dhidden * up * slope).astype(BF16)
+    dup = (dhidden * silu_val).astype(BF16)
+    dnormed_two = collect(
+        lambda r: jnp.dot(cut(dgate, r, 0), gate_w, preferred_element_type=F32)
+        + jnp.dot(cut(dup, r, 0), up_w, preferred_element_type=F32),
+        tok,
+    )
+    branch = collect(
+        lambda r: jnp.dot(cut(hidden, r, 0), down_w, preferred_element_type=F32), tok
+    )
+    block_out = (mid + branch).astype(BF16)
+    gate_grad, up_grad, down_grad = (
+        lax.psum_scatter(
+            outer_sum(left, right).astype(BF16), NEAR, scatter_dimension=0, tiled=True
+        ).astype(F32)
+        for left, right in ((dgate, rows_two), (dup, rows_two), (hidden, dy_rows))
+    )
+    dy = cotangent.astype(F32)
+    gain_two_term = jnp.sum(dnormed_two * mid * scale_two, axis=0)
+    scaled_two = gain_two * dnormed_two
+    dmid = (
+        dy
+        + scale_two * scaled_two
+        - mid * scale_two**3 * jnp.mean(scaled_two * mid, axis=-1, keepdims=True)
+    )
+    dmid_rows = spread(dmid.astype(BF16))
+    dattn = jnp.einsum("ed,td->et", out_rows, dmid_rows, preferred_element_type=F32).astype(BF16)
+    dattn_head = lax.all_to_all(
+        dattn.reshape(near, HD, rows_here), NEAR, split_axis=0, concat_axis=0, tiled=True
+    )
+    out_grad = lax.psum_scatter(
+        jnp.einsum("et,td->ed", attn, dmid_rows, preferred_element_type=F32).astype(BF16),
+        NEAR,
+        scatter_dimension=0,
+        tiled=True,
+    ).astype(F32)
+    dqkv_head = attn_bwd(block_slot, seq, o32, lse, dattn_head, seq_cos, seq_sin, far)
+    dqkv = lax.all_to_all(dqkv_head, NEAR, split_axis=0, concat_axis=0, tiled=True)
+    dqkv = dqkv.reshape(near, 3, HD, rows_here).transpose(1, 0, 2, 3).reshape(3 * group, rows_here)
+    scaled_one = collect(
+        lambda r: jnp.einsum("et,de->td", cut(dqkv, r, 1), w_heads, preferred_element_type=F32), tok
+    )
+    input_grad = (
+        dmid
+        + scale_one * scaled_one
+        - x32 * scale_one**3 * jnp.mean(scaled_one * x32, axis=-1, keepdims=True)
+    )
+    heads_grad = jnp.concatenate(
+        [
+            jnp.einsum("td,et->de", rows_one, dqkv, preferred_element_type=F32),
+            jnp.broadcast_to(gain_two_term[:, None], (width, 128)),
+        ],
+        axis=1,
+    ).astype(BF16)
+    heads_grad = lax.psum_scatter(
+        heads_grad.reshape(far, near * own_in, 3 * group + 128),
+        NEAR,
+        scatter_dimension=1,
+        tiled=True,
+    )
+    back = lax.all_to_all(heads_grad, FAR, split_axis=0, concat_axis=0, tiled=True).astype(F32)
+    raw = [
+        back[:, :, i * group : (i + 1) * group].transpose(1, 0, 2).reshape(own_in, -1)
+        for i in range(3)
+    ]
+    gain_attn_grad = sum(
+        jnp.sum(w.astype(F32) * g, axis=1)
+        for w, g in zip((w_query, w_key, w_value), raw, strict=True)
+    )
+    query_grad, key_grad, value_grad = (g * gain_one for g in raw)
+    gain_ffn_grad = jnp.sum(back[:, :, 3 * group], axis=0)
+    return (
+        block_out,
+        input_grad,
+        gain_attn_grad,
+        query_grad,
+        key_grad,
+        value_grad,
+        out_grad,
+        gain_ffn_grad,
+        gate_grad,
+        up_grad,
+        down_grad,
+    )
+
+
 def solution(mesh):
-    placed = (
-        P(("ctx", "fsdp"), None),
-        P(),
-        P(("ctx", "fsdp")),
-        P(("ctx", "fsdp"), None),
-        P(("ctx", "fsdp"), None),
-        P(("ctx", "fsdp"), None),
-        P(("ctx", "fsdp"), None),
-        P(("ctx", "fsdp")),
-        P(("ctx", "fsdp"), None),
-        P(("ctx", "fsdp"), None),
-        P(("ctx", "fsdp"), None),
-        P(("ctx", "fsdp"), None),
-    )
-    return jax.shard_map(
-        per_device,
-        mesh=mesh,
-        in_specs=placed,
-        out_specs=(
-            P(("ctx", "fsdp"), None),
-            P(("ctx", "fsdp"), None),
-            P(("ctx", "fsdp")),
-            P(("ctx", "fsdp"), None),
-            P(("ctx", "fsdp"), None),
-            P(("ctx", "fsdp"), None),
-            P(("ctx", "fsdp"), None),
-            P(("ctx", "fsdp")),
-            P(("ctx", "fsdp"), None),
-            P(("ctx", "fsdp"), None),
-            P(("ctx", "fsdp"), None),
-        ),
-        check_vma=False,
-    )
+    n_ctx, n_fsdp = mesh.shape["ctx"], mesh.shape["fsdp"]
+
+    def step(*args):
+        if n_fsdp == 8 and n_ctx * n_fsdp * HD == args[3].shape[1]:
+            body, axes = per_device_split, FAR + NEAR
+            over = Mesh(np.asarray(mesh.devices).reshape(n_ctx, 2, 2, 2), axes)
+        else:
+            body, axes, over = per_device_any, ("ctx", "fsdp"), mesh
+        rows, line = P(axes, None), P(axes)
+        return jax.shard_map(
+            body,
+            mesh=over,
+            in_specs=(rows, P(), line, rows, rows, rows, rows, line, rows, rows, rows, rows),
+            out_specs=(rows, rows, line, rows, rows, rows, rows, line, rows, rows, rows),
+            check_vma=False,
+        )(*args)
+
+    return step

time: 2110 us -> 828 us (0.39)
  waiting for transfers between devices: 1400 us -> 447 us
  blocking collectives: 151 us -> 0 us
  matrix products: 245 us -> 99.6 us
  starting transfers between devices: 20.7 us -> 123 us
  local copies, waits for them, and re-layouts: 114 us -> 36.6 us
  loops' own time: 64.6 us -> 0 us
  Pallas kernels: 0 us -> 58.1 us
  other arithmetic: 80.6 us -> 42.2 us
    reduce_scatter x11 -> x5, waiting for transfers between devices: 985 us -> 95.4 us  [the longest x3 95.4 us: per_device_split(): lax.psum_scatter(outer_sum(left, right).astype(BF16), NEAR, scatter_dimen...]
    all_gather x11 -> x4, waiting for transfers between devices: 381 us -> 0.02 us  [the longest x1 0.02 us: per_device_split(): out_rows = lax.all_gather(w_out, NEAR, axis=0, tiled=True)]
    ppermute x0 -> x59, waiting for transfers between devices: none -> 294 us  [the longest x24 154 us: shift(): return lax.ppermute(v, 'ctx', [(i, (i + by) % n) for i in range(n)])]
    dot_general x78 -> x14, matrix products: 183 us -> 38.4 us  [the longest x1 5.69 us: per_device_split(): jnp.einsum('td,et->de', rows_one, dqkv, preferred_element_type=F32)]
    ppermute x0 -> x59, starting transfers between devices: none -> 96.7 us  [the longest x24 55.6 us: shift(): return lax.ppermute(v, 'ctx', [(i, (i + by) % n) for i in range(n)])]
    unnamed x2 -> x0, blocking collectives: 87.8 us -> none
    another operation x51 -> x0, loops' own time: 64.6 us -> none  [the longest x1 21.4 us: per_device(): lax.scan(back_pass, dquery_start, (key_tiles, value_tiles, key_place_tiles))]
    all_to_all x5 -> x0, blocking collectives: 63.5 us -> none  [the longest x1 13.9 us: per_device(): lax.all_to_all(key, 'fsdp', split_axis=1, concat_axis=0, tiled=True)]
  transfers between devices with their start and end apart: 25 -> 74, of which waited for: 20 -> 49; matrix products, arithmetic and copies ran while one was open for 15% -> 17% of each run, Pallas kernels for 0% -> 3%
where the time goes in v1:
time: 828 us; the launch traced here: 821 us
  waiting for transfers between devices  447 us (54%)
  starting transfers between devices  123 us (15%)
  matrix products  99.6 us (12%)
  Pallas kernels  58.1 us (7%)
  other arithmetic  42.2 us (5%)
  local copies, waits for them, and re-layouts  36.6 us (4%)
  between operations  15 us (2%)
    ppermute x24, waiting for transfers between devices, shift(): return lax.ppermute(v, 'ctx', [(i, (i + by) % n) for i in range(n)])  154 us
    ppermute x35, waiting for transfers between devices, swap(): return lax.ppermute(v, axis, [(0, 1), (1, 0)])  141 us
    reduce_scatter x3, waiting for transfers between devices, per_device_split(): lax.psum_scatter(outer_sum(left, right).astype(BF16), NEAR, scatter_dimen...  95.4 us
    ppermute x24, starting transfers between devices, shift(): return lax.ppermute(v, 'ctx', [(i, (i + by) % n) for i in range(n)])  55.6 us
    ppermute x35, starting transfers between devices, swap(): return lax.ppermute(v, axis, [(0, 1), (1, 0)])  41.1 us
    pallas_call x1, Pallas kernels, attn_bwd(): pl.pallas_call(functools.partial(attn_bwd_kernel, blocks=blocks, width=co...  34.7 us
    dot_general x3, matrix products, rows_by(): jnp.einsum('td,fd->tf', left, right, preferred_element_type=jnp.float32)  32.4 us
    dot_general x3, matrix products, outer_sum(): jnp.einsum('tf,td->fd', left, right, preferred_element_type=jnp.float32)  28.8 us
  transfers between devices with their start and end apart: 74, of which 49 were waited for; matrix products, arithmetic and copies ran while one was open for 17% of the time, Pallas kernels for 3%

profile of v1, /device:TPU:0, one launch (start us, length us, event | category | flops | bytes accessed | tf_op | source)
XLA Modules:
  0.0 820.7 jit_solution(10912208709293545460)
XLA Ops:
  12.1 7.3 all-to-all-start
  25.4 24.2 %collective-permute-done.3 = bf16[128,2048]{1,0:T(8,128)(2,1)S(1)} collective-permute-done((bf16[128,2048]{1,0:T(8,128)(2,1)S(1)}, bf16[128,2048]{1,0:T(8,128)(2,1)S(1)}, u32[]{:S(2)}, u32[]{:S(2)}) %collective-permute-start.3) | collective-permute-done | bytes 524320 | tf_op jit(solution)/shard_map/ppermute | solution.py:576
  52.0 12.1 %collective-permute-done.4 = bf16[128,2048]{1,0:T(8,128)(2,1)} collective-permute-done((bf16[128,2048]{1,0:T(8,128)(2,1)S(1)}, bf16[128,2048]{1,0:T(8,128)(2,1)}, u32[]{:S(2)}, u32[]{:S(2)}) %collective-permute-start.4) | collective-permute-done | bytes 524320 | tf_op jit(solution)/shard_map/ppermute | solution.py:576
  73.3 6.1 collective-permute-done.5
  88.7 5.9 collective-permute-done.8
  95.4 8.1 collective-permute-done.9
  118.9 25.8 %all-to-all-done.1.qkv_ref = bf16[4,192,1024]{2,1,0:T(8,128)(2,1)S(1)} async-done(((bf16[4,192,1024]{2,1,0:T(8,128)(2,1)}), bf16[4,192,1024]{2,1,0:T(8,128)(2,1)S(1)}, u32[]{:S(2)}, u32[]{:S(2)}) %all-to-all-start.1) | async-done | bytes 1572896 | tf_op jit(solution)/shard_map/all_to_all | solution.py:684
  144.6 23.5 %attn_fwd.1 = (bf16[4,64,1024]{2,1,0:T(8,128)(2,1)}, f32[64,4096]{1,0:T(8,128)S(1)}, f32[1,4096]{1,0:T(1,128)S(1)}, bf16[192,4096]{1,0:T(8,128)(2,1)S(1)}) custom-call(s32[8]{0:T(128)S(1)} %select_reduce_fusion.slot_ref, bf16[4,192,1024]{2,1,0:T(8,128)(2,1)S(1)} %all-to-all-done.1.qkv_ref), custom_call_target="tpu_custom_call" | custom-call | flops 8589934592 | bytes 8388608 | tf_op jit(solution)/shard_map/attn_fwd/pallas_call | solution.py:434
  172.7 8.7 %all-to-all-done.2 = bf16[4,64,1024]{2,1,0:T(8,128)(2,1)S(1)} async-done(((bf16[4,64,1024]{2,1,0:T(8,128)(2,1)}), bf16[4,64,1024]{2,1,0:T(8,128)(2,1)S(1)}, u32[]{:S(2)}, u32[]{:S(2)}) %all-to-all-start.2) | async-done | bytes 524320 | tf_op jit(solution)/shard_map/all_to_all | solution.py:686
  187.4 12.0 %collective-permute-done.13 = bf16[128,2048]{1,0:T(8,128)(2,1)S(1)} collective-permute-done((bf16[128,2048]{1,0:T(8,128)(2,1)S(1)}, bf16[128,2048]{1,0:T(8,128)(2,1)S(1)}, u32[]{:S(2)}, u32[]{:S(2)}) %collective-permute-start.13) | collective-permute-done | bytes 524320 | tf_op jit(solution)/shard_map/ppermute | solution.py:571
  205.4 5.2 collective-permute-done.12
  210.6 12.4 %collective-permute-done.14 = bf16[128,2048]{1,0:T(8,128)(2,1)S(1)} collective-permute-done((bf16[128,2048]{1,0:T(8,128)(2,1)S(1)}, bf16[128,2048]{1,0:T(8,128)(2,1)S(1)}, u32[]{:S(2)}, u32[]{:S(2)}) %collective-permute-start.14) | collective-permute-done | bytes 524320 | tf_op jit(solution)/shard_map/ppermute | solution.py:576
  223.2 4.8 collective-permute-done.31
  230.1 17.4 %collective-permute-done.15 = bf16[128,2048]{1,0:T(8,128)(2,1)S(1)} collective-permute-done((bf16[128,2048]{1,0:T(8,128)(2,1)S(1)}, bf16[128,2048]{1,0:T(8,128)(2,1)S(1)}, u32[]{:S(2)}, u32[]{:S(2)}) %collective-permute-start.15) | collective-permute-done | bytes 524320 | tf_op jit(solution)/shard_map/ppermute | solution.py:576
  256.7 9.2 %collective-permute-done.16 = bf16[128,2048]{1,0:T(8,128)(2,1)} collective-permute-done((bf16[128,2048]{1,0:T(8,128)(2,1)S(1)}, bf16[128,2048]{1,0:T(8,128)(2,1)}, u32[]{:S(2)}, u32[]{:S(2)}) %collective-permute-start.16) | collective-permute-done | bytes 524320 | tf_op jit(solution)/shard_map/ppermute | solution.py:576
  268.9 22.3 %collective-permute-start.17 = (bf16[128,2048]{1,0:T(8,128)(2,1)S(1)}, bf16[128,2048]{1,0:T(8,128)(2,1)S(1)}, u32[]{:S(2)}, u32[]{:S(2)}) collective-permute-start(bf16[128,2048]{1,0:T(8,128)(2,1)S(1)} %get-tuple-element.25), channel_id=1, source_target_pairs={{0,8},{8,16},{16,24},{24,0},{1,9},{9,17},{17,25},{25,1},{2,10},{10... | collective-permute-start | bytes 1572872 | tf_op jit(solution)/shard_map/ppermute | solution.py:576
  302.1 5.3 collective-permute-done.36
  310.3 8.4 %collective-permute-done.37 = bf16[128,2048]{1,0:T(8,128)(2,1)S(1)} collective-permute-done((bf16[128,2048]{1,0:T(8,128)(2,1)S(1)}, bf16[128,2048]{1,0:T(8,128)(2,1)S(1)}, u32[]{:S(2)}, u32[]{:S(2)}) %collective-permute-start.37) | collective-permute-done | bytes 524320 | tf_op jit(solution)/shard_map/ppermute | solution.py:571
  329.7 4.8 collective-permute-done.21
  335.3 4.8 collective-permute-done.22
  341.0 4.8 collective-permute-done.23
  346.6 10.0 %fusion.68 = f32[1024,1024]{1,0:T(8,128)} fusion(bf16[1024,2048]{1,0:T(8,128)(2,1)} %constant_dynamic-update-slice_fusion.8, bf16[1024,2048]{1,0:T(8,128)(2,1)} %all-gather.9.cloned.1.call-done), kind=kOutput, calls=%fused_computation.197 | convolution fusion | flops 4294967296 | bytes 12582912 | tf_op jit(solution)/shard_map/td,fd->tf/dot_general | solution.py:55
  356.6 10.1 %fusion.67 = f32[1024,1024]{1,0:T(8,128)} fusion(bf16[1024,2048]{1,0:T(8,128)(2,1)} %constant_dynamic-update-slice_fusion.8, bf16[1024,2048]{1,0:T(8,128)(2,1)} %all-gather.7.cloned.1.call-done), kind=kOutput, calls=%fused_computation.196 | convolution fusion | flops 4294967296 | bytes 12582912 | tf_op jit(solution)/shard_map/td,fd->tf/dot_general | solution.py:55
  366.6 12.4 %multiply_convert_fusion = (bf16[1024,1024]{1,0:T(8,128)(2,1)S(1)}, bf16[1024,1024]{1,0:T(8,128)(2,1)S(1)}, bf16[1024,1024]{1,0:T(8,128)(2,1)S(1)}) fusion(f32[1024,1024]{1,0:T(8,128)} %fusion.67, f32[1024,1024]{1,0:T(8,128)} %fusion.68, bf16[1024,2048]{1,0:T(8,128)(2,1)} %copy-done.20, bf16[1024,2048]{1,0:T(8,128)(2,1)} %all-gather.11.cloned.1.call-done), kind=kOutput, calls=%fused_computation.1 | convolution fusion | flops 4310695936 | bytes 23068672 | tf_op jit(solution)/shard_map/td,fd->tf/dot_general | solution.py:55
  399.0 19.9 %collective-permute-done.41 = bf16[128,2048]{1,0:T(8,128)(2,1)S(1)} collective-permute-done((bf16[128,2048]{1,0:T(8,128)(2,1)S(1)}, bf16[128,2048]{1,0:T(8,128)(2,1)S(1)}, u32[]{:S(2)}, u32[]{:S(2)}) %collective-permute-start.41) | collective-permute-done | bytes 524320 | tf_op jit(solution)/shard_map/ppermute | solution.py:571
  423.1 7.1 collective-permute-done.40
  447.0 5.6 collective-permute-done.24
  452.6 9.4 %collective-permute-done.44 = bf16[128,2048]{1,0:T(8,128)(2,1)S(1)} collective-permute-done((bf16[128,2048]{1,0:T(8,128)(2,1)S(1)}, bf16[128,2048]{1,0:T(8,128)(2,1)S(1)}, u32[]{:S(2)}, u32[]{:S(2)}) %collective-permute-start.44) | collective-permute-done | bytes 524320 | tf_op jit(solution)/shard_map/ppermute | solution.py:576
  466.0 11.8 %collective-permute-done.45 = bf16[128,2048]{1,0:T(8,128)(2,1)S(1)} collective-permute-done((bf16[128,2048]{1,0:T(8,128)(2,1)S(1)}, bf16[128,2048]{1,0:T(8,128)(2,1)S(1)}, u32[]{:S(2)}, u32[]{:S(2)}) %collective-permute-start.45) | collective-permute-done | bytes 524320 | tf_op jit(solution)/shard_map/ppermute | solution.py:576
  478.2 10.6 %collective-permute-done.46 = bf16[128,2048]{1,0:T(8,128)(2,1)S(1)} collective-permute-done((bf16[128,2048]{1,0:T(8,128)(2,1)S(1)}, bf16[128,2048]{1,0:T(8,128)(2,1)S(1)}, u32[]{:S(2)}, u32[]{:S(2)}) %collective-permute-start.46) | collective-permute-done | bytes 524320 | tf_op jit(solution)/shard_map/ppermute | solution.py:576
  492.4 7.3 collective-permute-done.47
  503.6 5.6 collective-permute-done.50
  509.2 5.6 collective-permute-done.51
  522.4 6.9 all-to-all-done.3.do_ref
  530.5 34.7 %attn_bwd.1 = bf16[4,192,1024]{2,1,0:T(8,128)(2,1)} custom-call(s32[8]{0:T(128)S(1)} %select_reduce_fusion.slot_ref, bf16[192,4096]{1,0:T(8,128)(2,1)S(1)} %get-tuple-element.16.seq_ref, f32[64,4096]{1,0:T(8,128)S(1)} %copy-done.1, f32[1,4096]{1,0:T(1,128)S(1)} %get-tuple-element.18.lse_ref, bf16[4,64,1024]{2,1,0:T(8,128)(2,1)S(1)} %all-to-all-done.3.do_ref, ...), custom_call_target="tpu_custom_call" | custom-call | flops 21474836480 | bytes 8388608 | tf_op jit(solution)/shard_map/attn_bwd/pallas_call | solution.py:545
  568.8 6.4 copy.72
  575.2 13.6 %all-to-all-done.4 = bf16[4,192,1024]{2,1,0:T(8,128)(2,1)S(1)} async-done(((bf16[4,192,1024]{2,1,0:T(8,128)(2,1)}), bf16[4,192,1024]{2,1,0:T(8,128)(2,1)S(1)}, u32[]{:S(2)}, u32[]{:S(2)}) %all-to-all-start.4) | async-done | bytes 1572896 | tf_op jit(solution)/shard_map/all_to_all | solution.py:742
  588.9 5.7 convolution_convert_fusion.7
  601.9 10.1 %convolution_convert_fusion.1 = bf16[1024,2048]{1,0:T(8,128)(2,1)} fusion(bf16[1024,1024]{1,0:T(8,128)(2,1)} %copy-done.30, bf16[1024,2048]{1,0:T(8,128)(2,1)} %constant_dynamic-update-slice_fusion.8), kind=kOutput, calls=%fused_computation.7 | convolution fusion | flops 4297064448 | bytes 10485760 | tf_op jit(solution)/shard_map/tf,td->fd/dot_general | solution.py:59
  612.2 9.4 %convolution_convert_fusion.2 = bf16[1024,2048]{1,0:T(8,128)(2,1)} fusion(bf16[1024,1024]{1,0:T(8,128)(2,1)} %copy-done.32, bf16[1024,2048]{1,0:T(8,128)(2,1)} %constant_dynamic-update-slice_fusion.8), kind=kOutput, calls=%fused_computation.8 | convolution fusion | flops 4297064448 | bytes 10485760 | tf_op jit(solution)/shard_map/tf,td->fd/dot_general | solution.py:59
  621.7 9.4 %convolution_convert_fusion = bf16[1024,2048]{1,0:T(8,128)(2,1)} fusion(bf16[1024,1024]{1,0:T(8,128)(2,1)} %copy-done.31, bf16[1024,2048]{1,0:T(8,128)(2,1)} %copy-done.20), kind=kOutput, calls=%fused_computation.6 | convolution fusion | flops 4297064448 | bytes 10485760 | tf_op jit(solution)/shard_map/tf,td->fd/dot_general | solution.py:59
  639.8 10.9 %collective-permute-done.55 = bf16[128,2048]{1,0:T(8,128)(2,1)S(1)} collective-permute-done((bf16[128,2048]{1,0:T(8,128)(2,1)S(1)}, bf16[128,2048]{1,0:T(8,128)(2,1)S(1)}, u32[]{:S(2)}, u32[]{:S(2)}) %collective-permute-start.55) | collective-permute-done | bytes 524320 | tf_op jit(solution)/shard_map/ppermute | solution.py:571
  656.4 5.6 collective-permute-done.54
  673.9 7.6 collective-permute-done.57
  690.3 12.6 %collective-permute-done.58 = bf16[128,2048]{1,0:T(8,128)(2,1)S(1)} collective-permute-done((bf16[128,2048]{1,0:T(8,128)(2,1)}, bf16[128,2048]{1,0:T(8,128)(2,1)S(1)}, u32[]{:S(2)}, u32[]{:S(2)}) %collective-permute-start.58) | collective-permute-done | bytes 524320 | tf_op jit(solution)/shard_map/ppermute | solution.py:576
  707.1 6.7 reduce-scatter.12.cloned.1.call-done
  716.6 44.4 %reduce-scatter.10.cloned.1.call-done = bf16[256,2048]{1,0:T(8,128)(2,1)} async-done(((bf16[1024,2048]{1,0:T(8,128)(2,1)}), bf16[256,2048]{1,0:T(8,128)(2,1)}) %reduce-scatter.10.cloned.1.call-update) | async-done | bytes 1048592 | tf_op jit(solution)/shard_map/reduce_scatter | solution.py:717
  763.8 44.3 %reduce-scatter.14.cloned.1.call-done = bf16[256,2048]{1,0:T(8,128)(2,1)} async-done(((bf16[1024,2048]{1,0:T(8,128)(2,1)}), bf16[256,2048]{1,0:T(8,128)(2,1)}) %reduce-scatter.14.cloned.1.call-update) | async-done | bytes 1048592 | tf_op jit(solution)/shard_map/reduce_scatter | solution.py:717
  (295 shorter events, 229.2 us)
Async XLA Ops:
  7.2 165.5 %all-gather.5.cloned.1.call-start = ((), (), s32[]{:S(2)}) async-start(), calls=%async_computation.11 | async-start | bytes 1310720 | tf_op jit(solution)/shard_map/all_gather | solution.py:672
  12.1 53.7 %all-to-all-start = ((bf16[8,64,896]{2,1,0:T(8,128)(2,1)}), bf16[8,64,896]{2,1,0:T(8,128)(2,1)S(1)}, u32[]{:S(2)}, u32[]{:S(2)}) async-start(bf16[8,64,896]{2,1,0:T(8,128)(2,1)} %copy.60), calls=%async_computation | async-start | bytes 1835008 | tf_op jit(solution)/shard_map/all_to_all | solution.py:661
  19.3 327.3 %all-gather.9.cloned.1.call-start = ((), (), s32[]{:S(2)}) async-start(), calls=%async_computation.13 | async-start | bytes 5242880 | tf_op jit(solution)/shard_map/all_gather | solution.py:674
  21.8 27.8 %collective-permute-start.3 = (bf16[128,2048]{1,0:T(8,128)(2,1)S(1)}, bf16[128,2048]{1,0:T(8,128)(2,1)S(1)}, u32[]{:S(2)}, u32[]{:S(2)}) collective-permute-start(bf16[128,2048]{1,0:T(8,128)(2,1)S(1)} %get-tuple-element.31), channel_id=1, source_target_pairs={{0,8},{8,16},{16,24},{24,0},{1,9},{9,17},{17,25},{25,1},{2,10},{10... | collective-permute-start | bytes 1572872 | tf_op jit(solution)/shard_map/ppermute | solution.py:576
  23.8 59.5 %collective-permute-start.6 = (bf16[128,2048]{1,0:T(8,128)(2,1)S(1)}, bf16[128,2048]{1,0:T(8,128)(2,1)S(1)}, u32[]{:S(2)}, u32[]{:S(2)}) collective-permute-start(bf16[128,2048]{1,0:T(8,128)(2,1)S(1)} %get-tuple-element.31), channel_id=1, source_target_pairs={{0,4},{4,0},{1,5},{5,1},{2,6},{6,2},{3,7},{7,3},{8,12},{12,8},{9,1... | collective-permute-start | bytes 1572872 | tf_op jit(solution)/shard_map/ppermute | solution.py:571
  65.8 21.2 %collective-permute-start.1 = (bf16[8,64,896]{2,1,0:T(8,128)(2,1)S(1)}, bf16[8,64,896]{2,1,0:T(8,128)(2,1)S(1)}, u32[]{:S(2)}, u32[]{:S(2)}) collective-permute-start(bf16[8,64,896]{2,1,0:T(8,128)(2,1)S(1)} %all-to-all-done), channel_id=1, source_target_pairs={{0,2},{2,0},{1,3},{3,1},{4,6},{6,4},{5,7},{7,5},{8,10},{10,8},{9,1... | collective-permute-start | bytes 2752520 | tf_op jit(solution)/shard_map/ppermute | solution.py:571
  68.4 19.4 %collective-permute-start.7 = (bf16[128,2048]{1,0:T(8,128)(2,1)S(1)}, bf16[128,2048]{1,0:T(8,128)(2,1)S(1)}, u32[]{:S(2)}, u32[]{:S(2)}) collective-permute-start(bf16[128,2048]{1,0:T(8,128)(2,1)S(1)} %collective-permute-done.3), channel_id=1, source_target_pairs={{0,4},{4,0},{1,5},{5,1},{2,6},{6,2},{3,7},{7,3},{8,12},{12,8},{9,1... | collective-permute-start | bytes 1572872 | tf_op jit(solution)/shard_map/ppermute | solution.py:571
  71.1 23.4 %collective-permute-start.8 = (bf16[128,2048]{1,0:T(8,128)(2,1)}, bf16[128,2048]{1,0:T(8,128)(2,1)S(1)}, u32[]{:S(2)}, u32[]{:S(2)}) collective-permute-start(bf16[128,2048]{1,0:T(8,128)(2,1)} %collective-permute-done.4), channel_id=1, source_target_pairs={{0,4},{4,0},{1,5},{5,1},{2,6},{6,2},{3,7},{7,3},{8,12},{12,8},{9,1... | collective-permute-start | bytes 1572872 | tf_op jit(solution)/shard_map/ppermute | solution.py:571
  79.4 24.2 %collective-permute-start.9 = (bf16[128,2048]{1,0:T(8,128)(2,1)}, bf16[128,2048]{1,0:T(8,128)(2,1)S(1)}, u32[]{:S(2)}, u32[]{:S(2)}) collective-permute-start(bf16[128,2048]{1,0:T(8,128)(2,1)} %collective-permute-done.5), channel_id=1, source_target_pairs={{0,4},{4,0},{1,5},{5,1},{2,6},{6,2},{3,7},{7,3},{8,12},{12,8},{9,1... | collective-permute-start | bytes 1572872 | tf_op jit(solution)/shard_map/ppermute | solution.py:571
  83.2 21.2 %collective-permute-start = (bf16[8,64,896]{2,1,0:T(8,128)(2,1)S(1)}, bf16[8,64,896]{2,1,0:T(8,128)(2,1)S(1)}, u32[]{:S(2)}, u32[]{:S(2)}) collective-permute-start(bf16[8,64,896]{2,1,0:T(8,128)(2,1)S(1)} %all-to-all-done), channel_id=1, source_target_pairs={{0,1},{1,0},{2,3},{3,2},{4,5},{5,4},{6,7},{7,6},{8,9},{9,8},{10,11... | collective-permute-start | bytes 2752520 | tf_op jit(solution)/shard_map/ppermute | solution.py:571
  86.9 17.5 %collective-permute-start.2 = (bf16[8,64,896]{2,1,0:T(8,128)(2,1)S(1)}, bf16[8,64,896]{2,1,0:T(8,128)(2,1)S(1)}, u32[]{:S(2)}, u32[]{:S(2)}) collective-permute-start(bf16[8,64,896]{2,1,0:T(8,128)(2,1)S(1)} %collective-permute-done.1), channel_id=1, source_target_pairs={{0,1},{1,0},{2,3},{3,2},{4,5},{5,4},{6,7},{7,6},{8,9},{9,8},{10,11... | collective-permute-start | bytes 2752520 | tf_op jit(solution)/shard_map/ppermute | solution.py:571
  114.4 30.2 %all-to-all-start.1 = ((bf16[4,192,1024]{2,1,0:T(8,128)(2,1)}), bf16[4,192,1024]{2,1,0:T(8,128)(2,1)S(1)}, u32[]{:S(2)}, u32[]{:S(2)}) async-start(bf16[4,192,1024]{2,1,0:T(8,128)(2,1)} %bitcast.14), calls=%async_computation.1 | async-start | bytes 3145728 | tf_op jit(solution)/shard_map/all_to_all | solution.py:684
  118.0 238.6 %all-gather.7.cloned.1.call-start = ((), (), s32[]{:S(2)}) async-start(), calls=%async_computation.12 | async-start | bytes 5242880 | tf_op jit(solution)/shard_map/all_gather | solution.py:674
  172.6 194.0 %all-gather.11.cloned.1.call-start = ((), (), s32[]{:S(2)}) async-start(), calls=%async_computation.14 | async-start | bytes 5242880 | tf_op jit(solution)/shard_map/all_gather | solution.py:674
  186.6 24.0 %collective-permute-start.12 = (bf16[128,2048]{1,0:T(8,128)(2,1)S(1)}, bf16[128,2048]{1,0:T(8,128)(2,1)S(1)}, u32[]{:S(2)}, u32[]{:S(2)}) collective-permute-start(bf16[128,2048]{1,0:T(8,128)(2,1)S(1)} %get-tuple-element.57), channel_id=1, source_target_pairs={{0,4},{4,0},{1,5},{5,1},{2,6},{6,2},{3,7},{7,3},{8,12},{12,8},{9,1... | collective-permute-start | bytes 1572872 | tf_op jit(solution)/shard_map/ppermute | solution.py:571
  199.5 23.5 %collective-permute-start.14 = (bf16[128,2048]{1,0:T(8,128)(2,1)S(1)}, bf16[128,2048]{1,0:T(8,128)(2,1)S(1)}, u32[]{:S(2)}, u32[]{:S(2)}) collective-permute-start(bf16[128,2048]{1,0:T(8,128)(2,1)S(1)} %fusion.40), channel_id=1, source_target_pairs={{0,24},{8,0},{16,8},{24,16},{1,25},{9,1},{17,9},{25,17},{2,26},{10... | collective-permute-start | bytes 1572872 | tf_op jit(solution)/shard_map/ppermute | solution.py:576
  201.0 27.1 %collective-permute-start.31 = (bf16[128,2048]{1,0:T(8,128)(2,1)}, bf16[128,2048]{1,0:T(8,128)(2,1)}, u32[]{:S(2)}, u32[]{:S(2)}) collective-permute-start(bf16[128,2048]{1,0:T(8,128)(2,1)} %param.23), channel_id=1, source_target_pairs={{0,8},{8,16},{16,24},{24,0},{1,9},{9,17},{17,25},{25,1},{2,10},{10... | collective-permute-start | bytes 1572872 | tf_op jit(solution)/shard_map/ppermute | solution.py:576
  203.3 26.8 %collective-permute-start.11 = (bf16[128,2048]{1,0:T(8,128)(2,1)S(1)}, bf16[128,2048]{1,0:T(8,128)(2,1)S(1)}, u32[]{:S(2)}, u32[]{:S(2)}) collective-permute-start(bf16[128,2048]{1,0:T(8,128)(2,1)S(1)} %get-tuple-element.58), channel_id=1, source_target_pairs={{0,4},{4,0},{1,5},{5,1},{2,6},{6,2},{3,7},{7,3},{8,12},{12,8},{9,1... | collective-permute-start | bytes 1572872 | tf_op jit(solution)/shard_map/ppermute | solution.py:571
  223.2 24.4 %collective-permute-start.15 = (bf16[128,2048]{1,0:T(8,128)(2,1)S(1)}, bf16[128,2048]{1,0:T(8,128)(2,1)S(1)}, u32[]{:S(2)}, u32[]{:S(2)}) collective-permute-start(bf16[128,2048]{1,0:T(8,128)(2,1)S(1)} %fusion.42), channel_id=1, source_target_pairs={{0,24},{8,0},{16,8},{24,16},{1,25},{9,1},{17,9},{25,17},{2,26},{10... | collective-permute-start | bytes 1572872 | tf_op jit(solution)/shard_map/ppermute | solution.py:576
  228.1 23.4 %collective-permute-start.32 = (bf16[128,2048]{1,0:T(8,128)(2,1)}, bf16[128,2048]{1,0:T(8,128)(2,1)}, u32[]{:S(2)}, u32[]{:S(2)}) collective-permute-start(bf16[128,2048]{1,0:T(8,128)(2,1)} %collective-permute-done.31), channel_id=1, source_target_pairs={{0,8},{8,16},{16,24},{24,0},{1,9},{9,17},{17,25},{25,1},{2,10},{10... | collective-permute-start | bytes 1572872 | tf_op jit(solution)/shard_map/ppermute | solution.py:576
  228.1 28.7 %collective-permute-start.10 = (bf16[128,2048]{1,0:T(8,128)(2,1)}, bf16[128,2048]{1,0:T(8,128)(2,1)}, u32[]{:S(2)}, u32[]{:S(2)}) collective-permute-start(bf16[128,2048]{1,0:T(8,128)(2,1)} %get-tuple-element.55), channel_id=1, source_target_pairs={{0,4},{4,0},{1,5},{5,1},{2,6},{6,2},{3,7},{7,3},{8,12},{12,8},{9,1... | collective-permute-start | bytes 1572872 | tf_op jit(solution)/shard_map/ppermute | solution.py:571
  247.7 18.2 %collective-permute-start.16 = (bf16[128,2048]{1,0:T(8,128)(2,1)S(1)}, bf16[128,2048]{1,0:T(8,128)(2,1)}, u32[]{:S(2)}, u32[]{:S(2)}) collective-permute-start(bf16[128,2048]{1,0:T(8,128)(2,1)S(1)} %fusion.44), channel_id=1, source_target_pairs={{0,24},{8,0},{16,8},{24,16},{1,25},{9,1},{17,9},{25,17},{2,26},{10... | collective-permute-start | bytes 1572872 | tf_op jit(solution)/shard_map/ppermute | solution.py:576
  247.8 53.1 %collective-permute-start.34 = (bf16[128,2048]{1,0:T(8,128)(2,1)}, bf16[128,2048]{1,0:T(8,128)(2,1)}, u32[]{:S(2)}, u32[]{:S(2)}) collective-permute-start(bf16[128,2048]{1,0:T(8,128)(2,1)} %param.23), channel_id=1, source_target_pairs={{0,4},{4,0},{1,5},{5,1},{2,6},{6,2},{3,7},{7,3},{8,12},{12,8},{9,1... | collective-permute-start | bytes 1572872 | tf_op jit(solution)/shard_map/ppermute | solution.py:571
  251.1 51.0 %collective-permute-start.35 = (bf16[128,2048]{1,0:T(8,128)(2,1)}, bf16[128,2048]{1,0:T(8,128)(2,1)S(1)}, u32[]{:S(2)}, u32[]{:S(2)}) collective-permute-start(bf16[128,2048]{1,0:T(8,128)(2,1)} %collective-permute-done.31), channel_id=1, source_target_pairs={{0,4},{4,0},{1,5},{5,1},{2,6},{6,2},{3,7},{7,3},{8,12},{12,8},{9,1... | collective-permute-start | bytes 1572872 | tf_op jit(solution)/shard_map/ppermute | solution.py:571
  251.5 43.4 %collective-permute-start.33 = (bf16[128,2048]{1,0:T(8,128)(2,1)}, bf16[128,2048]{1,0:T(8,128)(2,1)S(1)}, u32[]{:S(2)}, u32[]{:S(2)}) collective-permute-start(bf16[128,2048]{1,0:T(8,128)(2,1)} %collective-permute-done.32), channel_id=1, source_target_pairs={{0,8},{8,16},{16,24},{24,0},{1,9},{9,17},{17,25},{25,1},{2,10},{10... | collective-permute-start | bytes 1572872 | tf_op jit(solution)/shard_map/ppermute | solution.py:576
  268.9 29.6 %collective-permute-start.17 = (bf16[128,2048]{1,0:T(8,128)(2,1)S(1)}, bf16[128,2048]{1,0:T(8,128)(2,1)S(1)}, u32[]{:S(2)}, u32[]{:S(2)}) collective-permute-start(bf16[128,2048]{1,0:T(8,128)(2,1)S(1)} %get-tuple-element.25), channel_id=1, source_target_pairs={{0,8},{8,16},{16,24},{24,0},{1,9},{9,17},{17,25},{25,1},{2,10},{10... | collective-permute-start | bytes 1572872 | tf_op jit(solution)/shard_map/ppermute | solution.py:576
  294.9 23.7 %collective-permute-start.37 = (bf16[128,2048]{1,0:T(8,128)(2,1)S(1)}, bf16[128,2048]{1,0:T(8,128)(2,1)S(1)}, u32[]{:S(2)}, u32[]{:S(2)}) collective-permute-start(bf16[128,2048]{1,0:T(8,128)(2,1)S(1)} %collective-permute-done.33), channel_id=1, source_target_pairs={{0,4},{4,0},{1,5},{5,1},{2,6},{6,2},{3,7},{7,3},{8,12},{12,8},{9,1... | collective-permute-start | bytes 1572872 | tf_op jit(solution)/shard_map/ppermute | solution.py:571
  321.6 18.5 %collective-permute-start.22 = (bf16[128,2048]{1,0:T(8,128)(2,1)S(1)}, bf16[128,2048]{1,0:T(8,128)(2,1)S(1)}, u32[]{:S(2)}, u32[]{:S(2)}) collective-permute-start(bf16[128,2048]{1,0:T(8,128)(2,1)S(1)} %collective-permute-done.18), channel_id=1, source_target_pairs={{0,4},{4,0},{1,5},{5,1},{2,6},{6,2},{3,7},{7,3},{8,12},{12,8},{9,1... | collective-permute-start | bytes 1572872 | tf_op jit(solution)/shard_map/ppermute | solution.py:571
  324.0 21.8 %collective-permute-start.23 = (bf16[128,2048]{1,0:T(8,128)(2,1)S(1)}, bf16[128,2048]{1,0:T(8,128)(2,1)S(1)}, u32[]{:S(2)}, u32[]{:S(2)}) collective-permute-start(bf16[128,2048]{1,0:T(8,128)(2,1)S(1)} %collective-permute-done.19), channel_id=1, source_target_pairs={{0,4},{4,0},{1,5},{5,1},{2,6},{6,2},{3,7},{7,3},{8,12},{12,8},{9,1... | collective-permute-start | bytes 1572872 | tf_op jit(solution)/shard_map/ppermute | solution.py:571
  383.1 37.6 %collective-permute-start.26 = (bf16[128,2048]{1,0:T(8,128)(2,1)S(1)}, bf16[128,2048]{1,0:T(8,128)(2,1)S(1)}, u32[]{:S(2)}, u32[]{:S(2)}) collective-permute-start(bf16[128,2048]{1,0:T(8,128)(2,1)S(1)} %get-tuple-element.53), channel_id=1, source_target_pairs={{0,4},{4,0},{1,5},{5,1},{2,6},{6,2},{3,7},{7,3},{8,12},{12,8},{9,1... | collective-permute-start | bytes 1572872 | tf_op jit(solution)/shard_map/ppermute | solution.py:571
  388.6 30.3 %collective-permute-start.41 = (bf16[128,2048]{1,0:T(8,128)(2,1)S(1)}, bf16[128,2048]{1,0:T(8,128)(2,1)S(1)}, u32[]{:S(2)}, u32[]{:S(2)}) collective-permute-start(bf16[128,2048]{1,0:T(8,128)(2,1)S(1)} %get-tuple-element.48), channel_id=1, source_target_pairs={{0,4},{4,0},{1,5},{5,1},{2,6},{6,2},{3,7},{7,3},{8,12},{12,8},{9,1... | collective-permute-start | bytes 1572872 | tf_op jit(solution)/shard_map/ppermute | solution.py:571
  390.2 40.0 %collective-permute-start.40 = (bf16[128,2048]{1,0:T(8,128)(2,1)S(1)}, bf16[128,2048]{1,0:T(8,128)(2,1)S(1)}, u32[]{:S(2)}, u32[]{:S(2)}) collective-permute-start(bf16[128,2048]{1,0:T(8,128)(2,1)S(1)} %get-tuple-element.49), channel_id=1, source_target_pairs={{0,4},{4,0},{1,5},{5,1},{2,6},{6,2},{3,7},{7,3},{8,12},{12,8},{9,1... | collective-permute-start | bytes 1572872 | tf_op jit(solution)/shard_map/ppermute | solution.py:571
  396.6 24.6 %collective-permute-start.28 = (bf16[128,2048]{1,0:T(8,128)(2,1)S(1)}, bf16[128,2048]{1,0:T(8,128)(2,1)S(1)}, u32[]{:S(2)}, u32[]{:S(2)}) collective-permute-start(bf16[128,2048]{1,0:T(8,128)(2,1)S(1)} %fusion.29), channel_id=1, source_target_pairs={{0,24},{8,0},{16,8},{24,16},{1,25},{9,1},{17,9},{25,17},{2,26},{10... | collective-permute-start | bytes 1572872 | tf_op jit(solution)/shard_map/ppermute | solution.py:576
  420.7 20.7 %collective-permute-start.39 = (bf16[128,2048]{1,0:T(8,128)(2,1)S(1)}, bf16[128,2048]{1,0:T(8,128)(2,1)S(1)}, u32[]{:S(2)}, u32[]{:S(2)}) collective-permute-start(bf16[128,2048]{1,0:T(8,128)(2,1)S(1)} %get-tuple-element.50), channel_id=1, source_target_pairs={{0,4},{4,0},{1,5},{5,1},{2,6},{6,2},{3,7},{7,3},{8,12},{12,8},{9,1... | collective-permute-start | bytes 1572872 | tf_op jit(solution)/shard_map/ppermute | solution.py:571
  442.9 19.2 %collective-permute-start.44 = (bf16[128,2048]{1,0:T(8,128)(2,1)S(1)}, bf16[128,2048]{1,0:T(8,128)(2,1)S(1)}, u32[]{:S(2)}, u32[]{:S(2)}) collective-permute-start(bf16[128,2048]{1,0:T(8,128)(2,1)S(1)} %fusion.21), channel_id=1, source_target_pairs={{0,24},{8,0},{16,8},{24,16},{1,25},{9,1},{17,9},{25,17},{2,26},{10... | collective-permute-start | bytes 1572872 | tf_op jit(solution)/shard_map/ppermute | solution.py:576
  490.8 18.4 %collective-permute-start.50 = (bf16[128,2048]{1,0:T(8,128)(2,1)S(1)}, bf16[128,2048]{1,0:T(8,128)(2,1)S(1)}, u32[]{:S(2)}, u32[]{:S(2)}) collective-permute-start(bf16[128,2048]{1,0:T(8,128)(2,1)S(1)} %collective-permute-done.46), channel_id=1, source_target_pairs={{0,4},{4,0},{1,5},{5,1},{2,6},{6,2},{3,7},{7,3},{8,12},{12,8},{9,1... | collective-permute-start | bytes 1572872 | tf_op jit(solution)/shard_map/ppermute | solution.py:571
  565.2 23.6 %all-to-all-start.4 = ((bf16[4,192,1024]{2,1,0:T(8,128)(2,1)}), bf16[4,192,1024]{2,1,0:T(8,128)(2,1)S(1)}, u32[]{:S(2)}, u32[]{:S(2)}) async-start(bf16[4,192,1024]{2,1,0:T(8,128)(2,1)} %attn_bwd.1), calls=%async_computation.4 | async-start | bytes 3145728 | tf_op jit(solution)/shard_map/all_to_all | solution.py:742
  568.8 101.6 %reduce-scatter.6.cloned.1.call-start = ((), (), s32[]{:S(2)}) async-start(), calls=%async_computation.15 | async-start | bytes 4587520 | tf_op jit(solution)/shard_map/reduce_scatter | solution.py:759
  597.3 90.8 %reduce-scatter.8.cloned.1.call-start = ((), (), s32[]{:S(2)}) async-start(), calls=%async_computation.16 | async-start | bytes 1310720 | tf_op jit(solution)/shard_map/reduce_scatter | solution.py:735
  601.8 112.0 %reduce-scatter.12.cloned.1.call-start = ((), (), s32[]{:S(2)}) async-start(), calls=%async_computation.18 | async-start | bytes 5242880 | tf_op jit(solution)/shard_map/reduce_scatter | solution.py:717
  612.0 149.0 %reduce-scatter.10.cloned.1.call-start = ((), (), s32[]{:S(2)}) async-start(), calls=%async_computation.17 | async-start | bytes 5242880 | tf_op jit(solution)/shard_map/reduce_scatter | solution.py:717
  621.6 186.5 %reduce-scatter.14.cloned.1.call-start = ((), (), s32[]{:S(2)}) async-start(), calls=%async_computation.19 | async-start | bytes 5242880 | tf_op jit(solution)/shard_map/reduce_scatter | solution.py:717
  637.5 24.6 %collective-permute-start.54 = (bf16[128,2048]{1,0:T(8,128)(2,1)S(1)}, bf16[128,2048]{1,0:T(8,128)(2,1)S(1)}, u32[]{:S(2)}, u32[]{:S(2)}) collective-permute-start(bf16[128,2048]{1,0:T(8,128)(2,1)S(1)} %get-tuple-element.45), channel_id=1, source_target_pairs={{0,4},{4,0},{1,5},{5,1},{2,6},{6,2},{3,7},{7,3},{8,12},{12,8},{9,1... | collective-permute-start | bytes 1572872 | tf_op jit(solution)/shard_map/ppermute | solution.py:571
  654.8 19.1 %collective-permute-start.53 = (bf16[128,2048]{1,0:T(8,128)(2,1)}, bf16[128,2048]{1,0:T(8,128)(2,1)S(1)}, u32[]{:S(2)}, u32[]{:S(2)}) collective-permute-start(bf16[128,2048]{1,0:T(8,128)(2,1)} %get-tuple-element.46), channel_id=1, source_target_pairs={{0,4},{4,0},{1,5},{5,1},{2,6},{6,2},{3,7},{7,3},{8,12},{12,8},{9,1... | collective-permute-start | bytes 1572872 | tf_op jit(solution)/shard_map/ppermute | solution.py:571
  664.5 17.0 %collective-permute-start.57 = (bf16[128,2048]{1,0:T(8,128)(2,1)}, bf16[128,2048]{1,0:T(8,128)(2,1)}, u32[]{:S(2)}, u32[]{:S(2)}) collective-permute-start(bf16[128,2048]{1,0:T(8,128)(2,1)} %fusion.13), channel_id=1, source_target_pairs={{0,24},{8,0},{16,8},{24,16},{1,25},{9,1},{17,9},{25,17},{2,26},{10... | collective-permute-start | bytes 1572872 | tf_op jit(solution)/shard_map/ppermute | solution.py:576
  668.8 21.5 %collective-permute-start.52 = (bf16[128,2048]{1,0:T(8,128)(2,1)}, bf16[128,2048]{1,0:T(8,128)(2,1)S(1)}, u32[]{:S(2)}, u32[]{:S(2)}) collective-permute-start(bf16[128,2048]{1,0:T(8,128)(2,1)} %get-tuple-element.43), channel_id=1, source_target_pairs={{0,4},{4,0},{1,5},{5,1},{2,6},{6,2},{3,7},{7,3},{8,12},{12,8},{9,1... | collective-permute-start | bytes 1572872 | tf_op jit(solution)/shard_map/ppermute | solution.py:571
  670.3 140.6 %all-to-all-start.5 = ((bf16[8,64,896]{2,1,0:T(8,128)(2,1)}), bf16[8,64,896]{2,1,0:T(8,128)(2,1)S(1)}, u32[]{:S(2)}, u32[]{:S(2)}) async-start(bf16[8,64,896]{2,1,0:T(8,128)(2,1)} %reduce-scatter.6.cloned.1.call-done), calls=%async_computation.6 | async-start | bytes 1835008 | tf_op jit(solution)/shard_map/all_to_all | solution.py:765
  683.9 19.0 %collective-permute-start.58 = (bf16[128,2048]{1,0:T(8,128)(2,1)}, bf16[128,2048]{1,0:T(8,128)(2,1)S(1)}, u32[]{:S(2)}, u32[]{:S(2)}) collective-permute-start(bf16[128,2048]{1,0:T(8,128)(2,1)} %fusion.15), channel_id=1, source_target_pairs={{0,24},{8,0},{16,8},{24,16},{1,25},{9,1},{17,9},{25,17},{2,26},{10... | collective-permute-start | bytes 1572872 | tf_op jit(solution)/shard_map/ppermute | solution.py:576
  (59 other events, 930.7 us)
Sparse Core Ops, SparseCore 0:
  9.6 19.4 all-gather.4
  30.6 34.4 all-gather.8
  120.4 41.6 all-gather.6
  250.1 35.8 all-gather.10
  597.4 41.7 reduce-scatter.5
  641.8 24.8 reduce-scatter.7
  669.2 44.4 reduce-scatter.11
  716.5 44.4 reduce-scatter.9
  763.5 44.5 reduce-scatter.13

commit v2 on v1

--- a/solution.py
+++ b/solution.py
@@ -576,25 +576,34 @@
     return lax.ppermute(v, "ctx", [(i, (i + by) % n) for i in range(n)])
 
 
-def spread(v):
-    parts = [v]
-    for _ in range(lax.axis_size("ctx") - 1):
-        parts.append(shift(parts[-1], 1))
-    return jnp.concatenate(parts + [swap(p, "row") for p in parts], axis=0)
-
-
-def collect(terms, tok):
+def spread(v, *beside):
+    own, other, held = [v], [], None
+    for i in range(lax.axis_size("ctx") - 1):
+        more = beside[i](held) if i < len(beside) else held
+        ahead, across, held = lax.optimization_barrier(
+            (shift(own[-1], 1), swap(own[-1], "row"), more)
+        )
+        own.append(ahead)
+        other.append(across)
+    rows = jnp.concatenate(own + other + [swap(own[-1], "row")], axis=0)
+    return (rows, held) if beside else rows
+
+
+def collect(other, own, tok):
     n = lax.axis_size("ctx")
-    other = terms(1).astype(BF16).reshape(n, tok, -1)
-    crossed = [swap(other[c], "row") for c in reversed(range(n))][::-1]
-    own = terms(0).reshape(n, tok, -1)
-    total = None
-    for c in reversed(range(n)):
-        part = own[c] + crossed[c].astype(F32)
-        if total is not None:
-            part = part + shift(total.astype(BF16), -1).astype(F32)
-        total = part
+    other = other.astype(BF16).reshape(n, tok, -1)
+    own = own.astype(F32).reshape(n, tok, -1)
+    total = own[n - 1] + swap(other[n - 1], "row").astype(F32)
+    for c in reversed(range(n - 1)):
+        ahead, across = lax.optimization_barrier(
+            (shift(total.astype(BF16), -1), swap(other[c], "row"))
+        )
+        total = own[c] + across.astype(F32) + ahead.astype(F32)
     return total
+
+
+def after(v, first):
+    return lax.optimization_barrier((v, first))[0]
 
 
 def by_side(index, mine, theirs):
@@ -657,9 +666,11 @@
     ).transpose(1, 0, 2)
     x32 = tokens.astype(F32)
     scale_one = lax.rsqrt(jnp.mean(x32 * x32, axis=-1, keepdims=True) + EPS)
-    rows_one = spread((x32 * scale_one).astype(BF16))
-    mine = lax.all_to_all(send, FAR, split_axis=0, concat_axis=0, tiled=True)
-    other = swap(mine, "col")
+    rows_one, (mine, other) = spread(
+        (x32 * scale_one).astype(BF16),
+        lambda _: lax.all_to_all(send, FAR, split_axis=0, concat_axis=0, tiled=True),
+        lambda mine: (mine, swap(mine, "col")),
+    )
     mine_pair = by_side(core_at, mine, swap(mine, "core"))
     other_pair = by_side(core_at, other, swap(other, "core"))
     halves = [by_side(col_at, a, b) for a, b in zip(mine_pair, other_pair, strict=True)]
@@ -669,6 +680,16 @@
     w_heads = w_ext[:, : 3 * group]
     gain_two = w_ext[:, 3 * group].astype(F32)[None, :]
 
+    dy_all = lax.all_gather(after(cotangent, rows_one), FAR, axis=0)
+    dy_rows = jnp.concatenate(
+        [
+            lax.dynamic_index_in_dim(
+                dy_all.reshape(far, tok, width), 2 * slot_ctx[i] + slot_row[i], keepdims=False
+            )
+            for i in range(far)
+        ],
+        axis=0,
+    )
     out_rows = lax.all_gather(w_out, NEAR, axis=0, tiled=True)
     gate_w, up_w, down_w = (
         lax.all_gather(w, NEAR, axis=0, tiled=True) for w in (w_gate, w_up, w_down)
@@ -690,13 +711,17 @@
     def cut(v, r, axis):
         return lax.slice_in_dim(v, r * rows_half, (r + 1) * rows_half, axis=axis)
 
-    mid = x32 + collect(
-        lambda r: jnp.einsum("et,ed->td", cut(attn, r, 1), out_rows, preferred_element_type=F32), tok
-    )
+    def halves_of(term, axis, *parts):
+        return [term(*(cut(p, r, axis) for p in parts)) for r in (1, 0)]
+
+    def out_term(rows):
+        return jnp.einsum("et,ed->td", rows, out_rows, preferred_element_type=F32)
+
+    mid = x32 + collect(*halves_of(out_term, 1, attn), tok)
     scale_two = lax.rsqrt(jnp.mean(mid * mid, axis=-1, keepdims=True) + EPS)
     normed_two = (mid * scale_two * gain_two).astype(BF16)
+    normed_two, dy_rows = lax.optimization_barrier((normed_two, dy_rows))
     rows_two = spread(normed_two)
-    dy_rows = spread(cotangent)
     gate = rows_by(rows_two, gate_w)
     up = rows_by(rows_two, up_w)
     silu_val, slope = silu_parts(gate)
@@ -704,15 +729,20 @@
     dhidden = rows_by(dy_rows, down_w)
     dgate = (dhidden * up * slope).astype(BF16)
     dup = (dhidden * silu_val).astype(BF16)
-    dnormed_two = collect(
-        lambda r: jnp.dot(cut(dgate, r, 0), gate_w, preferred_element_type=F32)
-        + jnp.dot(cut(dup, r, 0), up_w, preferred_element_type=F32),
-        tok,
-    )
-    branch = collect(
-        lambda r: jnp.dot(cut(hidden, r, 0), down_w, preferred_element_type=F32), tok
-    )
-    block_out = (mid + branch).astype(BF16)
+
+    def rows_term(dgate, dup):
+        return jnp.dot(dgate, gate_w, preferred_element_type=F32) + jnp.dot(
+            dup, up_w, preferred_element_type=F32
+        )
+
+    def branch_term(hidden):
+        return jnp.dot(hidden, down_w, preferred_element_type=F32).astype(BF16)
+
+    dn_other, dn_own = halves_of(rows_term, 0, dgate, dup)
+    dn_other, dgate, dup, hidden = lax.optimization_barrier((dn_other, dgate, dup, hidden))
+    dnormed_two = collect(dn_other, dn_own, tok)
+    branch_terms = halves_of(branch_term, 0, hidden)
+    dnormed_two, branch_terms = lax.optimization_barrier((dnormed_two, branch_terms))
     gate_grad, up_grad, down_grad = (
         lax.psum_scatter(
             outer_sum(left, right).astype(BF16), NEAR, scatter_dimension=0, tiled=True
@@ -727,23 +757,32 @@
         + scale_two * scaled_two
         - mid * scale_two**3 * jnp.mean(scaled_two * mid, axis=-1, keepdims=True)
     )
-    dmid_rows = spread(dmid.astype(BF16))
+    dmid_rows, gate_grad = lax.optimization_barrier((spread(dmid.astype(BF16)), gate_grad))
+    branch = collect(*after(branch_terms, dmid_rows), tok)
+    block_out = (mid + branch).astype(BF16)
     dattn = jnp.einsum("ed,td->et", out_rows, dmid_rows, preferred_element_type=F32).astype(BF16)
     dattn_head = lax.all_to_all(
         dattn.reshape(near, HD, rows_here), NEAR, split_axis=0, concat_axis=0, tiled=True
     )
+    dattn_head, up_grad = lax.optimization_barrier((dattn_head, up_grad))
+    dqkv_head = attn_bwd(block_slot, seq, o32, lse, dattn_head, seq_cos, seq_sin, far)
+    dqkv_head, down_grad = lax.optimization_barrier((dqkv_head, down_grad))
+    dqkv = lax.all_to_all(dqkv_head, NEAR, split_axis=0, concat_axis=0, tiled=True)
+    dqkv = dqkv.reshape(near, 3, HD, rows_here).transpose(1, 0, 2, 3).reshape(3 * group, rows_here)
+    dqkv, block_out = lax.optimization_barrier((dqkv, block_out))
+
+    def heads_term(rows):
+        return jnp.einsum("et,de->td", rows, w_heads, preferred_element_type=F32)
+
+    dx_other, dx_own = halves_of(heads_term, 1, dqkv)
+    dx_other, dqkv, attn, dmid_rows = lax.optimization_barrier((dx_other, dqkv, attn, dmid_rows))
+    scaled_one = collect(dx_other, dx_own, tok)
     out_grad = lax.psum_scatter(
         jnp.einsum("et,td->ed", attn, dmid_rows, preferred_element_type=F32).astype(BF16),
         NEAR,
         scatter_dimension=0,
         tiled=True,
     ).astype(F32)
-    dqkv_head = attn_bwd(block_slot, seq, o32, lse, dattn_head, seq_cos, seq_sin, far)
-    dqkv = lax.all_to_all(dqkv_head, NEAR, split_axis=0, concat_axis=0, tiled=True)
-    dqkv = dqkv.reshape(near, 3, HD, rows_here).transpose(1, 0, 2, 3).reshape(3 * group, rows_here)
-    scaled_one = collect(
-        lambda r: jnp.einsum("et,de->td", cut(dqkv, r, 1), w_heads, preferred_element_type=F32), tok
-    )
     input_grad = (
         dmid
         + scale_one * scaled_one

time: 828 us -> 675 us (0.82)
  waiting for transfers between devices: 447 us -> 245 us
  local copies, waits for them, and re-layouts: 36.6 us -> 51 us
  other arithmetic: 42.2 us -> 55.8 us
  between operations: 15 us -> 25.5 us
    reduce_scatter x3, waiting for transfers between devices: 95.4 us -> 0.01 us  [per_device_split(): lax.psum_scatter(outer_sum(left, right).astype(BF16), NEAR, scatter_dimen...]
    ppermute x35 -> x31, waiting for transfers between devices: 141 us -> 78.6 us  [swap(): return lax.ppermute(v, axis, [(0, 1), (1, 0)])]
    ppermute x24 -> x21, waiting for transfers between devices: 154 us -> 104 us  [shift(): return lax.ppermute(v, 'ctx', [(i, (i + by) % n) for i in range(n)])]
    convert_element_type x12 -> x15, other arithmetic: 4.92 us -> 18.8 us  [the longest x12 13.5 us: collect(): total.astype(BF16)]
    reduce_scatter x1, waiting for transfers between devices: 0.01 us -> 12.9 us  [per_device_split(): lax.psum_scatter(jnp.einsum('et,td->ed', attn, dmid_rows, preferred_eleme...]
    unnamed x95 -> x132, local copies, waits for them, and re-layouts: 23.2 us -> 35.8 us
    ppermute x24 -> x21, starting transfers between devices: 55.6 us -> 45.5 us  [shift(): return lax.ppermute(v, 'ctx', [(i, (i + by) % n) for i in range(n)])]
    dot_general x10, matrix products: 22.7 us -> 32 us  [the longest x2 9.85 us: branch_term(): return jnp.dot(hidden, down_w, preferred_element_type=F32).astype(BF16)]
  transfers between devices with their start and end apart: 74 -> 68, of which waited for: 49 -> 37; matrix products, arithmetic and copies ran while one was open for 17% -> 23% of each run, Pallas kernels for 3% -> 9%
where the time goes in v2:
time: 675 us; the launch traced here: 665 us
  waiting for transfers between devices  245 us (36%)
  starting transfers between devices  123 us (18%)
  matrix products  106 us (16%)
  Pallas kernels  57.9 us (9%)
  other arithmetic  55.8 us (8%)
  local copies, waits for them, and re-layouts  51 us (8%)
  between operations  25.5 us (4%)
    ppermute x21, waiting for transfers between devices, shift(): return lax.ppermute(v, 'ctx', [(i, (i + by) % n) for i in range(n)])  104 us
    ppermute x31, waiting for transfers between devices, swap(): return lax.ppermute(v, axis, [(0, 1), (1, 0)])  78.6 us
    ppermute x21, starting transfers between devices, shift(): return lax.ppermute(v, 'ctx', [(i, (i + by) % n) for i in range(n)])  45.5 us
    ppermute x31, starting transfers between devices, swap(): return lax.ppermute(v, axis, [(0, 1), (1, 0)])  42.6 us
    unnamed x132, local copies, waits for them, and re-layouts  35.8 us
    pallas_call x1, Pallas kernels, attn_bwd(): pl.pallas_call(functools.partial(attn_bwd_kernel, blocks=blocks, width=co...  34.4 us
    dot_general x3, matrix products, rows_by(): jnp.einsum('td,fd->tf', left, right, preferred_element_type=jnp.float32)  33.9 us
    dot_general x3, matrix products, outer_sum(): jnp.einsum('tf,td->fd', left, right, preferred_element_type=jnp.float32)  24.4 us
  transfers between devices with their start and end apart: 68, of which 37 were waited for; matrix products, arithmetic and copies ran while one was open for 23% of the time, Pallas kernels for 9%

profile of v2, /device:TPU:0, one launch (start us, length us, event | category | flops | bytes accessed | tf_op | source)
XLA Modules:
  0.0 664.5 jit_solution(5414568249651830459)
XLA Ops:
  11.4 7.3 %all-to-all-start = ((bf16[8,64,896]{2,1,0:T(8,128)(2,1)}), bf16[8,64,896]{2,1,0:T(8,128)(2,1)S(1)}, u32[]{:S(2)}, u32[]{:S(2)}) async-start(bf16[8,64,896]{2,1,0:T(8,128)(2,1)} %copy.58), calls=%async_computation | async-start | bytes 1835008 | tf_op jit(solution)/shard_map/all_to_all | solution.py:671
  23.8 25.0 %collective-permute-done = bf16[128,2048]{1,0:T(8,128)(2,1)S(1)} collective-permute-done((bf16[128,2048]{1,0:T(8,128)(2,1)S(1)}, bf16[128,2048]{1,0:T(8,128)(2,1)S(1)}, u32[]{:S(2)}, u32[]{:S(2)}) %collective-permute-start) | collective-permute-done | bytes 524320 | tf_op jit(solution)/shard_map/ppermute | solution.py:576
  48.8 4.1 all-to-all-done
  55.7 12.6 %collective-permute-done.2 = bf16[128,2048]{1,0:T(8,128)(2,1)} collective-permute-done((bf16[128,2048]{1,0:T(8,128)(2,1)S(1)}, bf16[128,2048]{1,0:T(8,128)(2,1)}, u32[]{:S(2)}, u32[]{:S(2)}) %collective-permute-start.2) | collective-permute-done | bytes 524320 | tf_op jit(solution)/shard_map/ppermute | solution.py:576
  68.3 5.3 collective-permute-done.4
  78.4 8.7 %collective-permute-done.5 = bf16[128,2048]{1,0:T(8,128)(2,1)} collective-permute-done((bf16[128,2048]{1,0:T(8,128)(2,1)}, bf16[128,2048]{1,0:T(8,128)(2,1)}, u32[]{:S(2)}, u32[]{:S(2)}) %collective-permute-start.5) | collective-permute-done | bytes 524320 | tf_op jit(solution)/shard_map/ppermute | solution.py:576
  95.2 4.0 collective-permute-done.9
  120.1 19.4 %all-to-all-done.1.qkv_ref = bf16[4,192,1024]{2,1,0:T(8,128)(2,1)S(1)} async-done(((bf16[4,192,1024]{2,1,0:T(8,128)(2,1)}), bf16[4,192,1024]{2,1,0:T(8,128)(2,1)S(1)}, u32[]{:S(2)}, u32[]{:S(2)}) %all-to-all-start.1) | async-done | bytes 1572896 | tf_op jit(solution)/shard_map/all_to_all | solution.py:705
  139.4 23.5 %attn_fwd.1 = (bf16[4,64,1024]{2,1,0:T(8,128)(2,1)}, f32[64,4096]{1,0:T(8,128)S(1)}, f32[1,4096]{1,0:T(1,128)S(1)}, bf16[192,4096]{1,0:T(8,128)(2,1)S(1)}) custom-call(s32[8]{0:T(128)S(1)} %select_reduce_fusion.slot_ref, bf16[4,192,1024]{2,1,0:T(8,128)(2,1)S(1)} %all-to-all-done.1.qkv_ref), custom_call_target="tpu_custom_call" | custom-call | flops 8589934592 | bytes 8388608 | tf_op jit(solution)/shard_map/attn_fwd/pallas_call | solution.py:434
  167.5 8.7 %all-to-all-done.2 = bf16[4,64,1024]{2,1,0:T(8,128)(2,1)S(1)} async-done(((bf16[4,64,1024]{2,1,0:T(8,128)(2,1)}), bf16[4,64,1024]{2,1,0:T(8,128)(2,1)S(1)}, u32[]{:S(2)}, u32[]{:S(2)}) %all-to-all-start.2) | async-done | bytes 524320 | tf_op jit(solution)/shard_map/all_to_all | solution.py:707
  182.2 12.0 %collective-permute-done.10 = bf16[128,2048]{1,0:T(8,128)(2,1)S(1)} collective-permute-done((bf16[128,2048]{1,0:T(8,128)(2,1)S(1)}, bf16[128,2048]{1,0:T(8,128)(2,1)S(1)}, u32[]{:S(2)}, u32[]{:S(2)}) %collective-permute-start.10) | collective-permute-done | bytes 524320 | tf_op jit(solution)/shard_map/ppermute | solution.py:571
  197.9 7.6 %collective-permute-done.12 = bf16[128,2048]{1,0:T(8,128)(2,1)S(1)} collective-permute-done((bf16[128,2048]{1,0:T(8,128)(2,1)S(1)}, bf16[128,2048]{1,0:T(8,128)(2,1)S(1)}, u32[]{:S(2)}, u32[]{:S(2)}) %collective-permute-start.12) | collective-permute-done | bytes 524320 | tf_op jit(solution)/shard_map/ppermute | solution.py:571
  211.2 5.5 collective-permute-done.14
  217.6 4.3 collective-permute-start.15
  243.9 9.5 %collective-permute-done.17 = bf16[128,2048]{1,0:T(8,128)(2,1)} collective-permute-done((bf16[128,2048]{1,0:T(8,128)(2,1)S(1)}, bf16[128,2048]{1,0:T(8,128)(2,1)}, u32[]{:S(2)}, u32[]{:S(2)}) %collective-permute-start.17) | collective-permute-done | bytes 524320 | tf_op jit(solution)/shard_map/ppermute | solution.py:576
  256.0 10.0 %fusion.69 = f32[1024,1024]{1,0:T(8,128)} fusion(bf16[1024,2048]{1,0:T(8,128)(2,1)} %copy-done.33, bf16[1024,2048]{1,0:T(8,128)(2,1)} %all-gather.9.cloned.1.call-done), kind=kOutput, calls=%fused_computation.198 | convolution fusion | flops 4294967296 | bytes 12582912 | tf_op jit(solution)/shard_map/td,fd->tf/dot_general | solution.py:55
  290.4 10.0 %fusion.70 = f32[1024,1024]{1,0:T(8,128)} fusion(bf16[1024,2048]{1,0:T(8,128)(2,1)} %constant_dynamic-update-slice_fusion.8, bf16[1024,2048]{1,0:T(8,128)(2,1)} %all-gather.13.cloned.1.call-done), kind=kOutput, calls=%fused_computation.199 | convolution fusion | flops 4294967296 | bytes 12582912 | tf_op jit(solution)/shard_map/td,fd->tf/dot_general | solution.py:55
  300.4 14.0 %multiply_convert_fusion = (bf16[1024,1024]{1,0:T(8,128)(2,1)}, bf16[1024,1024]{1,0:T(8,128)(2,1)}, bf16[1024,1024]{1,0:T(8,128)(2,1)S(1)}) fusion(f32[1024,1024]{1,0:T(8,128)} %fusion.70, f32[1024,1024]{1,0:T(8,128)} %fusion.69, bf16[1024,2048]{1,0:T(8,128)(2,1)} %constant_dynamic-update-slice_fusion.8, bf16[1024,2048]{1,0:T(8,128)(2,1)} %all-gather.11.cloned.1.call-done), kind=kOutput, calls=%fused_computation | convolution fusion | flops 4310695936 | bytes 23068672 | tf_op jit(solution)/shard_map/td,fd->tf/dot_general | solution.py:55
  314.4 4.4 fusion.27
  322.5 8.6 %convolution_convert_fusion.2 = bf16[1024,2048]{1,0:T(8,128)(2,1)} fusion(bf16[1024,1024]{1,0:T(8,128)(2,1)S(1)} %copy-done.50, bf16[1024,2048]{1,0:T(8,128)(2,1)} %constant_dynamic-update-slice_fusion.8), kind=kOutput, calls=%fused_computation.7 | convolution fusion | flops 4297064448 | bytes 10485760 | tf_op jit(solution)/shard_map/tf,td->fd/dot_general | solution.py:59
  331.2 9.4 %convolution_convert_fusion.1 = bf16[1024,2048]{1,0:T(8,128)(2,1)} fusion(bf16[1024,1024]{1,0:T(8,128)(2,1)} %copy-done.46, bf16[1024,2048]{1,0:T(8,128)(2,1)} %constant_dynamic-update-slice_fusion.8), kind=kOutput, calls=%fused_computation.6 | convolution fusion | flops 4297064448 | bytes 10485760 | tf_op jit(solution)/shard_map/tf,td->fd/dot_general | solution.py:59
  348.1 3.7 fusion.36
  354.3 4.6 collective-permute-done.24
  359.8 5.2 collective-permute-start.25
  365.0 6.5 convolution_convert_fusion
  371.5 4.4 collective-permute-done.25
  377.6 4.4 collective-permute-start.27
  382.0 6.2 convolution_convert_fusion.5
  390.7 4.3 collective-permute-start.29
  398.8 6.7 %collective-permute-done.29 = bf16[128,2048]{1,0:T(8,128)(2,1)S(1)} collective-permute-done((bf16[128,2048]{1,0:T(8,128)(2,1)S(1)}, bf16[128,2048]{1,0:T(8,128)(2,1)S(1)}, u32[]{:S(2)}, u32[]{:S(2)}) %collective-permute-start.29) | collective-permute-done | bytes 524320 | tf_op jit(solution)/shard_map/ppermute | solution.py:576
  411.1 8.7 %collective-permute-done.31 = bf16[128,2048]{1,0:T(8,128)(2,1)S(1)} collective-permute-done((bf16[128,2048]{1,0:T(8,128)(2,1)S(1)}, bf16[128,2048]{1,0:T(8,128)(2,1)S(1)}, u32[]{:S(2)}, u32[]{:S(2)}) %collective-permute-start.31) | collective-permute-done | bytes 524320 | tf_op jit(solution)/shard_map/ppermute | solution.py:576
  422.1 8.7 %collective-permute-done.33 = bf16[128,2048]{1,0:T(8,128)(2,1)S(1)} collective-permute-done((bf16[128,2048]{1,0:T(8,128)(2,1)S(1)}, bf16[128,2048]{1,0:T(8,128)(2,1)S(1)}, u32[]{:S(2)}, u32[]{:S(2)}) %collective-permute-start.33) | collective-permute-done | bytes 524320 | tf_op jit(solution)/shard_map/ppermute | solution.py:576
  430.8 4.3 collective-permute-start.35
  450.2 5.3 collective-permute-done.37
  462.4 4.3 convolution_convert_fusion.8
  466.6 11.5 %all-to-all-start.3 = ((bf16[4,64,1024]{2,1,0:T(8,128)(2,1)}), bf16[4,64,1024]{2,1,0:T(8,128)(2,1)S(1)}, u32[]{:S(2)}, u32[]{:S(2)}) async-start(bf16[4,64,1024]{2,1,0:T(8,128)(2,1)} %bitcast.34), calls=%async_computation.4 | async-start | bytes 1048576 | tf_op jit(solution)/shard_map/all_to_all | solution.py:764
  482.5 3.9 collective-permute-start.39
  501.0 4.7 collective-permute-start.41
  506.9 34.4 %attn_bwd.1 = bf16[4,192,1024]{2,1,0:T(8,128)(2,1)} custom-call(s32[8]{0:T(128)S(1)} %select_reduce_fusion.slot_ref, bf16[192,4096]{1,0:T(8,128)(2,1)S(1)} %get-tuple-element.97.seq_ref, f32[64,4096]{1,0:T(8,128)S(1)} %copy-done.1, f32[1,4096]{1,0:T(1,128)S(1)} %get-tuple-element.99.lse_ref, bf16[4,64,1024]{2,1,0:T(8,128)(2,1)S(1)} %all-to-all-done.3.do_ref, ...), custom_call_target="tpu_custom_call" | custom-call | flops 21474836480 | bytes 8388608 | tf_op jit(solution)/shard_map/attn_bwd/pallas_call | solution.py:545
  548.4 16.7 %all-to-all-done.4 = bf16[4,192,1024]{2,1,0:T(8,128)(2,1)S(1)} async-done(((bf16[4,192,1024]{2,1,0:T(8,128)(2,1)}), bf16[4,192,1024]{2,1,0:T(8,128)(2,1)S(1)}, u32[]{:S(2)}, u32[]{:S(2)}) %all-to-all-start.4) | async-done | bytes 1572896 | tf_op jit(solution)/shard_map/all_to_all | solution.py:770
  584.8 10.9 %collective-permute-done.45 = bf16[128,2048]{1,0:T(8,128)(2,1)S(1)} collective-permute-done((bf16[128,2048]{1,0:T(8,128)(2,1)S(1)}, bf16[128,2048]{1,0:T(8,128)(2,1)S(1)}, u32[]{:S(2)}, u32[]{:S(2)}) %collective-permute-start.45) | collective-permute-done | bytes 524320 | tf_op jit(solution)/shard_map/ppermute | solution.py:571
  595.9 4.4 convolution_convert_fusion.7
  601.4 5.5 collective-permute-done.47
  611.3 7.0 %collective-permute-done.49 = bf16[128,2048]{1,0:T(8,128)(2,1)} collective-permute-done((bf16[128,2048]{1,0:T(8,128)(2,1)}, bf16[128,2048]{1,0:T(8,128)(2,1)}, u32[]{:S(2)}, u32[]{:S(2)}) %collective-permute-start.49) | collective-permute-done | bytes 524320 | tf_op jit(solution)/shard_map/ppermute | solution.py:571
  619.9 4.6 all-to-all-start.5
  627.0 3.9 collective-permute-start.50
  630.8 12.9 %reduce-scatter.14.cloned.1.call-done = bf16[64,2048]{1,0:T(8,128)(2,1)} async-done(((bf16[256,2048]{1,0:T(8,128)(2,1)}), bf16[64,2048]{1,0:T(8,128)(2,1)}) %reduce-scatter.14.cloned.1.call-update) | async-done | bytes 262160 | tf_op jit(solution)/shard_map/reduce_scatter | solution.py:780
  645.5 4.4 collective-permute-done.50
  (325 shorter events, 223.6 us)
Async XLA Ops:
  11.4 41.5 %all-to-all-start = ((bf16[8,64,896]{2,1,0:T(8,128)(2,1)}), bf16[8,64,896]{2,1,0:T(8,128)(2,1)S(1)}, u32[]{:S(2)}, u32[]{:S(2)}) async-start(bf16[8,64,896]{2,1,0:T(8,128)(2,1)} %copy.58), calls=%async_computation | async-start | bytes 1835008 | tf_op jit(solution)/shard_map/all_to_all | solution.py:671
  18.6 148.8 %all-gather.7.cloned.1.call-start = ((), (), s32[]{:S(2)}) async-start(), calls=%async_computation.11 | async-start | bytes 1310720 | tf_op jit(solution)/shard_map/all_gather | solution.py:693
  20.4 28.4 %collective-permute-start = (bf16[128,2048]{1,0:T(8,128)(2,1)S(1)}, bf16[128,2048]{1,0:T(8,128)(2,1)S(1)}, u32[]{:S(2)}, u32[]{:S(2)}) collective-permute-start(bf16[128,2048]{1,0:T(8,128)(2,1)S(1)} %get-tuple-element.171), channel_id=1, source_target_pairs={{0,8},{8,16},{16,24},{24,0},{1,9},{9,17},{17,25},{25,1},{2,10},{10... | collective-permute-start | bytes 1572872 | tf_op jit(solution)/shard_map/ppermute | solution.py:576
  22.4 26.5 %collective-permute-start.1 = (bf16[128,2048]{1,0:T(8,128)(2,1)S(1)}, bf16[128,2048]{1,0:T(8,128)(2,1)S(1)}, u32[]{:S(2)}, u32[]{:S(2)}) collective-permute-start(bf16[128,2048]{1,0:T(8,128)(2,1)S(1)} %get-tuple-element.171), channel_id=1, source_target_pairs={{0,4},{4,0},{1,5},{5,1},{2,6},{6,2},{3,7},{7,3},{8,12},{12,8},{9,1... | collective-permute-start | bytes 1572872 | tf_op jit(solution)/shard_map/ppermute | solution.py:571
  52.9 20.7 %collective-permute-start.4 = (bf16[8,64,896]{2,1,0:T(8,128)(2,1)S(1)}, bf16[8,64,896]{2,1,0:T(8,128)(2,1)S(1)}, u32[]{:S(2)}, u32[]{:S(2)}) collective-permute-start(bf16[8,64,896]{2,1,0:T(8,128)(2,1)S(1)} %all-to-all-done), channel_id=1, source_target_pairs={{0,2},{2,0},{1,3},{3,1},{4,6},{6,4},{5,7},{7,5},{8,10},{10,8},{9,1... | collective-permute-start | bytes 2752520 | tf_op jit(solution)/shard_map/ppermute | solution.py:571
  54.4 13.9 %collective-permute-start.2 = (bf16[128,2048]{1,0:T(8,128)(2,1)S(1)}, bf16[128,2048]{1,0:T(8,128)(2,1)}, u32[]{:S(2)}, u32[]{:S(2)}) collective-permute-start(bf16[128,2048]{1,0:T(8,128)(2,1)S(1)} %collective-permute-done), channel_id=1, source_target_pairs={{0,8},{8,16},{16,24},{24,0},{1,9},{9,17},{17,25},{25,1},{2,10},{10... | collective-permute-start | bytes 1572872 | tf_op jit(solution)/shard_map/ppermute | solution.py:576
  54.4 13.9 %collective-permute-start.3 = (bf16[128,2048]{1,0:T(8,128)(2,1)S(1)}, bf16[128,2048]{1,0:T(8,128)(2,1)S(1)}, u32[]{:S(2)}, u32[]{:S(2)}) collective-permute-start(bf16[128,2048]{1,0:T(8,128)(2,1)S(1)} %collective-permute-done), channel_id=1, source_target_pairs={{0,4},{4,0},{1,5},{5,1},{2,6},{6,2},{3,7},{7,3},{8,12},{12,8},{9,1... | collective-permute-start | bytes 1572872 | tf_op jit(solution)/shard_map/ppermute | solution.py:571
  73.6 13.5 %collective-permute-start.5 = (bf16[128,2048]{1,0:T(8,128)(2,1)}, bf16[128,2048]{1,0:T(8,128)(2,1)}, u32[]{:S(2)}, u32[]{:S(2)}) collective-permute-start(bf16[128,2048]{1,0:T(8,128)(2,1)} %collective-permute-done.2), channel_id=1, source_target_pairs={{0,8},{8,16},{16,24},{24,0},{1,9},{9,17},{17,25},{25,1},{2,10},{10... | collective-permute-start | bytes 1572872 | tf_op jit(solution)/shard_map/ppermute | solution.py:576
  73.6 13.5 %collective-permute-start.6 = (bf16[128,2048]{1,0:T(8,128)(2,1)}, bf16[128,2048]{1,0:T(8,128)(2,1)}, u32[]{:S(2)}, u32[]{:S(2)}) collective-permute-start(bf16[128,2048]{1,0:T(8,128)(2,1)} %collective-permute-done.2), channel_id=1, source_target_pairs={{0,4},{4,0},{1,5},{5,1},{2,6},{6,2},{3,7},{7,3},{8,12},{12,8},{9,1... | collective-permute-start | bytes 1572872 | tf_op jit(solution)/shard_map/ppermute | solution.py:571
  75.6 161.3 %all-gather.15.cloned.1.call-start = ((), (), s32[]{:S(2)}) async-start(), calls=%async_computation.20 | async-start | bytes 4718592 | tf_op jit(solution)/shard_map/all_gather | solution.py:683
  100.0 156.0 %all-gather.9.cloned.1.call-start = ((), (), s32[]{:S(2)}) async-start(), calls=%async_computation.12 | async-start | bytes 5242880 | tf_op jit(solution)/shard_map/all_gather | solution.py:695
  115.8 23.6 %all-to-all-start.1 = ((bf16[4,192,1024]{2,1,0:T(8,128)(2,1)}), bf16[4,192,1024]{2,1,0:T(8,128)(2,1)S(1)}, u32[]{:S(2)}, u32[]{:S(2)}) async-start(bf16[4,192,1024]{2,1,0:T(8,128)(2,1)} %bitcast.14), calls=%async_computation.1 | async-start | bytes 3145728 | tf_op jit(solution)/shard_map/all_to_all | solution.py:705
  119.4 171.0 %all-gather.13.cloned.1.call-start = ((), (), s32[]{:S(2)}) async-start(), calls=%async_computation.14 | async-start | bytes 5242880 | tf_op jit(solution)/shard_map/all_gather | solution.py:695
  163.9 12.3 %all-to-all-start.2 = ((bf16[4,64,1024]{2,1,0:T(8,128)(2,1)}), bf16[4,64,1024]{2,1,0:T(8,128)(2,1)S(1)}, u32[]{:S(2)}, u32[]{:S(2)}) async-start(bf16[4,64,1024]{2,1,0:T(8,128)(2,1)} %get-tuple-element.100), calls=%async_computation.2 | async-start | bytes 1048576 | tf_op jit(solution)/shard_map/all_to_all | solution.py:707
  167.4 133.0 %all-gather.11.cloned.1.call-start = ((), (), s32[]{:S(2)}) async-start(), calls=%async_computation.13 | async-start | bytes 5242880 | tf_op jit(solution)/shard_map/all_gather | solution.py:695
  179.4 14.8 %collective-permute-start.10 = (bf16[128,2048]{1,0:T(8,128)(2,1)S(1)}, bf16[128,2048]{1,0:T(8,128)(2,1)S(1)}, u32[]{:S(2)}, u32[]{:S(2)}) collective-permute-start(bf16[128,2048]{1,0:T(8,128)(2,1)S(1)} %get-tuple-element.198), channel_id=1, source_target_pairs={{0,4},{4,0},{1,5},{5,1},{2,6},{6,2},{3,7},{7,3},{8,12},{12,8},{9,1... | collective-permute-start | bytes 1572872 | tf_op jit(solution)/shard_map/ppermute | solution.py:571
  181.1 24.4 %collective-permute-start.12 = (bf16[128,2048]{1,0:T(8,128)(2,1)S(1)}, bf16[128,2048]{1,0:T(8,128)(2,1)S(1)}, u32[]{:S(2)}, u32[]{:S(2)}) collective-permute-start(bf16[128,2048]{1,0:T(8,128)(2,1)S(1)} %get-tuple-element.197), channel_id=1, source_target_pairs={{0,4},{4,0},{1,5},{5,1},{2,6},{6,2},{3,7},{7,3},{8,12},{12,8},{9,1... | collective-permute-start | bytes 1572872 | tf_op jit(solution)/shard_map/ppermute | solution.py:571
  196.2 20.5 %collective-permute-start.14 = (bf16[128,2048]{1,0:T(8,128)(2,1)S(1)}, bf16[128,2048]{1,0:T(8,128)(2,1)S(1)}, u32[]{:S(2)}, u32[]{:S(2)}) collective-permute-start(bf16[128,2048]{1,0:T(8,128)(2,1)S(1)} %get-tuple-element.196), channel_id=1, source_target_pairs={{0,4},{4,0},{1,5},{5,1},{2,6},{6,2},{3,7},{7,3},{8,12},{12,8},{9,1... | collective-permute-start | bytes 1572872 | tf_op jit(solution)/shard_map/ppermute | solution.py:571
  209.5 25.3 %collective-permute-start.16 = (bf16[128,2048]{1,0:T(8,128)(2,1)}, bf16[128,2048]{1,0:T(8,128)(2,1)}, u32[]{:S(2)}, u32[]{:S(2)}) collective-permute-start(bf16[128,2048]{1,0:T(8,128)(2,1)} %get-tuple-element.195), channel_id=1, source_target_pairs={{0,4},{4,0},{1,5},{5,1},{2,6},{6,2},{3,7},{7,3},{8,12},{12,8},{9,1... | collective-permute-start | bytes 1572872 | tf_op jit(solution)/shard_map/ppermute | solution.py:571
  217.6 17.2 %collective-permute-start.15 = (bf16[128,2048]{1,0:T(8,128)(2,1)S(1)}, bf16[128,2048]{1,0:T(8,128)(2,1)}, u32[]{:S(2)}, u32[]{:S(2)}) collective-permute-start(bf16[128,2048]{1,0:T(8,128)(2,1)S(1)} %fusion.42), channel_id=1, source_target_pairs={{0,24},{8,0},{16,8},{24,16},{1,25},{9,1},{17,9},{25,17},{2,26},{10... | collective-permute-start | bytes 1572872 | tf_op jit(solution)/shard_map/ppermute | solution.py:576
  221.9 234.4 %reduce-scatter.6.cloned.1.call-start = ((), (), s32[]{:S(2)}) async-start(), calls=%async_computation.15 | async-start | bytes 5242880 | tf_op jit(solution)/shard_map/reduce_scatter | solution.py:747
  266.4 13.7 %collective-permute-start.22 = (bf16[128,2048]{1,0:T(8,128)(2,1)}, bf16[128,2048]{1,0:T(8,128)(2,1)S(1)}, u32[]{:S(2)}, u32[]{:S(2)}) collective-permute-start(bf16[128,2048]{1,0:T(8,128)(2,1)} %collective-permute-done.19), channel_id=1, source_target_pairs={{0,4},{4,0},{1,5},{5,1},{2,6},{6,2},{3,7},{7,3},{8,12},{12,8},{9,1... | collective-permute-start | bytes 1572872 | tf_op jit(solution)/shard_map/ppermute | solution.py:571
  331.1 158.0 %reduce-scatter.8.cloned.1.call-start = ((), (), s32[]{:S(2)}) async-start(), calls=%async_computation.16 | async-start | bytes 5242880 | tf_op jit(solution)/shard_map/reduce_scatter | solution.py:747
  340.5 151.4 %reduce-scatter.10.cloned.1.call-start = ((), (), s32[]{:S(2)}) async-start(), calls=%async_computation.17 | async-start | bytes 5242880 | tf_op jit(solution)/shard_map/reduce_scatter | solution.py:747
  344.1 14.9 %collective-permute-start.24 = (bf16[128,2048]{1,0:T(8,128)(2,1)S(1)}, bf16[128,2048]{1,0:T(8,128)(2,1)S(1)}, u32[]{:S(2)}, u32[]{:S(2)}) collective-permute-start(bf16[128,2048]{1,0:T(8,128)(2,1)S(1)} %get-tuple-element.194), channel_id=1, source_target_pairs={{0,4},{4,0},{1,5},{5,1},{2,6},{6,2},{3,7},{7,3},{8,12},{12,8},{9,1... | collective-permute-start | bytes 1572872 | tf_op jit(solution)/shard_map/ppermute | solution.py:571
  346.1 25.5 %collective-permute-start.26 = (bf16[128,2048]{1,0:T(8,128)(2,1)}, bf16[128,2048]{1,0:T(8,128)(2,1)}, u32[]{:S(2)}, u32[]{:S(2)}) collective-permute-start(bf16[128,2048]{1,0:T(8,128)(2,1)} %get-tuple-element.193), channel_id=1, source_target_pairs={{0,4},{4,0},{1,5},{5,1},{2,6},{6,2},{3,7},{7,3},{8,12},{12,8},{9,1... | collective-permute-start | bytes 1572872 | tf_op jit(solution)/shard_map/ppermute | solution.py:571
  346.1 42.0 %collective-permute-start.28 = (bf16[128,2048]{1,0:T(8,128)(2,1)}, bf16[128,2048]{1,0:T(8,128)(2,1)S(1)}, u32[]{:S(2)}, u32[]{:S(2)}) collective-permute-start(bf16[128,2048]{1,0:T(8,128)(2,1)} %get-tuple-element.192), channel_id=1, source_target_pairs={{0,4},{4,0},{1,5},{5,1},{2,6},{6,2},{3,7},{7,3},{8,12},{12,8},{9,1... | collective-permute-start | bytes 1572872 | tf_op jit(solution)/shard_map/ppermute | solution.py:571
  348.1 50.7 %collective-permute-start.30 = (bf16[128,2048]{1,0:T(8,128)(2,1)}, bf16[128,2048]{1,0:T(8,128)(2,1)}, u32[]{:S(2)}, u32[]{:S(2)}) collective-permute-start(bf16[128,2048]{1,0:T(8,128)(2,1)} %get-tuple-element.191), channel_id=1, source_target_pairs={{0,4},{4,0},{1,5},{5,1},{2,6},{6,2},{3,7},{7,3},{8,12},{12,8},{9,1... | collective-permute-start | bytes 1572872 | tf_op jit(solution)/shard_map/ppermute | solution.py:571
  359.8 16.0 %collective-permute-start.25 = (bf16[128,2048]{1,0:T(8,128)(2,1)}, bf16[128,2048]{1,0:T(8,128)(2,1)}, u32[]{:S(2)}, u32[]{:S(2)}) collective-permute-start(bf16[128,2048]{1,0:T(8,128)(2,1)} %fusion.29), channel_id=1, source_target_pairs={{0,24},{8,0},{16,8},{24,16},{1,25},{9,1},{17,9},{25,17},{2,26},{10... | collective-permute-start | bytes 1572872 | tf_op jit(solution)/shard_map/ppermute | solution.py:576
  377.6 12.9 %collective-permute-start.27 = (bf16[128,2048]{1,0:T(8,128)(2,1)S(1)}, bf16[128,2048]{1,0:T(8,128)(2,1)S(1)}, u32[]{:S(2)}, u32[]{:S(2)}) collective-permute-start(bf16[128,2048]{1,0:T(8,128)(2,1)S(1)} %fusion.31), channel_id=1, source_target_pairs={{0,24},{8,0},{16,8},{24,16},{1,25},{9,1},{17,9},{25,17},{2,26},{10... | collective-permute-start | bytes 1572872 | tf_op jit(solution)/shard_map/ppermute | solution.py:576
  390.7 14.8 %collective-permute-start.29 = (bf16[128,2048]{1,0:T(8,128)(2,1)S(1)}, bf16[128,2048]{1,0:T(8,128)(2,1)S(1)}, u32[]{:S(2)}, u32[]{:S(2)}) collective-permute-start(bf16[128,2048]{1,0:T(8,128)(2,1)S(1)} %fusion.33), channel_id=1, source_target_pairs={{0,24},{8,0},{16,8},{24,16},{1,25},{9,1},{17,9},{25,17},{2,26},{10... | collective-permute-start | bytes 1572872 | tf_op jit(solution)/shard_map/ppermute | solution.py:576
  460.6 19.8 %collective-permute-start.38 = (bf16[128,2048]{1,0:T(8,128)(2,1)}, bf16[128,2048]{1,0:T(8,128)(2,1)S(1)}, u32[]{:S(2)}, u32[]{:S(2)}) collective-permute-start(bf16[128,2048]{1,0:T(8,128)(2,1)} %get-tuple-element.190), channel_id=1, source_target_pairs={{0,4},{4,0},{1,5},{5,1},{2,6},{6,2},{3,7},{7,3},{8,12},{12,8},{9,1... | collective-permute-start | bytes 1572872 | tf_op jit(solution)/shard_map/ppermute | solution.py:571
  466.6 28.1 %all-to-all-start.3 = ((bf16[4,64,1024]{2,1,0:T(8,128)(2,1)}), bf16[4,64,1024]{2,1,0:T(8,128)(2,1)S(1)}, u32[]{:S(2)}, u32[]{:S(2)}) async-start(bf16[4,64,1024]{2,1,0:T(8,128)(2,1)} %bitcast.34), calls=%async_computation.4 | async-start | bytes 1048576 | tf_op jit(solution)/shard_map/all_to_all | solution.py:764
  480.3 15.1 %collective-permute-start.40 = (bf16[128,2048]{1,0:T(8,128)(2,1)}, bf16[128,2048]{1,0:T(8,128)(2,1)}, u32[]{:S(2)}, u32[]{:S(2)}) collective-permute-start(bf16[128,2048]{1,0:T(8,128)(2,1)} %get-tuple-element.189), channel_id=1, source_target_pairs={{0,4},{4,0},{1,5},{5,1},{2,6},{6,2},{3,7},{7,3},{8,12},{12,8},{9,1... | collective-permute-start | bytes 1572872 | tf_op jit(solution)/shard_map/ppermute | solution.py:571
  482.5 16.0 %collective-permute-start.39 = (bf16[128,2048]{1,0:T(8,128)(2,1)}, bf16[128,2048]{1,0:T(8,128)(2,1)}, u32[]{:S(2)}, u32[]{:S(2)}) collective-permute-start(bf16[128,2048]{1,0:T(8,128)(2,1)} %fusion.18), channel_id=1, source_target_pairs={{0,24},{8,0},{16,8},{24,16},{1,25},{9,1},{17,9},{25,17},{2,26},{10... | collective-permute-start | bytes 1572872 | tf_op jit(solution)/shard_map/ppermute | solution.py:576
  488.2 57.4 %collective-permute-start.42 = (bf16[128,2048]{1,0:T(8,128)(2,1)}, bf16[128,2048]{1,0:T(8,128)(2,1)}, u32[]{:S(2)}, u32[]{:S(2)}) collective-permute-start(bf16[128,2048]{1,0:T(8,128)(2,1)} %get-tuple-element.188), channel_id=1, source_target_pairs={{0,4},{4,0},{1,5},{5,1},{2,6},{6,2},{3,7},{7,3},{8,12},{12,8},{9,1... | collective-permute-start | bytes 1572872 | tf_op jit(solution)/shard_map/ppermute | solution.py:571
  501.0 44.7 %collective-permute-start.41 = (bf16[128,2048]{1,0:T(8,128)(2,1)}, bf16[128,2048]{1,0:T(8,128)(2,1)}, u32[]{:S(2)}, u32[]{:S(2)}) collective-permute-start(bf16[128,2048]{1,0:T(8,128)(2,1)} %fusion.20), channel_id=1, source_target_pairs={{0,24},{8,0},{16,8},{24,16},{1,25},{9,1},{17,9},{25,17},{2,26},{10... | collective-permute-start | bytes 1572872 | tf_op jit(solution)/shard_map/ppermute | solution.py:576
  541.3 23.7 %all-to-all-start.4 = ((bf16[4,192,1024]{2,1,0:T(8,128)(2,1)}), bf16[4,192,1024]{2,1,0:T(8,128)(2,1)S(1)}, u32[]{:S(2)}, u32[]{:S(2)}) async-start(bf16[4,192,1024]{2,1,0:T(8,128)(2,1)} %attn_bwd.1), calls=%async_computation.7 | async-start | bytes 3145728 | tf_op jit(solution)/shard_map/all_to_all | solution.py:770
  545.0 74.9 %reduce-scatter.12.cloned.1.call-start = ((), (), s32[]{:S(2)}) async-start(), calls=%async_computation.18 | async-start | bytes 4587520 | tf_op jit(solution)/shard_map/reduce_scatter | solution.py:798
  545.0 20.2 %collective-permute-start.44 = (bf16[128,2048]{1,0:T(8,128)(2,1)}, bf16[128,2048]{1,0:T(8,128)(2,1)S(1)}, u32[]{:S(2)}, u32[]{:S(2)}) collective-permute-start(bf16[128,2048]{1,0:T(8,128)(2,1)} %get-tuple-element.187), channel_id=1, source_target_pairs={{0,4},{4,0},{1,5},{5,1},{2,6},{6,2},{3,7},{7,3},{8,12},{12,8},{9,1... | collective-permute-start | bytes 1572872 | tf_op jit(solution)/shard_map/ppermute | solution.py:571
  548.2 17.0 %collective-permute-start.43 = (bf16[128,2048]{1,0:T(8,128)(2,1)}, bf16[128,2048]{1,0:T(8,128)(2,1)}, u32[]{:S(2)}, u32[]{:S(2)}) collective-permute-start(bf16[128,2048]{1,0:T(8,128)(2,1)} %fusion.22), channel_id=1, source_target_pairs={{0,24},{8,0},{16,8},{24,16},{1,25},{9,1},{17,9},{25,17},{2,26},{10... | collective-permute-start | bytes 1572872 | tf_op jit(solution)/shard_map/ppermute | solution.py:576
  577.9 65.8 %reduce-scatter.14.cloned.1.call-start = ((), (), s32[]{:S(2)}) async-start(), calls=%async_computation.19 | async-start | bytes 1310720 | tf_op jit(solution)/shard_map/reduce_scatter | solution.py:780
  580.9 14.8 %collective-permute-start.45 = (bf16[128,2048]{1,0:T(8,128)(2,1)S(1)}, bf16[128,2048]{1,0:T(8,128)(2,1)S(1)}, u32[]{:S(2)}, u32[]{:S(2)}) collective-permute-start(bf16[128,2048]{1,0:T(8,128)(2,1)S(1)} %get-tuple-element.186), channel_id=1, source_target_pairs={{0,4},{4,0},{1,5},{5,1},{2,6},{6,2},{3,7},{7,3},{8,12},{12,8},{9,1... | collective-permute-start | bytes 1572872 | tf_op jit(solution)/shard_map/ppermute | solution.py:571
  581.4 25.5 %collective-permute-start.47 = (bf16[128,2048]{1,0:T(8,128)(2,1)}, bf16[128,2048]{1,0:T(8,128)(2,1)S(1)}, u32[]{:S(2)}, u32[]{:S(2)}) collective-permute-start(bf16[128,2048]{1,0:T(8,128)(2,1)} %get-tuple-element.185), channel_id=1, source_target_pairs={{0,4},{4,0},{1,5},{5,1},{2,6},{6,2},{3,7},{7,3},{8,12},{12,8},{9,1... | collective-permute-start | bytes 1572872 | tf_op jit(solution)/shard_map/ppermute | solution.py:571
  600.4 17.9 %collective-permute-start.49 = (bf16[128,2048]{1,0:T(8,128)(2,1)}, bf16[128,2048]{1,0:T(8,128)(2,1)}, u32[]{:S(2)}, u32[]{:S(2)}) collective-permute-start(bf16[128,2048]{1,0:T(8,128)(2,1)} %get-tuple-element.184), channel_id=1, source_target_pairs={{0,4},{4,0},{1,5},{5,1},{2,6},{6,2},{3,7},{7,3},{8,12},{12,8},{9,1... | collective-permute-start | bytes 1572872 | tf_op jit(solution)/shard_map/ppermute | solution.py:571
  610.7 34.8 %collective-permute-start.51 = (bf16[128,2048]{1,0:T(8,128)(2,1)}, bf16[128,2048]{1,0:T(8,128)(2,1)S(1)}, u32[]{:S(2)}, u32[]{:S(2)}) collective-permute-start(bf16[128,2048]{1,0:T(8,128)(2,1)} %get-tuple-element.183), channel_id=1, source_target_pairs={{0,4},{4,0},{1,5},{5,1},{2,6},{6,2},{3,7},{7,3},{8,12},{12,8},{9,1... | collective-permute-start | bytes 1572872 | tf_op jit(solution)/shard_map/ppermute | solution.py:571
  619.9 34.6 %all-to-all-start.5 = ((bf16[8,64,896]{2,1,0:T(8,128)(2,1)}), bf16[8,64,896]{2,1,0:T(8,128)(2,1)S(1)}, u32[]{:S(2)}, u32[]{:S(2)}) async-start(bf16[8,64,896]{2,1,0:T(8,128)(2,1)} %reduce-scatter.12.cloned.1.call-done), calls=%async_computation.9 | async-start | bytes 1835008 | tf_op jit(solution)/shard_map/all_to_all | solution.py:804
  627.0 22.9 %collective-permute-start.50 = (bf16[128,2048]{1,0:T(8,128)(2,1)}, bf16[128,2048]{1,0:T(8,128)(2,1)}, u32[]{:S(2)}, u32[]{:S(2)}) collective-permute-start(bf16[128,2048]{1,0:T(8,128)(2,1)} %fusion.16), channel_id=1, source_target_pairs={{0,24},{8,0},{16,8},{24,16},{1,25},{9,1},{17,9},{25,17},{2,26},{10... | collective-permute-start | bytes 1572872 | tf_op jit(solution)/shard_map/ppermute | solution.py:576
  (71 other events, 1052.3 us)
Sparse Core Ops, SparseCore 0:
  75.7 17.2 all-gather.6
  100.1 73.0 all-gather.14
  174.8 32.8 all-gather.8
  209.1 34.4 all-gather.12
  245.0 34.4 all-gather.10
  331.2 46.9 reduce-scatter.5
  380.9 44.5 reduce-scatter.7
  428.0 44.4 reduce-scatter.9
  578.1 37.7 reduce-scatter.11
  618.8 24.8 reduce-scatter.13

commit v3 on v1

--- a/solution.py
+++ b/solution.py
@@ -379,13 +379,26 @@
 
 
 def attn_fwd_kernel(
-    slot_ref, qkv_ref, out_ref, o32_ref, lse_ref, seq_ref, k_scr, m_scr, l_scr, acc_scr, *, blocks, width
+    place_ref,
+    qkv_ref,
+    extra_ref,
+    out_ref,
+    o32_ref,
+    lse_ref,
+    seq_ref,
+    k_scr,
+    m_scr,
+    l_scr,
+    acc_scr,
+    *,
+    blocks,
+    width,
 ):
     pieces = qkv_ref.shape[0]
     blk = pieces * width
     coef = LOG2E * HD**-0.5
     for s in range(blocks):
-        at = pl.multiple_of(slot_ref[s] * width, width)
+        at = pl.multiple_of(place_ref[0, s] * width, width)
         for j in range(pieces):
             lo = s * blk + j * width
             piece = qkv_ref[j, :, pl.ds(at, width)]
@@ -421,25 +434,26 @@
         o = acc_scr[...] / l_scr[...]
         o32_ref[:, lo : lo + blk] = o
         lse_ref[:, lo : lo + blk] = m_scr[...] + jnp.log2(l_scr[...])
-        at = pl.multiple_of(slot_ref[qb] * width, width)
         low = o.astype(BF16)
         for j in range(pieces):
-            out_ref[j, :, pl.ds(at, width)] = low[:, j * width : (j + 1) * width]
-
-
-def attn_fwd(slot, qkv, blocks):
+            owner = place_ref[1, qb] * pieces + j
+            out_ref[owner, :HD] = low[:, j * width : (j + 1) * width]
+            out_ref[owner, HD:] = extra_ref[...]
+
+
+def attn_fwd(place, qkv, extra, blocks):
     pieces, _, cols = qkv.shape
     total = pieces * cols
     blk = total // blocks
     return pl.pallas_call(
         functools.partial(attn_fwd_kernel, blocks=blocks, width=cols // blocks),
         out_shape=(
-            jax.ShapeDtypeStruct((pieces, HD, cols), BF16),
+            jax.ShapeDtypeStruct((blocks * pieces, HD + extra.shape[0], cols // blocks), BF16),
             jax.ShapeDtypeStruct((HD, total), F32),
             jax.ShapeDtypeStruct((1, total), F32),
             jax.ShapeDtypeStruct((3 * HD, total), BF16),
         ),
-        in_specs=[pl.BlockSpec(memory_space=pltpu.SMEM), VMEM],
+        in_specs=[pl.BlockSpec(memory_space=pltpu.SMEM), VMEM, VMEM],
         out_specs=(VMEM,) * 4,
         scratch_shapes=[
             pltpu.VMEM((total, HD), BF16),
@@ -452,11 +466,11 @@
             flops=8 * total * total * HD, bytes_accessed=8 << 20, transcendentals=total * total // 2
         ),
         name="attn_fwd",
-    )(slot, qkv)
+    )(place, qkv, extra)
 
 
 def attn_bwd_kernel(
-    slot_ref,
+    place_ref,
     seq_ref,
     o32_ref,
     lse_ref,
@@ -477,16 +491,15 @@
     blocks,
     width,
 ):
-    pieces = do_ref.shape[0]
+    pieces = out_ref.shape[0]
     blk = pieces * width
     scale = HD**-0.5
     coef = LOG2E * scale
     half = HD // 2
     for s in range(blocks):
-        at = pl.multiple_of(slot_ref[s] * width, width)
         for j in range(pieces):
             lo = s * blk + j * width
-            piece = do_ref[j, :, pl.ds(at, width)]
+            piece = do_ref[place_ref[1, s] * pieces + j, :HD]
             dot_scr[:, lo : lo + width] = piece
             do_scr[lo : lo + width, :] = piece.T
             delta_scr[:, lo : lo + width] = jnp.sum(
@@ -504,7 +517,7 @@
         return jnp.concatenate([a * c + b * n, b * c - a * n], axis=0).astype(BF16)
 
     def put(v, s, row):
-        at = pl.multiple_of(slot_ref[s] * width, width)
+        at = pl.multiple_of(place_ref[0, s] * width, width)
         for j in range(pieces):
             out_ref[j, row * HD : (row + 1) * HD, pl.ds(at, width)] = v[:, j * width : (j + 1) * width]
 
@@ -538,12 +551,11 @@
         put(dv_scr[...].T.astype(BF16), kb, 2)
 
 
-def attn_bwd(slot, seq, o32, lse, do, cos, sin, blocks):
-    pieces, _, cols = do.shape
-    total = pieces * cols
-    blk = total // blocks
+def attn_bwd(place, seq, o32, lse, do, cos, sin, blocks):
+    pieces, width = do.shape[0] // blocks, do.shape[2]
+    cols, total, blk = blocks * width, seq.shape[1], pieces * width
     return pl.pallas_call(
-        functools.partial(attn_bwd_kernel, blocks=blocks, width=cols // blocks),
+        functools.partial(attn_bwd_kernel, blocks=blocks, width=width),
         out_shape=jax.ShapeDtypeStruct((pieces, 3 * HD, cols), BF16),
         in_specs=[pl.BlockSpec(memory_space=pltpu.SMEM)] + [VMEM] * 6,
         out_specs=VMEM,
@@ -560,7 +572,170 @@
             flops=20 * total * total * HD, bytes_accessed=8 << 20, transcendentals=total * total // 2
         ),
         name="attn_bwd",
-    )(slot, seq, o32, lse, do, cos, sin)
+    )(place, seq, o32, lse, do, cos, sin)
+
+
+ANY = pl.BlockSpec(memory_space=pl.ANY)
+
+
+def mxu_nt(a, b):
+    return lax.dot_general(a, b, (((1,), (1,)), ((), ())), preferred_element_type=F32)
+
+
+def mxu_tn(a, b):
+    return lax.dot_general(a, b, (((0,), (0,)), ((), ())), preferred_element_type=F32)
+
+
+def ffn_kernel(*refs, count, step):
+    x, dy = refs[:count], refs[count : 2 * count]
+    w_hbm = refs[2 * count : 2 * count + 3]
+    dn, br = refs[2 * count + 3 : 3 * count + 3], refs[3 * count + 3 : 4 * count + 3]
+    kept = refs[4 * count + 3 : 4 * count + 6]
+    x_scr, dy_scr, gate_w, up_w, down_w, hid_scr, dgate_scr, dup_scr, act_scr, dn_scr, br_scr, in_sem, w_sem, out_sem, keep_sem = refs[4 * count + 6 :]
+    tok, width = x[0].shape
+    hidden = gate_w.shape[0]
+    rows_in = [
+        pltpu.make_async_copy(src[i], dst.at[i * tok : (i + 1) * tok], in_sem.at[k, i])
+        for k, (src, dst) in enumerate(((x, x_scr), (dy, dy_scr)))
+        for i in range(count)
+    ]
+    w_in = [
+        pltpu.make_async_copy(src, dst, w_sem.at[k])
+        for k, (src, dst) in enumerate(zip(w_hbm, (gate_w, up_w, down_w)))
+    ]
+    for c in rows_in[:count] + w_in[:2] + rows_in[count:] + w_in[2:]:
+        c.start()
+    for c in rows_in[:count] + w_in[:2]:
+        c.wait()
+    half = hidden // 2
+    for h in range(2):
+        part = slice(h * half, (h + 1) * half)
+        gate = mxu_nt(x_scr[...], gate_w[part, :])
+        up = mxu_nt(x_scr[...], up_w[part, :])
+        sig = jax.nn.sigmoid(gate)
+        act = gate * sig
+        hid_scr[:, part] = (act * up).astype(BF16)
+        act_scr[:, part] = act
+        dgate_scr[:, part] = up * (sig * (1.0 + gate * (1.0 - sig)))
+    for c in rows_in[count:] + w_in[2:]:
+        c.wait()
+    for h in range(2):
+        part = slice(h * half, (h + 1) * half)
+        dhidden = mxu_nt(dy_scr[...], down_w[part, :])
+        dup_scr[1, :, part] = (dhidden * act_scr[:, part]).astype(BF16)
+        dup_scr[0, :, part] = (dhidden * dgate_scr[:, part]).astype(BF16)
+    keep = [
+        pltpu.make_async_copy(src, dst, keep_sem.at[k])
+        for k, (src, dst) in enumerate(zip((hid_scr, dup_scr.at[0], dup_scr.at[1]), kept))
+    ]
+    for c in keep:
+        c.start()
+    sent = []
+    for n in range(width // step):
+        part = slice(n * step, (n + 1) * step)
+        total = mxu(dup_scr[0], gate_w[:, part]) + mxu(dup_scr[1], up_w[:, part])
+        dn_scr[:, part] = total.astype(BF16)
+        br_scr[:, part] = mxu(hid_scr[...], down_w[:, part]).astype(BF16)
+        for i in range(count):
+            rows = slice(i * tok, (i + 1) * tok)
+            for k, (src, dst) in enumerate(((dn_scr, dn[i]), (br_scr, br[i]))):
+                sent.append(pltpu.make_async_copy(src.at[rows, part], dst.at[:, part], out_sem.at[k, i, n]))
+                sent[-1].start()
+    for c in keep + sent:
+        c.wait()
+
+
+def ffn(x, dy, gate_w, up_w, down_w):
+    count, (tok, width), hidden = len(x), x[0].shape, gate_w.shape[0]
+    rows, step = count * tok, width // 4
+    out = pl.pallas_call(
+        functools.partial(ffn_kernel, count=count, step=step),
+        in_specs=[ANY] * (2 * count + 3),
+        out_specs=[ANY] * (2 * count + 3),
+        out_shape=[jax.ShapeDtypeStruct((tok, width), BF16)] * (2 * count)
+        + [jax.ShapeDtypeStruct((rows, hidden), BF16)] * 3,
+        scratch_shapes=[pltpu.VMEM((rows, width), BF16)] * 2
+        + [pltpu.VMEM((hidden, width), BF16)] * 3
+        + [
+            pltpu.VMEM((rows, hidden), BF16),
+            pltpu.VMEM((rows, hidden), F32),
+            pltpu.VMEM((2, rows, hidden), BF16),
+            pltpu.VMEM((rows, hidden), F32),
+            pltpu.VMEM((rows, width), BF16),
+            pltpu.VMEM((rows, width), BF16),
+            pltpu.SemaphoreType.DMA((2, count)),
+            pltpu.SemaphoreType.DMA((3,)),
+            pltpu.SemaphoreType.DMA((2, count, width // step)),
+            pltpu.SemaphoreType.DMA((3,)),
+        ],
+        compiler_params=pltpu.CompilerParams(vmem_limit_bytes=60 << 20),
+        cost_estimate=pl.CostEstimate(
+            flops=12 * rows * hidden * width, bytes_accessed=6 * hidden * width + 16 * rows * width, transcendentals=rows * hidden
+        ),
+        name="ffn",
+    )(*x, *dy, gate_w, up_w, down_w)
+    return out[:count], out[count : 2 * count], out[2 * count :]
+
+
+def outer_kernel(*refs, lefts, rights):
+    order = refs[0]
+    left, right = refs[1 : 1 + lefts], refs[1 + lefts : 1 + lefts + rights]
+    send, keep, l_scr, r_scr, l_sem, r_sem = refs[1 + lefts + rights :]
+    i = pl.program_id(0)
+
+    def into(parts, scr, sem):
+        at, out = 0, []
+        for k, part in enumerate(parts):
+            out.append(pltpu.make_async_copy(part, scr.at[at : at + part.shape[0]], sem.at[k]))
+            at += part.shape[0]
+        return out
+
+    @pl.when(i == 0)
+    def _():
+        copies = into(left, l_scr, l_sem) + into(right, r_scr, r_sem)
+        for c in copies:
+            c.start()
+        for c in copies:
+            c.wait()
+
+    tile = send.shape[1]
+    l = l_scr[:, pl.ds(pl.multiple_of(order[i] * tile, tile), tile)]
+    v = mxu_tn(l, r_scr[...]).astype(BF16)
+
+    @pl.when(i < 2)
+    def _():
+        send[0] = v
+
+    @pl.when(i >= 2)
+    def _():
+        keep[0] = v
+
+
+def outer(order, left, right):
+    cols, width = left[0].shape[1], right[0].shape[1]
+    rows = sum(p.shape[0] for p in left)
+    tile = cols // 4
+    return pl.pallas_call(
+        functools.partial(outer_kernel, lefts=len(left), rights=len(right)),
+        grid=(4,),
+        in_specs=[pl.BlockSpec(memory_space=pltpu.SMEM)] + [ANY] * (len(left) + len(right)),
+        out_specs=[
+            pl.BlockSpec((1, tile, width), lambda i: (jnp.minimum(i, 1), 0, 0)),
+            pl.BlockSpec((1, tile, width), lambda i: (jnp.maximum(i - 2, 0), 0, 0)),
+        ],
+        out_shape=[jax.ShapeDtypeStruct((2, tile, width), BF16)] * 2,
+        scratch_shapes=[
+            pltpu.VMEM((rows, cols), BF16),
+            pltpu.VMEM((rows, width), BF16),
+            pltpu.SemaphoreType.DMA((len(left),)),
+            pltpu.SemaphoreType.DMA((len(right),)),
+        ],
+        compiler_params=pltpu.CompilerParams(vmem_limit_bytes=60 << 20),
+        cost_estimate=pl.CostEstimate(
+            flops=2 * rows * cols * width, bytes_accessed=2 * (rows * (cols + width) + cols * width), transcendentals=0
+        ),
+        name="outer",
+    )(order, *left, *right)
 
 
 FAR = ("ctx", "row")
@@ -571,34 +746,119 @@
     return lax.ppermute(v, axis, [(0, 1), (1, 0)])
 
 
-def shift(v, by):
+def shift(v):
     n = lax.axis_size("ctx")
-    return lax.ppermute(v, "ctx", [(i, (i + by) % n) for i in range(n)])
-
-
-def spread(v):
-    parts = [v]
-    for _ in range(lax.axis_size("ctx") - 1):
-        parts.append(shift(parts[-1], 1))
-    return jnp.concatenate(parts + [swap(p, "row") for p in parts], axis=0)
-
-
-def collect(terms, tok):
+    return lax.ppermute(v, "ctx", [(i, (i + 1) % n) for i in range(n)])
+
+
+class Flow:
+    def __init__(self, steps):
+        self.steps = steps
+        self.result = None
+        self.pending = next(steps)
+
+    def take(self, got):
+        try:
+            self.pending = self.steps.send(got)
+        except StopIteration as end:
+            self.pending, self.result = None, end.value
+
+    def run_on(self):
+        self.take(self.pending)
+
+
+def stage(flows, values=(), then=None):
+    got, values = lax.optimization_barrier(([f.pending for f in flows], values))
+    if then is not None:
+        then(values)
+    for f, g in zip(flows, got, strict=True):
+        f.take(g)
+    return values
+
+
+def spread(v, slots):
+    slots[0, 0] = v
     n = lax.axis_size("ctx")
-    other = terms(1).astype(BF16).reshape(n, tok, -1)
-    crossed = [swap(other[c], "row") for c in reversed(range(n))][::-1]
-    own = terms(0).reshape(n, tok, -1)
+    for c in range(n - 1):
+        slots[c + 1, 0], slots[c, 1] = yield shift(slots[c, 0]), swap(slots[c, 0], "row")
+    slots[n - 1, 1] = yield swap(slots[n - 1, 0], "row")
+    return slots
+
+
+def collect(terms, marks):
+    n = lax.axis_size("ctx")
     total = None
-    for c in reversed(range(n)):
-        part = own[c] + crossed[c].astype(F32)
-        if total is not None:
-            part = part + shift(total.astype(BF16), -1).astype(F32)
-        total = part
+    for c in [*range(1, n), 0]:
+        if total is None:
+            across = yield swap(terms[c, 1], "row")
+            total = terms[c, 0].astype(F32) + across.astype(F32)
+        else:
+            marks.append(total.astype(BF16))
+            across, ahead = yield swap(terms[c, 1], "row"), shift(marks[-1])
+            total = terms[c, 0].astype(F32) + across.astype(F32) + ahead.astype(F32)
     return total
+
+
+def reduce_near(send, keep):
+    got = yield swap(send, "core")
+    rows = keep.shape[1] // 2
+    upper, lower = (
+        (keep[0, p].astype(F32) + got[0, p].astype(F32)).astype(BF16)
+        for p in (slice(0, rows), slice(rows, None))
+    )
+    upper = yield swap(upper, "col")
+    lower = yield swap(lower, "col")
+    return keep[1], got[1], upper, lower
+
+
+def add_terms(keep, got, upper, lower):
+    return keep.astype(F32) + got.astype(F32) + jnp.concatenate([upper, lower], axis=0).astype(F32)
+
+
+def after(v, first):
+    return lax.optimization_barrier((v, first))[0]
+
+
+def beside(v, tok):
+    return jnp.pad(v.reshape(*v.shape[:-1], 1, -1), [(0, 0)] * (v.ndim - 1) + [(0, 15), (0, tok - v.shape[-1])])
 
 
 def by_side(index, mine, theirs):
     return jnp.where(index == 0, mine, theirs), jnp.where(index == 0, theirs, mine)
+
+
+def to_near(v, col_at, core_at):
+    keep, give = by_side(col_at, v[0], v[1])
+    got = yield swap(give, "col")
+    both = jnp.stack(by_side(col_at, keep, got))
+    keep, give = by_side(core_at, both[:, 0], both[:, 1])
+    got = yield swap(give, "core")
+    return jnp.stack(by_side(core_at, keep, got), axis=1)
+
+
+def sum_near(v, col_at, core_at):
+    keep, give = by_side(core_at, v[:, :, 0], v[:, :, 1])
+    got = yield swap(give, "core")
+    total = keep.astype(F32) + got.astype(F32)
+    keep, give = by_side(col_at, total[:, 0], total[:, 1])
+    give = give.astype(BF16)
+    rows = give.shape[1] // 2
+    upper = yield swap(give[:, :rows], "col")
+    lower = yield swap(give[:, rows:], "col")
+    return keep + jnp.concatenate([upper, lower], axis=1).astype(F32)
+
+
+def gather_heads(send, col_at, core_at):
+    mine = yield lax.all_to_all(send, FAR, split_axis=0, concat_axis=0, tiled=True)
+    part = mine.shape[0] // 2
+    upper = yield swap(mine[:part], "col")
+    lower = yield swap(mine[part:], "col")
+    other = jnp.concatenate([upper, lower], axis=0)
+    mine_two, other_two = yield swap(mine, "core"), swap(other, "core")
+    mine_pair = by_side(core_at, mine, mine_two)
+    other_pair = by_side(core_at, other, other_two)
+    halves = [by_side(col_at, a, b) for a, b in zip(mine_pair, other_pair, strict=True)]
+    return jnp.stack([halves[0][0], halves[1][0], halves[0][1], halves[1][1]], axis=1)
 
 
 def per_device_split(
@@ -627,21 +887,22 @@
     group = near * HD
 
     slots = jnp.arange(far, dtype=jnp.int32)
-    slot_ctx = (ctx_at - slots % n_ctx + n_ctx) % n_ctx
-    slot_row = row_at ^ (slots // n_ctx)
-    pair = jnp.sum(
-        jnp.where(
-            slot_ctx[:, None] == jnp.arange(n_ctx, dtype=jnp.int32)[None, :], pair_index[None, :], 0
-        ),
-        axis=1,
-    )
-    slot_block = jnp.where(slot_row == 0, pair, far - 1 - pair)
-    block_slot = jnp.sum(jnp.where(slot_block[None, :] == slots[:, None], slots[None, :], 0), axis=1)
+    ctxs = jnp.arange(n_ctx, dtype=jnp.int32)
+
+    def block_of(ctx, row):
+        pair = jnp.sum(jnp.where(ctx[:, None] == ctxs[None, :], pair_index[None, :], 0), axis=1)
+        return jnp.where(row == 0, pair, far - 1 - pair)
+
+    def place_of_block(block):
+        return jnp.sum(jnp.where(block[None, :] == slots[:, None], slots[None, :], 0), axis=1)
+
+    slot_block = block_of((ctx_at - slots % n_ctx + n_ctx) % n_ctx, row_at ^ (slots // n_ctx))
+    places = jnp.stack([place_of_block(slot_block), place_of_block(block_of(slots // 2, slots % 2))])
     freq = jnp.exp(jnp.arange(HD // 2, dtype=F32) * (-2.0 * math.log(THETA) / HD))
-    places = (
+    token_places = (
         slot_block[:, None] * blk + near_at * tok + jnp.arange(tok, dtype=jnp.int32)[None, :]
     ).reshape(rows_here)
-    angle = freq[:, None] * places.astype(F32)[None, :]
+    angle = freq[:, None] * token_places.astype(F32)[None, :]
     cosine, sine = jnp.cos(angle), jnp.sin(angle)
     seq_angle = freq[:, None] * jnp.arange(far * blk, dtype=jnp.int32).astype(F32)[None, :]
     seq_cos, seq_sin = jnp.cos(seq_angle), jnp.sin(seq_angle)
@@ -651,74 +912,95 @@
         [
             (w.astype(F32) * gain_one).astype(BF16).reshape(own_in, far, group)
             for w in (w_query, w_key, w_value)
-        ]
-        + [jnp.broadcast_to(gain_ffn[:, None, None], (own_in, far, 128))],
+        ],
         axis=2,
     ).transpose(1, 0, 2)
     x32 = tokens.astype(F32)
     scale_one = lax.rsqrt(jnp.mean(x32 * x32, axis=-1, keepdims=True) + EPS)
-    rows_one = spread((x32 * scale_one).astype(BF16))
-    mine = lax.all_to_all(send, FAR, split_axis=0, concat_axis=0, tiled=True)
-    other = swap(mine, "col")
-    mine_pair = by_side(core_at, mine, swap(mine, "core"))
-    other_pair = by_side(core_at, other, swap(other, "core"))
-    halves = [by_side(col_at, a, b) for a, b in zip(mine_pair, other_pair, strict=True)]
-    w_ext = jnp.stack(
-        [halves[0][0], halves[1][0], halves[0][1], halves[1][1]], axis=1
-    ).reshape(width, 3 * group + 128)
-    w_heads = w_ext[:, : 3 * group]
-    gain_two = w_ext[:, 3 * group].astype(F32)[None, :]
-
-    out_rows = lax.all_gather(w_out, NEAR, axis=0, tiled=True)
-    gate_w, up_w, down_w = (
-        lax.all_gather(w, NEAR, axis=0, tiled=True) for w in (w_gate, w_up, w_down)
-    )
+    gate_w = lax.all_gather(w_gate, NEAR, axis=0, tiled=True)
+
+    def rows_of(by_slot):
+        return jnp.concatenate([by_slot[c, r] for r in range(2) for c in range(n_ctx)], axis=0)
+
+    one_flow = Flow(spread((x32 * scale_one).astype(BF16), {}))
+    heads_flow = Flow(gather_heads(send, col_at, core_at))
+    w_out = stage([one_flow, heads_flow], w_out)
+    out_w = lax.all_gather(w_out, FAR + NEAR, axis=0, tiled=True)
+    for _ in range(n_ctx - 2):
+        stage([one_flow, heads_flow])
+    w_up, dy_low = stage([one_flow, heads_flow], (w_up, cotangent))
+    up_w = lax.all_gather(w_up, NEAR, axis=0, tiled=True)
+    w_heads = heads_flow.result.reshape(width, 3 * group)
+    rows_one = rows_of(one_flow.result)
 
     half = HD // 2
+    dy_by = {}
+    dy_flow = Flow(spread(dy_low, dy_by))
     flat = jnp.einsum("de,td->et", w_heads, rows_one, preferred_element_type=F32)
     qkv = flat.reshape(3, near, 2, half, rows_here)
     first, second = qkv[:2, :, 0], qkv[:2, :, 1]
     turned = jnp.stack([first * cosine - second * sine, second * cosine + first * sine], axis=2)
     qkv = jnp.concatenate([turned, qkv[2:]], axis=0).astype(BF16)
     qkv = qkv.transpose(1, 0, 2, 3, 4).reshape(near, 3 * HD, rows_here)
-    qkv_head = lax.all_to_all(qkv, NEAR, split_axis=0, concat_axis=0, tiled=True)
-    attn_head, o32, lse, seq = attn_fwd(block_slot, qkv_head, far)
-    attn = lax.all_to_all(attn_head, NEAR, split_axis=0, concat_axis=0, tiled=True)
-    attn = attn.reshape(group, rows_here)
-    rows_half = rows_here // 2
-
-    def cut(v, r, axis):
-        return lax.slice_in_dim(v, r * rows_half, (r + 1) * rows_half, axis=axis)
-
-    mid = x32 + collect(
-        lambda r: jnp.einsum("et,ed->td", cut(attn, r, 1), out_rows, preferred_element_type=F32), tok
-    )
+    qkv = stage([dy_flow], qkv)
+    qkv_head, gate_w, out_w = stage(
+        [dy_flow],
+        (lax.all_to_all(qkv, NEAR, split_axis=0, concat_axis=0, tiled=True), gate_w, out_w),
+    )
+    down_w = lax.all_gather(after(w_down, qkv_head), NEAR, axis=0, tiled=True)
+    attn_head, o32, lse, seq = stage(
+        [dy_flow], attn_fwd(places, qkv_head, beside(gain_ffn, tok), far)
+    )
+    attn, up_w = stage(
+        [dy_flow],
+        (lax.all_to_all(attn_head, FAR + NEAR, split_axis=0, concat_axis=0, tiled=True), up_w),
+    )
+    gain_two = attn[:, HD, :own_in].reshape(1, width).astype(F32)
+    attn = attn[:, :HD].reshape(width, tok)
+
+    mid = x32 + jnp.einsum("et,ed->td", attn, out_w, preferred_element_type=F32)
     scale_two = lax.rsqrt(jnp.mean(mid * mid, axis=-1, keepdims=True) + EPS)
     normed_two = (mid * scale_two * gain_two).astype(BF16)
-    rows_two = spread(normed_two)
-    dy_rows = spread(cotangent)
-    gate = rows_by(rows_two, gate_w)
-    up = rows_by(rows_two, up_w)
-    silu_val, slope = silu_parts(gate)
-    hidden = (silu_val * up).astype(BF16)
-    dhidden = rows_by(dy_rows, down_w)
-    dgate = (dhidden * up * slope).astype(BF16)
-    dup = (dhidden * silu_val).astype(BF16)
-    dnormed_two = collect(
-        lambda r: jnp.dot(cut(dgate, r, 0), gate_w, preferred_element_type=F32)
-        + jnp.dot(cut(dup, r, 0), up_w, preferred_element_type=F32),
-        tok,
-    )
-    branch = collect(
-        lambda r: jnp.dot(cut(hidden, r, 0), down_w, preferred_element_type=F32), tok
-    )
-    block_out = (mid + branch).astype(BF16)
-    gate_grad, up_grad, down_grad = (
-        lax.psum_scatter(
-            outer_sum(left, right).astype(BF16), NEAR, scatter_dimension=0, tiled=True
-        ).astype(F32)
-        for left, right in ((dgate, rows_two), (dup, rows_two), (hidden, dy_rows))
-    )
+    side_flow = Flow(
+        to_near(attn_head[:, :HD].reshape(far, 2, 2, HD, tok).transpose(1, 2, 3, 0, 4), col_at, core_at)
+    )
+
+    two, dn_by, br_by, kept = {}, {}, {}, []
+    two_flow = Flow(spread(normed_two, two))
+
+    def feed(cs):
+        names = [(c, r) for c in cs for r in range(2)]
+        dn, br, lefts = ffn(
+            [two[k] for k in names], [dy_by[k] for k in names], gate_w, up_w, down_w
+        )
+        return dict(zip(names, dn, strict=True)), dict(zip(names, br, strict=True)), lefts
+
+    def fed(results):
+        dn, br, lefts = results
+        dn_by.update(dn)
+        br_by.update(br)
+        kept.append(lefts)
+
+    stage([two_flow, side_flow])
+    stage([two_flow, side_flow], feed([0]), fed)
+    for c in range(1, n_ctx - 1):
+        stage([two_flow], feed([c]), fed)
+    marks = []
+    dn_flow = Flow(collect(dn_by, marks))
+    stage([dn_flow], feed([n_ctx - 1]), fed)
+    names = [(c, r) for c in range(n_ctx) for r in range(2)]
+    two_rows, dy_rows = [two[k] for k in names], [dy_by[k] for k in names]
+    tiles = near_at ^ jnp.array([3, 1, 2, 0], jnp.int32)
+    lefts = [[k[i] for k in kept] for i in range(3)]
+    gate_terms = outer(tiles, *after((lefts[1], two_rows), marks[-1]))
+    gate_flow = Flow(reduce_near(*stage([dn_flow], gate_terms)))
+    up_terms = outer(tiles, *after((lefts[2], two_rows), marks[-1]))
+    up_flow = Flow(reduce_near(*stage([dn_flow, gate_flow], up_terms)))
+    down_terms = outer(tiles, *after((lefts[0], dy_rows), marks[-1]))
+    down_terms, br_by = stage([dn_flow, up_flow], (down_terms, br_by))
+    down_flow = Flow(reduce_near(*down_terms))
+    dnormed_two = dn_flow.result
+
     dy = cotangent.astype(F32)
     gain_two_term = jnp.sum(dnormed_two * mid * scale_two, axis=0)
     scaled_two = gain_two * dnormed_two
@@ -727,42 +1009,84 @@
         + scale_two * scaled_two
         - mid * scale_two**3 * jnp.mean(scaled_two * mid, axis=-1, keepdims=True)
     )
-    dmid_rows = spread(dmid.astype(BF16))
-    dattn = jnp.einsum("ed,td->et", out_rows, dmid_rows, preferred_element_type=F32).astype(BF16)
-    dattn_head = lax.all_to_all(
-        dattn.reshape(near, HD, rows_here), NEAR, split_axis=0, concat_axis=0, tiled=True
-    )
-    out_grad = lax.psum_scatter(
-        jnp.einsum("et,td->ed", attn, dmid_rows, preferred_element_type=F32).astype(BF16),
-        NEAR,
-        scatter_dimension=0,
-        tiled=True,
-    ).astype(F32)
-    dqkv_head = attn_bwd(block_slot, seq, o32, lse, dattn_head, seq_cos, seq_sin, far)
-    dqkv = lax.all_to_all(dqkv_head, NEAR, split_axis=0, concat_axis=0, tiled=True)
+    dmid_low = dmid.astype(BF16)
+    dattn = jnp.einsum("ed,td->et", out_w, dmid_low, preferred_element_type=F32).astype(BF16)
+    gain_high = gain_two_term.astype(BF16)
+    gain_low = (gain_two_term - gain_high.astype(F32)).astype(BF16)
+    dattn = jnp.concatenate(
+        [
+            dattn.reshape(far * near, HD, tok),
+            beside(
+                jnp.concatenate(
+                    [v.reshape(far * near, own_in) for v in (gain_high, gain_low)], axis=1
+                ),
+                tok,
+            ),
+        ],
+        axis=1,
+    )
+    br_flow = Flow(collect(br_by, []))
+    gate_flow.run_on()
+    br_first = br_flow.pending
+    br_flow.run_on()
+    dattn_head, dmid_low, _ = stage(
+        [gate_flow, down_flow, br_flow],
+        (
+            lax.all_to_all(dattn, FAR + NEAR, split_axis=0, concat_axis=0, tiled=True),
+            dmid_low,
+            br_first,
+        ),
+    )
+    gain_parts = dattn_head[:, HD, : 2 * own_in].astype(F32)
+    dmid_side = lax.all_gather(dmid_low, FAR, axis=0, tiled=True)
+    up_flow.run_on()
+    dqkv_head = stage(
+        [up_flow, down_flow, br_flow],
+        attn_bwd(places, seq, o32, lse, dattn_head, seq_cos, seq_sin, far),
+    )
+    rows_one = after(rows_one, dqkv_head)
+    dqkv = stage(
+        [br_flow, down_flow],
+        lax.all_to_all(dqkv_head, NEAR, split_axis=0, concat_axis=0, tiled=True),
+    )
     dqkv = dqkv.reshape(near, 3, HD, rows_here).transpose(1, 0, 2, 3).reshape(3 * group, rows_here)
-    scaled_one = collect(
-        lambda r: jnp.einsum("et,de->td", cut(dqkv, r, 1), w_heads, preferred_element_type=F32), tok
-    )
+    half_rows = rows_here // 2
+
+    def dx_of(r, dqkv):
+        rows = lax.slice_in_dim(dqkv, r * half_rows, (r + 1) * half_rows, axis=1)
+        return jnp.einsum("et,de->td", rows, w_heads, preferred_element_type=F32).astype(BF16)
+
+    dx_other, dqkv = lax.optimization_barrier((dx_of(1, dqkv), dqkv))
+    dx_own, dqkv = lax.optimization_barrier((dx_of(0, dqkv), dqkv))
+    dx = [v.reshape(n_ctx, tok, width) for v in (dx_own, dx_other)]
+    dx_flow = Flow(collect({(c, r): dx[r][c] for c in range(n_ctx) for r in range(2)}, marks))
+    heads_grad = jnp.einsum("td,et->de", rows_one, dqkv, preferred_element_type=F32).astype(BF16)
+    heads_flow = Flow(
+        sum_near(heads_grad.reshape(far, 2, 2, own_in, 3 * group), col_at, core_at)
+    )
+    dmid_side = stage([dx_flow, heads_flow], dmid_side)
+    attn_side, dmid_side = after(
+        (side_flow.result.reshape(group, rows_here), dmid_side), marks[-1]
+    )
+    out_term = jnp.einsum("et,td->ed", attn_side, dmid_side, preferred_element_type=F32)
+    heads_first = heads_flow.pending
+    heads_flow.run_on()
+    ffn_terms, out_term, _ = stage(
+        [dx_flow, heads_flow],
+        ([f.result for f in (gate_flow, up_flow, down_flow)], out_term.astype(BF16), heads_first),
+    )
+    gate_grad, up_grad, down_grad = (add_terms(*terms) for terms in ffn_terms)
+    out_flow = Flow(sum_near(out_term.reshape(1, 2, 2, own_in, width), col_at, core_at))
+    for _ in range(n_ctx - 2):
+        stage([dx_flow, out_flow])
+    out_flow.run_on()
+    scaled_one = dx_flow.result
     input_grad = (
         dmid
         + scale_one * scaled_one
         - x32 * scale_one**3 * jnp.mean(scaled_one * x32, axis=-1, keepdims=True)
     )
-    heads_grad = jnp.concatenate(
-        [
-            jnp.einsum("td,et->de", rows_one, dqkv, preferred_element_type=F32),
-            jnp.broadcast_to(gain_two_term[:, None], (width, 128)),
-        ],
-        axis=1,
-    ).astype(BF16)
-    heads_grad = lax.psum_scatter(
-        heads_grad.reshape(far, near * own_in, 3 * group + 128),
-        NEAR,
-        scatter_dimension=1,
-        tiled=True,
-    )
-    back = lax.all_to_all(heads_grad, FAR, split_axis=0, concat_axis=0, tiled=True).astype(F32)
+    back = lax.all_to_all(heads_flow.result.astype(BF16), FAR, split_axis=0, concat_axis=0, tiled=True).astype(F32)
     raw = [
         back[:, :, i * group : (i + 1) * group].transpose(1, 0, 2).reshape(own_in, -1)
         for i in range(3)
@@ -772,15 +1096,15 @@
         for w, g in zip((w_query, w_key, w_value), raw, strict=True)
     )
     query_grad, key_grad, value_grad = (g * gain_one for g in raw)
-    gain_ffn_grad = jnp.sum(back[:, :, 3 * group], axis=0)
+    gain_ffn_grad = jnp.sum(gain_parts[:, :own_in] + gain_parts[:, own_in:], axis=0)
     return (
-        block_out,
+        (mid + br_flow.result).astype(BF16),
         input_grad,
         gain_attn_grad,
         query_grad,
         key_grad,
         value_grad,
-        out_grad,
+        out_flow.result[0],
         gain_ffn_grad,
         gate_grad,
         up_grad,
@@ -792,7 +1116,7 @@
     n_ctx, n_fsdp = mesh.shape["ctx"], mesh.shape["fsdp"]
 
     def step(*args):
-        if n_fsdp == 8 and n_ctx * n_fsdp * HD == args[3].shape[1]:
+        if n_fsdp == 8 and n_ctx == 4 and n_ctx * n_fsdp * HD == args[3].shape[1]:
             body, axes = per_device_split, FAR + NEAR
             over = Mesh(np.asarray(mesh.devices).reshape(n_ctx, 2, 2, 2), axes)
         else:

time: 828 us -> 619 us (0.75)
  waiting for transfers between devices: 447 us -> 232 us
  Pallas kernels: 58.1 us -> 138 us
  matrix products: 99.6 us -> 24.3 us
  other arithmetic: 42.2 us -> 63.7 us
  starting transfers between devices: 123 us -> 103 us
    reduce_scatter x5 -> x0, waiting for transfers between devices: 95.4 us -> none  [the longest x3 95.4 us: per_device_split(): lax.psum_scatter(outer_sum(left, right).astype(BF16), NEAR, scatter_dimen...]
    pallas_call x1 -> x8, Pallas kernels: 34.7 us -> 114 us  [the longest x4 47.5 us: ffn(): pl.pallas_call(functools.partial(ffn_kernel, count=count, step=step), in_...]
    dot_general x18 -> x5, matrix products: 90.5 us -> 17 us  [the longest x1 5.94 us: per_device_split(): jnp.einsum('ed,td->et', out_w, dmid_low, preferred_element_type=F32)]
    ppermute x24 -> x18, waiting for transfers between devices: 154 us -> 96.9 us  [shift(): return lax.ppermute(v, 'ctx', [(i, (i + 1) % n) for i in range(n)])]
    ppermute x24 -> x18, starting transfers between devices: 55.6 us -> 27.7 us  [shift(): return lax.ppermute(v, 'ctx', [(i, (i + 1) % n) for i in range(n)])]
    ppermute x35 -> x45, waiting for transfers between devices: 141 us -> 116 us  [swap(): return lax.ppermute(v, axis, [(0, 1), (1, 0)])]
    all_to_all x1, waiting for transfers between devices: 25.8 us -> 2.01 us  [per_device_split(): lax.all_to_all(qkv, NEAR, split_axis=0, concat_axis=0, tiled=True)]
    convert_element_type x19 -> x23, other arithmetic: 16.6 us -> 31.1 us  [the longest x9 14.4 us: collect(): marks.append(total.astype(BF16))]
  transfers between devices with their start and end apart: 74 -> 74, of which waited for: 49 -> 31; matrix products, arithmetic and copies ran while one was open for 17% -> 18% of each run, Pallas kernels for 3% -> 22%
where the time goes in v3:
time: 619 us; the launch traced here: 615 us
  waiting for transfers between devices  232 us (37%)
  Pallas kernels  138 us (22%)
  starting transfers between devices  103 us (17%)
  other arithmetic  63.7 us (10%)
  local copies, waits for them, and re-layouts  38.9 us (6%)
  matrix products  24.3 us (4%)
  between operations  15.1 us (2%)
    ppermute x45, waiting for transfers between devices, swap(): return lax.ppermute(v, axis, [(0, 1), (1, 0)])  116 us
    ppermute x18, waiting for transfers between devices, shift(): return lax.ppermute(v, 'ctx', [(i, (i + 1) % n) for i in range(n)])  96.9 us
    pallas_call x4, Pallas kernels, ffn(): pl.pallas_call(functools.partial(ffn_kernel, count=count, step=step), in_...  47.5 us
    ppermute x45, starting transfers between devices, swap(): return lax.ppermute(v, axis, [(0, 1), (1, 0)])  47.1 us
    pallas_call x1, Pallas kernels, attn_bwd(): pl.pallas_call(functools.partial(attn_bwd_kernel, blocks=blocks, width=wi...  34.6 us
    pallas_call x3, Pallas kernels, outer(): pl.pallas_call(functools.partial(outer_kernel, lefts=len(left), rights=le...  32.2 us
    ppermute x18, starting transfers between devices, shift(): return lax.ppermute(v, 'ctx', [(i, (i + 1) % n) for i in range(n)])  27.7 us
    pallas_call x1, Pallas kernels, attn_fwd(): pl.pallas_call(functools.partial(attn_fwd_kernel, blocks=blocks, width=co...  23.5 us
  transfers between devices with their start and end apart: 74, of which 31 were waited for; matrix products, arithmetic and copies ran while one was open for 18% of the time, Pallas kernels for 22%

profile of v3, /device:TPU:0, one launch (start us, length us, event | category | flops | bytes accessed | tf_op | source)
XLA Modules:
  0.0 614.8 jit_solution(14550959583570137417)
XLA Ops:
  11.2 7.3 %all-to-all-start = ((bf16[8,64,768]{2,1,0:T(8,128)(2,1)}), bf16[8,64,768]{2,1,0:T(8,128)(2,1)S(1)}, u32[]{:S(2)}, u32[]{:S(2)}) async-start(bf16[8,64,768]{2,1,0:T(8,128)(2,1)} %copy.119), calls=%async_computation | async-start | bytes 1572864 | tf_op jit(solution)/shard_map/all_to_all | solution.py:852
  23.1 23.5 %collective-permute-done = bf16[128,2048]{1,0:T(8,128)(2,1)S(1)} collective-permute-done((bf16[128,2048]{1,0:T(8,128)(2,1)S(1)}, bf16[128,2048]{1,0:T(8,128)(2,1)S(1)}, u32[]{:S(2)}, u32[]{:S(2)}) %collective-permute-start) | collective-permute-done | bytes 524320 | tf_op jit(solution)/shard_map/ppermute | solution.py:751
  46.6 3.3 all-to-all-done
  53.1 9.2 %collective-permute-done.4 = bf16[4,64,768]{2,1,0:T(8,128)(2,1)S(1)} collective-permute-done((bf16[4,64,768]{2,1,0:T(8,128)(2,1)S(1)}, bf16[4,64,768]{2,1,0:T(8,128)(2,1)S(1)}, u32[]{:S(2)}, u32[]{:S(2)}) %collective-permute-start.4) | collective-permute-done | bytes 393248 | tf_op jit(solution)/shard_map/ppermute | solution.py:746
  62.3 3.7 collective-permute-done.2
  70.7 6.6 %collective-permute-done.7 = bf16[4,64,768]{2,1,0:T(8,128)(2,1)S(1)} collective-permute-done((bf16[4,64,768]{2,1,0:T(8,128)(2,1)S(1)}, bf16[4,64,768]{2,1,0:T(8,128)(2,1)S(1)}, u32[]{:S(2)}, u32[]{:S(2)}) %collective-permute-start.7) | collective-permute-done | bytes 393248 | tf_op jit(solution)/shard_map/ppermute | solution.py:746
  77.3 3.7 collective-permute-done.5
  83.1 16.3 %collective-permute-done.8 = bf16[128,2048]{1,0:T(8,128)(2,1)S(1)} collective-permute-done((bf16[128,2048]{1,0:T(8,128)(2,1)S(1)}, bf16[128,2048]{1,0:T(8,128)(2,1)S(1)}, u32[]{:S(2)}, u32[]{:S(2)}) %collective-permute-start.8) | collective-permute-done | bytes 524320 | tf_op jit(solution)/shard_map/ppermute | solution.py:746
  116.7 3.5 fusion.44
  122.1 14.7 %collective-permute-done.11.refs_2_.refs_7_ = bf16[128,2048]{1,0:T(8,128)(2,1)S(1)} collective-permute-done((bf16[128,2048]{1,0:T(8,128)(2,1)S(1)}, bf16[128,2048]{1,0:T(8,128)(2,1)S(1)}, u32[]{:S(2)}, u32[]{:S(2)}) %collective-permute-start.11) | collective-permute-done | bytes 524320 | tf_op jit(solution)/shard_map/ppermute | solution.py:751
  138.4 3.7 all-to-all-start.1
  144.1 16.1 %collective-permute-done.13.refs_2_.refs_9_ = bf16[128,2048]{1,0:T(8,128)(2,1)} collective-permute-done((bf16[128,2048]{1,0:T(8,128)(2,1)S(1)}, bf16[128,2048]{1,0:T(8,128)(2,1)}, u32[]{:S(2)}, u32[]{:S(2)}) %collective-permute-start.13) | collective-permute-done | bytes 524320 | tf_op jit(solution)/shard_map/ppermute | solution.py:751
  162.5 11.1 %collective-permute-start.15 = (bf16[128,2048]{1,0:T(8,128)(2,1)}, bf16[128,2048]{1,0:T(8,128)(2,1)}, u32[]{:S(2)}, u32[]{:S(2)}) collective-permute-start(bf16[128,2048]{1,0:T(8,128)(2,1)} %collective-permute-done.13.refs_2_.refs_9_), channel_id=1, source_target_pairs={{0,8},{8,16},{16,24},{24,0},{1,9},{9,17},{17,25},{25,1},{2,10},{10... | collective-permute-start | bytes 1572872 | tf_op jit(solution)/shard_map/ppermute | solution.py:751
  175.8 23.5 %attn_fwd.1 = (bf16[32,80,128]{2,1,0:T(8,128)(2,1)}, f32[64,4096]{1,0:T(8,128)S(1)}, f32[1,4096]{1,0:T(1,128)S(1)}, bf16[192,4096]{1,0:T(8,128)(2,1)S(1)}) custom-call(s32[2,8]{1,0:T(2,128)S(1)} %pad_add_fusion.place_ref, bf16[4,192,1024]{2,1,0:T(8,128)(2,1)S(1)} %all-to-all-done.1.qkv_ref, bf16[16,128]{1,0:T(8,128)(2,1)S(1)} %pad.8.extra_ref), custom_call_target="tpu_custom_call" | custom-call | flops 8589934592 | bytes 8388608 | tf_op jit(solution)/shard_map/attn_fwd/pallas_call | solution.py:448
  200.3 4.1 all-to-all-start.2
  206.2 19.3 %collective-permute-done.17.refs_3_.refs_12_ = bf16[128,2048]{1,0:T(8,128)(2,1)S(1)} collective-permute-done((bf16[128,2048]{1,0:T(8,128)(2,1)}, bf16[128,2048]{1,0:T(8,128)(2,1)S(1)}, u32[]{:S(2)}, u32[]{:S(2)}) %collective-permute-start.17) | collective-permute-done | bytes 524320 | tf_op jit(solution)/shard_map/ppermute | solution.py:746
  226.5 4.8 multiply_reduce_fusion.2
  236.6 6.5 %collective-permute-done.20 = bf16[2,64,8,128]{3,2,1,0:T(8,128)(2,1)S(1)} collective-permute-done((bf16[2,64,8,128]{3,2,1,0:T(8,128)(2,1)S(1)}, bf16[2,64,8,128]{3,2,1,0:T(8,128)(2,1)S(1)}, u32[]{:S(2)}, u32[]{:S(2)}) %collective-permute-start.20) | collective-permute-done | bytes 262176 | tf_op jit(solution)/shard_map/ppermute | solution.py:746
  243.0 4.0 collective-permute-done.18.refs_0_.refs_7_
  249.3 11.8 %ffn.4 = (bf16[128,2048]{1,0:T(8,128)(2,1)}, bf16[128,2048]{1,0:T(8,128)(2,1)}, bf16[128,2048]{1,0:T(8,128)(2,1)}, bf16[128,2048]{1,0:T(8,128)(2,1)}, bf16[256,1...) custom-call(bf16[128,2048]{1,0:T(8,128)(2,1)} %copy-done.29, bf16[128,2048]{1,0:T(8,128)(2,1)} %copy-done.63, ...), custom_call_target="tpu_custom_call" | custom-call | flops 6442450944 | bytes 20971520 | tf_op jit(solution)/shard_map/ffn/pallas_call | solution.py:651
  263.9 11.8 %ffn.5 = (bf16[128,2048]{1,0:T(8,128)(2,1)}, bf16[128,2048]{1,0:T(8,128)(2,1)}, bf16[128,2048]{1,0:T(8,128)(2,1)}, bf16[128,2048]{1,0:T(8,128)(2,1)}, bf16[256,1...) custom-call(bf16[128,2048]{1,0:T(8,128)(2,1)} %collective-permute-done.18.refs_0_.refs_7_, ...), custom_call_target="tpu_custom_call" | custom-call | flops 6442450944 | bytes 20971520 | tf_op jit(solution)/shard_map/ffn/pallas_call | solution.py:651
  280.0 11.8 %ffn.6 = (bf16[128,2048]{1,0:T(8,128)(2,1)}, bf16[128,2048]{1,0:T(8,128)(2,1)}, bf16[128,2048]{1,0:T(8,128)(2,1)}, bf16[128,2048]{1,0:T(8,128)(2,1)}, bf16[256,1...) custom-call(bf16[128,2048]{1,0:T(8,128)(2,1)} %collective-permute-done.21.refs_0_.refs_9_, ...), custom_call_target="tpu_custom_call" | custom-call | flops 6442450944 | bytes 20971520 | tf_op jit(solution)/shard_map/ffn/pallas_call | solution.py:651
  293.0 12.0 %ffn.7 = (bf16[128,2048]{1,0:T(8,128)(2,1)}, bf16[128,2048]{1,0:T(8,128)(2,1)}, bf16[128,2048]{1,0:T(8,128)(2,1)}, bf16[128,2048]{1,0:T(8,128)(2,1)}, bf16[256,1...) custom-call(bf16[128,2048]{1,0:T(8,128)(2,1)} %copy-done.64, ...), custom_call_target="tpu_custom_call" | custom-call | flops 6442450944 | bytes 20971520 | tf_op jit(solution)/shard_map/ffn/pallas_call | solution.py:651
  306.7 10.7 %outer.3 = (bf16[2,256,2048]{2,1,0:T(8,128)(2,1)}, bf16[2,256,2048]{2,1,0:T(8,128)(2,1)}) custom-call(s32[4]{0:T(128)} %broadcast_xor_fusion.refs_0_, bf16[256,1024]{1,0:T(8,128)(2,1)} %get-tuple-element.307.refs_1_, bf16[256,1024]{1,0:T(8,128)(2,1)} %get-tuple-element.308.refs_2_, bf16[256,1024]{1,0:T(8,128)(2,1)} %get-tuple-element.309.refs_3_, ...), custom_call_target="tpu_custom_call" | custom-call | flops 4294967296 | bytes 10485760 | tf_op jit(solution)/shard_map/outer/pallas_call | solution.py:718
  327.1 10.8 %outer.4 = (bf16[2,256,2048]{2,1,0:T(8,128)(2,1)}, bf16[2,256,2048]{2,1,0:T(8,128)(2,1)}) custom-call(s32[4]{0:T(128)} %broadcast_xor_fusion.refs_0_, bf16[256,1024]{1,0:T(8,128)(2,1)} %get-tuple-element.328.refs_1_, bf16[256,1024]{1,0:T(8,128)(2,1)} %get-tuple-element.329.refs_2_, bf16[256,1024]{1,0:T(8,128)(2,1)} %get-tuple-element.330.refs_3_, ...), custom_call_target="tpu_custom_call" | custom-call | flops 4294967296 | bytes 10485760 | tf_op jit(solution)/shard_map/outer/pallas_call | solution.py:718
  340.4 7.3 %collective-permute-done.29 = bf16[128,2048]{1,0:T(8,128)(2,1)} collective-permute-done((bf16[128,2048]{1,0:T(8,128)(2,1)}, bf16[128,2048]{1,0:T(8,128)(2,1)}, u32[]{:S(2)}, u32[]{:S(2)}) %collective-permute-start.29) | collective-permute-done | bytes 524320 | tf_op jit(solution)/shard_map/ppermute | solution.py:746
  358.2 10.7 %outer.5 = (bf16[2,256,2048]{2,1,0:T(8,128)(2,1)}, bf16[2,256,2048]{2,1,0:T(8,128)(2,1)}) custom-call(s32[4]{0:T(128)} %broadcast_xor_fusion.refs_0_, bf16[256,1024]{1,0:T(8,128)(2,1)} %get-tuple-element.349.refs_1_, bf16[256,1024]{1,0:T(8,128)(2,1)} %get-tuple-element.350.refs_2_, bf16[256,1024]{1,0:T(8,128)(2,1)} %get-tuple-element.351.refs_3_, ...), custom_call_target="tpu_custom_call" | custom-call | flops 4294967296 | bytes 10485760 | tf_op jit(solution)/shard_map/outer/pallas_call | solution.py:718
  374.6 3.3 fusion.37
  377.9 5.9 convolution_convert_fusion.4
  384.8 4.2 all-to-all-start.3
  399.2 10.4 %collective-permute-done.40 = bf16[128,2048]{1,0:T(8,128)(2,1)S(1)} collective-permute-done((bf16[128,2048]{1,0:T(8,128)(2,1)}, bf16[128,2048]{1,0:T(8,128)(2,1)S(1)}, u32[]{:S(2)}, u32[]{:S(2)}) %collective-permute-start.40) | collective-permute-done | bytes 524320 | tf_op jit(solution)/shard_map/ppermute | solution.py:746
  410.4 5.1 collective-permute-done.42
  425.3 34.6 %attn_bwd.1 = bf16[4,192,1024]{2,1,0:T(8,128)(2,1)} custom-call(s32[2,8]{1,0:T(2,128)S(1)} %pad_add_fusion.place_ref, bf16[192,4096]{1,0:T(8,128)(2,1)S(1)} %get-tuple-element.391.seq_ref, f32[64,4096]{1,0:T(8,128)S(1)} %copy-done.1, f32[1,4096]{1,0:T(1,128)S(1)} %get-tuple-element.393.lse_ref, bf16[32,80,128]{2,1,0:T(8,128)(2,1)S(1)} %all-to-all-done.3.do_ref, ...), custom_call_target="tpu_custom_call" | custom-call | flops 21474836480 | bytes 8388608 | tf_op jit(solution)/shard_map/attn_bwd/pallas_call | solution.py:557
  463.0 3.6 all-to-all-start.4
  471.6 14.3 %collective-permute-done.36 = bf16[128,2048]{1,0:T(8,128)(2,1)} collective-permute-done((bf16[128,2048]{1,0:T(8,128)(2,1)}, bf16[128,2048]{1,0:T(8,128)(2,1)}, u32[]{:S(2)}, u32[]{:S(2)}) %collective-permute-start.36) | collective-permute-done | bytes 524320 | tf_op jit(solution)/shard_map/ppermute | solution.py:746
  487.2 4.5 collective-permute-done.46
  491.7 10.5 %all-to-all-done.4 = bf16[4,192,1024]{2,1,0:T(8,128)(2,1)S(1)} async-done(((bf16[4,192,1024]{2,1,0:T(8,128)(2,1)}), bf16[4,192,1024]{2,1,0:T(8,128)(2,1)S(1)}, u32[]{:S(2)}, u32[]{:S(2)}) %all-to-all-start.4) | async-done | bytes 1572896 | tf_op jit(solution)/shard_map/all_to_all | solution.py:1050
  506.0 3.2 convolution_convert_fusion.1
  509.1 3.8 convolution_convert_fusion
  521.4 10.7 %collective-permute-done.51 = bf16[128,2048]{1,0:T(8,128)(2,1)} collective-permute-done((bf16[128,2048]{1,0:T(8,128)(2,1)S(1)}, bf16[128,2048]{1,0:T(8,128)(2,1)}, u32[]{:S(2)}, u32[]{:S(2)}) %collective-permute-start.51) | collective-permute-done | bytes 524320 | tf_op jit(solution)/shard_map/ppermute | solution.py:746
  545.0 4.1 collective-permute-done.54
  549.1 6.4 %collective-permute-done.57 = bf16[8,32,768]{2,1,0:T(8,128)(2,1)S(1)} collective-permute-done((bf16[8,32,768]{2,1,0:T(8,128)(2,1)S(1)}, bf16[8,32,768]{2,1,0:T(8,128)(2,1)S(1)}, u32[]{:S(2)}, u32[]{:S(2)}) %collective-permute-start.57) | collective-permute-done | bytes 393248 | tf_op jit(solution)/shard_map/ppermute | solution.py:746
  560.0 5.4 all-to-all-start.5
  565.4 3.2 convert_add_fusion.1
  568.5 3.0 convert_add_fusion.2
  571.6 3.8 collective-permute-done.58
  580.3 3.0 convert_add_fusion.3
  584.6 14.3 %collective-permute-done.60 = bf16[128,2048]{1,0:T(8,128)(2,1)S(1)} collective-permute-done((bf16[128,2048]{1,0:T(8,128)(2,1)S(1)}, bf16[128,2048]{1,0:T(8,128)(2,1)S(1)}, u32[]{:S(2)}, u32[]{:S(2)}) %collective-permute-start.60) | collective-permute-done | bytes 524320 | tf_op jit(solution)/shard_map/ppermute | solution.py:751
  (362 shorter events, 170.8 us)
Async XLA Ops:
  7.2 155.0 %all-gather.6.cloned.1.call-start = ((), (), s32[]{:S(2)}) async-start(), calls=%async_computation.6 | async-start | bytes 5242880 | tf_op jit(solution)/shard_map/all_gather | solution.py:920
  11.2 38.7 %all-to-all-start = ((bf16[8,64,768]{2,1,0:T(8,128)(2,1)}), bf16[8,64,768]{2,1,0:T(8,128)(2,1)S(1)}, u32[]{:S(2)}, u32[]{:S(2)}) async-start(bf16[8,64,768]{2,1,0:T(8,128)(2,1)} %copy.119), calls=%async_computation | async-start | bytes 1572864 | tf_op jit(solution)/shard_map/all_to_all | solution.py:852
  18.5 143.7 %all-gather.8.cloned.1.call-start = ((), (), s32[]{:S(2)}) async-start(), calls=%async_computation.7 | async-start | bytes 8650752 | tf_op jit(solution)/shard_map/all_gather | solution.py:928
  19.7 26.9 %collective-permute-start = (bf16[128,2048]{1,0:T(8,128)(2,1)S(1)}, bf16[128,2048]{1,0:T(8,128)(2,1)S(1)}, u32[]{:S(2)}, u32[]{:S(2)}) collective-permute-start(bf16[128,2048]{1,0:T(8,128)(2,1)S(1)} %get-tuple-element.450), channel_id=1, source_target_pairs={{0,8},{8,16},{16,24},{24,0},{1,9},{9,17},{17,25},{25,1},{2,10},{10... | collective-permute-start | bytes 1572872 | tf_op jit(solution)/shard_map/ppermute | solution.py:751
  21.6 24.9 %collective-permute-start.1 = (bf16[128,2048]{1,0:T(8,128)(2,1)S(1)}, bf16[128,2048]{1,0:T(8,128)(2,1)}, u32[]{:S(2)}, u32[]{:S(2)}) collective-permute-start(bf16[128,2048]{1,0:T(8,128)(2,1)S(1)} %get-tuple-element.450), channel_id=1, source_target_pairs={{0,4},{4,0},{1,5},{5,1},{2,6},{6,2},{3,7},{7,3},{8,12},{12,8},{9,1... | collective-permute-start | bytes 1572872 | tf_op jit(solution)/shard_map/ppermute | solution.py:746
  49.9 156.3 %all-gather.10.cloned.1.call-start = ((), (), s32[]{:S(2)}) async-start(), calls=%async_computation.8 | async-start | bytes 5242880 | tf_op jit(solution)/shard_map/all_gather | solution.py:932
  81.0 19.2 %collective-permute-start.10 = (bf16[8,64,768]{2,1,0:T(8,128)(2,1)S(1)}, bf16[8,64,768]{2,1,0:T(8,128)(2,1)S(1)}, u32[]{:S(2)}, u32[]{:S(2)}) collective-permute-start(bf16[8,64,768]{2,1,0:T(8,128)(2,1)S(1)} %constant_dynamic-update-slice_fusion), channel_id=1, source_target_pairs={{0,1},{1,0},{2,3},{3,2},{4,5},{5,4},{6,7},{7,6},{8,9},{9,8},{10,11... | collective-permute-start | bytes 2359304 | tf_op jit(solution)/shard_map/ppermute | solution.py:746
  81.1 18.3 %collective-permute-start.8 = (bf16[128,2048]{1,0:T(8,128)(2,1)S(1)}, bf16[128,2048]{1,0:T(8,128)(2,1)S(1)}, u32[]{:S(2)}, u32[]{:S(2)}) collective-permute-start(bf16[128,2048]{1,0:T(8,128)(2,1)S(1)} %collective-permute-done.5), channel_id=1, source_target_pairs={{0,4},{4,0},{1,5},{5,1},{2,6},{6,2},{3,7},{7,3},{8,12},{12,8},{9,1... | collective-permute-start | bytes 1572872 | tf_op jit(solution)/shard_map/ppermute | solution.py:746
  109.4 27.4 %collective-permute-start.11 = (bf16[128,2048]{1,0:T(8,128)(2,1)S(1)}, bf16[128,2048]{1,0:T(8,128)(2,1)S(1)}, u32[]{:S(2)}, u32[]{:S(2)}) collective-permute-start(bf16[128,2048]{1,0:T(8,128)(2,1)S(1)} %copy-done.50), channel_id=1, source_target_pairs={{0,8},{8,16},{16,24},{24,0},{1,9},{9,17},{17,25},{25,1},{2,10},{10... | collective-permute-start | bytes 1572872 | tf_op jit(solution)/shard_map/ppermute | solution.py:751
  110.4 26.4 %collective-permute-start.12 = (bf16[128,2048]{1,0:T(8,128)(2,1)S(1)}, bf16[128,2048]{1,0:T(8,128)(2,1)S(1)}, u32[]{:S(2)}, u32[]{:S(2)}) collective-permute-start(bf16[128,2048]{1,0:T(8,128)(2,1)S(1)} %copy-done.50), channel_id=1, source_target_pairs={{0,4},{4,0},{1,5},{5,1},{2,6},{6,2},{3,7},{7,3},{8,12},{12,8},{9,1... | collective-permute-start | bytes 1572872 | tf_op jit(solution)/shard_map/ppermute | solution.py:746
  138.4 23.7 %all-to-all-start.1 = ((bf16[4,192,1024]{2,1,0:T(8,128)(2,1)}), bf16[4,192,1024]{2,1,0:T(8,128)(2,1)S(1)}, u32[]{:S(2)}, u32[]{:S(2)}) async-start(bf16[4,192,1024]{2,1,0:T(8,128)(2,1)} %bitcast.14), calls=%async_computation.1 | async-start | bytes 3145728 | tf_op jit(solution)/shard_map/all_to_all | solution.py:948
  142.1 107.2 %all-gather.12.cloned.1.call-start = ((), (), s32[]{:S(2)}) async-start(), calls=%async_computation.9 | async-start | bytes 5242880 | tf_op jit(solution)/shard_map/all_gather | solution.py:950
  142.2 18.0 %collective-permute-start.13 = (bf16[128,2048]{1,0:T(8,128)(2,1)S(1)}, bf16[128,2048]{1,0:T(8,128)(2,1)}, u32[]{:S(2)}, u32[]{:S(2)}) collective-permute-start(bf16[128,2048]{1,0:T(8,128)(2,1)S(1)} %copy-done.59), channel_id=1, source_target_pairs={{0,8},{8,16},{16,24},{24,0},{1,9},{9,17},{17,25},{25,1},{2,10},{10... | collective-permute-start | bytes 1572872 | tf_op jit(solution)/shard_map/ppermute | solution.py:751
  162.5 37.8 %collective-permute-start.15 = (bf16[128,2048]{1,0:T(8,128)(2,1)}, bf16[128,2048]{1,0:T(8,128)(2,1)}, u32[]{:S(2)}, u32[]{:S(2)}) collective-permute-start(bf16[128,2048]{1,0:T(8,128)(2,1)} %collective-permute-done.13.refs_2_.refs_9_), channel_id=1, source_target_pairs={{0,8},{8,16},{16,24},{24,0},{1,9},{9,17},{17,25},{25,1},{2,10},{10... | collective-permute-start | bytes 1572872 | tf_op jit(solution)/shard_map/ppermute | solution.py:751
  173.6 26.7 %collective-permute-start.16 = (bf16[128,2048]{1,0:T(8,128)(2,1)}, bf16[128,2048]{1,0:T(8,128)(2,1)}, u32[]{:S(2)}, u32[]{:S(2)}) collective-permute-start(bf16[128,2048]{1,0:T(8,128)(2,1)} %collective-permute-done.13.refs_2_.refs_9_), channel_id=1, source_target_pairs={{0,4},{4,0},{1,5},{5,1},{2,6},{6,2},{3,7},{7,3},{8,12},{12,8},{9,1... | collective-permute-start | bytes 1572872 | tf_op jit(solution)/shard_map/ppermute | solution.py:746
  200.3 26.0 %all-to-all-start.2 = ((bf16[32,80,128]{2,1,0:T(8,128)(2,1)}), bf16[32,80,128]{2,1,0:T(8,128)(2,1)S(1)}, u32[]{:S(2)}, u32[]{:S(2)}) async-start(bf16[32,80,128]{2,1,0:T(8,128)(2,1)} %get-tuple-element.248), calls=%async_computation.2 | async-start | bytes 1310720 | tf_op jit(solution)/shard_map/all_to_all | solution.py:956
  204.4 21.1 %collective-permute-start.17 = (bf16[128,2048]{1,0:T(8,128)(2,1)}, bf16[128,2048]{1,0:T(8,128)(2,1)S(1)}, u32[]{:S(2)}, u32[]{:S(2)}) collective-permute-start(bf16[128,2048]{1,0:T(8,128)(2,1)} %collective-permute-done.15.refs_2_.refs_11_), channel_id=1, source_target_pairs={{0,4},{4,0},{1,5},{5,1},{2,6},{6,2},{3,7},{7,3},{8,12},{12,8},{9,1... | collective-permute-start | bytes 1572872 | tf_op jit(solution)/shard_map/ppermute | solution.py:746
  278.8 26.2 %collective-permute-start.27 = (bf16[128,2048]{1,0:T(8,128)(2,1)}, bf16[128,2048]{1,0:T(8,128)(2,1)S(1)}, u32[]{:S(2)}, u32[]{:S(2)}) collective-permute-start(bf16[128,2048]{1,0:T(8,128)(2,1)} %get-tuple-element.277), channel_id=1, source_target_pairs={{0,4},{4,0},{1,5},{5,1},{2,6},{6,2},{3,7},{7,3},{8,12},{12,8},{9,1... | collective-permute-start | bytes 1572872 | tf_op jit(solution)/shard_map/ppermute | solution.py:746
  319.0 28.8 %collective-permute-start.33 = (bf16[2,256,2048]{2,1,0:T(8,128)(2,1)}, bf16[2,256,2048]{2,1,0:T(8,128)(2,1)}, u32[]{:S(2)}, u32[]{:S(2)}) collective-permute-start(bf16[2,256,2048]{2,1,0:T(8,128)(2,1)} %get-tuple-element.323), channel_id=1, source_target_pairs={{0,1},{1,0},{2,3},{3,2},{4,5},{5,4},{6,7},{7,6},{8,9},{9,8},{10,11... | collective-permute-start | bytes 6291464 | tf_op jit(solution)/shard_map/ppermute | solution.py:746
  321.9 49.5 %collective-permute-start.24 = (bf16[128,2048]{1,0:T(8,128)(2,1)}, bf16[128,2048]{1,0:T(8,128)(2,1)S(1)}, u32[]{:S(2)}, u32[]{:S(2)}) collective-permute-start(bf16[128,2048]{1,0:T(8,128)(2,1)} %get-tuple-element.266), channel_id=1, source_target_pairs={{0,4},{4,0},{1,5},{5,1},{2,6},{6,2},{3,7},{7,3},{8,12},{12,8},{9,1... | collective-permute-start | bytes 1572872 | tf_op jit(solution)/shard_map/ppermute | solution.py:746
  322.5 25.3 %collective-permute-start.29 = (bf16[128,2048]{1,0:T(8,128)(2,1)}, bf16[128,2048]{1,0:T(8,128)(2,1)}, u32[]{:S(2)}, u32[]{:S(2)}) collective-permute-start(bf16[128,2048]{1,0:T(8,128)(2,1)} %get-tuple-element.298), channel_id=1, source_target_pairs={{0,4},{4,0},{1,5},{5,1},{2,6},{6,2},{3,7},{7,3},{8,12},{12,8},{9,1... | collective-permute-start | bytes 1572872 | tf_op jit(solution)/shard_map/ppermute | solution.py:746
  326.0 21.8 %collective-permute-start.32 = (bf16[128,2048]{1,0:T(8,128)(2,1)}, bf16[128,2048]{1,0:T(8,128)(2,1)}, u32[]{:S(2)}, u32[]{:S(2)}) collective-permute-start(bf16[128,2048]{1,0:T(8,128)(2,1)} %add_convert_fusion.14), channel_id=1, source_target_pairs={{0,8},{8,16},{16,24},{24,0},{1,9},{9,17},{17,25},{25,1},{2,10},{10... | collective-permute-start | bytes 1572872 | tf_op jit(solution)/shard_map/ppermute | solution.py:751
  347.8 23.6 %collective-permute-start.35 = (bf16[2,256,2048]{2,1,0:T(8,128)(2,1)}, bf16[2,256,2048]{2,1,0:T(8,128)(2,1)}, u32[]{:S(2)}, u32[]{:S(2)}) collective-permute-start(bf16[2,256,2048]{2,1,0:T(8,128)(2,1)} %get-tuple-element.344), channel_id=1, source_target_pairs={{0,1},{1,0},{2,3},{3,2},{4,5},{5,4},{6,7},{7,6},{8,9},{9,8},{10,11... | collective-permute-start | bytes 6291464 | tf_op jit(solution)/shard_map/ppermute | solution.py:746
  350.0 21.4 %collective-permute-start.34 = (bf16[128,2048]{1,0:T(8,128)(2,1)}, bf16[128,2048]{1,0:T(8,128)(2,1)}, u32[]{:S(2)}, u32[]{:S(2)}) collective-permute-start(bf16[128,2048]{1,0:T(8,128)(2,1)} %add_convert_fusion.13), channel_id=1, source_target_pairs={{0,8},{8,16},{16,24},{24,0},{1,9},{9,17},{17,25},{25,1},{2,10},{10... | collective-permute-start | bytes 1572872 | tf_op jit(solution)/shard_map/ppermute | solution.py:751
  353.9 43.8 %collective-permute-start.38 = (bf16[128,2048]{1,0:T(8,128)(2,1)}, bf16[128,2048]{1,0:T(8,128)(2,1)}, u32[]{:S(2)}, u32[]{:S(2)}) collective-permute-start(bf16[128,2048]{1,0:T(8,128)(2,1)} %get-tuple-element.454), channel_id=1, source_target_pairs={{0,2},{2,0},{1,3},{3,1},{4,6},{6,4},{5,7},{7,5},{8,10},{10,8},{9,1... | collective-permute-start | bytes 1572872 | tf_op jit(solution)/shard_map/ppermute | solution.py:746
  355.5 182.1 %collective-permute-start.55 = (bf16[128,2048]{1,0:T(8,128)(2,1)}, bf16[128,2048]{1,0:T(8,128)(2,1)}, u32[]{:S(2)}, u32[]{:S(2)}) collective-permute-start(bf16[128,2048]{1,0:T(8,128)(2,1)} %get-tuple-element.453), channel_id=1, source_target_pairs={{0,2},{2,0},{1,3},{3,1},{4,6},{6,4},{5,7},{7,5},{8,10},{10,8},{9,1... | collective-permute-start | bytes 1572872 | tf_op jit(solution)/shard_map/ppermute | solution.py:746
  374.6 43.6 %collective-permute-start.39 = (bf16[2,256,2048]{2,1,0:T(8,128)(2,1)}, bf16[2,256,2048]{2,1,0:T(8,128)(2,1)}, u32[]{:S(2)}, u32[]{:S(2)}) collective-permute-start(bf16[2,256,2048]{2,1,0:T(8,128)(2,1)} %get-tuple-element.379), channel_id=1, source_target_pairs={{0,1},{1,0},{2,3},{3,2},{4,5},{5,4},{6,7},{7,6},{8,9},{9,8},{10,11... | collective-permute-start | bytes 6291464 | tf_op jit(solution)/shard_map/ppermute | solution.py:746
  384.8 33.4 %all-to-all-start.3 = ((bf16[32,80,128]{2,1,0:T(8,128)(2,1)}), bf16[32,80,128]{2,1,0:T(8,128)(2,1)S(1)}, u32[]{:S(2)}, u32[]{:S(2)}) async-start(bf16[32,80,128]{2,1,0:T(8,128)(2,1)} %fusion.13), calls=%async_computation.3 | async-start | bytes 1310720 | tf_op jit(solution)/shard_map/all_to_all | solution.py:1035
  389.0 143.1 %all-gather.14.cloned.1.call-start = ((), (), s32[]{:S(2)}) async-start(), calls=%async_computation.10 | async-start | bytes 4718592 | tf_op jit(solution)/shard_map/all_gather | solution.py:1041
  389.0 20.6 %collective-permute-start.40 = (bf16[128,2048]{1,0:T(8,128)(2,1)}, bf16[128,2048]{1,0:T(8,128)(2,1)S(1)}, u32[]{:S(2)}, u32[]{:S(2)}) collective-permute-start(bf16[128,2048]{1,0:T(8,128)(2,1)} %get-tuple-element.380), channel_id=1, source_target_pairs={{0,4},{4,0},{1,5},{5,1},{2,6},{6,2},{3,7},{7,3},{8,12},{12,8},{9,1... | collective-permute-start | bytes 1572872 | tf_op jit(solution)/shard_map/ppermute | solution.py:746
  392.2 23.4 %collective-permute-start.42 = (bf16[128,2048]{1,0:T(8,128)(2,1)S(1)}, bf16[128,2048]{1,0:T(8,128)(2,1)}, u32[]{:S(2)}, u32[]{:S(2)}) collective-permute-start(bf16[128,2048]{1,0:T(8,128)(2,1)S(1)} %add_convert_fusion.10), channel_id=1, source_target_pairs={{0,8},{8,16},{16,24},{24,0},{1,9},{9,17},{17,25},{25,1},{2,10},{10... | collective-permute-start | bytes 1572872 | tf_op jit(solution)/shard_map/ppermute | solution.py:751
  397.7 62.2 %collective-permute-start.37 = (bf16[128,2048]{1,0:T(8,128)(2,1)}, bf16[128,2048]{1,0:T(8,128)(2,1)}, u32[]{:S(2)}, u32[]{:S(2)}) collective-permute-start(bf16[128,2048]{1,0:T(8,128)(2,1)} %get-tuple-element.452), channel_id=1, source_target_pairs={{0,2},{2,0},{1,3},{3,1},{4,6},{6,4},{5,7},{7,5},{8,10},{10,8},{9,1... | collective-permute-start | bytes 1572872 | tf_op jit(solution)/shard_map/ppermute | solution.py:746
  409.6 51.3 %collective-permute-start.44 = (bf16[128,2048]{1,0:T(8,128)(2,1)}, bf16[128,2048]{1,0:T(8,128)(2,1)}, u32[]{:S(2)}, u32[]{:S(2)}) collective-permute-start(bf16[128,2048]{1,0:T(8,128)(2,1)} %get-tuple-element.387), channel_id=1, source_target_pairs={{0,4},{4,0},{1,5},{5,1},{2,6},{6,2},{3,7},{7,3},{8,12},{12,8},{9,1... | collective-permute-start | bytes 1572872 | tf_op jit(solution)/shard_map/ppermute | solution.py:746
  420.6 41.9 %collective-permute-start.45 = (bf16[128,2048]{1,0:T(8,128)(2,1)}, bf16[128,2048]{1,0:T(8,128)(2,1)}, u32[]{:S(2)}, u32[]{:S(2)}) collective-permute-start(bf16[128,2048]{1,0:T(8,128)(2,1)} %add_convert_fusion.8), channel_id=1, source_target_pairs={{0,8},{8,16},{16,24},{24,0},{1,9},{9,17},{17,25},{25,1},{2,10},{10... | collective-permute-start | bytes 1572872 | tf_op jit(solution)/shard_map/ppermute | solution.py:751
  424.8 38.1 %collective-permute-start.43 = (bf16[128,2048]{1,0:T(8,128)(2,1)S(1)}, bf16[128,2048]{1,0:T(8,128)(2,1)}, u32[]{:S(2)}, u32[]{:S(2)}) collective-permute-start(bf16[128,2048]{1,0:T(8,128)(2,1)S(1)} %get-tuple-element.456), channel_id=1, source_target_pairs={{0,2},{2,0},{1,3},{3,1},{4,6},{6,4},{5,7},{7,5},{8,10},{10,8},{9,1... | collective-permute-start | bytes 1572872 | tf_op jit(solution)/shard_map/ppermute | solution.py:746
  459.9 26.0 %collective-permute-start.36 = (bf16[128,2048]{1,0:T(8,128)(2,1)}, bf16[128,2048]{1,0:T(8,128)(2,1)}, u32[]{:S(2)}, u32[]{:S(2)}) collective-permute-start(bf16[128,2048]{1,0:T(8,128)(2,1)} %get-tuple-element.372), channel_id=1, source_target_pairs={{0,4},{4,0},{1,5},{5,1},{2,6},{6,2},{3,7},{7,3},{8,12},{12,8},{9,1... | collective-permute-start | bytes 1572872 | tf_op jit(solution)/shard_map/ppermute | solution.py:746
  460.9 79.4 %collective-permute-start.56 = (bf16[128,2048]{1,0:T(8,128)(2,1)}, bf16[128,2048]{1,0:T(8,128)(2,1)}, u32[]{:S(2)}, u32[]{:S(2)}) collective-permute-start(bf16[128,2048]{1,0:T(8,128)(2,1)} %get-tuple-element.451), channel_id=1, source_target_pairs={{0,2},{2,0},{1,3},{3,1},{4,6},{6,4},{5,7},{7,5},{8,10},{10,8},{9,1... | collective-permute-start | bytes 1572872 | tf_op jit(solution)/shard_map/ppermute | solution.py:746
  462.5 24.7 %collective-permute-start.47 = (bf16[128,2048]{1,0:T(8,128)(2,1)}, bf16[128,2048]{1,0:T(8,128)(2,1)S(1)}, u32[]{:S(2)}, u32[]{:S(2)}) collective-permute-start(bf16[128,2048]{1,0:T(8,128)(2,1)} %get-tuple-element.455), channel_id=1, source_target_pairs={{0,2},{2,0},{1,3},{3,1},{4,6},{6,4},{5,7},{7,5},{8,10},{10,8},{9,1... | collective-permute-start | bytes 1572872 | tf_op jit(solution)/shard_map/ppermute | solution.py:746
  463.0 39.2 %all-to-all-start.4 = ((bf16[4,192,1024]{2,1,0:T(8,128)(2,1)}), bf16[4,192,1024]{2,1,0:T(8,128)(2,1)S(1)}, u32[]{:S(2)}, u32[]{:S(2)}) async-start(bf16[4,192,1024]{2,1,0:T(8,128)(2,1)} %attn_bwd.1), calls=%async_computation.4 | async-start | bytes 3145728 | tf_op jit(solution)/shard_map/all_to_all | solution.py:1050
  468.0 23.7 %collective-permute-start.46 = (bf16[128,2048]{1,0:T(8,128)(2,1)S(1)}, bf16[128,2048]{1,0:T(8,128)(2,1)S(1)}, u32[]{:S(2)}, u32[]{:S(2)}) collective-permute-start(bf16[128,2048]{1,0:T(8,128)(2,1)S(1)} %add_convert_fusion.7), channel_id=1, source_target_pairs={{0,8},{8,16},{16,24},{24,0},{1,9},{9,17},{17,25},{25,1},{2,10},{10... | collective-permute-start | bytes 1572872 | tf_op jit(solution)/shard_map/ppermute | solution.py:751
  513.1 19.0 %collective-permute-start.52 = (bf16[8,2,64,768]{3,2,1,0:T(8,128)(2,1)S(1)}, bf16[8,2,64,768]{3,2,1,0:T(8,128)(2,1)}, u32[]{:S(2)}, u32[]{:S(2)}) collective-permute-start(bf16[8,2,64,768]{3,2,1,0:T(8,128)(2,1)S(1)} %fusion.2), channel_id=1, source_target_pairs={{0,1},{1,0},{2,3},{3,2},{4,5},{5,4},{6,7},{7,6},{8,9},{9,8},{10,11... | collective-permute-start | bytes 4718600 | tf_op jit(solution)/shard_map/ppermute | solution.py:746
  518.9 24.4 %collective-permute-start.50 = (bf16[128,2048]{1,0:T(8,128)(2,1)}, bf16[128,2048]{1,0:T(8,128)(2,1)}, u32[]{:S(2)}, u32[]{:S(2)}) collective-permute-start(bf16[128,2048]{1,0:T(8,128)(2,1)} %get-tuple-element.466), channel_id=1, source_target_pairs={{0,4},{4,0},{1,5},{5,1},{2,6},{6,2},{3,7},{7,3},{8,12},{12,8},{9,1... | collective-permute-start | bytes 1572872 | tf_op jit(solution)/shard_map/ppermute | solution.py:746
  535.6 19.9 %collective-permute-start.53 = (bf16[128,2048]{1,0:T(8,128)(2,1)S(1)}, bf16[128,2048]{1,0:T(8,128)(2,1)S(1)}, u32[]{:S(2)}, u32[]{:S(2)}) collective-permute-start(bf16[128,2048]{1,0:T(8,128)(2,1)S(1)} %add_convert_fusion.4), channel_id=1, source_target_pairs={{0,8},{8,16},{16,24},{24,0},{1,9},{9,17},{17,25},{25,1},{2,10},{10... | collective-permute-start | bytes 1572872 | tf_op jit(solution)/shard_map/ppermute | solution.py:751
  537.6 17.9 %collective-permute-start.57 = (bf16[8,32,768]{2,1,0:T(8,128)(2,1)S(1)}, bf16[8,32,768]{2,1,0:T(8,128)(2,1)S(1)}, u32[]{:S(2)}, u32[]{:S(2)}) collective-permute-start(bf16[8,32,768]{2,1,0:T(8,128)(2,1)S(1)} %get-tuple-element.472), channel_id=1, source_target_pairs={{0,2},{2,0},{1,3},{3,1},{4,6},{6,4},{5,7},{7,5},{8,10},{10,8},{9,1... | collective-permute-start | bytes 1179656 | tf_op jit(solution)/shard_map/ppermute | solution.py:746
  540.4 31.2 %collective-permute-start.49 = (bf16[128,2048]{1,0:T(8,128)(2,1)}, bf16[128,2048]{1,0:T(8,128)(2,1)}, u32[]{:S(2)}, u32[]{:S(2)}) collective-permute-start(bf16[128,2048]{1,0:T(8,128)(2,1)} %get-tuple-element.467), channel_id=1, source_target_pairs={{0,4},{4,0},{1,5},{5,1},{2,6},{6,2},{3,7},{7,3},{8,12},{12,8},{9,1... | collective-permute-start | bytes 1572872 | tf_op jit(solution)/shard_map/ppermute | solution.py:746
  543.3 41.2 %collective-permute-start.48 = (bf16[128,2048]{1,0:T(8,128)(2,1)}, bf16[128,2048]{1,0:T(8,128)(2,1)}, u32[]{:S(2)}, u32[]{:S(2)}) collective-permute-start(bf16[128,2048]{1,0:T(8,128)(2,1)} %get-tuple-element.468), channel_id=1, source_target_pairs={{0,4},{4,0},{1,5},{5,1},{2,6},{6,2},{3,7},{7,3},{8,12},{12,8},{9,1... | collective-permute-start | bytes 1572872 | tf_op jit(solution)/shard_map/ppermute | solution.py:746
  560.0 43.6 %all-to-all-start.5 = ((bf16[8,64,768]{2,1,0:T(8,128)(2,1)}), bf16[8,64,768]{2,1,0:T(8,128)(2,1)}, u32[]{:S(2)}, u32[]{:S(2)}) async-start(bf16[8,64,768]{2,1,0:T(8,128)(2,1)} %fusion.3), calls=%async_computation.5 | async-start | bytes 1572864 | tf_op jit(solution)/shard_map/all_to_all | solution.py:1089
  578.8 20.1 %collective-permute-start.60 = (bf16[128,2048]{1,0:T(8,128)(2,1)S(1)}, bf16[128,2048]{1,0:T(8,128)(2,1)S(1)}, u32[]{:S(2)}, u32[]{:S(2)}) collective-permute-start(bf16[128,2048]{1,0:T(8,128)(2,1)S(1)} %add_convert_fusion), channel_id=1, source_target_pairs={{0,8},{8,16},{16,24},{24,0},{1,9},{9,17},{17,25},{25,1},{2,10},{10... | collective-permute-start | bytes 1572872 | tf_op jit(solution)/shard_map/ppermute | solution.py:751
  (93 other events, 914.4 us)
Sparse Core Ops, SparseCore 0:
  9.6 37.1 all-gather.5
  50.0 100.1 all-gather.7
  151.8 34.4 all-gather.9
  187.7 41.4 all-gather.11
  422.1 85.5 all-gather.13

commit v4 on v3

--- a/solution.py
+++ b/solution.py
@@ -366,6 +366,7 @@
 F32 = jnp.float32
 LOG2E = math.log2(math.e)
 VMEM = pl.BlockSpec(memory_space=pltpu.VMEM)
+ANY = pl.BlockSpec(memory_space=pl.ANY)
 
 
 def mxu(a, b):
@@ -383,9 +384,13 @@
     qkv_ref,
     extra_ref,
     out_ref,
+    o32_hbm,
+    lse_ref,
+    seq_hbm,
+    seq_ref,
     o32_ref,
-    lse_ref,
-    seq_ref,
+    seq_sem,
+    o32_sem,
     k_scr,
     m_scr,
     l_scr,
@@ -405,9 +410,12 @@
             seq_ref[:, lo : lo + width] = piece
             k_scr[lo : lo + width, :] = piece[HD : 2 * HD].T
 
-    def tile(kb, q_t, masked):
-        at = pl.multiple_of(kb * blk, blk)
-        score = mxu(k_scr[pl.ds(at, blk), :], q_t) * coef
+    leaving = [pltpu.make_async_copy(seq_ref, seq_hbm, seq_sem)]
+    leaving[0].start()
+
+    def tile(kb, q_t, masked, wide=1):
+        keys = pl.ds(pl.multiple_of(kb * blk, blk), wide * blk)
+        score = mxu(k_scr[keys, :], q_t) * coef
         if masked:
             score = jnp.where(causal(blk), score, -1e30)
         old = m_scr[...]
@@ -416,7 +424,7 @@
         fade = jnp.exp2(old - new)
         m_scr[...] = new
         l_scr[...] = l_scr[...] * fade + jnp.sum(p, axis=0, keepdims=True)
-        acc_scr[...] = acc_scr[...] * fade + mxu(seq_ref[2 * HD :, pl.ds(at, blk)], p.astype(BF16))
+        acc_scr[...] = acc_scr[...] * fade + mxu(seq_ref[2 * HD :, keys], p.astype(BF16))
 
     for qb in range(blocks):
         lo = qb * blk
@@ -425,20 +433,28 @@
         l_scr[...] = jnp.zeros_like(l_scr)
         acc_scr[...] = jnp.zeros_like(acc_scr)
         tile(qb, q_t, True)
-        if qb > 0:
-
-            @pl.loop(0, qb)
-            def _(kb):
-                tile(kb, q_t, False)
+        kb = 0
+        while kb < qb:
+            wide = min(4, qb - kb)
+            tile(kb, q_t, False, wide)
+            kb += wide
 
         o = acc_scr[...] / l_scr[...]
         o32_ref[:, lo : lo + blk] = o
+        leaving.append(
+            pltpu.make_async_copy(
+                o32_ref.at[:, lo : lo + blk], o32_hbm.at[:, lo : lo + blk], o32_sem.at[qb]
+            )
+        )
+        leaving[-1].start()
         lse_ref[:, lo : lo + blk] = m_scr[...] + jnp.log2(l_scr[...])
         low = o.astype(BF16)
         for j in range(pieces):
             owner = place_ref[1, qb] * pieces + j
             out_ref[owner, :HD] = low[:, j * width : (j + 1) * width]
             out_ref[owner, HD:] = extra_ref[...]
+    for c in leaving:
+        c.wait()
 
 
 def attn_fwd(place, qkv, extra, blocks):
@@ -454,14 +470,18 @@
             jax.ShapeDtypeStruct((3 * HD, total), BF16),
         ),
         in_specs=[pl.BlockSpec(memory_space=pltpu.SMEM), VMEM, VMEM],
-        out_specs=(VMEM,) * 4,
+        out_specs=(VMEM, ANY, VMEM, ANY),
         scratch_shapes=[
+            pltpu.VMEM((3 * HD, total), BF16),
+            pltpu.VMEM((HD, total), F32),
+            pltpu.SemaphoreType.DMA,
+            pltpu.SemaphoreType.DMA((blocks,)),
             pltpu.VMEM((total, HD), BF16),
             pltpu.VMEM((1, blk), F32),
             pltpu.VMEM((1, blk), F32),
             pltpu.VMEM((HD, blk), F32),
         ],
-        compiler_params=pltpu.CompilerParams(vmem_limit_bytes=40 << 20),
+        compiler_params=pltpu.CompilerParams(vmem_limit_bytes=60 << 20),
         cost_estimate=pl.CostEstimate(
             flops=8 * total * total * HD, bytes_accessed=8 << 20, transcendentals=total * total // 2
         ),
@@ -471,13 +491,18 @@
 
 def attn_bwd_kernel(
     place_ref,
+    seq_hbm,
+    o32_hbm,
+    lse_ref,
+    do_ref,
+    cos_hbm,
+    sin_hbm,
+    out_ref,
     seq_ref,
     o32_ref,
-    lse_ref,
-    do_ref,
     cos_ref,
     sin_ref,
-    out_ref,
+    in_sem,
     q_scr,
     k_scr,
     v_scr,
@@ -496,6 +521,16 @@
     scale = HD**-0.5
     coef = LOG2E * scale
     half = HD // 2
+    arriving = [
+        pltpu.make_async_copy(src, dst, in_sem.at[i])
+        for i, (src, dst) in enumerate(
+            ((seq_hbm, seq_ref), (o32_hbm, o32_ref), (cos_hbm, cos_ref), (sin_hbm, sin_ref))
+        )
+    ]
+    for c in arriving:
+        c.start()
+    for c in arriving[:2]:
+        c.wait()
     for s in range(blocks):
         for j in range(pieces):
             lo = s * blk + j * width
@@ -509,6 +544,8 @@
             k_scr[lo : lo + width, :] = seq_ref[HD : 2 * HD, lo : lo + width].T
             v_scr[lo : lo + width, :] = seq_ref[2 * HD :, lo : lo + width].T
     dq_scr[...] = jnp.zeros_like(dq_scr)
+    for c in arriving[2:]:
+        c.wait()
 
     def turn_back(v, s):
         c = cos_ref[:, s * blk : (s + 1) * blk]
@@ -527,8 +564,8 @@
         v = v_scr[lo : lo + blk, :]
         k_t = seq_ref[HD : 2 * HD, lo : lo + blk]
 
-        def tile(qb, masked):
-            here = pl.ds(pl.multiple_of(qb * blk, blk), blk)
+        def tile(qb, masked, wide=1):
+            here = pl.ds(pl.multiple_of(qb * blk, blk), wide * blk)
             p = jnp.exp2(mxu(k, seq_ref[:HD, here]) * coef - lse_ref[:, here])
             if masked:
                 p = jnp.where(causal(blk), p, 0.0)
@@ -538,13 +575,17 @@
             return mxu(ds, q_scr[here, :]), mxu(p.astype(BF16), do_scr[here, :])
 
         dk_scr[...], dv_scr[...] = tile(kb, True)
-        if kb < blocks - 1:
-
-            @pl.loop(kb + 1, blocks)
-            def _(qb):
-                dk, dv = tile(qb, False)
-                dk_scr[...] += dk
-                dv_scr[...] += dv
+
+        def add_tile(qb, wide):
+            dk, dv = tile(qb, False, wide)
+            dk_scr[...] += dk
+            dv_scr[...] += dv
+
+        qb = kb + 1
+        while qb < blocks:
+            wide = min(2, blocks - qb)
+            add_tile(qb, wide)
+            qb += wide
 
         put(turn_back(dq_scr[:, lo : lo + blk] * scale, kb), kb, 0)
         put(turn_back((dk_scr[...] * scale).T, kb), kb, 1)
@@ -557,9 +598,16 @@
     return pl.pallas_call(
         functools.partial(attn_bwd_kernel, blocks=blocks, width=width),
         out_shape=jax.ShapeDtypeStruct((pieces, 3 * HD, cols), BF16),
-        in_specs=[pl.BlockSpec(memory_space=pltpu.SMEM)] + [VMEM] * 6,
+        in_specs=[pl.BlockSpec(memory_space=pltpu.SMEM), ANY, ANY, VMEM, VMEM, ANY, ANY],
         out_specs=VMEM,
-        scratch_shapes=[pltpu.VMEM((total, HD), BF16)] * 4
+        scratch_shapes=[
+            pltpu.VMEM(seq.shape, BF16),
+            pltpu.VMEM(o32.shape, F32),
+            pltpu.VMEM(cos.shape, F32),
+            pltpu.VMEM(sin.shape, F32),
+            pltpu.SemaphoreType.DMA((4,)),
+        ]
+        + [pltpu.VMEM((total, HD), BF16)] * 4
         + [
             pltpu.VMEM((HD, total), BF16),
             pltpu.VMEM((1, total), F32),
@@ -567,15 +615,12 @@
             pltpu.VMEM((blk, HD), F32),
             pltpu.VMEM((blk, HD), F32),
         ],
-        compiler_params=pltpu.CompilerParams(vmem_limit_bytes=48 << 20),
+        compiler_params=pltpu.CompilerParams(vmem_limit_bytes=60 << 20),
         cost_estimate=pl.CostEstimate(
             flops=20 * total * total * HD, bytes_accessed=8 << 20, transcendentals=total * total // 2
         ),
         name="attn_bwd",
     )(place, seq, o32, lse, do, cos, sin)
-
-
-ANY = pl.BlockSpec(memory_space=pl.ANY)
 
 
 def mxu_nt(a, b):
@@ -738,6 +783,247 @@
     )(order, *left, *right)
 
 
+def qkv_kernel(near_ref, *refs, count):
+    x, parts = refs[:count], refs[count : count + 4]
+    cos_ref, sin_ref, out_ref, rows_ref, w_ref, x_scr, w_scr, x_sem, w_sem, out_sem = refs[count + 4 :]
+    tok = x[0].shape[0]
+    groups, depth, cols = parts[0].shape
+    heads, half = out_ref.shape[0], HD // 2
+    x_in = [
+        pltpu.make_async_copy(x[i], x_scr.at[i * tok : (i + 1) * tok], x_sem.at[i])
+        for i in range(count)
+    ]
+    w_in = [
+        pltpu.make_async_copy(
+            parts[r].at[g],
+            w_scr.at[pl.ds(pl.multiple_of((g * 4 + (near_ref[0] ^ r)) * depth, depth), depth)],
+            w_sem.at[r, g],
+        )
+        for r in range(4)
+        for g in range(groups)
+    ]
+    for c in w_in + x_in:
+        c.start()
+    for c in w_in + x_in:
+        c.wait()
+    out = [
+        pltpu.make_async_copy(x_scr, rows_ref, out_sem.at[0]),
+        pltpu.make_async_copy(w_scr, w_ref, out_sem.at[1]),
+    ]
+    for c in out:
+        c.start()
+    group = heads * HD
+    for i in range(3):
+        y = mxu(x_scr[...], w_scr[:, i * group : (i + 1) * group]).T
+        for h in range(heads):
+            at = slice(i * HD, (i + 1) * HD)
+            a, b = y[h * HD : h * HD + half], y[h * HD + half : (h + 1) * HD]
+            if i < 2:
+                c, s = cos_ref[...], sin_ref[...]
+                a, b = a * c - b * s, b * c + a * s
+            out_ref[h, at] = jnp.concatenate([a, b], axis=0).astype(BF16)
+    for c in out:
+        c.wait()
+
+
+def qkv_of(near, x, parts, cos, sin):
+    count, (tok, width) = len(x), x[0].shape
+    groups, depth, cols = parts[0].shape
+    heads = cols // (3 * HD)
+    return pl.pallas_call(
+        functools.partial(qkv_kernel, count=count),
+        in_specs=[pl.BlockSpec(memory_space=pltpu.SMEM)] + [ANY] * (count + 4) + [VMEM] * 2,
+        out_specs=[VMEM, ANY, ANY],
+        out_shape=[
+            jax.ShapeDtypeStruct((heads, 3 * HD, count * tok), BF16),
+            jax.ShapeDtypeStruct((count * tok, width), BF16),
+            jax.ShapeDtypeStruct((width, cols), BF16),
+        ],
+        scratch_shapes=[
+            pltpu.VMEM((count * tok, width), BF16),
+            pltpu.VMEM((width, cols), BF16),
+            pltpu.SemaphoreType.DMA((count,)),
+            pltpu.SemaphoreType.DMA((4, groups)),
+            pltpu.SemaphoreType.DMA((2,)),
+        ],
+        compiler_params=pltpu.CompilerParams(vmem_limit_bytes=60 << 20),
+        cost_estimate=pl.CostEstimate(
+            flops=2 * count * tok * width * cols,
+            bytes_accessed=4 * (count * tok * width + width * cols),
+            transcendentals=0,
+        ),
+        name="qkv",
+    )(near, *x, *parts, cos, sin)
+
+
+def turned_rows(d_ref, d_scr, at, rows):
+    heads = d_ref.shape[0]
+    for i in range(3):
+        for h in range(heads):
+            top = (i * heads + h) * HD
+            d_scr[top : top + HD] = d_ref[h, i * HD : (i + 1) * HD, at : at + rows]
+
+
+def input_rows_kernel(d_hbm, w_hbm, out_ref, w_scr, d_scr, t_scr, sem, *, slot):
+    rows = out_ref.shape[0]
+    d_in = pltpu.make_async_copy(d_hbm.at[:, :, slot * rows : (slot + 1) * rows], d_scr, sem.at[0])
+    w_in = pltpu.make_async_copy(w_hbm, w_scr, sem.at[1])
+    d_in.start()
+    w_in.start()
+    d_in.wait()
+    turned_rows(d_scr, t_scr, 0, rows)
+    d = t_scr[...].T
+    w_in.wait()
+    out_ref[...] = mxu_nt(d, w_scr[...]).astype(BF16)
+
+
+def input_rows(dqkv, w, slot, tok):
+    width, cols = w.shape
+    return pl.pallas_call(
+        functools.partial(input_rows_kernel, slot=slot),
+        in_specs=[ANY, ANY],
+        out_specs=VMEM,
+        out_shape=jax.ShapeDtypeStruct((tok, width), BF16),
+        scratch_shapes=[
+            pltpu.VMEM((width, cols), BF16),
+            pltpu.VMEM((*dqkv.shape[:2], tok), BF16),
+            pltpu.VMEM((cols, tok), BF16),
+            pltpu.SemaphoreType.DMA((2,)),
+        ],
+        compiler_params=pltpu.CompilerParams(vmem_limit_bytes=60 << 20),
+        cost_estimate=pl.CostEstimate(
+            flops=2 * tok * width * cols, bytes_accessed=2 * width * cols, transcendentals=0
+        ),
+        name="input_rows",
+    )(dqkv, w)
+
+
+def heads_back_kernel(near_ref, d_ref, x_hbm, w_hbm, *refs, slots, step):
+    count = len(slots)
+    give_ref, keep_ref = refs[:2]
+    out = refs[2 : 2 + count]
+    x_scr, w_scr, d_scr, t_scr, y_scr, o_scr, in_sem, out_sem = refs[2 + count :]
+    groups, depth = keep_ref.shape[1:3]
+    tok, width = out[0].shape
+    x_in = pltpu.make_async_copy(x_hbm, x_scr, in_sem.at[0])
+    w_in = pltpu.make_async_copy(w_hbm, w_scr, in_sem.at[1])
+    w_in.start()
+    x_in.start()
+    turned_rows(d_ref, d_scr, 0, d_scr.shape[1])
+    t_scr[...] = d_scr[...].T
+    w_in.wait()
+    sent = []
+    for n in range(width // step):
+        part = slice(n * step, (n + 1) * step)
+        o_scr[:, part] = mxu_nt(t_scr[...], w_scr[part, :]).astype(BF16)
+        for i, slot in enumerate(slots):
+            sent.append(
+                pltpu.make_async_copy(
+                    o_scr.at[slot * tok : (slot + 1) * tok, part],
+                    out[i].at[:, part],
+                    out_sem.at[n, i],
+                )
+            )
+            sent[-1].start()
+    x_in.wait()
+    tile = 4 * depth
+    for g in range(groups):
+        y_scr[...] = mxu(d_scr[...], x_scr[:, g * tile : (g + 1) * tile]).astype(BF16).T
+        for r in range(4):
+            rows = pl.ds(pl.multiple_of((near_ref[0] ^ r) * depth, depth), depth)
+            (give_ref if r % 2 else keep_ref)[r // 2, g] = y_scr[rows, :]
+    for c in sent:
+        c.wait()
+
+
+def heads_back(near, dqkv, x, w, slots, tok):
+    rows, width = x.shape
+    cols = w.shape[1]
+    depth = HD
+    groups = width // (4 * depth)
+    step = width // 4
+    shape = jax.ShapeDtypeStruct((2, groups, depth, cols), BF16)
+    out = pl.pallas_call(
+        functools.partial(heads_back_kernel, slots=slots, step=step),
+        in_specs=[pl.BlockSpec(memory_space=pltpu.SMEM), VMEM, ANY, ANY],
+        out_specs=[VMEM, VMEM] + [ANY] * len(slots),
+        out_shape=[shape, shape] + [jax.ShapeDtypeStruct((tok, width), BF16)] * len(slots),
+        scratch_shapes=[
+            pltpu.VMEM((rows, width), BF16),
+            pltpu.VMEM((width, cols), BF16),
+            pltpu.VMEM((cols, rows), BF16),
+            pltpu.VMEM((rows, cols), BF16),
+            pltpu.VMEM((4 * depth, cols), BF16),
+            pltpu.VMEM((rows, width), BF16),
+            pltpu.SemaphoreType.DMA((2,)),
+            pltpu.SemaphoreType.DMA((width // step, len(slots))),
+        ],
+        compiler_params=pltpu.CompilerParams(vmem_limit_bytes=60 << 20),
+        cost_estimate=pl.CostEstimate(
+            flops=4 * rows * width * cols,
+            bytes_accessed=2 * (2 * width * cols + rows * (2 * width + cols)),
+            transcendentals=0,
+        ),
+        name="heads_back",
+    )(near, dqkv, x, w)
+    return out[:2], out[2:]
+
+
+def mid_grad_kernel(
+    own_ref, across_ref, ahead_ref, mid_ref, dy_ref, scale_ref, gain_ref, w_hbm, dmid_ref, low_ref, out_ref, w_scr, sem
+):
+    tiles = sem.shape[0]
+    width = mid_ref.shape[1]
+    rows = w_scr.shape[0] // tiles
+    w_in = [
+        pltpu.make_async_copy(w_hbm.at[i * rows : (i + 1) * rows], w_scr.at[i * rows : (i + 1) * rows], sem.at[i])
+        for i in range(tiles)
+    ]
+    for c in w_in:
+        c.start()
+    dn = own_ref[...].astype(F32) + across_ref[...].astype(F32) + ahead_ref[...].astype(F32)
+    mid, scale = mid_ref[...], scale_ref[...]
+    scaled = gain_ref[...] * dn
+    mean = jnp.sum(scaled * mid, axis=-1, keepdims=True) * (1.0 / width)
+    dmid = dy_ref[...].astype(F32) + scale * scaled - mid * (scale * scale * scale * mean)
+    dmid_ref[...] = dmid
+    low = dmid.astype(BF16)
+    low_ref[...] = low
+    gain_term = jnp.sum(dn * mid * scale, axis=0, keepdims=True)
+    high = gain_term.astype(BF16)
+    rest = (gain_term - high.astype(F32)).astype(BF16)
+    out_ref[:, HD:] = jnp.zeros((out_ref.shape[0], out_ref.shape[1] - HD, out_ref.shape[2]), BF16)
+    for h in range(out_ref.shape[0]):
+        at = slice(h * HD, (h + 1) * HD)
+        out_ref[h, HD : HD + 1, : 2 * HD] = jnp.concatenate([high[:, at], rest[:, at]], axis=1)
+    for i in range(tiles):
+        w_in[i].wait()
+        v = mxu_nt(w_scr[i * rows : (i + 1) * rows, :], low).astype(BF16)
+        for j in range(rows // HD):
+            out_ref[i * (rows // HD) + j, :HD] = v[j * HD : (j + 1) * HD]
+
+
+def mid_grad(terms, mid, dy, scale, gain, w):
+    tok, width = mid.shape
+    owners = w.shape[0] // HD
+    return pl.pallas_call(
+        mid_grad_kernel,
+        in_specs=[VMEM] * 7 + [ANY],
+        out_specs=[VMEM] * 3,
+        out_shape=[
+            jax.ShapeDtypeStruct((tok, width), F32),
+            jax.ShapeDtypeStruct((tok, width), BF16),
+            jax.ShapeDtypeStruct((owners, HD + 16, tok), BF16),
+        ],
+        scratch_shapes=[pltpu.VMEM(w.shape, BF16), pltpu.SemaphoreType.DMA((4,))],
+        compiler_params=pltpu.CompilerParams(vmem_limit_bytes=60 << 20),
+        cost_estimate=pl.CostEstimate(
+            flops=2 * tok * width * w.shape[0], bytes_accessed=2 * width * w.shape[0], transcendentals=0
+        ),
+        name="mid_grad",
+    )(*terms, mid, dy, scale, gain, w)
+
+
 FAR = ("ctx", "row")
 NEAR = ("col", "core")
 
@@ -785,34 +1071,61 @@
     return slots
 
 
-def collect(terms, marks):
+def spread_late(v, slots):
+    slots[0, 0] = v
     n = lax.axis_size("ctx")
-    total = None
-    for c in [*range(1, n), 0]:
-        if total is None:
-            across = yield swap(terms[c, 1], "row")
-            total = terms[c, 0].astype(F32) + across.astype(F32)
+    slots[1, 0] = yield shift(v)
+    for c in range(1, n - 2):
+        slots[c + 1, 0], slots[c - 1, 1] = yield shift(slots[c, 0]), swap(slots[c - 1, 0], "row")
+    slots[n - 1, 0], slots[n - 3, 1], slots[n - 2, 1] = yield (
+        shift(slots[n - 2, 0]),
+        swap(slots[n - 3, 0], "row"),
+        swap(slots[n - 2, 0], "row"),
+    )
+    slots[n - 1, 1] = yield swap(slots[n - 1, 0], "row")
+    return slots
+
+
+def collect(terms, marks, early=False, open_end=False):
+    n = lax.axis_size("ctx")
+    across = yield swap(terms[1, 1], "row")
+    total = terms[1, 0].astype(F32) + across.astype(F32)
+    for c in [*range(2, n), 0]:
+        send = total.astype(BF16)
+        marks.append(send)
+        if early and c == 2:
+            ahead, across, last = yield (
+                shift(send),
+                swap(after(terms[c, 1], send), "row"),
+                swap(after(terms[0, 1], send), "row"),
+            )
+        elif early and c == 0:
+            ahead, across = (yield shift(send)), last
         else:
-            marks.append(total.astype(BF16))
-            across, ahead = yield swap(terms[c, 1], "row"), shift(marks[-1])
-            total = terms[c, 0].astype(F32) + across.astype(F32) + ahead.astype(F32)
+            ahead, across = yield shift(send), swap(after(terms[c, 1], send), "row")
+        if open_end and c == 0:
+            return terms[0, 0], across, ahead
+        total = terms[c, 0].astype(F32) + across.astype(F32) + ahead.astype(F32)
     return total
 
 
 def reduce_near(send, keep):
     got = yield swap(send, "core")
-    rows = keep.shape[1] // 2
-    upper, lower = (
-        (keep[0, p].astype(F32) + got[0, p].astype(F32)).astype(BF16)
-        for p in (slice(0, rows), slice(rows, None))
-    )
-    upper = yield swap(upper, "col")
-    lower = yield swap(lower, "col")
-    return keep[1], got[1], upper, lower
-
-
-def add_terms(keep, got, upper, lower):
-    return keep.astype(F32) + got.astype(F32) + jnp.concatenate([upper, lower], axis=0).astype(F32)
+    (give,) = yield for_column(keep, got, 1)
+    across = yield swap(give, "col")
+    return keep, got, [across]
+
+
+def for_column(keep, got, pieces):
+    rows = keep.shape[1] // pieces
+    return [
+        (keep[0, p : p + rows].astype(F32) + got[0, p : p + rows].astype(F32)).astype(BF16)
+        for p in range(0, keep.shape[1], rows)
+    ]
+
+
+def add_terms(keep, got, across):
+    return keep[1].astype(F32) + got[1].astype(F32) + jnp.concatenate(across, axis=0).astype(F32)
 
 
 def after(v, first):
@@ -836,29 +1149,21 @@
     return jnp.stack(by_side(core_at, keep, got), axis=1)
 
 
-def sum_near(v, col_at, core_at):
-    keep, give = by_side(core_at, v[:, :, 0], v[:, :, 1])
+def sum_near(give, keep):
     got = yield swap(give, "core")
-    total = keep.astype(F32) + got.astype(F32)
-    keep, give = by_side(col_at, total[:, 0], total[:, 1])
-    give = give.astype(BF16)
-    rows = give.shape[1] // 2
-    upper = yield swap(give[:, :rows], "col")
-    lower = yield swap(give[:, rows:], "col")
-    return keep + jnp.concatenate([upper, lower], axis=1).astype(F32)
-
-
-def gather_heads(send, col_at, core_at):
+    other = (keep[1].astype(F32) + got[1].astype(F32)).astype(BF16)
+    across = yield swap(other, "col")
+    return keep[0].astype(F32) + got[0].astype(F32) + across.astype(F32)
+
+
+def gather_heads(send):
     mine = yield lax.all_to_all(send, FAR, split_axis=0, concat_axis=0, tiled=True)
     part = mine.shape[0] // 2
-    upper = yield swap(mine[:part], "col")
+    upper, mine_two = yield swap(mine[:part], "col"), swap(mine, "core")
     lower = yield swap(mine[part:], "col")
     other = jnp.concatenate([upper, lower], axis=0)
-    mine_two, other_two = yield swap(mine, "core"), swap(other, "core")
-    mine_pair = by_side(core_at, mine, mine_two)
-    other_pair = by_side(core_at, other, other_two)
-    halves = [by_side(col_at, a, b) for a, b in zip(mine_pair, other_pair, strict=True)]
-    return jnp.stack([halves[0][0], halves[1][0], halves[0][1], halves[1][1]], axis=1)
+    other_two = yield swap(other, "core")
+    return mine, mine_two, other, other_two
 
 
 def per_device_split(
@@ -919,60 +1224,61 @@
     scale_one = lax.rsqrt(jnp.mean(x32 * x32, axis=-1, keepdims=True) + EPS)
     gate_w = lax.all_gather(w_gate, NEAR, axis=0, tiled=True)
 
-    def rows_of(by_slot):
-        return jnp.concatenate([by_slot[c, r] for r in range(2) for c in range(n_ctx)], axis=0)
-
     one_flow = Flow(spread((x32 * scale_one).astype(BF16), {}))
-    heads_flow = Flow(gather_heads(send, col_at, core_at))
+    heads_flow = Flow(gather_heads(send))
     w_out = stage([one_flow, heads_flow], w_out)
     out_w = lax.all_gather(w_out, FAR + NEAR, axis=0, tiled=True)
-    for _ in range(n_ctx - 2):
-        stage([one_flow, heads_flow])
-    w_up, dy_low = stage([one_flow, heads_flow], (w_up, cotangent))
+    for _ in range(n_ctx - 3):
+        cosine, sine = stage([one_flow, heads_flow], (cosine, sine))
+    dy_low = stage([one_flow, heads_flow], cotangent)
+    dy_by = {}
+    dy_flow = Flow(spread_late(dy_low, dy_by))
+    w_up = stage([one_flow, heads_flow], w_up)
+    dy_flow.run_on()
     up_w = lax.all_gather(w_up, NEAR, axis=0, tiled=True)
-    w_heads = heads_flow.result.reshape(width, 3 * group)
-    rows_one = rows_of(one_flow.result)
-
-    half = HD // 2
-    dy_by = {}
-    dy_flow = Flow(spread(dy_low, dy_by))
-    flat = jnp.einsum("de,td->et", w_heads, rows_one, preferred_element_type=F32)
-    qkv = flat.reshape(3, near, 2, half, rows_here)
-    first, second = qkv[:2, :, 0], qkv[:2, :, 1]
-    turned = jnp.stack([first * cosine - second * sine, second * cosine + first * sine], axis=2)
-    qkv = jnp.concatenate([turned, qkv[2:]], axis=0).astype(BF16)
-    qkv = qkv.transpose(1, 0, 2, 3, 4).reshape(near, 3 * HD, rows_here)
-    qkv = stage([dy_flow], qkv)
-    qkv_head, gate_w, out_w = stage(
+    slot_names = [(c, r) for r in range(2) for c in range(n_ctx)]
+    qkv, rows_one, w_heads = qkv_of(
+        near_at.reshape(1),
+        [one_flow.result[k] for k in slot_names],
+        heads_flow.result,
+        cosine,
+        sine,
+    )
+    qkv_head, gate_w, seq_cos, seq_sin = stage(
         [dy_flow],
-        (lax.all_to_all(qkv, NEAR, split_axis=0, concat_axis=0, tiled=True), gate_w, out_w),
+        (
+            lax.all_to_all(qkv, NEAR, split_axis=0, concat_axis=0, tiled=True),
+            gate_w,
+            seq_cos,
+            seq_sin,
+        ),
     )
     down_w = lax.all_gather(after(w_down, qkv_head), NEAR, axis=0, tiled=True)
-    attn_head, o32, lse, seq = stage(
-        [dy_flow], attn_fwd(places, qkv_head, beside(gain_ffn, tok), far)
+    (attn_head, o32, lse, seq), out_w = stage(
+        [dy_flow], (attn_fwd(places, qkv_head, beside(gain_ffn, tok), far), out_w)
     )
     attn, up_w = stage(
         [dy_flow],
         (lax.all_to_all(attn_head, FAR + NEAR, split_axis=0, concat_axis=0, tiled=True), up_w),
     )
     gain_two = attn[:, HD, :own_in].reshape(1, width).astype(F32)
-    attn = attn[:, :HD].reshape(width, tok)
+    attn_all = attn[:, :HD]
+    attn = attn_all.reshape(width, tok)
 
     mid = x32 + jnp.einsum("et,ed->td", attn, out_w, preferred_element_type=F32)
     scale_two = lax.rsqrt(jnp.mean(mid * mid, axis=-1, keepdims=True) + EPS)
     normed_two = (mid * scale_two * gain_two).astype(BF16)
     side_flow = Flow(
-        to_near(attn_head[:, :HD].reshape(far, 2, 2, HD, tok).transpose(1, 2, 3, 0, 4), col_at, core_at)
+        to_near(attn_all.reshape(far, 2, 2, HD, tok).transpose(1, 2, 0, 3, 4), col_at, core_at)
     )
 
     two, dn_by, br_by, kept = {}, {}, {}, []
     two_flow = Flow(spread(normed_two, two))
 
-    def feed(cs):
+    def feed(cs, first=()):
         names = [(c, r) for c in cs for r in range(2)]
-        dn, br, lefts = ffn(
-            [two[k] for k in names], [dy_by[k] for k in names], gate_w, up_w, down_w
-        )
+        rows = after([two[k] for k in names], first)
+        dn, br, lefts = ffn(rows, [dy_by[k] for k in names], gate_w, up_w, down_w)
         return dict(zip(names, dn, strict=True)), dict(zip(names, br, strict=True)), lefts
 
     def fed(results):
@@ -983,110 +1289,97 @@
 
     stage([two_flow, side_flow])
     stage([two_flow, side_flow], feed([0]), fed)
-    for c in range(1, n_ctx - 1):
+    for c in range(1, n_ctx - 2):
         stage([two_flow], feed([c]), fed)
     marks = []
-    dn_flow = Flow(collect(dn_by, marks))
-    stage([dn_flow], feed([n_ctx - 1]), fed)
+    dn_flow = Flow(collect(dn_by, marks, open_end=True))
+    stage([two_flow, dn_flow], feed([n_ctx - 2]), fed)
+    last = feed([n_ctx - 1], marks[-1])
+    stage([dn_flow], last, fed)
     names = [(c, r) for c in range(n_ctx) for r in range(2)]
     two_rows, dy_rows = [two[k] for k in names], [dy_by[k] for k in names]
     tiles = near_at ^ jnp.array([3, 1, 2, 0], jnp.int32)
     lefts = [[k[i] for k in kept] for i in range(3)]
+    for _ in range(n_ctx - 4):
+        stage([dn_flow])
     gate_terms = outer(tiles, *after((lefts[1], two_rows), marks[-1]))
     gate_flow = Flow(reduce_near(*stage([dn_flow], gate_terms)))
     up_terms = outer(tiles, *after((lefts[2], two_rows), marks[-1]))
-    up_flow = Flow(reduce_near(*stage([dn_flow, gate_flow], up_terms)))
-    down_terms = outer(tiles, *after((lefts[0], dy_rows), marks[-1]))
-    down_terms, br_by = stage([dn_flow, up_flow], (down_terms, br_by))
-    down_flow = Flow(reduce_near(*down_terms))
-    dnormed_two = dn_flow.result
-
-    dy = cotangent.astype(F32)
-    gain_two_term = jnp.sum(dnormed_two * mid * scale_two, axis=0)
-    scaled_two = gain_two * dnormed_two
-    dmid = (
-        dy
-        + scale_two * scaled_two
-        - mid * scale_two**3 * jnp.mean(scaled_two * mid, axis=-1, keepdims=True)
-    )
-    dmid_low = dmid.astype(BF16)
-    dattn = jnp.einsum("ed,td->et", out_w, dmid_low, preferred_element_type=F32).astype(BF16)
-    gain_high = gain_two_term.astype(BF16)
-    gain_low = (gain_two_term - gain_high.astype(F32)).astype(BF16)
-    dattn = jnp.concatenate(
-        [
-            dattn.reshape(far * near, HD, tok),
-            beside(
-                jnp.concatenate(
-                    [v.reshape(far * near, own_in) for v in (gain_high, gain_low)], axis=1
-                ),
-                tok,
-            ),
-        ],
-        axis=1,
-    )
-    br_flow = Flow(collect(br_by, []))
-    gate_flow.run_on()
-    br_first = br_flow.pending
-    br_flow.run_on()
-    dattn_head, dmid_low, _ = stage(
-        [gate_flow, down_flow, br_flow],
+    up_terms, br_by = stage([dn_flow, gate_flow], (up_terms, br_by))
+    up_send, up_keep = up_terms
+    dmid, dmid_low, dattn = mid_grad(dn_flow.result, mid, cotangent, scale_two, gain_two, out_w)
+    dmid_near = lax.all_gather(dmid_low, NEAR, axis=0, tiled=True)
+    br_marks = []
+    br_flow = Flow(collect(br_by, br_marks, early=True, open_end=True))
+    down_terms = outer(tiles, *after((lefts[0], dy_rows), dattn))
+    gate_flow.pending = after(gate_flow.pending, dattn)
+    attn_side = side_flow.result.transpose(2, 3, 0, 1, 4).reshape(far, HD, blk)
+    out_term = jnp.einsum(
+        "gft,td->gfd", after(attn_side, dattn), dmid_near, preferred_element_type=F32
+    )
+    dattn_head, down_terms, out_term, up_got = stage(
+        [gate_flow, br_flow],
         (
             lax.all_to_all(dattn, FAR + NEAR, split_axis=0, concat_axis=0, tiled=True),
-            dmid_low,
-            br_first,
+            down_terms,
+            out_term.astype(BF16),
+            swap(up_send, "core"),
         ),
     )
+    out_grad = lax.psum_scatter(
+        out_term.reshape(far * HD, width), FAR, scatter_dimension=0, tiled=True
+    )
+    down_send, down_keep = down_terms
     gain_parts = dattn_head[:, HD, : 2 * own_in].astype(F32)
-    dmid_side = lax.all_gather(dmid_low, FAR, axis=0, tiled=True)
-    up_flow.run_on()
-    dqkv_head = stage(
-        [up_flow, down_flow, br_flow],
-        attn_bwd(places, seq, o32, lse, dattn_head, seq_cos, seq_sin, far),
-    )
-    rows_one = after(rows_one, dqkv_head)
-    dqkv = stage(
-        [br_flow, down_flow],
-        lax.all_to_all(dqkv_head, NEAR, split_axis=0, concat_axis=0, tiled=True),
-    )
-    dqkv = dqkv.reshape(near, 3, HD, rows_here).transpose(1, 0, 2, 3).reshape(3 * group, rows_here)
-    half_rows = rows_here // 2
-
-    def dx_of(r, dqkv):
-        rows = lax.slice_in_dim(dqkv, r * half_rows, (r + 1) * half_rows, axis=1)
-        return jnp.einsum("et,de->td", rows, w_heads, preferred_element_type=F32).astype(BF16)
-
-    dx_other, dqkv = lax.optimization_barrier((dx_of(1, dqkv), dqkv))
-    dx_own, dqkv = lax.optimization_barrier((dx_of(0, dqkv), dqkv))
-    dx = [v.reshape(n_ctx, tok, width) for v in (dx_own, dx_other)]
-    dx_flow = Flow(collect({(c, r): dx[r][c] for c in range(n_ctx) for r in range(2)}, marks))
-    heads_grad = jnp.einsum("td,et->de", rows_one, dqkv, preferred_element_type=F32).astype(BF16)
-    heads_flow = Flow(
-        sum_near(heads_grad.reshape(far, 2, 2, own_in, 3 * group), col_at, core_at)
-    )
-    dmid_side = stage([dx_flow, heads_flow], dmid_side)
-    attn_side, dmid_side = after(
-        (side_flow.result.reshape(group, rows_here), dmid_side), marks[-1]
-    )
-    out_term = jnp.einsum("et,td->ed", attn_side, dmid_side, preferred_element_type=F32)
-    heads_first = heads_flow.pending
-    heads_flow.run_on()
-    ffn_terms, out_term, _ = stage(
-        [dx_flow, heads_flow],
-        ([f.result for f in (gate_flow, up_flow, down_flow)], out_term.astype(BF16), heads_first),
-    )
-    gate_grad, up_grad, down_grad = (add_terms(*terms) for terms in ffn_terms)
-    out_flow = Flow(sum_near(out_term.reshape(1, 2, 2, own_in, width), col_at, core_at))
-    for _ in range(n_ctx - 2):
-        stage([dx_flow, out_flow])
-    out_flow.run_on()
+    dqkv_head, down_got = stage(
+        [gate_flow, br_flow],
+        (
+            attn_bwd(places, seq, o32, lse, dattn_head, seq_cos, seq_sin, far),
+            swap(down_send, "core"),
+        ),
+    )
+    exchange = lax.all_to_all(dqkv_head, NEAR, split_axis=0, concat_axis=0, tiled=True)
+    up_give = for_column(*after((up_keep, up_got), br_marks[-1]), 2)
+    (down_keep, down_got) = after((down_keep, down_got), br_marks[-1])
+    dqkv, up_give, down_give = stage(
+        [br_flow], (exchange, up_give, for_column(down_keep, down_got, 1)[0])
+    )
+    dx = {(1, 1): input_rows(dqkv, w_heads, slot_names.index((1, 1)), tok)}
+    dx_flow = Flow(collect(dx, marks))
+    up_first, up_second = up_give
+    rest = [i for i in range(far) if slot_names[i] != (1, 1)]
+
+    def add_rows(values):
+        dx.update({slot_names[i]: v for i, v in zip(rest, values[1], strict=True)})
+
+    heads_terms, _, up_first = stage(
+        [dx_flow, br_flow],
+        (*heads_back(near_at.reshape(1), after(dqkv, dx[1, 1]), rows_one, w_heads, rest, tok), swap(up_first, "col")),
+        add_rows,
+    )
+    heads_flow = Flow(sum_near(*heads_terms))
+    stage([heads_flow])
+    gate_terms, out_grad, up_second = stage(
+        [dx_flow, heads_flow], (gate_flow.result, out_grad, up_second)
+    )
+    back = lax.all_to_all(
+        heads_flow.result.astype(BF16), FAR, split_axis=0, concat_axis=0, tiled=True
+    )
+    gate_terms, down_give, up_second, branch = stage(
+        [dx_flow], (gate_terms, down_give, swap(up_second, "col"), br_flow.result)
+    )
+    up_terms = up_keep, up_got, [up_first, up_second]
+    gate_terms, up_terms, branch = after((gate_terms, up_terms, branch), marks[-1])
+    gate_grad, up_grad = add_terms(*gate_terms), add_terms(*up_terms)
+    back, down_across = stage([dx_flow], (back, swap(down_give, "col")))
+    down_grad = add_terms(down_keep, down_got, [down_across])
     scaled_one = dx_flow.result
     input_grad = (
         dmid
         + scale_one * scaled_one
         - x32 * scale_one**3 * jnp.mean(scaled_one * x32, axis=-1, keepdims=True)
     )
-    back = lax.all_to_all(heads_flow.result.astype(BF16), FAR, split_axis=0, concat_axis=0, tiled=True).astype(F32)
+    back = back.astype(F32)
     raw = [
         back[:, :, i * group : (i + 1) * group].transpose(1, 0, 2).reshape(own_in, -1)
         for i in range(3)
@@ -1098,13 +1391,13 @@
     query_grad, key_grad, value_grad = (g * gain_one for g in raw)
     gain_ffn_grad = jnp.sum(gain_parts[:, :own_in] + gain_parts[:, own_in:], axis=0)
     return (
-        (mid + br_flow.result).astype(BF16),
+        (mid + sum(v.astype(F32) for v in branch)).astype(BF16),
         input_grad,
         gain_attn_grad,
         query_grad,
         key_grad,
         value_grad,
-        out_flow.result[0],
+        out_grad.astype(F32),
         gain_ffn_grad,
         gate_grad,
         up_grad,

time: 619 us -> 561 us (0.906)
  Pallas kernels: 138 us -> 166 us
  local copies, waits for them, and re-layouts: 38.9 us -> 16.1 us
  waiting for transfers between devices: 232 us -> 210 us
  starting transfers between devices: 103 us -> 82.9 us
  matrix products: 24.3 us -> 9.64 us
  other arithmetic: 63.7 us -> 54.3 us
    ppermute x18, waiting for transfers between devices: 96.9 us -> 44.1 us  [shift(): return lax.ppermute(v, 'ctx', [(i, (i + 1) % n) for i in range(n)])]
    pallas_call x0 -> x4, Pallas kernels: none -> 35.2 us  [the longest x1 12.6 us: heads_back(): pl.pallas_call(functools.partial(heads_back_kernel, slots=slots, step=ste...]
    dot_general x6 -> x1, matrix products: 19.5 us -> 4.17 us  [per_device_split(): jnp.einsum('gft,td->gfd', after(attn_side, dattn), dmid_near, preferred_e...]
    all_gather x1, waiting for transfers between devices: 0.01 us -> 13.7 us  [per_device_split(): up_w = lax.all_gather(w_up, NEAR, axis=0, tiled=True)]
    squeeze x6 -> x0, local copies, waits for them, and re-layouts: 13 us -> none  [reduce_near(): return (keep[1], got[1], upper, lower)]
    ppermute x45 -> x39, waiting for transfers between devices: 116 us -> 128 us  [swap(): return lax.ppermute(v, axis, [(0, 1), (1, 0)])]
    ppermute x18, starting transfers between devices: 27.7 us -> 16 us  [shift(): return lax.ppermute(v, 'ctx', [(i, (i + 1) % n) for i in range(n)])]
    all_to_all x1, waiting for transfers between devices: 10.5 us -> 0.82 us  [per_device_split(): lax.all_to_all(dqkv_head, NEAR, split_axis=0, concat_axis=0, tiled=True)]
  transfers between devices with their start and end apart: 74 -> 69, of which waited for: 31 -> 34; matrix products, arithmetic and copies ran while one was open for 18% -> 10% of each run, Pallas kernels for 22% -> 28%
where the time goes in v4:
time: 561 us; the launch traced here: 555 us
  waiting for transfers between devices  210 us (37%)
  Pallas kernels  166 us (30%)
  starting transfers between devices  82.9 us (15%)
  other arithmetic  54.3 us (10%)
  local copies, waits for them, and re-layouts  16.1 us (3%)
  between operations  15.4 us (3%)
  matrix products  9.64 us (2%)
    ppermute x39, waiting for transfers between devices, swap(): return lax.ppermute(v, axis, [(0, 1), (1, 0)])  128 us
    pallas_call x4, Pallas kernels, ffn(): pl.pallas_call(functools.partial(ffn_kernel, count=count, step=step), in_...  47.2 us
    ppermute x18, waiting for transfers between devices, shift(): return lax.ppermute(v, 'ctx', [(i, (i + 1) % n) for i in range(n)])  44.1 us
    ppermute x39, starting transfers between devices, swap(): return lax.ppermute(v, axis, [(0, 1), (1, 0)])  39 us
    pallas_call x3, Pallas kernels, outer(): pl.pallas_call(functools.partial(outer_kernel, lefts=len(left), rights=le...  32.4 us
    pallas_call x1, Pallas kernels, attn_bwd(): pl.pallas_call(functools.partial(attn_bwd_kernel, blocks=blocks, width=wi...  31.9 us
    pallas_call x1, Pallas kernels, attn_fwd(): pl.pallas_call(functools.partial(attn_fwd_kernel, blocks=blocks, width=co...  19.1 us
    ppermute x18, starting transfers between devices, shift(): return lax.ppermute(v, 'ctx', [(i, (i + 1) % n) for i in range(n)])  16 us
  transfers between devices with their start and end apart: 69, of which 34 were waited for; matrix products, arithmetic and copies ran while one was open for 10% of the time, Pallas kernels for 28%

profile of v4, /device:TPU:0, one launch (start us, length us, event | category | flops | bytes accessed | tf_op | source)
XLA Modules:
  0.0 554.5 jit_solution(146445121627869028)
XLA Ops:
  10.9 7.4 %all-to-all-start = ((bf16[8,64,768]{2,1,0:T(8,128)(2,1)}), bf16[8,64,768]{2,1,0:T(8,128)(2,1)S(1)}, u32[]{:S(2)}, u32[]{:S(2)}) async-start(bf16[8,64,768]{2,1,0:T(8,128)(2,1)} %maximum_bitcast_fusion), calls=%async_computation | async-start | bytes 1572864 | tf_op jit(solution)/shard_map/all_to_all | solution.py:1160
  22.8 17.6 %collective-permute-done.1.refs_4_ = bf16[128,2048]{1,0:T(8,128)(2,1)S(1)} collective-permute-done((bf16[128,2048]{1,0:T(8,128)(2,1)S(1)}, bf16[128,2048]{1,0:T(8,128)(2,1)S(1)}, u32[]{:S(2)}, u32[]{:S(2)}) %collective-permute-start.1) | collective-permute-done | bytes 524320 | tf_op jit(solution)/shard_map/ppermute | solution.py:1032
  41.2 5.4 collective-permute-done.refs_1_
  46.6 3.2 all-to-all-done.refs_8_
  54.4 10.6 %collective-permute-done.4 = bf16[4,64,768]{2,1,0:T(8,128)(2,1)S(1)} collective-permute-done((bf16[4,64,768]{2,1,0:T(8,128)(2,1)S(1)}, bf16[4,64,768]{2,1,0:T(8,128)(2,1)S(1)}, u32[]{:S(2)}, u32[]{:S(2)}) %collective-permute-start.4) | collective-permute-done | bytes 393248 | tf_op jit(solution)/shard_map/ppermute | solution.py:1032
  65.0 4.2 collective-permute-done.2.refs_2_
  70.1 3.0 collective-permute-start.8
  73.1 5.7 %collective-permute-done.8 = bf16[4,64,768]{2,1,0:T(8,128)(2,1)S(1)} collective-permute-done((bf16[4,64,768]{2,1,0:T(8,128)(2,1)S(1)}, bf16[4,64,768]{2,1,0:T(8,128)(2,1)S(1)}, u32[]{:S(2)}, u32[]{:S(2)}) %collective-permute-start.8) | collective-permute-done | bytes 393248 | tf_op jit(solution)/shard_map/ppermute | solution.py:1032
  78.8 4.2 collective-permute-done.6.refs_3_
  84.6 16.7 %collective-permute-done.12.refs_7_ = bf16[128,2048]{1,0:T(8,128)(2,1)S(1)} collective-permute-done((bf16[128,2048]{1,0:T(8,128)(2,1)S(1)}, bf16[128,2048]{1,0:T(8,128)(2,1)S(1)}, u32[]{:S(2)}, u32[]{:S(2)}) %collective-permute-start.12) | collective-permute-done | bytes 524320 | tf_op jit(solution)/shard_map/ppermute | solution.py:1032
  102.3 9.3 %qkv.1 = (bf16[4,192,1024]{2,1,0:T(8,128)(2,1)}, bf16[1024,2048]{1,0:T(8,128)(2,1)}, bf16[2048,768]{1,0:T(8,128)(2,1)}) custom-call(s32[1]{0:T(128)} %bitcast.2.near_ref, bf16[128,2048]{1,0:T(8,128)(2,1)} %copy-done.33, bf16[128,2048]{1,0:T(8,128)(2,1)} %collective-permute-done.refs_1_, bf16[128,2048]{1,0:T(8,128)(2,1)} %copy-done.62, ...), custom_call_target="tpu_custom_call" | custom-call | flops 3221225472 | bytes 14680064 | tf_op jit(solution)/shard_map/qkv/pallas_call | solution.py:833
  111.6 3.6 all-to-all-start.1
  116.7 6.1 %collective-permute-done.9.refs_2_.refs_7_ = bf16[128,2048]{1,0:T(8,128)(2,1)} collective-permute-done((bf16[128,2048]{1,0:T(8,128)(2,1)S(1)}, bf16[128,2048]{1,0:T(8,128)(2,1)}, u32[]{:S(2)}, u32[]{:S(2)}) %collective-permute-start.9) | collective-permute-done | bytes 524320 | tf_op jit(solution)/shard_map/ppermute | solution.py:1037
  125.6 12.6 %collective-permute-done.11.refs_3_.refs_6_ = bf16[128,2048]{1,0:T(8,128)(2,1)S(1)} collective-permute-done((bf16[128,2048]{1,0:T(8,128)(2,1)S(1)}, bf16[128,2048]{1,0:T(8,128)(2,1)S(1)}, u32[]{:S(2)}, u32[]{:S(2)}) %collective-permute-start.11) | collective-permute-done | bytes 524320 | tf_op jit(solution)/shard_map/ppermute | solution.py:1032
  138.2 11.4 %collective-permute-done.10.refs_2_.refs_9_ = bf16[128,2048]{1,0:T(8,128)(2,1)} collective-permute-done((bf16[128,2048]{1,0:T(8,128)(2,1)}, bf16[128,2048]{1,0:T(8,128)(2,1)}, u32[]{:S(2)}, u32[]{:S(2)}) %collective-permute-start.10) | collective-permute-done | bytes 524320 | tf_op jit(solution)/shard_map/ppermute | solution.py:1037
  153.5 19.1 %attn_fwd.1 = (bf16[32,80,128]{2,1,0:T(8,128)(2,1)}, f32[64,4096]{1,0:T(8,128)}, f32[1,4096]{1,0:T(1,128)}, bf16[192,4096]{1,0:T(8,128)(2,1)}) custom-call(s32[2,8]{1,0:T(2,128)} %pad_add_fusion.place_ref, bf16[4,192,1024]{2,1,0:T(8,128)(2,1)} %copy-done.15, bf16[16,128]{1,0:T(8,128)(2,1)} %pad.4.extra_ref), custom_call_target="tpu_custom_call" | custom-call | flops 8589934592 | bytes 8388608 | tf_op jit(solution)/shard_map/attn_fwd/pallas_call | solution.py:464
  172.7 5.2 all-to-all-start.2
  179.8 13.7 %all-gather.10.cloned.1.call-done.refs_5_ = bf16[1024,2048]{1,0:T(8,128)(2,1)} async-done(((bf16[256,2048]{1,0:T(8,128)(2,1)}), bf16[1024,2048]{1,0:T(8,128)(2,1)}) %all-gather.10.cloned.1.call-update) | async-done | bytes 4194320 | tf_op jit(solution)/shard_map/all_gather | solution.py:1238
  193.5 5.6 %collective-permute-done.17.refs_3_.refs_12_ = bf16[128,2048]{1,0:T(8,128)(2,1)S(1)} collective-permute-done((bf16[128,2048]{1,0:T(8,128)(2,1)}, bf16[128,2048]{1,0:T(8,128)(2,1)S(1)}, u32[]{:S(2)}, u32[]{:S(2)}) %collective-permute-start.17) | collective-permute-done | bytes 524320 | tf_op jit(solution)/shard_map/ppermute | solution.py:1032
  200.1 5.5 multiply_reduce_fusion
  210.3 13.4 %collective-permute-done.20 = bf16[2,8,64,128]{3,2,0,1:T(8,128)(2,1)S(1)} collective-permute-done((bf16[2,8,64,128]{3,2,0,1:T(8,128)(2,1)}, bf16[2,8,64,128]{3,2,0,1:T(8,128)(2,1)S(1)}, u32[]{:S(2)}, u32[]{:S(2)}) %collective-permute-start.20) | collective-permute-done | bytes 262176 | tf_op jit(solution)/shard_map/ppermute | solution.py:1032
  226.6 8.5 %all-gather.12.cloned.1.call-done.refs_6_ = bf16[1024,2048]{1,0:T(8,128)(2,1)} async-done(((bf16[256,2048]{1,0:T(8,128)(2,1)}), bf16[1024,2048]{1,0:T(8,128)(2,1)}) %all-gather.12.cloned.1.call-update) | async-done | bytes 4194320 | tf_op jit(solution)/shard_map/all_gather | solution.py:1256
  235.1 11.8 %ffn.4 = (bf16[128,2048]{1,0:T(8,128)(2,1)}, bf16[128,2048]{1,0:T(8,128)(2,1)}, bf16[128,2048]{1,0:T(8,128)(2,1)}, bf16[128,2048]{1,0:T(8,128)(2,1)}, bf16[256,1...) custom-call(bf16[128,2048]{1,0:T(8,128)(2,1)} %copy-done.31, ...), custom_call_target="tpu_custom_call" | custom-call | flops 6442450944 | bytes 20971520 | tf_op jit(solution)/shard_map/ffn/pallas_call | solution.py:696
  250.2 11.8 %ffn.5 = (bf16[128,2048]{1,0:T(8,128)(2,1)}, bf16[128,2048]{1,0:T(8,128)(2,1)}, bf16[128,2048]{1,0:T(8,128)(2,1)}, bf16[128,2048]{1,0:T(8,128)(2,1)}, bf16[256,1...) custom-call(bf16[128,2048]{1,0:T(8,128)(2,1)} %collective-permute-done.18.refs_0_.refs_7_, ...), custom_call_target="tpu_custom_call" | custom-call | flops 6442450944 | bytes 20971520 | tf_op jit(solution)/shard_map/ffn/pallas_call | solution.py:696
  266.5 11.8 %ffn.6 = (bf16[128,2048]{1,0:T(8,128)(2,1)}, bf16[128,2048]{1,0:T(8,128)(2,1)}, bf16[128,2048]{1,0:T(8,128)(2,1)}, bf16[128,2048]{1,0:T(8,128)(2,1)}, bf16[256,1...) custom-call(bf16[128,2048]{1,0:T(8,128)(2,1)} %collective-permute-done.21.refs_0_.refs_9_, ...), custom_call_target="tpu_custom_call" | custom-call | flops 6442450944 | bytes 20971520 | tf_op jit(solution)/shard_map/ffn/pallas_call | solution.py:696
  279.6 9.4 %collective-permute-done.26.refs_1_.refs_12_ = bf16[128,2048]{1,0:T(8,128)(2,1)} collective-permute-done((bf16[128,2048]{1,0:T(8,128)(2,1)S(1)}, bf16[128,2048]{1,0:T(8,128)(2,1)}, u32[]{:S(2)}, u32[]{:S(2)}) %collective-permute-start.26) | collective-permute-done | bytes 524320 | tf_op jit(solution)/shard_map/ppermute | solution.py:1032
  290.0 11.8 %ffn.7 = (bf16[128,2048]{1,0:T(8,128)(2,1)}, bf16[128,2048]{1,0:T(8,128)(2,1)}, bf16[128,2048]{1,0:T(8,128)(2,1)}, bf16[128,2048]{1,0:T(8,128)(2,1)}, bf16[256,1...) custom-call(bf16[128,2048]{1,0:T(8,128)(2,1)} %copy-done.59, ...), custom_call_target="tpu_custom_call" | custom-call | flops 6442450944 | bytes 20971520 | tf_op jit(solution)/shard_map/ffn/pallas_call | solution.py:696
  307.1 10.8 %outer.3 = (bf16[2,256,2048]{2,1,0:T(8,128)(2,1)}, bf16[2,256,2048]{2,1,0:T(8,128)(2,1)}) custom-call(s32[4]{0:T(128)} %broadcast_xor_fusion.refs_0_, bf16[256,1024]{1,0:T(8,128)(2,1)} %get-tuple-element.373.refs_1_, bf16[256,1024]{1,0:T(8,128)(2,1)} %get-tuple-element.374.refs_2_, bf16[256,1024]{1,0:T(8,128)(2,1)} %get-tuple-element.375.refs_3_, ...), custom_call_target="tpu_custom_call" | custom-call | flops 4294967296 | bytes 10485760 | tf_op jit(solution)/shard_map/outer/pallas_call | solution.py:763
  322.8 10.7 %outer.4 = (bf16[2,256,2048]{2,1,0:T(8,128)(2,1)}, bf16[2,256,2048]{2,1,0:T(8,128)(2,1)}) custom-call(s32[4]{0:T(128)} %broadcast_xor_fusion.refs_0_, bf16[256,1024]{1,0:T(8,128)(2,1)} %get-tuple-element.396.refs_1_, bf16[256,1024]{1,0:T(8,128)(2,1)} %get-tuple-element.397.refs_2_, bf16[256,1024]{1,0:T(8,128)(2,1)} %get-tuple-element.398.refs_3_, ...), custom_call_target="tpu_custom_call" | custom-call | flops 4294967296 | bytes 10485760 | tf_op jit(solution)/shard_map/outer/pallas_call | solution.py:763
  335.6 9.2 %mid_grad.1 = (f32[128,2048]{1,0:T(8,128)}, bf16[128,2048]{1,0:T(8,128)(2,1)}, bf16[32,80,128]{2,1,0:T(8,128)(2,1)}) custom-call(bf16[128,2048]{1,0:T(8,128)(2,1)} %get-tuple-element.421.own_ref, bf16[128,2048]{1,0:T(8,128)(2,1)} %copy-done.28, bf16[128,2048]{1,0:T(8,128)(2,1)} %copy-done.27, f32[128,2048]{1,0:T(8,128)} %copy-done, bf16[128,2048]{1,0:T(8,128)(2,1)} %refs_5_, ...), custom_call_target="tpu_custom_call" | custom-call | flops 1073741824 | bytes 8388608 | tf_op jit(solution)/shard_map/mid_grad/pallas_call | solution.py:1009
  346.7 3.0 all-to-all-start.3
  354.2 10.9 %outer.5 = (bf16[2,256,2048]{2,1,0:T(8,128)(2,1)}, bf16[2,256,2048]{2,1,0:T(8,128)(2,1)}) custom-call(s32[4]{0:T(128)} %broadcast_xor_fusion.refs_0_, bf16[256,1024]{1,0:T(8,128)(2,1)} %get-tuple-element.431.refs_1_, bf16[256,1024]{1,0:T(8,128)(2,1)} %get-tuple-element.432.refs_2_, bf16[256,1024]{1,0:T(8,128)(2,1)} %get-tuple-element.433.refs_3_, ...), custom_call_target="tpu_custom_call" | custom-call | flops 4294967296 | bytes 10485760 | tf_op jit(solution)/shard_map/outer/pallas_call | solution.py:763
  365.1 7.3 %all-gather.14.cloned.1.call-done = bf16[512,2048]{1,0:T(8,128)(2,1)} async-done(((bf16[128,2048]{1,0:T(8,128)(2,1)}), bf16[512,2048]{1,0:T(8,128)(2,1)}) %all-gather.14.cloned.1.call-update) | async-done | bytes 2097168 | tf_op jit(solution)/shard_map/all_gather | solution.py:1311
  372.3 4.2 convolution_convert_fusion
  383.3 31.9 %attn_bwd.1 = bf16[4,192,1024]{2,1,0:T(8,128)(2,1)} custom-call(s32[2,8]{1,0:T(2,128)} %pad_add_fusion.place_ref, bf16[192,4096]{1,0:T(8,128)(2,1)} %get-tuple-element.456.seq_hbm, f32[64,4096]{1,0:T(8,128)} %get-tuple-element.457.o32_hbm, f32[1,4096]{1,0:T(1,128)} %get-tuple-element.458.lse_ref, bf16[32,80,128]{2,1,0:T(8,128)(2,1)} %copy-done.23, ...), custom_call_target="tpu_custom_call" | custom-call | flops 21474836480 | bytes 8388608 | tf_op jit(solution)/shard_map/attn_bwd/pallas_call | solution.py:598
  417.3 3.6 all-to-all-start.4
  430.5 8.8 %collective-permute-done.43 = bf16[128,2048]{1,0:T(8,128)(2,1)S(1)} collective-permute-done((bf16[128,2048]{1,0:T(8,128)(2,1)}, bf16[128,2048]{1,0:T(8,128)(2,1)S(1)}, u32[]{:S(2)}, u32[]{:S(2)}) %collective-permute-start.43) | collective-permute-done | bytes 524320 | tf_op jit(solution)/shard_map/ppermute | solution.py:1032
  442.1 4.0 input_rows.1
  451.0 12.6 %heads_back.1 = (bf16[2,8,64,768]{3,2,1,0:T(8,128)(2,1)}, bf16[2,8,64,768]{3,2,1,0:T(8,128)(2,1)}, bf16[128,2048]{1,0:T(8,128)(2,1)}, bf16[128,2048]{1,0:T(8,128...) custom-call(s32[1]{0:T(128)} %bitcast.2.near_ref, ...), custom_call_target="tpu_custom_call" | custom-call | flops 6442450944 | bytes 16252928 | tf_op jit(solution)/shard_map/heads_back/pallas_call | solution.py:946
  464.3 3.6 collective-permute-done.49
  475.1 12.1 %collective-permute-done.48 = bf16[128,2048]{1,0:T(8,128)(2,1)S(1)} collective-permute-done((bf16[128,2048]{1,0:T(8,128)(2,1)}, bf16[128,2048]{1,0:T(8,128)(2,1)S(1)}, u32[]{:S(2)}, u32[]{:S(2)}) %collective-permute-start.48) | collective-permute-done | bytes 524320 | tf_op jit(solution)/shard_map/ppermute | solution.py:1032
  498.8 4.9 all-to-all-start.5
  514.8 3.4 bitcast_add_fusion.2
  518.2 3.4 bitcast_add_fusion.1
  522.7 5.1 collective-permute-done.55
  528.6 3.9 collective-permute-done.54
  532.5 4.1 all-to-all-done.5
  536.6 3.5 bitcast_add_fusion
  (316 shorter events, 129.7 us)
Async XLA Ops:
  7.2 142.4 %all-gather.6.cloned.1.call-start = ((), (), s32[]{:S(2)}) async-start(), calls=%async_computation.7 | async-start | bytes 5242880 | tf_op jit(solution)/shard_map/all_gather | solution.py:1225
  10.9 38.8 %all-to-all-start = ((bf16[8,64,768]{2,1,0:T(8,128)(2,1)}), bf16[8,64,768]{2,1,0:T(8,128)(2,1)S(1)}, u32[]{:S(2)}, u32[]{:S(2)}) async-start(bf16[8,64,768]{2,1,0:T(8,128)(2,1)} %maximum_bitcast_fusion), calls=%async_computation | async-start | bytes 1572864 | tf_op jit(solution)/shard_map/all_to_all | solution.py:1160
  18.4 154.3 %all-gather.8.cloned.1.call-start = ((), (), s32[]{:S(2)}) async-start(), calls=%async_computation.8 | async-start | bytes 8650752 | tf_op jit(solution)/shard_map/all_gather | solution.py:1230
  19.3 21.1 %collective-permute-start.1 = (bf16[128,2048]{1,0:T(8,128)(2,1)S(1)}, bf16[128,2048]{1,0:T(8,128)(2,1)S(1)}, u32[]{:S(2)}, u32[]{:S(2)}) collective-permute-start(bf16[128,2048]{1,0:T(8,128)(2,1)S(1)} %fusion.3.refs_0_), channel_id=1, source_target_pairs={{0,4},{4,0},{1,5},{5,1},{2,6},{6,2},{3,7},{7,3},{8,12},{12,8},{9,1... | collective-permute-start | bytes 1572872 | tf_op jit(solution)/shard_map/ppermute | solution.py:1032
  21.3 25.2 %collective-permute-start = (bf16[128,2048]{1,0:T(8,128)(2,1)S(1)}, bf16[128,2048]{1,0:T(8,128)(2,1)}, u32[]{:S(2)}, u32[]{:S(2)}) collective-permute-start(bf16[128,2048]{1,0:T(8,128)(2,1)S(1)} %fusion.3.refs_0_), channel_id=1, source_target_pairs={{0,8},{8,16},{16,24},{24,0},{1,9},{9,17},{17,25},{25,1},{2,10},{10... | collective-permute-start | bytes 1572872 | tf_op jit(solution)/shard_map/ppermute | solution.py:1037
  49.8 143.7 %all-gather.10.cloned.1.call-start = ((), (), s32[]{:S(2)}) async-start(), calls=%async_computation.9 | async-start | bytes 5242880 | tf_op jit(solution)/shard_map/all_gather | solution.py:1238
  51.5 17.7 %collective-permute-start.2 = (bf16[128,2048]{1,0:T(8,128)(2,1)}, bf16[128,2048]{1,0:T(8,128)(2,1)S(1)}, u32[]{:S(2)}, u32[]{:S(2)}) collective-permute-start(bf16[128,2048]{1,0:T(8,128)(2,1)} %collective-permute-done.refs_1_), channel_id=1, source_target_pairs={{0,8},{8,16},{16,24},{24,0},{1,9},{9,17},{17,25},{25,1},{2,10},{10... | collective-permute-start | bytes 1572872 | tf_op jit(solution)/shard_map/ppermute | solution.py:1037
  51.5 17.7 %collective-permute-start.5 = (bf16[8,64,768]{2,1,0:T(8,128)(2,1)S(1)}, bf16[8,64,768]{2,1,0:T(8,128)(2,1)S(1)}, u32[]{:S(2)}, u32[]{:S(2)}) collective-permute-start(bf16[8,64,768]{2,1,0:T(8,128)(2,1)S(1)} %all-to-all-done.refs_8_), channel_id=1, source_target_pairs={{0,1},{1,0},{2,3},{3,2},{4,5},{5,4},{6,7},{7,6},{8,9},{9,8},{10,11... | collective-permute-start | bytes 2359304 | tf_op jit(solution)/shard_map/ppermute | solution.py:1032
  83.1 19.1 %collective-permute-start.13 = (bf16[8,64,768]{2,1,0:T(8,128)(2,1)S(1)}, bf16[8,64,768]{2,1,0:T(8,128)(2,1)}, u32[]{:S(2)}, u32[]{:S(2)}) collective-permute-start(bf16[8,64,768]{2,1,0:T(8,128)(2,1)S(1)} %constant_dynamic-update-slice_fusion.refs_10_), channel_id=1, source_target_pairs={{0,1},{1,0},{2,3},{3,2},{4,5},{5,4},{6,7},{7,6},{8,9},{9,8},{10,11... | collective-permute-start | bytes 2359304 | tf_op jit(solution)/shard_map/ppermute | solution.py:1032
  83.2 18.1 %collective-permute-start.12 = (bf16[128,2048]{1,0:T(8,128)(2,1)S(1)}, bf16[128,2048]{1,0:T(8,128)(2,1)S(1)}, u32[]{:S(2)}, u32[]{:S(2)}) collective-permute-start(bf16[128,2048]{1,0:T(8,128)(2,1)S(1)} %collective-permute-done.6.refs_3_), channel_id=1, source_target_pairs={{0,4},{4,0},{1,5},{5,1},{2,6},{6,2},{3,7},{7,3},{8,12},{12,8},{9,1... | collective-permute-start | bytes 1572872 | tf_op jit(solution)/shard_map/ppermute | solution.py:1032
  102.2 20.6 %collective-permute-start.9 = (bf16[128,2048]{1,0:T(8,128)(2,1)S(1)}, bf16[128,2048]{1,0:T(8,128)(2,1)}, u32[]{:S(2)}, u32[]{:S(2)}) collective-permute-start(bf16[128,2048]{1,0:T(8,128)(2,1)S(1)} %copy-done.24), channel_id=1, source_target_pairs={{0,8},{8,16},{16,24},{24,0},{1,9},{9,17},{17,25},{25,1},{2,10},{10... | collective-permute-start | bytes 1572872 | tf_op jit(solution)/shard_map/ppermute | solution.py:1037
  111.6 38.0 %all-to-all-start.1 = ((bf16[4,192,1024]{2,1,0:T(8,128)(2,1)}), bf16[4,192,1024]{2,1,0:T(8,128)(2,1)S(1)}, u32[]{:S(2)}, u32[]{:S(2)}) async-start(bf16[4,192,1024]{2,1,0:T(8,128)(2,1)} %get-tuple-element.294), calls=%async_computation.1 | async-start | bytes 3145728 | tf_op jit(solution)/shard_map/all_to_all | solution.py:1250
  115.2 119.9 %all-gather.12.cloned.1.call-start = ((), (), s32[]{:S(2)}) async-start(), calls=%async_computation.10 | async-start | bytes 5242880 | tf_op jit(solution)/shard_map/all_gather | solution.py:1256
  115.3 22.9 %collective-permute-start.11 = (bf16[128,2048]{1,0:T(8,128)(2,1)S(1)}, bf16[128,2048]{1,0:T(8,128)(2,1)S(1)}, u32[]{:S(2)}, u32[]{:S(2)}) collective-permute-start(bf16[128,2048]{1,0:T(8,128)(2,1)S(1)} %copy-done.24), channel_id=1, source_target_pairs={{0,4},{4,0},{1,5},{5,1},{2,6},{6,2},{3,7},{7,3},{8,12},{12,8},{9,1... | collective-permute-start | bytes 1572872 | tf_op jit(solution)/shard_map/ppermute | solution.py:1032
  122.8 26.8 %collective-permute-start.10 = (bf16[128,2048]{1,0:T(8,128)(2,1)}, bf16[128,2048]{1,0:T(8,128)(2,1)}, u32[]{:S(2)}, u32[]{:S(2)}) collective-permute-start(bf16[128,2048]{1,0:T(8,128)(2,1)} %collective-permute-done.9.refs_2_.refs_7_), channel_id=1, source_target_pairs={{0,8},{8,16},{16,24},{24,0},{1,9},{9,17},{17,25},{25,1},{2,10},{10... | collective-permute-start | bytes 1572872 | tf_op jit(solution)/shard_map/ppermute | solution.py:1037
  151.2 21.5 %collective-permute-start.15 = (bf16[128,2048]{1,0:T(8,128)(2,1)}, bf16[128,2048]{1,0:T(8,128)(2,1)S(1)}, u32[]{:S(2)}, u32[]{:S(2)}) collective-permute-start(bf16[128,2048]{1,0:T(8,128)(2,1)} %collective-permute-done.9.refs_2_.refs_7_), channel_id=1, source_target_pairs={{0,4},{4,0},{1,5},{5,1},{2,6},{6,2},{3,7},{7,3},{8,12},{12,8},{9,1... | collective-permute-start | bytes 1572872 | tf_op jit(solution)/shard_map/ppermute | solution.py:1032
  152.3 20.4 %collective-permute-start.16 = (bf16[128,2048]{1,0:T(8,128)(2,1)}, bf16[128,2048]{1,0:T(8,128)(2,1)}, u32[]{:S(2)}, u32[]{:S(2)}) collective-permute-start(bf16[128,2048]{1,0:T(8,128)(2,1)} %collective-permute-done.10.refs_2_.refs_9_), channel_id=1, source_target_pairs={{0,4},{4,0},{1,5},{5,1},{2,6},{6,2},{3,7},{7,3},{8,12},{12,8},{9,1... | collective-permute-start | bytes 1572872 | tf_op jit(solution)/shard_map/ppermute | solution.py:1032
  153.2 19.5 %collective-permute-start.14 = (bf16[128,2048]{1,0:T(8,128)(2,1)}, bf16[128,2048]{1,0:T(8,128)(2,1)}, u32[]{:S(2)}, u32[]{:S(2)}) collective-permute-start(bf16[128,2048]{1,0:T(8,128)(2,1)} %collective-permute-done.10.refs_2_.refs_9_), channel_id=1, source_target_pairs={{0,8},{8,16},{16,24},{24,0},{1,9},{9,17},{17,25},{25,1},{2,10},{10... | collective-permute-start | bytes 1572872 | tf_op jit(solution)/shard_map/ppermute | solution.py:1037
  172.7 26.4 %all-to-all-start.2 = ((bf16[32,80,128]{2,1,0:T(8,128)(2,1)}), bf16[32,80,128]{2,1,0:T(8,128)(2,1)S(1)}, u32[]{:S(2)}, u32[]{:S(2)}) async-start(bf16[32,80,128]{2,1,0:T(8,128)(2,1)} %get-tuple-element.303), calls=%async_computation.2 | async-start | bytes 1310720 | tf_op jit(solution)/shard_map/all_to_all | solution.py:1262
  178.0 194.4 %all-gather.14.cloned.1.call-start = ((), (), s32[]{:S(2)}) async-start(), calls=%async_computation.11 | async-start | bytes 2621440 | tf_op jit(solution)/shard_map/all_gather | solution.py:1311
  178.0 21.1 %collective-permute-start.17 = (bf16[128,2048]{1,0:T(8,128)(2,1)}, bf16[128,2048]{1,0:T(8,128)(2,1)S(1)}, u32[]{:S(2)}, u32[]{:S(2)}) collective-permute-start(bf16[128,2048]{1,0:T(8,128)(2,1)} %collective-permute-done.14.refs_2_.refs_11_), channel_id=1, source_target_pairs={{0,4},{4,0},{1,5},{5,1},{2,6},{6,2},{3,7},{7,3},{8,12},{12,8},{9,1... | collective-permute-start | bytes 1572872 | tf_op jit(solution)/shard_map/ppermute | solution.py:1032
  206.3 17.4 %collective-permute-start.19 = (bf16[128,2048]{1,0:T(8,128)(2,1)S(1)}, bf16[128,2048]{1,0:T(8,128)(2,1)}, u32[]{:S(2)}, u32[]{:S(2)}) collective-permute-start(bf16[128,2048]{1,0:T(8,128)(2,1)S(1)} %multiply_convert_fusion.refs_0_.refs_5_), channel_id=1, source_target_pairs={{0,4},{4,0},{1,5},{5,1},{2,6},{6,2},{3,7},{7,3},{8,12},{12,8},{9,1... | collective-permute-start | bytes 1572872 | tf_op jit(solution)/shard_map/ppermute | solution.py:1032
  207.3 16.4 %collective-permute-start.18 = (bf16[128,2048]{1,0:T(8,128)(2,1)S(1)}, bf16[128,2048]{1,0:T(8,128)(2,1)}, u32[]{:S(2)}, u32[]{:S(2)}) collective-permute-start(bf16[128,2048]{1,0:T(8,128)(2,1)S(1)} %multiply_convert_fusion.refs_0_.refs_5_), channel_id=1, source_target_pairs={{0,8},{8,16},{16,24},{24,0},{1,9},{9,17},{17,25},{25,1},{2,10},{10... | collective-permute-start | bytes 1572872 | tf_op jit(solution)/shard_map/ppermute | solution.py:1037
  223.7 23.3 %collective-permute-start.22 = (bf16[128,2048]{1,0:T(8,128)(2,1)}, bf16[128,2048]{1,0:T(8,128)(2,1)}, u32[]{:S(2)}, u32[]{:S(2)}) collective-permute-start(bf16[128,2048]{1,0:T(8,128)(2,1)} %collective-permute-done.18.refs_0_.refs_7_), channel_id=1, source_target_pairs={{0,4},{4,0},{1,5},{5,1},{2,6},{6,2},{3,7},{7,3},{8,12},{12,8},{9,1... | collective-permute-start | bytes 1572872 | tf_op jit(solution)/shard_map/ppermute | solution.py:1032
  225.0 22.0 %collective-permute-start.21 = (bf16[128,2048]{1,0:T(8,128)(2,1)}, bf16[128,2048]{1,0:T(8,128)(2,1)}, u32[]{:S(2)}, u32[]{:S(2)}) collective-permute-start(bf16[128,2048]{1,0:T(8,128)(2,1)} %collective-permute-done.18.refs_0_.refs_7_), channel_id=1, source_target_pairs={{0,8},{8,16},{16,24},{24,0},{1,9},{9,17},{17,25},{25,1},{2,10},{10... | collective-permute-start | bytes 1572872 | tf_op jit(solution)/shard_map/ppermute | solution.py:1037
  226.5 20.4 %collective-permute-start.23 = (bf16[2,8,64,128]{3,2,1,0:T(8,128)(2,1)S(1)}, bf16[2,8,64,128]{3,2,1,0:T(8,128)(2,1)S(1)}, u32[]{:S(2)}, u32[]{:S(2)}) collective-permute-start(bf16[2,8,64,128]{3,2,1,0:T(8,128)(2,1)S(1)} %fusion.21), channel_id=1, source_target_pairs={{0,1},{1,0},{2,3},{3,2},{4,5},{5,4},{6,7},{7,6},{8,9},{9,8},{10,11... | collective-permute-start | bytes 786440 | tf_op jit(solution)/shard_map/ppermute | solution.py:1032
  248.5 16.0 %collective-permute-start.24 = (bf16[128,2048]{1,0:T(8,128)(2,1)}, bf16[128,2048]{1,0:T(8,128)(2,1)S(1)}, u32[]{:S(2)}, u32[]{:S(2)}) collective-permute-start(bf16[128,2048]{1,0:T(8,128)(2,1)} %collective-permute-done.21.refs_0_.refs_9_), channel_id=1, source_target_pairs={{0,8},{8,16},{16,24},{24,0},{1,9},{9,17},{17,25},{25,1},{2,10},{10... | collective-permute-start | bytes 1572872 | tf_op jit(solution)/shard_map/ppermute | solution.py:1037
  265.0 23.9 %collective-permute-start.26 = (bf16[128,2048]{1,0:T(8,128)(2,1)S(1)}, bf16[128,2048]{1,0:T(8,128)(2,1)}, u32[]{:S(2)}, u32[]{:S(2)}) collective-permute-start(bf16[128,2048]{1,0:T(8,128)(2,1)S(1)} %collective-permute-done.24.refs_0_.refs_11_), channel_id=1, source_target_pairs={{0,4},{4,0},{1,5},{5,1},{2,6},{6,2},{3,7},{7,3},{8,12},{12,8},{9,1... | collective-permute-start | bytes 1572872 | tf_op jit(solution)/shard_map/ppermute | solution.py:1032
  317.9 16.9 %collective-permute-start.34 = (bf16[2,256,2048]{2,1,0:T(8,128)(2,1)}, bf16[2,256,2048]{2,1,0:T(8,128)(2,1)}, u32[]{:S(2)}, u32[]{:S(2)}) collective-permute-start(bf16[2,256,2048]{2,1,0:T(8,128)(2,1)} %get-tuple-element.391), channel_id=1, source_target_pairs={{0,1},{1,0},{2,3},{3,2},{4,5},{5,4},{6,7},{7,6},{8,9},{9,8},{10,11... | collective-permute-start | bytes 6291464 | tf_op jit(solution)/shard_map/ppermute | solution.py:1032
  318.3 16.6 %collective-permute-start.32 = (bf16[128,2048]{1,0:T(8,128)(2,1)S(1)}, bf16[128,2048]{1,0:T(8,128)(2,1)S(1)}, u32[]{:S(2)}, u32[]{:S(2)}) collective-permute-start(bf16[128,2048]{1,0:T(8,128)(2,1)S(1)} %add_convert_fusion.12), channel_id=1, source_target_pairs={{0,8},{8,16},{16,24},{24,0},{1,9},{9,17},{17,25},{25,1},{2,10},{10... | collective-permute-start | bytes 1572872 | tf_op jit(solution)/shard_map/ppermute | solution.py:1037
  344.9 31.6 %collective-permute-start.36 = (bf16[2,256,2048]{2,1,0:T(8,128)(2,1)}, bf16[2,256,2048]{2,1,0:T(8,128)(2,1)}, u32[]{:S(2)}, u32[]{:S(2)}) collective-permute-start(bf16[2,256,2048]{2,1,0:T(8,128)(2,1)} %get-tuple-element.448), channel_id=1, source_target_pairs={{0,1},{1,0},{2,3},{3,2},{4,5},{5,4},{6,7},{7,6},{8,9},{9,8},{10,11... | collective-permute-start | bytes 6291464 | tf_op jit(solution)/shard_map/ppermute | solution.py:1032
  346.7 29.8 %all-to-all-start.3 = ((bf16[32,80,128]{2,1,0:T(8,128)(2,1)}), bf16[32,80,128]{2,1,0:T(8,128)(2,1)S(1)}, u32[]{:S(2)}, u32[]{:S(2)}) async-start(bf16[32,80,128]{2,1,0:T(8,128)(2,1)} %get-tuple-element.424), calls=%async_computation.3 | async-start | bytes 1310720 | tf_op jit(solution)/shard_map/all_to_all | solution.py:1323
  349.7 125.4 %reduce-scatter.2.cloned.1.call-start = ((), (), s32[]{:S(2)}) async-start(), calls=%async_computation.12 | async-start | bytes 2359296 | tf_op jit(solution)/shard_map/reduce_scatter | solution.py:1329
  349.7 26.8 %collective-permute-start.35 = (bf16[128,2048]{1,0:T(8,128)(2,1)}, bf16[128,2048]{1,0:T(8,128)(2,1)}, u32[]{:S(2)}, u32[]{:S(2)}) collective-permute-start(bf16[128,2048]{1,0:T(8,128)(2,1)} %get-tuple-element.426), channel_id=1, source_target_pairs={{0,4},{4,0},{1,5},{5,1},{2,6},{6,2},{3,7},{7,3},{8,12},{12,8},{9,1... | collective-permute-start | bytes 1572872 | tf_op jit(solution)/shard_map/ppermute | solution.py:1032
  376.5 39.4 %collective-permute-start.41 = (bf16[2,256,2048]{2,1,0:T(8,128)(2,1)}, bf16[2,256,2048]{2,1,0:T(8,128)(2,1)S(1)}, u32[]{:S(2)}, u32[]{:S(2)}) collective-permute-start(bf16[2,256,2048]{2,1,0:T(8,128)(2,1)} %get-tuple-element.462), channel_id=1, source_target_pairs={{0,1},{1,0},{2,3},{3,2},{4,5},{5,4},{6,7},{7,6},{8,9},{9,8},{10,11... | collective-permute-start | bytes 6291464 | tf_op jit(solution)/shard_map/ppermute | solution.py:1032
  379.0 36.2 %collective-permute-start.38 = (bf16[128,2048]{1,0:T(8,128)(2,1)}, bf16[128,2048]{1,0:T(8,128)(2,1)}, u32[]{:S(2)}, u32[]{:S(2)}) collective-permute-start(bf16[128,2048]{1,0:T(8,128)(2,1)} %add_convert_fusion.11), channel_id=1, source_target_pairs={{0,8},{8,16},{16,24},{24,0},{1,9},{9,17},{17,25},{25,1},{2,10},{10... | collective-permute-start | bytes 1572872 | tf_op jit(solution)/shard_map/ppermute | solution.py:1037
  380.6 34.5 %collective-permute-start.39 = (bf16[128,2048]{1,0:T(8,128)(2,1)}, bf16[128,2048]{1,0:T(8,128)(2,1)}, u32[]{:S(2)}, u32[]{:S(2)}) collective-permute-start(bf16[128,2048]{1,0:T(8,128)(2,1)} %get-tuple-element.453), channel_id=1, source_target_pairs={{0,4},{4,0},{1,5},{5,1},{2,6},{6,2},{3,7},{7,3},{8,12},{12,8},{9,1... | collective-permute-start | bytes 1572872 | tf_op jit(solution)/shard_map/ppermute | solution.py:1032
  382.1 33.0 %collective-permute-start.40 = (bf16[128,2048]{1,0:T(8,128)(2,1)}, bf16[128,2048]{1,0:T(8,128)(2,1)S(1)}, u32[]{:S(2)}, u32[]{:S(2)}) collective-permute-start(bf16[128,2048]{1,0:T(8,128)(2,1)} %get-tuple-element.455), channel_id=1, source_target_pairs={{0,4},{4,0},{1,5},{5,1},{2,6},{6,2},{3,7},{7,3},{8,12},{12,8},{9,1... | collective-permute-start | bytes 1572872 | tf_op jit(solution)/shard_map/ppermute | solution.py:1032
  382.7 33.3 %collective-permute-start.37 = (bf16[256,2048]{1,0:T(8,128)(2,1)}, bf16[256,2048]{1,0:T(8,128)(2,1)}, u32[]{:S(2)}, u32[]{:S(2)}) collective-permute-start(bf16[256,2048]{1,0:T(8,128)(2,1)} %fusion.7), channel_id=1, source_target_pairs={{0,2},{2,0},{1,3},{3,1},{4,6},{6,4},{5,7},{7,5},{8,10},{10,8},{9,1... | collective-permute-start | bytes 3145736 | tf_op jit(solution)/shard_map/ppermute | solution.py:1032
  417.3 23.6 %all-to-all-start.4 = ((bf16[4,192,1024]{2,1,0:T(8,128)(2,1)}), bf16[4,192,1024]{2,1,0:T(8,128)(2,1)S(1)}, u32[]{:S(2)}, u32[]{:S(2)}) async-start(bf16[4,192,1024]{2,1,0:T(8,128)(2,1)} %attn_bwd.1), calls=%async_computation.4 | async-start | bytes 3145728 | tf_op jit(solution)/shard_map/all_to_all | solution.py:1341
  422.5 17.6 %collective-permute-start.42 = (bf16[128,2048]{1,0:T(8,128)(2,1)S(1)}, bf16[128,2048]{1,0:T(8,128)(2,1)}, u32[]{:S(2)}, u32[]{:S(2)}) collective-permute-start(bf16[128,2048]{1,0:T(8,128)(2,1)S(1)} %add_convert_fusion.10), channel_id=1, source_target_pairs={{0,8},{8,16},{16,24},{24,0},{1,9},{9,17},{17,25},{25,1},{2,10},{10... | collective-permute-start | bytes 1572872 | tf_op jit(solution)/shard_map/ppermute | solution.py:1037
  446.1 17.5 %collective-permute-start.44 = (bf16[128,2048]{1,0:T(8,128)(2,1)}, bf16[128,2048]{1,0:T(8,128)(2,1)S(1)}, u32[]{:S(2)}, u32[]{:S(2)}) collective-permute-start(bf16[128,2048]{1,0:T(8,128)(2,1)} %input_rows.1), channel_id=1, source_target_pairs={{0,4},{4,0},{1,5},{5,1},{2,6},{6,2},{3,7},{7,3},{8,12},{12,8},{9,1... | collective-permute-start | bytes 1572872 | tf_op jit(solution)/shard_map/ppermute | solution.py:1032
  471.3 19.8 %collective-permute-start.50 = (bf16[8,64,768]{2,1,0:T(8,128)(2,1)}, bf16[8,64,768]{2,1,0:T(8,128)(2,1)S(1)}, u32[]{:S(2)}, u32[]{:S(2)}) collective-permute-start(bf16[8,64,768]{2,1,0:T(8,128)(2,1)} %fusion.9), channel_id=1, source_target_pairs={{0,2},{2,0},{1,3},{3,1},{4,6},{6,4},{5,7},{7,5},{8,10},{10,8},{9,1... | collective-permute-start | bytes 2359304 | tf_op jit(solution)/shard_map/ppermute | solution.py:1032
  493.3 17.0 %collective-permute-start.51 = (bf16[128,2048]{1,0:T(8,128)(2,1)}, bf16[128,2048]{1,0:T(8,128)(2,1)}, u32[]{:S(2)}, u32[]{:S(2)}) collective-permute-start(bf16[128,2048]{1,0:T(8,128)(2,1)} %add_convert_fusion.5), channel_id=1, source_target_pairs={{0,8},{8,16},{16,24},{24,0},{1,9},{9,17},{17,25},{25,1},{2,10},{10... | collective-permute-start | bytes 1572872 | tf_op jit(solution)/shard_map/ppermute | solution.py:1037
  494.5 15.7 %collective-permute-start.53 = (bf16[128,2048]{1,0:T(8,128)(2,1)}, bf16[128,2048]{1,0:T(8,128)(2,1)}, u32[]{:S(2)}, u32[]{:S(2)}) collective-permute-start(bf16[128,2048]{1,0:T(8,128)(2,1)} %get-tuple-element.511), channel_id=1, source_target_pairs={{0,2},{2,0},{1,3},{3,1},{4,6},{6,4},{5,7},{7,5},{8,10},{10,8},{9,1... | collective-permute-start | bytes 1572872 | tf_op jit(solution)/shard_map/ppermute | solution.py:1032
  498.8 37.7 %all-to-all-start.5 = ((bf16[8,64,768]{2,1,0:T(8,128)(2,1)}), bf16[8,64,768]{2,1,0:T(8,128)(2,1)S(1)}, u32[]{:S(2)}, u32[]{:S(2)}) async-start(bf16[8,64,768]{2,1,0:T(8,128)(2,1)} %fusion.1), calls=%async_computation.6 | async-start | bytes 1572864 | tf_op jit(solution)/shard_map/all_to_all | solution.py:1365
  511.9 20.6 %collective-permute-start.54 = (bf16[128,2048]{1,0:T(8,128)(2,1)S(1)}, bf16[128,2048]{1,0:T(8,128)(2,1)}, u32[]{:S(2)}, u32[]{:S(2)}) collective-permute-start(bf16[128,2048]{1,0:T(8,128)(2,1)S(1)} %add_convert_fusion.4), channel_id=1, source_target_pairs={{0,8},{8,16},{16,24},{24,0},{1,9},{9,17},{17,25},{25,1},{2,10},{10... | collective-permute-start | bytes 1572872 | tf_op jit(solution)/shard_map/ppermute | solution.py:1037
  513.1 23.5 %collective-permute-start.56 = (bf16[256,2048]{1,0:T(8,128)(2,1)}, bf16[256,2048]{1,0:T(8,128)(2,1)}, u32[]{:S(2)}, u32[]{:S(2)}) collective-permute-start(bf16[256,2048]{1,0:T(8,128)(2,1)} %fusion.8), channel_id=1, source_target_pairs={{0,2},{2,0},{1,3},{3,1},{4,6},{6,4},{5,7},{7,5},{8,10},{10,8},{9,1... | collective-permute-start | bytes 3145736 | tf_op jit(solution)/shard_map/ppermute | solution.py:1032
  (88 other events, 1048.5 us)
Sparse Core Ops, SparseCore 0:
  9.6 37.1 all-gather.5
  49.9 103.7 all-gather.7
  155.2 38.2 all-gather.9
  194.9 40.1 all-gather.11
  345.0 27.2 all-gather.13
  380.7 71.0 reduce-scatter.1

commit v5 on v4

--- a/solution.py
+++ b/solution.py
@@ -633,42 +633,80 @@
 
 def ffn_kernel(*refs, count, step):
     x, dy = refs[:count], refs[count : 2 * count]
-    w_hbm = refs[2 * count : 2 * count + 3]
-    dn, br = refs[2 * count + 3 : 3 * count + 3], refs[3 * count + 3 : 4 * count + 3]
-    kept = refs[4 * count + 3 : 4 * count + 6]
-    x_scr, dy_scr, gate_w, up_w, down_w, hid_scr, dgate_scr, dup_scr, act_scr, dn_scr, br_scr, in_sem, w_sem, out_sem, keep_sem = refs[4 * count + 6 :]
+    gate_hbm, rest_hbm = refs[2 * count : 2 * count + 2]
+    refs = refs[2 * count + 2 :]
+    dn, br, kept = refs[:count], refs[count : 2 * count], refs[2 * count : 2 * count + 3]
+    (
+        x_scr,
+        dy_scr,
+        gate_w,
+        up_w,
+        down_w,
+        hid_scr,
+        dgate_scr,
+        dup_scr,
+        act_scr,
+        dn_scr,
+        br_scr,
+        in_sem,
+        w_sem,
+        out_sem,
+        keep_sem,
+    ) = refs[2 * count + 3 :]
     tok, width = x[0].shape
-    hidden = gate_w.shape[0]
+    hidden, parts = gate_w.shape[0], w_sem.shape[1]
+    part = hidden // parts
     rows_in = [
         pltpu.make_async_copy(src[i], dst.at[i * tok : (i + 1) * tok], in_sem.at[k, i])
         for k, (src, dst) in enumerate(((x, x_scr), (dy, dy_scr)))
         for i in range(count)
     ]
-    w_in = [
-        pltpu.make_async_copy(src, dst, w_sem.at[k])
-        for k, (src, dst) in enumerate(zip(w_hbm, (gate_w, up_w, down_w)))
-    ]
-    for c in rows_in[:count] + w_in[:2] + rows_in[count:] + w_in[2:]:
+    gate_in, up_in, down_in = (
+        [
+            pltpu.make_async_copy(
+                src.at[at(j) * part : (at(j) + 1) * part],
+                dst.at[j * part : (j + 1) * part],
+                w_sem.at[i, j],
+            )
+            for j in range(parts)
+        ]
+        for i, (src, at, dst) in enumerate(
+            (
+                (gate_hbm, lambda j: j, gate_w),
+                (rest_hbm, lambda j: 2 * j, up_w),
+                (rest_hbm, lambda j: 2 * j + 1, down_w),
+            )
+        )
+    )
+    for c in rows_in[:count]:
         c.start()
-    for c in rows_in[:count] + w_in[:2]:
+    for pair in zip(gate_in, up_in, strict=True):
+        for c in pair:
+            c.start()
+    for c in rows_in[count:] + down_in:
+        c.start()
+    for c in rows_in[:count]:
         c.wait()
-    half = hidden // 2
-    for h in range(2):
-        part = slice(h * half, (h + 1) * half)
-        gate = mxu_nt(x_scr[...], gate_w[part, :])
-        up = mxu_nt(x_scr[...], up_w[part, :])
+    for lo, hi in ((0, parts // 2), (parts // 2, parts)):
+        for c in gate_in[lo:hi] + up_in[lo:hi]:
+            c.wait()
+        here = slice(lo * part, hi * part)
+        gate = mxu_nt(x_scr[...], gate_w[here, :])
+        up = mxu_nt(x_scr[...], up_w[here, :])
         sig = jax.nn.sigmoid(gate)
         act = gate * sig
-        hid_scr[:, part] = (act * up).astype(BF16)
-        act_scr[:, part] = act
-        dgate_scr[:, part] = up * (sig * (1.0 + gate * (1.0 - sig)))
-    for c in rows_in[count:] + w_in[2:]:
+        hid_scr[:, here] = (act * up).astype(BF16)
+        act_scr[:, here] = act
+        dgate_scr[:, here] = up * (sig * (1.0 + gate * (1.0 - sig)))
+    for c in rows_in[count:]:
         c.wait()
-    for h in range(2):
-        part = slice(h * half, (h + 1) * half)
-        dhidden = mxu_nt(dy_scr[...], down_w[part, :])
-        dup_scr[1, :, part] = (dhidden * act_scr[:, part]).astype(BF16)
-        dup_scr[0, :, part] = (dhidden * dgate_scr[:, part]).astype(BF16)
+    for lo, hi in ((0, parts // 2), (parts // 2, parts)):
+        for c in down_in[lo:hi]:
+            c.wait()
+        here = slice(lo * part, hi * part)
+        dhidden = mxu_nt(dy_scr[...], down_w[here, :])
+        dup_scr[1, :, here] = (dhidden * act_scr[:, here]).astype(BF16)
+        dup_scr[0, :, here] = (dhidden * dgate_scr[:, here]).astype(BF16)
     keep = [
         pltpu.make_async_copy(src, dst, keep_sem.at[k])
         for k, (src, dst) in enumerate(zip((hid_scr, dup_scr.at[0], dup_scr.at[1]), kept))
@@ -690,12 +728,12 @@
         c.wait()
 
 
-def ffn(x, dy, gate_w, up_w, down_w):
+def ffn(x, dy, gate_w, rest_w, parts):
     count, (tok, width), hidden = len(x), x[0].shape, gate_w.shape[0]
     rows, step = count * tok, width // 4
     out = pl.pallas_call(
         functools.partial(ffn_kernel, count=count, step=step),
-        in_specs=[ANY] * (2 * count + 3),
+        in_specs=[ANY] * (2 * count + 2),
         out_specs=[ANY] * (2 * count + 3),
         out_shape=[jax.ShapeDtypeStruct((tok, width), BF16)] * (2 * count)
         + [jax.ShapeDtypeStruct((rows, hidden), BF16)] * 3,
@@ -709,7 +747,7 @@
             pltpu.VMEM((rows, width), BF16),
             pltpu.VMEM((rows, width), BF16),
             pltpu.SemaphoreType.DMA((2, count)),
-            pltpu.SemaphoreType.DMA((3,)),
+            pltpu.SemaphoreType.DMA((3, parts)),
             pltpu.SemaphoreType.DMA((2, count, width // step)),
             pltpu.SemaphoreType.DMA((3,)),
         ],
@@ -718,7 +756,7 @@
             flops=12 * rows * hidden * width, bytes_accessed=6 * hidden * width + 16 * rows * width, transcendentals=rows * hidden
         ),
         name="ffn",
-    )(*x, *dy, gate_w, up_w, down_w)
+    )(*x, *dy, gate_w, rest_w)
     return out[:count], out[count : 2 * count], out[2 * count :]
 
 
@@ -1233,9 +1271,9 @@
     dy_low = stage([one_flow, heads_flow], cotangent)
     dy_by = {}
     dy_flow = Flow(spread_late(dy_low, dy_by))
-    w_up = stage([one_flow, heads_flow], w_up)
+    w_rest = stage([one_flow, heads_flow], jnp.concatenate([w_up, w_down], axis=0))
     dy_flow.run_on()
-    up_w = lax.all_gather(w_up, NEAR, axis=0, tiled=True)
+    rest_w = lax.all_gather(w_rest, NEAR, axis=0, tiled=True)
     slot_names = [(c, r) for r in range(2) for c in range(n_ctx)]
     qkv, rows_one, w_heads = qkv_of(
         near_at.reshape(1),
@@ -1253,13 +1291,11 @@
             seq_sin,
         ),
     )
-    down_w = lax.all_gather(after(w_down, qkv_head), NEAR, axis=0, tiled=True)
     (attn_head, o32, lse, seq), out_w = stage(
         [dy_flow], (attn_fwd(places, qkv_head, beside(gain_ffn, tok), far), out_w)
     )
-    attn, up_w = stage(
-        [dy_flow],
-        (lax.all_to_all(attn_head, FAR + NEAR, split_axis=0, concat_axis=0, tiled=True), up_w),
+    attn = stage(
+        [dy_flow], lax.all_to_all(attn_head, FAR + NEAR, split_axis=0, concat_axis=0, tiled=True)
     )
     gain_two = attn[:, HD, :own_in].reshape(1, width).astype(F32)
     attn_all = attn[:, :HD]
@@ -1278,7 +1314,7 @@
     def feed(cs, first=()):
         names = [(c, r) for c in cs for r in range(2)]
         rows = after([two[k] for k in names], first)
-        dn, br, lefts = ffn(rows, [dy_by[k] for k in names], gate_w, up_w, down_w)
+        dn, br, lefts = ffn(rows, [dy_by[k] for k in names], gate_w, rest_w, near)
         return dict(zip(names, dn, strict=True)), dict(zip(names, br, strict=True)), lefts
 
     def fed(results):
@@ -1287,15 +1323,15 @@
         br_by.update(br)
         kept.append(lefts)
 
-    stage([two_flow, side_flow])
-    stage([two_flow, side_flow], feed([0]), fed)
+    stage([two_flow])
+    stage([two_flow], feed([0]), fed)
     for c in range(1, n_ctx - 2):
         stage([two_flow], feed([c]), fed)
     marks = []
     dn_flow = Flow(collect(dn_by, marks, open_end=True))
-    stage([two_flow, dn_flow], feed([n_ctx - 2]), fed)
+    stage([two_flow, dn_flow, side_flow], feed([n_ctx - 2]), fed)
     last = feed([n_ctx - 1], marks[-1])
-    stage([dn_flow], last, fed)
+    stage([dn_flow, side_flow], last, fed)
     names = [(c, r) for c in range(n_ctx) for r in range(2)]
     two_rows, dy_rows = [two[k] for k in names], [dy_by[k] for k in names]
     tiles = near_at ^ jnp.array([3, 1, 2, 0], jnp.int32)

time: 561 us -> 555 us (0.989)
  waiting for transfers between devices: 210 us -> 203 us
    all_gather x2 -> x1, waiting for transfers between devices: 22.2 us -> 3.76 us  [per_device_split(): rest_w = lax.all_gather(w_rest, NEAR, axis=0, tiled=True)]
    ppermute x39, waiting for transfers between devices: 128 us -> 137 us  [swap(): return lax.ppermute(v, axis, [(0, 1), (1, 0)])]
    unnamed x136 -> x134, local copies, waits for them, and re-layouts: 11.5 us -> 11.4 us
  transfers between devices with their start and end apart: 69 -> 68, of which waited for: 34 -> 37; matrix products, arithmetic and copies ran while one was open for 10% -> 11% of each run, Pallas kernels for 28% -> 29%
where the time goes in v5:
time: 555 us; the launch traced here: 548 us
  waiting for transfers between devices  203 us (37%)
  Pallas kernels  168 us (30%)
  starting transfers between devices  80.3 us (14%)
  other arithmetic  56.1 us (10%)
  local copies, waits for them, and re-layouts  16.7 us (3%)
  between operations  14.9 us (3%)
  matrix products  8.91 us (2%)
    ppermute x39, waiting for transfers between devices, swap(): return lax.ppermute(v, axis, [(0, 1), (1, 0)])  137 us
    pallas_call x4, Pallas kernels, ffn(): pl.pallas_call(functools.partial(ffn_kernel, count=count, step=step), in_...  49.7 us
    ppermute x18, waiting for transfers between devices, shift(): return lax.ppermute(v, 'ctx', [(i, (i + 1) % n) for i in range(n)])  45.8 us
    ppermute x39, starting transfers between devices, swap(): return lax.ppermute(v, axis, [(0, 1), (1, 0)])  38.4 us
    pallas_call x3, Pallas kernels, outer(): pl.pallas_call(functools.partial(outer_kernel, lefts=len(left), rights=le...  32.4 us
    pallas_call x1, Pallas kernels, attn_bwd(): pl.pallas_call(functools.partial(attn_bwd_kernel, blocks=blocks, width=wi...  31.9 us
    pallas_call x1, Pallas kernels, attn_fwd(): pl.pallas_call(functools.partial(attn_fwd_kernel, blocks=blocks, width=co...  19.1 us
    ppermute x18, starting transfers between devices, shift(): return lax.ppermute(v, 'ctx', [(i, (i + 1) % n) for i in range(n)])  14.4 us
  transfers between devices with their start and end apart: 68, of which 37 were waited for; matrix products, arithmetic and copies ran while one was open for 11% of the time, Pallas kernels for 29%

profile of v5, /device:TPU:0, one launch (start us, length us, event | category | flops | bytes accessed | tf_op | source)
XLA Modules:
  0.0 547.7 jit_solution(12885208774960630309)
XLA Ops:
  10.9 7.4 %all-to-all-start = ((bf16[8,64,768]{2,1,0:T(8,128)(2,1)}), bf16[8,64,768]{2,1,0:T(8,128)(2,1)S(1)}, u32[]{:S(2)}, u32[]{:S(2)}) async-start(bf16[8,64,768]{2,1,0:T(8,128)(2,1)} %maximum_bitcast_fusion), calls=%async_computation | async-start | bytes 1572864 | tf_op jit(solution)/shard_map/all_to_all | solution.py:1198
  22.8 17.5 %collective-permute-done.1.refs_4_ = bf16[128,2048]{1,0:T(8,128)(2,1)S(1)} collective-permute-done((bf16[128,2048]{1,0:T(8,128)(2,1)S(1)}, bf16[128,2048]{1,0:T(8,128)(2,1)S(1)}, u32[]{:S(2)}, u32[]{:S(2)}) %collective-permute-start.1) | collective-permute-done | bytes 524320 | tf_op jit(solution)/shard_map/ppermute | solution.py:1070
  41.2 5.4 collective-permute-done.refs_1_
  46.6 3.2 all-to-all-done.refs_8_
  54.4 10.6 %collective-permute-done.4 = bf16[4,64,768]{2,1,0:T(8,128)(2,1)S(1)} collective-permute-done((bf16[4,64,768]{2,1,0:T(8,128)(2,1)S(1)}, bf16[4,64,768]{2,1,0:T(8,128)(2,1)S(1)}, u32[]{:S(2)}, u32[]{:S(2)}) %collective-permute-start.4) | collective-permute-done | bytes 393248 | tf_op jit(solution)/shard_map/ppermute | solution.py:1070
  65.0 4.2 collective-permute-done.2.refs_2_
  69.3 3.2 collective-permute-start.8
  73.2 5.0 collective-permute-done.8
  78.6 4.6 collective-permute-done.6.refs_3_
  86.8 15.6 %collective-permute-done.12.refs_7_ = bf16[128,2048]{1,0:T(8,128)(2,1)} collective-permute-done((bf16[128,2048]{1,0:T(8,128)(2,1)}, bf16[128,2048]{1,0:T(8,128)(2,1)}, u32[]{:S(2)}, u32[]{:S(2)}) %collective-permute-start.12) | collective-permute-done | bytes 524320 | tf_op jit(solution)/shard_map/ppermute | solution.py:1070
  102.6 9.3 %qkv.1 = (bf16[4,192,1024]{2,1,0:T(8,128)(2,1)}, bf16[1024,2048]{1,0:T(8,128)(2,1)}, bf16[2048,768]{1,0:T(8,128)(2,1)}) custom-call(s32[1]{0:T(128)} %bitcast.2.near_ref, bf16[128,2048]{1,0:T(8,128)(2,1)} %copy-done.35, bf16[128,2048]{1,0:T(8,128)(2,1)} %collective-permute-done.refs_1_, bf16[128,2048]{1,0:T(8,128)(2,1)} %copy-done.63, ...), custom_call_target="tpu_custom_call" | custom-call | flops 3221225472 | bytes 14680064 | tf_op jit(solution)/shard_map/qkv/pallas_call | solution.py:871
  112.0 3.6 all-to-all-start.1
  118.1 5.5 collective-permute-done.9.refs_2_.refs_7_
  123.6 2.8 multiply_sine_fusion
  127.6 10.5 %collective-permute-done.11.refs_3_.refs_6_ = bf16[128,2048]{1,0:T(8,128)(2,1)S(1)} collective-permute-done((bf16[128,2048]{1,0:T(8,128)(2,1)S(1)}, bf16[128,2048]{1,0:T(8,128)(2,1)S(1)}, u32[]{:S(2)}, u32[]{:S(2)}) %collective-permute-start.11) | collective-permute-done | bytes 524320 | tf_op jit(solution)/shard_map/ppermute | solution.py:1070
  139.0 11.2 %collective-permute-done.10.refs_2_.refs_9_ = bf16[128,2048]{1,0:T(8,128)(2,1)} collective-permute-done((bf16[128,2048]{1,0:T(8,128)(2,1)S(1)}, bf16[128,2048]{1,0:T(8,128)(2,1)}, u32[]{:S(2)}, u32[]{:S(2)}) %collective-permute-start.10) | collective-permute-done | bytes 524320 | tf_op jit(solution)/shard_map/ppermute | solution.py:1075
  151.9 19.1 %attn_fwd.1 = (bf16[32,80,128]{2,1,0:T(8,128)(2,1)}, f32[64,4096]{1,0:T(8,128)}, f32[1,4096]{1,0:T(1,128)}, bf16[192,4096]{1,0:T(8,128)(2,1)}) custom-call(s32[2,8]{1,0:T(2,128)} %pad_add_fusion.place_ref, bf16[4,192,1024]{2,1,0:T(8,128)(2,1)} %copy-done.15, bf16[16,128]{1,0:T(8,128)(2,1)} %pad.4.extra_ref), custom_call_target="tpu_custom_call" | custom-call | flops 8589934592 | bytes 8388608 | tf_op jit(solution)/shard_map/attn_fwd/pallas_call | solution.py:464
  171.1 5.2 all-to-all-start.2
  178.2 19.2 %collective-permute-done.17.refs_3_.refs_12_ = bf16[128,2048]{1,0:T(8,128)(2,1)S(1)} collective-permute-done((bf16[128,2048]{1,0:T(8,128)(2,1)S(1)}, bf16[128,2048]{1,0:T(8,128)(2,1)S(1)}, u32[]{:S(2)}, u32[]{:S(2)}) %collective-permute-start.17) | collective-permute-done | bytes 524320 | tf_op jit(solution)/shard_map/ppermute | solution.py:1070
  198.5 4.7 multiply_reduce_fusion
  208.2 9.5 %collective-permute-done.19.refs_1_.refs_6_ = bf16[128,2048]{1,0:T(8,128)(2,1)} collective-permute-done((bf16[128,2048]{1,0:T(8,128)(2,1)S(1)}, bf16[128,2048]{1,0:T(8,128)(2,1)}, u32[]{:S(2)}, u32[]{:S(2)}) %collective-permute-start.19) | collective-permute-done | bytes 524320 | tf_op jit(solution)/shard_map/ppermute | solution.py:1070
  221.2 3.8 all-gather.9.cloned.1.call-done.refs_5_
  225.0 12.4 %ffn.4 = (bf16[128,2048]{1,0:T(8,128)(2,1)}, bf16[128,2048]{1,0:T(8,128)(2,1)}, bf16[128,2048]{1,0:T(8,128)(2,1)}, bf16[128,2048]{1,0:T(8,128)(2,1)}, bf16[256,1...) custom-call(bf16[128,2048]{1,0:T(8,128)(2,1)} %copy-done.33, ...), custom_call_target="tpu_custom_call" | custom-call | flops 6442450944 | bytes 20971520 | tf_op jit(solution)/shard_map/ffn/pallas_call | solution.py:734
  240.6 12.4 %ffn.5 = (bf16[128,2048]{1,0:T(8,128)(2,1)}, bf16[128,2048]{1,0:T(8,128)(2,1)}, bf16[128,2048]{1,0:T(8,128)(2,1)}, bf16[128,2048]{1,0:T(8,128)(2,1)}, bf16[256,1...) custom-call(bf16[128,2048]{1,0:T(8,128)(2,1)} %collective-permute-done.18.refs_0_.refs_7_, ...), custom_call_target="tpu_custom_call" | custom-call | flops 6442450944 | bytes 20971520 | tf_op jit(solution)/shard_map/ffn/pallas_call | solution.py:734
  257.0 12.5 %ffn.6 = (bf16[128,2048]{1,0:T(8,128)(2,1)}, bf16[128,2048]{1,0:T(8,128)(2,1)}, bf16[128,2048]{1,0:T(8,128)(2,1)}, bf16[128,2048]{1,0:T(8,128)(2,1)}, bf16[256,1...) custom-call(bf16[128,2048]{1,0:T(8,128)(2,1)} %collective-permute-done.20.refs_0_.refs_9_, ...), custom_call_target="tpu_custom_call" | custom-call | flops 6442450944 | bytes 20971520 | tf_op jit(solution)/shard_map/ffn/pallas_call | solution.py:734
  270.0 9.4 %collective-permute-done.24.refs_1_.refs_12_ = bf16[128,2048]{1,0:T(8,128)(2,1)} collective-permute-done((bf16[128,2048]{1,0:T(8,128)(2,1)S(1)}, bf16[128,2048]{1,0:T(8,128)(2,1)}, u32[]{:S(2)}, u32[]{:S(2)}) %collective-permute-start.24) | collective-permute-done | bytes 524320 | tf_op jit(solution)/shard_map/ppermute | solution.py:1070
  281.3 12.4 %ffn.7 = (bf16[128,2048]{1,0:T(8,128)(2,1)}, bf16[128,2048]{1,0:T(8,128)(2,1)}, bf16[128,2048]{1,0:T(8,128)(2,1)}, bf16[128,2048]{1,0:T(8,128)(2,1)}, bf16[256,1...) custom-call(bf16[128,2048]{1,0:T(8,128)(2,1)} %copy-done.60, ...), custom_call_target="tpu_custom_call" | custom-call | flops 6442450944 | bytes 20971520 | tf_op jit(solution)/shard_map/ffn/pallas_call | solution.py:734
  299.0 10.8 %outer.3 = (bf16[2,256,2048]{2,1,0:T(8,128)(2,1)}, bf16[2,256,2048]{2,1,0:T(8,128)(2,1)}) custom-call(s32[4]{0:T(128)} %broadcast_xor_fusion.refs_0_, bf16[256,1024]{1,0:T(8,128)(2,1)} %get-tuple-element.369.refs_1_, bf16[256,1024]{1,0:T(8,128)(2,1)} %get-tuple-element.370.refs_2_, bf16[256,1024]{1,0:T(8,128)(2,1)} %get-tuple-element.371.refs_3_, ...), custom_call_target="tpu_custom_call" | custom-call | flops 4294967296 | bytes 10485760 | tf_op jit(solution)/shard_map/outer/pallas_call | solution.py:801
  315.5 10.7 %outer.4 = (bf16[2,256,2048]{2,1,0:T(8,128)(2,1)}, bf16[2,256,2048]{2,1,0:T(8,128)(2,1)}) custom-call(s32[4]{0:T(128)} %broadcast_xor_fusion.refs_0_, bf16[256,1024]{1,0:T(8,128)(2,1)} %get-tuple-element.392.refs_1_, bf16[256,1024]{1,0:T(8,128)(2,1)} %get-tuple-element.393.refs_2_, bf16[256,1024]{1,0:T(8,128)(2,1)} %get-tuple-element.394.refs_3_, ...), custom_call_target="tpu_custom_call" | custom-call | flops 4294967296 | bytes 10485760 | tf_op jit(solution)/shard_map/outer/pallas_call | solution.py:801
  329.6 9.3 %mid_grad.1 = (f32[128,2048]{1,0:T(8,128)}, bf16[128,2048]{1,0:T(8,128)(2,1)}, bf16[32,80,128]{2,1,0:T(8,128)(2,1)}) custom-call(bf16[128,2048]{1,0:T(8,128)(2,1)} %get-tuple-element.417.own_ref, bf16[128,2048]{1,0:T(8,128)(2,1)} %copy-done.31, bf16[128,2048]{1,0:T(8,128)(2,1)} %copy-done.30, f32[128,2048]{1,0:T(8,128)} %copy-done, bf16[128,2048]{1,0:T(8,128)(2,1)} %refs_5_, ...), custom_call_target="tpu_custom_call" | custom-call | flops 1073741824 | bytes 8388608 | tf_op jit(solution)/shard_map/mid_grad/pallas_call | solution.py:1047
  347.7 10.9 %outer.5 = (bf16[2,256,2048]{2,1,0:T(8,128)(2,1)}, bf16[2,256,2048]{2,1,0:T(8,128)(2,1)}) custom-call(s32[4]{0:T(128)} %broadcast_xor_fusion.refs_0_, bf16[256,1024]{1,0:T(8,128)(2,1)} %get-tuple-element.427.refs_1_, bf16[256,1024]{1,0:T(8,128)(2,1)} %get-tuple-element.428.refs_2_, bf16[256,1024]{1,0:T(8,128)(2,1)} %get-tuple-element.429.refs_3_, ...), custom_call_target="tpu_custom_call" | custom-call | flops 4294967296 | bytes 10485760 | tf_op jit(solution)/shard_map/outer/pallas_call | solution.py:801
  358.6 7.3 %all-gather.11.cloned.1.call-done = bf16[512,2048]{1,0:T(8,128)(2,1)} async-done(((bf16[128,2048]{1,0:T(8,128)(2,1)}), bf16[512,2048]{1,0:T(8,128)(2,1)}) %all-gather.11.cloned.1.call-update) | async-done | bytes 2097168 | tf_op jit(solution)/shard_map/all_gather | solution.py:1347
  365.9 4.2 convolution_convert_fusion
  376.8 31.9 %attn_bwd.1 = bf16[4,192,1024]{2,1,0:T(8,128)(2,1)} custom-call(s32[2,8]{1,0:T(2,128)} %pad_add_fusion.place_ref, bf16[192,4096]{1,0:T(8,128)(2,1)} %get-tuple-element.452.seq_hbm, f32[64,4096]{1,0:T(8,128)} %get-tuple-element.453.o32_hbm, f32[1,4096]{1,0:T(1,128)} %get-tuple-element.454.lse_ref, bf16[32,80,128]{2,1,0:T(8,128)(2,1)} %copy-done.25, ...), custom_call_target="tpu_custom_call" | custom-call | flops 21474836480 | bytes 8388608 | tf_op jit(solution)/shard_map/attn_bwd/pallas_call | solution.py:598
  410.9 3.6 all-to-all-start.4
  424.1 8.8 %collective-permute-done.43 = bf16[128,2048]{1,0:T(8,128)(2,1)S(1)} collective-permute-done((bf16[128,2048]{1,0:T(8,128)(2,1)}, bf16[128,2048]{1,0:T(8,128)(2,1)S(1)}, u32[]{:S(2)}, u32[]{:S(2)}) %collective-permute-start.43) | collective-permute-done | bytes 524320 | tf_op jit(solution)/shard_map/ppermute | solution.py:1070
  435.6 4.0 input_rows.1
  444.5 12.6 %heads_back.1 = (bf16[2,8,64,768]{3,2,1,0:T(8,128)(2,1)}, bf16[2,8,64,768]{3,2,1,0:T(8,128)(2,1)}, bf16[128,2048]{1,0:T(8,128)(2,1)}, bf16[128,2048]{1,0:T(8,128...) custom-call(s32[1]{0:T(128)} %bitcast.2.near_ref, ...), custom_call_target="tpu_custom_call" | custom-call | flops 6442450944 | bytes 16252928 | tf_op jit(solution)/shard_map/heads_back/pallas_call | solution.py:984
  457.9 3.6 collective-permute-done.49
  468.7 12.0 %collective-permute-done.48 = bf16[128,2048]{1,0:T(8,128)(2,1)S(1)} collective-permute-done((bf16[128,2048]{1,0:T(8,128)(2,1)}, bf16[128,2048]{1,0:T(8,128)(2,1)S(1)}, u32[]{:S(2)}, u32[]{:S(2)}) %collective-permute-start.48) | collective-permute-done | bytes 524320 | tf_op jit(solution)/shard_map/ppermute | solution.py:1070
  492.4 4.8 all-to-all-start.5
  499.1 3.0 collective-permute-done.52
  508.3 3.4 bitcast_add_fusion.2
  511.7 3.4 bitcast_add_fusion.1
  516.2 5.2 collective-permute-done.55
  522.1 3.9 collective-permute-done.54
  526.0 4.1 all-to-all-done.5
  530.1 3.5 bitcast_add_fusion
  (312 shorter events, 132.0 us)
Async XLA Ops:
  7.2 142.9 %all-gather.5.cloned.1.call-start = ((), (), s32[]{:S(2)}) async-start(), calls=%async_computation.7 | async-start | bytes 5242880 | tf_op jit(solution)/shard_map/all_gather | solution.py:1263
  10.9 38.8 %all-to-all-start = ((bf16[8,64,768]{2,1,0:T(8,128)(2,1)}), bf16[8,64,768]{2,1,0:T(8,128)(2,1)S(1)}, u32[]{:S(2)}, u32[]{:S(2)}) async-start(bf16[8,64,768]{2,1,0:T(8,128)(2,1)} %maximum_bitcast_fusion), calls=%async_computation | async-start | bytes 1572864 | tf_op jit(solution)/shard_map/all_to_all | solution.py:1198
  18.4 152.7 %all-gather.7.cloned.1.call-start = ((), (), s32[]{:S(2)}) async-start(), calls=%async_computation.8 | async-start | bytes 8650752 | tf_op jit(solution)/shard_map/all_gather | solution.py:1268
  19.3 21.0 %collective-permute-start.1 = (bf16[128,2048]{1,0:T(8,128)(2,1)S(1)}, bf16[128,2048]{1,0:T(8,128)(2,1)S(1)}, u32[]{:S(2)}, u32[]{:S(2)}) collective-permute-start(bf16[128,2048]{1,0:T(8,128)(2,1)S(1)} %fusion.3.refs_0_), channel_id=1, source_target_pairs={{0,4},{4,0},{1,5},{5,1},{2,6},{6,2},{3,7},{7,3},{8,12},{12,8},{9,1... | collective-permute-start | bytes 1572872 | tf_op jit(solution)/shard_map/ppermute | solution.py:1070
  21.4 25.2 %collective-permute-start = (bf16[128,2048]{1,0:T(8,128)(2,1)S(1)}, bf16[128,2048]{1,0:T(8,128)(2,1)}, u32[]{:S(2)}, u32[]{:S(2)}) collective-permute-start(bf16[128,2048]{1,0:T(8,128)(2,1)S(1)} %fusion.3.refs_0_), channel_id=1, source_target_pairs={{0,8},{8,16},{16,24},{24,0},{1,9},{9,17},{17,25},{25,1},{2,10},{10... | collective-permute-start | bytes 1572872 | tf_op jit(solution)/shard_map/ppermute | solution.py:1075
  49.8 175.2 %all-gather.9.cloned.1.call-start = ((), (), s32[]{:S(2)}) async-start(), calls=%async_computation.9 | async-start | bytes 10485760 | tf_op jit(solution)/shard_map/all_gather | solution.py:1276
  51.4 17.7 %collective-permute-start.2 = (bf16[128,2048]{1,0:T(8,128)(2,1)}, bf16[128,2048]{1,0:T(8,128)(2,1)S(1)}, u32[]{:S(2)}, u32[]{:S(2)}) collective-permute-start(bf16[128,2048]{1,0:T(8,128)(2,1)} %collective-permute-done.refs_1_), channel_id=1, source_target_pairs={{0,8},{8,16},{16,24},{24,0},{1,9},{9,17},{17,25},{25,1},{2,10},{10... | collective-permute-start | bytes 1572872 | tf_op jit(solution)/shard_map/ppermute | solution.py:1075
  51.4 17.7 %collective-permute-start.5 = (bf16[8,64,768]{2,1,0:T(8,128)(2,1)S(1)}, bf16[8,64,768]{2,1,0:T(8,128)(2,1)S(1)}, u32[]{:S(2)}, u32[]{:S(2)}) collective-permute-start(bf16[8,64,768]{2,1,0:T(8,128)(2,1)S(1)} %all-to-all-done.refs_8_), channel_id=1, source_target_pairs={{0,1},{1,0},{2,3},{3,2},{4,5},{5,4},{6,7},{7,6},{8,9},{9,8},{10,11... | collective-permute-start | bytes 2359304 | tf_op jit(solution)/shard_map/ppermute | solution.py:1070
  83.9 18.5 %collective-permute-start.13 = (bf16[8,64,768]{2,1,0:T(8,128)(2,1)}, bf16[8,64,768]{2,1,0:T(8,128)(2,1)}, u32[]{:S(2)}, u32[]{:S(2)}) collective-permute-start(bf16[8,64,768]{2,1,0:T(8,128)(2,1)} %constant_dynamic-update-slice_fusion.refs_10_), channel_id=1, source_target_pairs={{0,1},{1,0},{2,3},{3,2},{4,5},{5,4},{6,7},{7,6},{8,9},{9,8},{10,11... | collective-permute-start | bytes 2359304 | tf_op jit(solution)/shard_map/ppermute | solution.py:1070
  84.0 18.5 %collective-permute-start.12 = (bf16[128,2048]{1,0:T(8,128)(2,1)}, bf16[128,2048]{1,0:T(8,128)(2,1)}, u32[]{:S(2)}, u32[]{:S(2)}) collective-permute-start(bf16[128,2048]{1,0:T(8,128)(2,1)} %collective-permute-done.6.refs_3_), channel_id=1, source_target_pairs={{0,4},{4,0},{1,5},{5,1},{2,6},{6,2},{3,7},{7,3},{8,12},{12,8},{9,1... | collective-permute-start | bytes 1572872 | tf_op jit(solution)/shard_map/ppermute | solution.py:1070
  102.6 21.0 %collective-permute-start.9 = (bf16[128,2048]{1,0:T(8,128)(2,1)S(1)}, bf16[128,2048]{1,0:T(8,128)(2,1)S(1)}, u32[]{:S(2)}, u32[]{:S(2)}) collective-permute-start(bf16[128,2048]{1,0:T(8,128)(2,1)S(1)} %copy-done.26), channel_id=1, source_target_pairs={{0,8},{8,16},{16,24},{24,0},{1,9},{9,17},{17,25},{25,1},{2,10},{10... | collective-permute-start | bytes 1572872 | tf_op jit(solution)/shard_map/ppermute | solution.py:1075
  112.0 38.1 %all-to-all-start.1 = ((bf16[4,192,1024]{2,1,0:T(8,128)(2,1)}), bf16[4,192,1024]{2,1,0:T(8,128)(2,1)S(1)}, u32[]{:S(2)}, u32[]{:S(2)}) async-start(bf16[4,192,1024]{2,1,0:T(8,128)(2,1)} %get-tuple-element.292), calls=%async_computation.1 | async-start | bytes 3145728 | tf_op jit(solution)/shard_map/all_to_all | solution.py:1288
  116.8 21.3 %collective-permute-start.11 = (bf16[128,2048]{1,0:T(8,128)(2,1)S(1)}, bf16[128,2048]{1,0:T(8,128)(2,1)S(1)}, u32[]{:S(2)}, u32[]{:S(2)}) collective-permute-start(bf16[128,2048]{1,0:T(8,128)(2,1)S(1)} %copy-done.26), channel_id=1, source_target_pairs={{0,4},{4,0},{1,5},{5,1},{2,6},{6,2},{3,7},{7,3},{8,12},{12,8},{9,1... | collective-permute-start | bytes 1572872 | tf_op jit(solution)/shard_map/ppermute | solution.py:1070
  123.6 26.5 %collective-permute-start.10 = (bf16[128,2048]{1,0:T(8,128)(2,1)S(1)}, bf16[128,2048]{1,0:T(8,128)(2,1)}, u32[]{:S(2)}, u32[]{:S(2)}) collective-permute-start(bf16[128,2048]{1,0:T(8,128)(2,1)S(1)} %collective-permute-done.9.refs_2_.refs_7_), channel_id=1, source_target_pairs={{0,8},{8,16},{16,24},{24,0},{1,9},{9,17},{17,25},{25,1},{2,10},{10... | collective-permute-start | bytes 1572872 | tf_op jit(solution)/shard_map/ppermute | solution.py:1075
  126.4 44.6 %collective-permute-start.15 = (bf16[128,2048]{1,0:T(8,128)(2,1)S(1)}, bf16[128,2048]{1,0:T(8,128)(2,1)}, u32[]{:S(2)}, u32[]{:S(2)}) collective-permute-start(bf16[128,2048]{1,0:T(8,128)(2,1)S(1)} %collective-permute-done.9.refs_2_.refs_7_), channel_id=1, source_target_pairs={{0,4},{4,0},{1,5},{5,1},{2,6},{6,2},{3,7},{7,3},{8,12},{12,8},{9,1... | collective-permute-start | bytes 1572872 | tf_op jit(solution)/shard_map/ppermute | solution.py:1070
  150.1 20.9 %collective-permute-start.16 = (bf16[128,2048]{1,0:T(8,128)(2,1)}, bf16[128,2048]{1,0:T(8,128)(2,1)}, u32[]{:S(2)}, u32[]{:S(2)}) collective-permute-start(bf16[128,2048]{1,0:T(8,128)(2,1)} %collective-permute-done.10.refs_2_.refs_9_), channel_id=1, source_target_pairs={{0,4},{4,0},{1,5},{5,1},{2,6},{6,2},{3,7},{7,3},{8,12},{12,8},{9,1... | collective-permute-start | bytes 1572872 | tf_op jit(solution)/shard_map/ppermute | solution.py:1070
  151.6 19.4 %collective-permute-start.14 = (bf16[128,2048]{1,0:T(8,128)(2,1)}, bf16[128,2048]{1,0:T(8,128)(2,1)S(1)}, u32[]{:S(2)}, u32[]{:S(2)}) collective-permute-start(bf16[128,2048]{1,0:T(8,128)(2,1)} %collective-permute-done.10.refs_2_.refs_9_), channel_id=1, source_target_pairs={{0,8},{8,16},{16,24},{24,0},{1,9},{9,17},{17,25},{25,1},{2,10},{10... | collective-permute-start | bytes 1572872 | tf_op jit(solution)/shard_map/ppermute | solution.py:1075
  171.1 27.2 %all-to-all-start.2 = ((bf16[32,80,128]{2,1,0:T(8,128)(2,1)}), bf16[32,80,128]{2,1,0:T(8,128)(2,1)S(1)}, u32[]{:S(2)}, u32[]{:S(2)}) async-start(bf16[32,80,128]{2,1,0:T(8,128)(2,1)} %get-tuple-element.301), calls=%async_computation.2 | async-start | bytes 1310720 | tf_op jit(solution)/shard_map/all_to_all | solution.py:1298
  176.3 189.6 %all-gather.11.cloned.1.call-start = ((), (), s32[]{:S(2)}) async-start(), calls=%async_computation.10 | async-start | bytes 2621440 | tf_op jit(solution)/shard_map/all_gather | solution.py:1347
  176.4 21.1 %collective-permute-start.17 = (bf16[128,2048]{1,0:T(8,128)(2,1)S(1)}, bf16[128,2048]{1,0:T(8,128)(2,1)S(1)}, u32[]{:S(2)}, u32[]{:S(2)}) collective-permute-start(bf16[128,2048]{1,0:T(8,128)(2,1)S(1)} %collective-permute-done.14.refs_2_.refs_11_), channel_id=1, source_target_pairs={{0,4},{4,0},{1,5},{5,1},{2,6},{6,2},{3,7},{7,3},{8,12},{12,8},{9,1... | collective-permute-start | bytes 1572872 | tf_op jit(solution)/shard_map/ppermute | solution.py:1070
  206.9 62.6 %collective-permute-start.26 = (bf16[2,8,64,128]{3,2,0,1:T(8,128)(2,1)}, bf16[2,8,64,128]{3,2,0,1:T(8,128)(2,1)S(1)}, u32[]{:S(2)}, u32[]{:S(2)}) collective-permute-start(bf16[2,8,64,128]{3,2,0,1:T(8,128)(2,1)} %fusion.22), channel_id=1, source_target_pairs={{0,2},{2,0},{1,3},{3,1},{4,6},{6,4},{5,7},{7,5},{8,10},{10,8},{9,1... | collective-permute-start | bytes 786440 | tf_op jit(solution)/shard_map/ppermute | solution.py:1070
  220.3 17.2 %collective-permute-start.21 = (bf16[128,2048]{1,0:T(8,128)(2,1)}, bf16[128,2048]{1,0:T(8,128)(2,1)}, u32[]{:S(2)}, u32[]{:S(2)}) collective-permute-start(bf16[128,2048]{1,0:T(8,128)(2,1)} %collective-permute-done.18.refs_0_.refs_7_), channel_id=1, source_target_pairs={{0,4},{4,0},{1,5},{5,1},{2,6},{6,2},{3,7},{7,3},{8,12},{12,8},{9,1... | collective-permute-start | bytes 1572872 | tf_op jit(solution)/shard_map/ppermute | solution.py:1070
  221.2 16.2 %collective-permute-start.20 = (bf16[128,2048]{1,0:T(8,128)(2,1)}, bf16[128,2048]{1,0:T(8,128)(2,1)}, u32[]{:S(2)}, u32[]{:S(2)}) collective-permute-start(bf16[128,2048]{1,0:T(8,128)(2,1)} %collective-permute-done.18.refs_0_.refs_7_), channel_id=1, source_target_pairs={{0,8},{8,16},{16,24},{24,0},{1,9},{9,17},{17,25},{25,1},{2,10},{10... | collective-permute-start | bytes 1572872 | tf_op jit(solution)/shard_map/ppermute | solution.py:1075
  237.5 15.6 %collective-permute-start.23 = (bf16[128,2048]{1,0:T(8,128)(2,1)}, bf16[128,2048]{1,0:T(8,128)(2,1)S(1)}, u32[]{:S(2)}, u32[]{:S(2)}) collective-permute-start(bf16[128,2048]{1,0:T(8,128)(2,1)} %collective-permute-done.20.refs_0_.refs_9_), channel_id=1, source_target_pairs={{0,4},{4,0},{1,5},{5,1},{2,6},{6,2},{3,7},{7,3},{8,12},{12,8},{9,1... | collective-permute-start | bytes 1572872 | tf_op jit(solution)/shard_map/ppermute | solution.py:1070
  239.0 16.0 %collective-permute-start.22 = (bf16[128,2048]{1,0:T(8,128)(2,1)}, bf16[128,2048]{1,0:T(8,128)(2,1)S(1)}, u32[]{:S(2)}, u32[]{:S(2)}) collective-permute-start(bf16[128,2048]{1,0:T(8,128)(2,1)} %collective-permute-done.20.refs_0_.refs_9_), channel_id=1, source_target_pairs={{0,8},{8,16},{16,24},{24,0},{1,9},{9,17},{17,25},{25,1},{2,10},{10... | collective-permute-start | bytes 1572872 | tf_op jit(solution)/shard_map/ppermute | solution.py:1075
  255.5 24.0 %collective-permute-start.24 = (bf16[128,2048]{1,0:T(8,128)(2,1)S(1)}, bf16[128,2048]{1,0:T(8,128)(2,1)}, u32[]{:S(2)}, u32[]{:S(2)}) collective-permute-start(bf16[128,2048]{1,0:T(8,128)(2,1)S(1)} %collective-permute-done.22.refs_0_.refs_11_), channel_id=1, source_target_pairs={{0,4},{4,0},{1,5},{5,1},{2,6},{6,2},{3,7},{7,3},{8,12},{12,8},{9,1... | collective-permute-start | bytes 1572872 | tf_op jit(solution)/shard_map/ppermute | solution.py:1070
  279.7 15.6 %collective-permute-start.27 = (bf16[128,2048]{1,0:T(8,128)(2,1)S(1)}, bf16[128,2048]{1,0:T(8,128)(2,1)S(1)}, u32[]{:S(2)}, u32[]{:S(2)}) collective-permute-start(bf16[128,2048]{1,0:T(8,128)(2,1)S(1)} %add_convert_fusion.14), channel_id=1, source_target_pairs={{0,8},{8,16},{16,24},{24,0},{1,9},{9,17},{17,25},{25,1},{2,10},{10... | collective-permute-start | bytes 1572872 | tf_op jit(solution)/shard_map/ppermute | solution.py:1075
  311.9 16.8 %collective-permute-start.34 = (bf16[2,256,2048]{2,1,0:T(8,128)(2,1)}, bf16[2,256,2048]{2,1,0:T(8,128)(2,1)}, u32[]{:S(2)}, u32[]{:S(2)}) collective-permute-start(bf16[2,256,2048]{2,1,0:T(8,128)(2,1)} %get-tuple-element.387), channel_id=1, source_target_pairs={{0,1},{1,0},{2,3},{3,2},{4,5},{5,4},{6,7},{7,6},{8,9},{9,8},{10,11... | collective-permute-start | bytes 6291464 | tf_op jit(solution)/shard_map/ppermute | solution.py:1070
  312.2 16.6 %collective-permute-start.32 = (bf16[128,2048]{1,0:T(8,128)(2,1)S(1)}, bf16[128,2048]{1,0:T(8,128)(2,1)S(1)}, u32[]{:S(2)}, u32[]{:S(2)}) collective-permute-start(bf16[128,2048]{1,0:T(8,128)(2,1)S(1)} %add_convert_fusion.12), channel_id=1, source_target_pairs={{0,8},{8,16},{16,24},{24,0},{1,9},{9,17},{17,25},{25,1},{2,10},{10... | collective-permute-start | bytes 1572872 | tf_op jit(solution)/shard_map/ppermute | solution.py:1075
  338.9 31.2 %collective-permute-start.36 = (bf16[2,256,2048]{2,1,0:T(8,128)(2,1)}, bf16[2,256,2048]{2,1,0:T(8,128)(2,1)}, u32[]{:S(2)}, u32[]{:S(2)}) collective-permute-start(bf16[2,256,2048]{2,1,0:T(8,128)(2,1)} %get-tuple-element.444), channel_id=1, source_target_pairs={{0,1},{1,0},{2,3},{3,2},{4,5},{5,4},{6,7},{7,6},{8,9},{9,8},{10,11... | collective-permute-start | bytes 6291464 | tf_op jit(solution)/shard_map/ppermute | solution.py:1070
  340.6 29.4 %all-to-all-start.3 = ((bf16[32,80,128]{2,1,0:T(8,128)(2,1)}), bf16[32,80,128]{2,1,0:T(8,128)(2,1)S(1)}, u32[]{:S(2)}, u32[]{:S(2)}) async-start(bf16[32,80,128]{2,1,0:T(8,128)(2,1)} %get-tuple-element.420), calls=%async_computation.3 | async-start | bytes 1310720 | tf_op jit(solution)/shard_map/all_to_all | solution.py:1359
  343.3 125.4 %reduce-scatter.2.cloned.1.call-start = ((), (), s32[]{:S(2)}) async-start(), calls=%async_computation.11 | async-start | bytes 2359296 | tf_op jit(solution)/shard_map/reduce_scatter | solution.py:1365
  343.3 26.7 %collective-permute-start.35 = (bf16[128,2048]{1,0:T(8,128)(2,1)}, bf16[128,2048]{1,0:T(8,128)(2,1)}, u32[]{:S(2)}, u32[]{:S(2)}) collective-permute-start(bf16[128,2048]{1,0:T(8,128)(2,1)} %get-tuple-element.422), channel_id=1, source_target_pairs={{0,4},{4,0},{1,5},{5,1},{2,6},{6,2},{3,7},{7,3},{8,12},{12,8},{9,1... | collective-permute-start | bytes 1572872 | tf_op jit(solution)/shard_map/ppermute | solution.py:1070
  370.1 39.4 %collective-permute-start.41 = (bf16[2,256,2048]{2,1,0:T(8,128)(2,1)}, bf16[2,256,2048]{2,1,0:T(8,128)(2,1)S(1)}, u32[]{:S(2)}, u32[]{:S(2)}) collective-permute-start(bf16[2,256,2048]{2,1,0:T(8,128)(2,1)} %get-tuple-element.458), channel_id=1, source_target_pairs={{0,1},{1,0},{2,3},{3,2},{4,5},{5,4},{6,7},{7,6},{8,9},{9,8},{10,11... | collective-permute-start | bytes 6291464 | tf_op jit(solution)/shard_map/ppermute | solution.py:1070
  372.5 36.2 %collective-permute-start.38 = (bf16[128,2048]{1,0:T(8,128)(2,1)}, bf16[128,2048]{1,0:T(8,128)(2,1)}, u32[]{:S(2)}, u32[]{:S(2)}) collective-permute-start(bf16[128,2048]{1,0:T(8,128)(2,1)} %add_convert_fusion.11), channel_id=1, source_target_pairs={{0,8},{8,16},{16,24},{24,0},{1,9},{9,17},{17,25},{25,1},{2,10},{10... | collective-permute-start | bytes 1572872 | tf_op jit(solution)/shard_map/ppermute | solution.py:1075
  374.1 34.5 %collective-permute-start.39 = (bf16[128,2048]{1,0:T(8,128)(2,1)}, bf16[128,2048]{1,0:T(8,128)(2,1)}, u32[]{:S(2)}, u32[]{:S(2)}) collective-permute-start(bf16[128,2048]{1,0:T(8,128)(2,1)} %get-tuple-element.449), channel_id=1, source_target_pairs={{0,4},{4,0},{1,5},{5,1},{2,6},{6,2},{3,7},{7,3},{8,12},{12,8},{9,1... | collective-permute-start | bytes 1572872 | tf_op jit(solution)/shard_map/ppermute | solution.py:1070
  375.7 33.0 %collective-permute-start.40 = (bf16[128,2048]{1,0:T(8,128)(2,1)}, bf16[128,2048]{1,0:T(8,128)(2,1)S(1)}, u32[]{:S(2)}, u32[]{:S(2)}) collective-permute-start(bf16[128,2048]{1,0:T(8,128)(2,1)} %get-tuple-element.451), channel_id=1, source_target_pairs={{0,4},{4,0},{1,5},{5,1},{2,6},{6,2},{3,7},{7,3},{8,12},{12,8},{9,1... | collective-permute-start | bytes 1572872 | tf_op jit(solution)/shard_map/ppermute | solution.py:1070
  376.2 33.3 %collective-permute-start.37 = (bf16[256,2048]{1,0:T(8,128)(2,1)}, bf16[256,2048]{1,0:T(8,128)(2,1)}, u32[]{:S(2)}, u32[]{:S(2)}) collective-permute-start(bf16[256,2048]{1,0:T(8,128)(2,1)} %fusion.7), channel_id=1, source_target_pairs={{0,2},{2,0},{1,3},{3,1},{4,6},{6,4},{5,7},{7,5},{8,10},{10,8},{9,1... | collective-permute-start | bytes 3145736 | tf_op jit(solution)/shard_map/ppermute | solution.py:1070
  410.9 23.6 %all-to-all-start.4 = ((bf16[4,192,1024]{2,1,0:T(8,128)(2,1)}), bf16[4,192,1024]{2,1,0:T(8,128)(2,1)S(1)}, u32[]{:S(2)}, u32[]{:S(2)}) async-start(bf16[4,192,1024]{2,1,0:T(8,128)(2,1)} %attn_bwd.1), calls=%async_computation.4 | async-start | bytes 3145728 | tf_op jit(solution)/shard_map/all_to_all | solution.py:1377
  416.1 17.6 %collective-permute-start.42 = (bf16[128,2048]{1,0:T(8,128)(2,1)S(1)}, bf16[128,2048]{1,0:T(8,128)(2,1)}, u32[]{:S(2)}, u32[]{:S(2)}) collective-permute-start(bf16[128,2048]{1,0:T(8,128)(2,1)S(1)} %add_convert_fusion.10), channel_id=1, source_target_pairs={{0,8},{8,16},{16,24},{24,0},{1,9},{9,17},{17,25},{25,1},{2,10},{10... | collective-permute-start | bytes 1572872 | tf_op jit(solution)/shard_map/ppermute | solution.py:1075
  439.7 17.5 %collective-permute-start.44 = (bf16[128,2048]{1,0:T(8,128)(2,1)}, bf16[128,2048]{1,0:T(8,128)(2,1)S(1)}, u32[]{:S(2)}, u32[]{:S(2)}) collective-permute-start(bf16[128,2048]{1,0:T(8,128)(2,1)} %input_rows.1), channel_id=1, source_target_pairs={{0,4},{4,0},{1,5},{5,1},{2,6},{6,2},{3,7},{7,3},{8,12},{12,8},{9,1... | collective-permute-start | bytes 1572872 | tf_op jit(solution)/shard_map/ppermute | solution.py:1070
  464.8 19.8 %collective-permute-start.50 = (bf16[8,64,768]{2,1,0:T(8,128)(2,1)}, bf16[8,64,768]{2,1,0:T(8,128)(2,1)S(1)}, u32[]{:S(2)}, u32[]{:S(2)}) collective-permute-start(bf16[8,64,768]{2,1,0:T(8,128)(2,1)} %fusion.9), channel_id=1, source_target_pairs={{0,2},{2,0},{1,3},{3,1},{4,6},{6,4},{5,7},{7,5},{8,10},{10,8},{9,1... | collective-permute-start | bytes 2359304 | tf_op jit(solution)/shard_map/ppermute | solution.py:1070
  486.8 17.0 %collective-permute-start.51 = (bf16[128,2048]{1,0:T(8,128)(2,1)}, bf16[128,2048]{1,0:T(8,128)(2,1)}, u32[]{:S(2)}, u32[]{:S(2)}) collective-permute-start(bf16[128,2048]{1,0:T(8,128)(2,1)} %add_convert_fusion.5), channel_id=1, source_target_pairs={{0,8},{8,16},{16,24},{24,0},{1,9},{9,17},{17,25},{25,1},{2,10},{10... | collective-permute-start | bytes 1572872 | tf_op jit(solution)/shard_map/ppermute | solution.py:1075
  488.1 15.7 %collective-permute-start.53 = (bf16[128,2048]{1,0:T(8,128)(2,1)}, bf16[128,2048]{1,0:T(8,128)(2,1)}, u32[]{:S(2)}, u32[]{:S(2)}) collective-permute-start(bf16[128,2048]{1,0:T(8,128)(2,1)} %get-tuple-element.507), channel_id=1, source_target_pairs={{0,2},{2,0},{1,3},{3,1},{4,6},{6,4},{5,7},{7,5},{8,10},{10,8},{9,1... | collective-permute-start | bytes 1572872 | tf_op jit(solution)/shard_map/ppermute | solution.py:1070
  492.4 37.7 %all-to-all-start.5 = ((bf16[8,64,768]{2,1,0:T(8,128)(2,1)}), bf16[8,64,768]{2,1,0:T(8,128)(2,1)S(1)}, u32[]{:S(2)}, u32[]{:S(2)}) async-start(bf16[8,64,768]{2,1,0:T(8,128)(2,1)} %fusion.1), calls=%async_computation.6 | async-start | bytes 1572864 | tf_op jit(solution)/shard_map/all_to_all | solution.py:1401
  505.4 20.6 %collective-permute-start.54 = (bf16[128,2048]{1,0:T(8,128)(2,1)S(1)}, bf16[128,2048]{1,0:T(8,128)(2,1)}, u32[]{:S(2)}, u32[]{:S(2)}) collective-permute-start(bf16[128,2048]{1,0:T(8,128)(2,1)S(1)} %add_convert_fusion.4), channel_id=1, source_target_pairs={{0,8},{8,16},{16,24},{24,0},{1,9},{9,17},{17,25},{25,1},{2,10},{10... | collective-permute-start | bytes 1572872 | tf_op jit(solution)/shard_map/ppermute | solution.py:1075
  505.7 15.7 %collective-permute-start.55 = (bf16[128,2048]{1,0:T(8,128)(2,1)S(1)}, bf16[128,2048]{1,0:T(8,128)(2,1)S(1)}, u32[]{:S(2)}, u32[]{:S(2)}) collective-permute-start(bf16[128,2048]{1,0:T(8,128)(2,1)S(1)} %copy-done.61), channel_id=1, source_target_pairs={{0,4},{4,0},{1,5},{5,1},{2,6},{6,2},{3,7},{7,3},{8,12},{12,8},{9,1... | collective-permute-start | bytes 1572872 | tf_op jit(solution)/shard_map/ppermute | solution.py:1070
  506.6 23.5 %collective-permute-start.56 = (bf16[256,2048]{1,0:T(8,128)(2,1)}, bf16[256,2048]{1,0:T(8,128)(2,1)}, u32[]{:S(2)}, u32[]{:S(2)}) collective-permute-start(bf16[256,2048]{1,0:T(8,128)(2,1)} %fusion.8), channel_id=1, source_target_pairs={{0,2},{2,0},{1,3},{3,1},{4,6},{6,4},{5,7},{7,5},{8,10},{10,8},{9,1... | collective-permute-start | bytes 3145736 | tf_op jit(solution)/shard_map/ppermute | solution.py:1070
  (86 other events, 1026.1 us)
Sparse Core Ops, SparseCore 0:
  9.6 37.1 all-gather.4
  49.9 104.2 all-gather.6
  156.3 68.5 all-gather.8
  339.0 26.8 all-gather.10
  374.3 70.8 reduce-scatter.1

commit v6 on v5

--- a/solution.py
+++ b/solution.py
@@ -1349,10 +1349,8 @@
     br_flow = Flow(collect(br_by, br_marks, early=True, open_end=True))
     down_terms = outer(tiles, *after((lefts[0], dy_rows), dattn))
     gate_flow.pending = after(gate_flow.pending, dattn)
-    attn_side = side_flow.result.transpose(2, 3, 0, 1, 4).reshape(far, HD, blk)
-    out_term = jnp.einsum(
-        "gft,td->gfd", after(attn_side, dattn), dmid_near, preferred_element_type=F32
-    )
+    attn_side = after(side_flow.result, dattn).transpose(2, 3, 0, 1, 4).reshape(far, HD, blk)
+    out_term = jnp.einsum("gft,td->gfd", attn_side, dmid_near, preferred_element_type=F32)
     dattn_head, down_terms, out_term, up_got = stage(
         [gate_flow, br_flow],
         (
@@ -1407,7 +1405,7 @@
     up_terms = up_keep, up_got, [up_first, up_second]
     gate_terms, up_terms, branch = after((gate_terms, up_terms, branch), marks[-1])
     gate_grad, up_grad = add_terms(*gate_terms), add_terms(*up_terms)
-    back, down_across = stage([dx_flow], (back, swap(down_give, "col")))
+    down_across = stage([dx_flow], swap(down_give, "col"))
     down_grad = add_terms(down_keep, down_got, [down_across])
     scaled_one = dx_flow.result
     input_grad = (
@@ -1415,6 +1413,7 @@
         + scale_one * scaled_one
         - x32 * scale_one**3 * jnp.mean(scaled_one * x32, axis=-1, keepdims=True)
     )
+    back, input_grad, down_grad = lax.optimization_barrier((back, input_grad, down_grad))
     back = back.astype(F32)
     raw = [
         back[:, :, i * group : (i + 1) * group].transpose(1, 0, 2).reshape(own_in, -1)

time: 555 us -> 549 us (0.989)
  no operation moved by 1% of the time
where the time goes in v6:
time: 549 us; the launch traced here: 542 us
  waiting for transfers between devices  200 us (36%)
  Pallas kernels  168 us (31%)
  starting transfers between devices  80.4 us (15%)
  other arithmetic  53 us (10%)
  local copies, waits for them, and re-layouts  16.9 us (3%)
  between operations  15 us (3%)
  matrix products  8.91 us (2%)
    ppermute x39, waiting for transfers between devices, swap(): return lax.ppermute(v, axis, [(0, 1), (1, 0)])  138 us
    pallas_call x4, Pallas kernels, ffn(): pl.pallas_call(functools.partial(ffn_kernel, count=count, step=step), in_...  49.7 us
    ppermute x18, waiting for transfers between devices, shift(): return lax.ppermute(v, 'ctx', [(i, (i + 1) % n) for i in range(n)])  46.5 us
    ppermute x39, starting transfers between devices, swap(): return lax.ppermute(v, axis, [(0, 1), (1, 0)])  38.5 us
    pallas_call x3, Pallas kernels, outer(): pl.pallas_call(functools.partial(outer_kernel, lefts=len(left), rights=le...  32.2 us
    pallas_call x1, Pallas kernels, attn_bwd(): pl.pallas_call(functools.partial(attn_bwd_kernel, blocks=blocks, width=wi...  31.9 us
    pallas_call x1, Pallas kernels, attn_fwd(): pl.pallas_call(functools.partial(attn_fwd_kernel, blocks=blocks, width=co...  19.1 us
    ppermute x18, starting transfers between devices, shift(): return lax.ppermute(v, 'ctx', [(i, (i + 1) % n) for i in range(n)])  14.4 us
  transfers between devices with their start and end apart: 68, of which 37 were waited for; matrix products, arithmetic and copies ran while one was open for 11% of the time, Pallas kernels for 29%

profile of v6, /device:TPU:0, one launch (start us, length us, event | category | flops | bytes accessed | tf_op | source)
XLA Modules:
  0.0 542.0 jit_solution(13560698653009278695)
XLA Ops:
  10.9 7.4 %all-to-all-start = ((bf16[8,64,768]{2,1,0:T(8,128)(2,1)}), bf16[8,64,768]{2,1,0:T(8,128)(2,1)S(1)}, u32[]{:S(2)}, u32[]{:S(2)}) async-start(bf16[8,64,768]{2,1,0:T(8,128)(2,1)} %maximum_bitcast_fusion), calls=%async_computation | async-start | bytes 1572864 | tf_op jit(solution)/shard_map/all_to_all | solution.py:1198
  22.8 17.5 %collective-permute-done.1.refs_4_ = bf16[128,2048]{1,0:T(8,128)(2,1)S(1)} collective-permute-done((bf16[128,2048]{1,0:T(8,128)(2,1)S(1)}, bf16[128,2048]{1,0:T(8,128)(2,1)S(1)}, u32[]{:S(2)}, u32[]{:S(2)}) %collective-permute-start.1) | collective-permute-done | bytes 524320 | tf_op jit(solution)/shard_map/ppermute | solution.py:1070
  41.2 5.4 collective-permute-done.refs_1_
  46.6 3.2 all-to-all-done.refs_8_
  54.4 10.6 %collective-permute-done.4 = bf16[4,64,768]{2,1,0:T(8,128)(2,1)S(1)} collective-permute-done((bf16[4,64,768]{2,1,0:T(8,128)(2,1)S(1)}, bf16[4,64,768]{2,1,0:T(8,128)(2,1)S(1)}, u32[]{:S(2)}, u32[]{:S(2)}) %collective-permute-start.4) | collective-permute-done | bytes 393248 | tf_op jit(solution)/shard_map/ppermute | solution.py:1070
  65.0 4.2 collective-permute-done.2.refs_2_
  69.3 3.2 collective-permute-start.8
  73.2 5.0 collective-permute-done.8
  78.6 4.6 collective-permute-done.6.refs_3_
  86.8 15.6 %collective-permute-done.12.refs_7_ = bf16[128,2048]{1,0:T(8,128)(2,1)} collective-permute-done((bf16[128,2048]{1,0:T(8,128)(2,1)}, bf16[128,2048]{1,0:T(8,128)(2,1)}, u32[]{:S(2)}, u32[]{:S(2)}) %collective-permute-start.12) | collective-permute-done | bytes 524320 | tf_op jit(solution)/shard_map/ppermute | solution.py:1070
  102.6 9.3 %qkv.1 = (bf16[4,192,1024]{2,1,0:T(8,128)(2,1)}, bf16[1024,2048]{1,0:T(8,128)(2,1)}, bf16[2048,768]{1,0:T(8,128)(2,1)}) custom-call(s32[1]{0:T(128)} %bitcast.2.near_ref, bf16[128,2048]{1,0:T(8,128)(2,1)} %copy-done.34, bf16[128,2048]{1,0:T(8,128)(2,1)} %collective-permute-done.refs_1_, bf16[128,2048]{1,0:T(8,128)(2,1)} %copy-done.63, ...), custom_call_target="tpu_custom_call" | custom-call | flops 3221225472 | bytes 14680064 | tf_op jit(solution)/shard_map/qkv/pallas_call | solution.py:871
  112.0 3.6 all-to-all-start.1
  118.1 5.5 %collective-permute-done.9.refs_2_.refs_7_ = bf16[128,2048]{1,0:T(8,128)(2,1)S(1)} collective-permute-done((bf16[128,2048]{1,0:T(8,128)(2,1)S(1)}, bf16[128,2048]{1,0:T(8,128)(2,1)S(1)}, u32[]{:S(2)}, u32[]{:S(2)}) %collective-permute-start.9) | collective-permute-done | bytes 524320 | tf_op jit(solution)/shard_map/ppermute | solution.py:1075
  123.6 2.8 multiply_sine_fusion
  127.6 10.5 %collective-permute-done.11.refs_3_.refs_6_ = bf16[128,2048]{1,0:T(8,128)(2,1)S(1)} collective-permute-done((bf16[128,2048]{1,0:T(8,128)(2,1)S(1)}, bf16[128,2048]{1,0:T(8,128)(2,1)S(1)}, u32[]{:S(2)}, u32[]{:S(2)}) %collective-permute-start.11) | collective-permute-done | bytes 524320 | tf_op jit(solution)/shard_map/ppermute | solution.py:1070
  139.0 11.2 %collective-permute-done.10.refs_2_.refs_9_ = bf16[128,2048]{1,0:T(8,128)(2,1)} collective-permute-done((bf16[128,2048]{1,0:T(8,128)(2,1)S(1)}, bf16[128,2048]{1,0:T(8,128)(2,1)}, u32[]{:S(2)}, u32[]{:S(2)}) %collective-permute-start.10) | collective-permute-done | bytes 524320 | tf_op jit(solution)/shard_map/ppermute | solution.py:1075
  151.9 19.1 %attn_fwd.1 = (bf16[32,80,128]{2,1,0:T(8,128)(2,1)}, f32[64,4096]{1,0:T(8,128)}, f32[1,4096]{1,0:T(1,128)}, bf16[192,4096]{1,0:T(8,128)(2,1)}) custom-call(s32[2,8]{1,0:T(2,128)} %pad_add_fusion.place_ref, bf16[4,192,1024]{2,1,0:T(8,128)(2,1)} %copy-done.13, bf16[16,128]{1,0:T(8,128)(2,1)} %pad.4.extra_ref), custom_call_target="tpu_custom_call" | custom-call | flops 8589934592 | bytes 8388608 | tf_op jit(solution)/shard_map/attn_fwd/pallas_call | solution.py:464
  171.1 5.3 all-to-all-start.2
  178.2 19.2 %collective-permute-done.17.refs_3_.refs_12_ = bf16[128,2048]{1,0:T(8,128)(2,1)S(1)} collective-permute-done((bf16[128,2048]{1,0:T(8,128)(2,1)S(1)}, bf16[128,2048]{1,0:T(8,128)(2,1)S(1)}, u32[]{:S(2)}, u32[]{:S(2)}) %collective-permute-start.17) | collective-permute-done | bytes 524320 | tf_op jit(solution)/shard_map/ppermute | solution.py:1070
  198.5 4.7 multiply_reduce_fusion
  208.2 9.5 %collective-permute-done.19.refs_1_.refs_6_ = bf16[128,2048]{1,0:T(8,128)(2,1)} collective-permute-done((bf16[128,2048]{1,0:T(8,128)(2,1)S(1)}, bf16[128,2048]{1,0:T(8,128)(2,1)}, u32[]{:S(2)}, u32[]{:S(2)}) %collective-permute-start.19) | collective-permute-done | bytes 524320 | tf_op jit(solution)/shard_map/ppermute | solution.py:1070
  221.3 3.7 all-gather.9.cloned.1.call-done.refs_5_
  225.0 12.4 %ffn.4 = (bf16[128,2048]{1,0:T(8,128)(2,1)}, bf16[128,2048]{1,0:T(8,128)(2,1)}, bf16[128,2048]{1,0:T(8,128)(2,1)}, bf16[128,2048]{1,0:T(8,128)(2,1)}, bf16[256,1...) custom-call(bf16[128,2048]{1,0:T(8,128)(2,1)} %copy-done.33, ...), custom_call_target="tpu_custom_call" | custom-call | flops 6442450944 | bytes 20971520 | tf_op jit(solution)/shard_map/ffn/pallas_call | solution.py:734
  240.6 12.4 %ffn.5 = (bf16[128,2048]{1,0:T(8,128)(2,1)}, bf16[128,2048]{1,0:T(8,128)(2,1)}, bf16[128,2048]{1,0:T(8,128)(2,1)}, bf16[128,2048]{1,0:T(8,128)(2,1)}, bf16[256,1...) custom-call(bf16[128,2048]{1,0:T(8,128)(2,1)} %collective-permute-done.18.refs_0_.refs_7_, ...), custom_call_target="tpu_custom_call" | custom-call | flops 6442450944 | bytes 20971520 | tf_op jit(solution)/shard_map/ffn/pallas_call | solution.py:734
  257.0 12.5 %ffn.6 = (bf16[128,2048]{1,0:T(8,128)(2,1)}, bf16[128,2048]{1,0:T(8,128)(2,1)}, bf16[128,2048]{1,0:T(8,128)(2,1)}, bf16[128,2048]{1,0:T(8,128)(2,1)}, bf16[256,1...) custom-call(bf16[128,2048]{1,0:T(8,128)(2,1)} %collective-permute-done.20.refs_0_.refs_9_, ...), custom_call_target="tpu_custom_call" | custom-call | flops 6442450944 | bytes 20971520 | tf_op jit(solution)/shard_map/ffn/pallas_call | solution.py:734
  270.0 9.4 %collective-permute-done.24.refs_1_.refs_12_ = bf16[128,2048]{1,0:T(8,128)(2,1)} collective-permute-done((bf16[128,2048]{1,0:T(8,128)(2,1)S(1)}, bf16[128,2048]{1,0:T(8,128)(2,1)}, u32[]{:S(2)}, u32[]{:S(2)}) %collective-permute-start.24) | collective-permute-done | bytes 524320 | tf_op jit(solution)/shard_map/ppermute | solution.py:1070
  281.3 12.4 %ffn.7 = (bf16[128,2048]{1,0:T(8,128)(2,1)}, bf16[128,2048]{1,0:T(8,128)(2,1)}, bf16[128,2048]{1,0:T(8,128)(2,1)}, bf16[128,2048]{1,0:T(8,128)(2,1)}, bf16[256,1...) custom-call(bf16[128,2048]{1,0:T(8,128)(2,1)} %copy-done.60, ...), custom_call_target="tpu_custom_call" | custom-call | flops 6442450944 | bytes 20971520 | tf_op jit(solution)/shard_map/ffn/pallas_call | solution.py:734
  299.0 10.8 %outer.3 = (bf16[2,256,2048]{2,1,0:T(8,128)(2,1)}, bf16[2,256,2048]{2,1,0:T(8,128)(2,1)}) custom-call(s32[4]{0:T(128)} %broadcast_xor_fusion.refs_0_, bf16[256,1024]{1,0:T(8,128)(2,1)} %get-tuple-element.371.refs_1_, bf16[256,1024]{1,0:T(8,128)(2,1)} %get-tuple-element.372.refs_2_, bf16[256,1024]{1,0:T(8,128)(2,1)} %get-tuple-element.373.refs_3_, ...), custom_call_target="tpu_custom_call" | custom-call | flops 4294967296 | bytes 10485760 | tf_op jit(solution)/shard_map/outer/pallas_call | solution.py:801
  315.5 10.7 %outer.4 = (bf16[2,256,2048]{2,1,0:T(8,128)(2,1)}, bf16[2,256,2048]{2,1,0:T(8,128)(2,1)}) custom-call(s32[4]{0:T(128)} %broadcast_xor_fusion.refs_0_, bf16[256,1024]{1,0:T(8,128)(2,1)} %get-tuple-element.394.refs_1_, bf16[256,1024]{1,0:T(8,128)(2,1)} %get-tuple-element.395.refs_2_, bf16[256,1024]{1,0:T(8,128)(2,1)} %get-tuple-element.396.refs_3_, ...), custom_call_target="tpu_custom_call" | custom-call | flops 4294967296 | bytes 10485760 | tf_op jit(solution)/shard_map/outer/pallas_call | solution.py:801
  329.6 9.3 %mid_grad.1 = (f32[128,2048]{1,0:T(8,128)}, bf16[128,2048]{1,0:T(8,128)(2,1)}, bf16[32,80,128]{2,1,0:T(8,128)(2,1)}) custom-call(bf16[128,2048]{1,0:T(8,128)(2,1)} %get-tuple-element.419.own_ref, bf16[128,2048]{1,0:T(8,128)(2,1)} %copy-done.31, bf16[128,2048]{1,0:T(8,128)(2,1)} %copy-done.30, f32[128,2048]{1,0:T(8,128)} %copy-done, bf16[128,2048]{1,0:T(8,128)(2,1)} %refs_5_, ...), custom_call_target="tpu_custom_call" | custom-call | flops 1073741824 | bytes 8388608 | tf_op jit(solution)/shard_map/mid_grad/pallas_call | solution.py:1047
  339.1 2.6 all-to-all-start.3
  343.6 3.1 fusion.7
  346.7 10.7 %outer.5 = (bf16[2,256,2048]{2,1,0:T(8,128)(2,1)}, bf16[2,256,2048]{2,1,0:T(8,128)(2,1)}) custom-call(s32[4]{0:T(128)} %broadcast_xor_fusion.refs_0_, bf16[256,1024]{1,0:T(8,128)(2,1)} %get-tuple-element.429.refs_1_, bf16[256,1024]{1,0:T(8,128)(2,1)} %get-tuple-element.430.refs_2_, bf16[256,1024]{1,0:T(8,128)(2,1)} %get-tuple-element.431.refs_3_, ...), custom_call_target="tpu_custom_call" | custom-call | flops 4294967296 | bytes 10485760 | tf_op jit(solution)/shard_map/outer/pallas_call | solution.py:801
  358.2 6.2 %all-gather.11.cloned.1.call-done = bf16[512,2048]{1,0:T(8,128)(2,1)} async-done(((bf16[128,2048]{1,0:T(8,128)(2,1)}), bf16[512,2048]{1,0:T(8,128)(2,1)}) %all-gather.11.cloned.1.call-update) | async-done | bytes 2097168 | tf_op jit(solution)/shard_map/all_gather | solution.py:1347
  364.4 4.2 convolution_convert_fusion
  376.0 31.9 %attn_bwd.1 = bf16[4,192,1024]{2,1,0:T(8,128)(2,1)} custom-call(s32[2,8]{1,0:T(2,128)} %pad_add_fusion.place_ref, bf16[192,4096]{1,0:T(8,128)(2,1)} %get-tuple-element.454.seq_hbm, f32[64,4096]{1,0:T(8,128)} %get-tuple-element.455.o32_hbm, f32[1,4096]{1,0:T(1,128)} %get-tuple-element.456.lse_ref, bf16[32,80,128]{2,1,0:T(8,128)(2,1)} %copy-done.24, ...), custom_call_target="tpu_custom_call" | custom-call | flops 21474836480 | bytes 8388608 | tf_op jit(solution)/shard_map/attn_bwd/pallas_call | solution.py:598
  410.0 3.6 all-to-all-start.4
  423.2 8.8 %collective-permute-done.43 = bf16[128,2048]{1,0:T(8,128)(2,1)S(1)} collective-permute-done((bf16[128,2048]{1,0:T(8,128)(2,1)}, bf16[128,2048]{1,0:T(8,128)(2,1)S(1)}, u32[]{:S(2)}, u32[]{:S(2)}) %collective-permute-start.43) | collective-permute-done | bytes 524320 | tf_op jit(solution)/shard_map/ppermute | solution.py:1070
  434.8 4.0 input_rows.1
  443.7 12.6 %heads_back.1 = (bf16[2,8,64,768]{3,2,1,0:T(8,128)(2,1)}, bf16[2,8,64,768]{3,2,1,0:T(8,128)(2,1)}, bf16[128,2048]{1,0:T(8,128)(2,1)}, bf16[128,2048]{1,0:T(8,128...) custom-call(s32[1]{0:T(128)} %bitcast.2.near_ref, ...), custom_call_target="tpu_custom_call" | custom-call | flops 6442450944 | bytes 16252928 | tf_op jit(solution)/shard_map/heads_back/pallas_call | solution.py:984
  457.0 3.6 collective-permute-done.49
  467.8 12.0 %collective-permute-done.48 = bf16[128,2048]{1,0:T(8,128)(2,1)S(1)} collective-permute-done((bf16[128,2048]{1,0:T(8,128)(2,1)}, bf16[128,2048]{1,0:T(8,128)(2,1)S(1)}, u32[]{:S(2)}, u32[]{:S(2)}) %collective-permute-start.48) | collective-permute-done | bytes 524320 | tf_op jit(solution)/shard_map/ppermute | solution.py:1070
  491.7 4.8 all-to-all-start.5
  498.4 2.8 collective-permute-done.52
  507.6 3.4 bitcast_add_fusion.1
  511.0 3.4 bitcast_add_fusion
  515.5 5.0 collective-permute-done.55
  520.5 4.5 collective-permute-done.54
  (312 shorter events, 128.7 us)
Async XLA Ops:
  7.2 142.9 %all-gather.5.cloned.1.call-start = ((), (), s32[]{:S(2)}) async-start(), calls=%async_computation.7 | async-start | bytes 5242880 | tf_op jit(solution)/shard_map/all_gather | solution.py:1263
  10.9 38.8 %all-to-all-start = ((bf16[8,64,768]{2,1,0:T(8,128)(2,1)}), bf16[8,64,768]{2,1,0:T(8,128)(2,1)S(1)}, u32[]{:S(2)}, u32[]{:S(2)}) async-start(bf16[8,64,768]{2,1,0:T(8,128)(2,1)} %maximum_bitcast_fusion), calls=%async_computation | async-start | bytes 1572864 | tf_op jit(solution)/shard_map/all_to_all | solution.py:1198
  18.4 152.7 %all-gather.7.cloned.1.call-start = ((), (), s32[]{:S(2)}) async-start(), calls=%async_computation.8 | async-start | bytes 8650752 | tf_op jit(solution)/shard_map/all_gather | solution.py:1268
  19.3 21.0 %collective-permute-start.1 = (bf16[128,2048]{1,0:T(8,128)(2,1)S(1)}, bf16[128,2048]{1,0:T(8,128)(2,1)S(1)}, u32[]{:S(2)}, u32[]{:S(2)}) collective-permute-start(bf16[128,2048]{1,0:T(8,128)(2,1)S(1)} %fusion.3.refs_0_), channel_id=1, source_target_pairs={{0,4},{4,0},{1,5},{5,1},{2,6},{6,2},{3,7},{7,3},{8,12},{12,8},{9,1... | collective-permute-start | bytes 1572872 | tf_op jit(solution)/shard_map/ppermute | solution.py:1070
  21.4 25.2 %collective-permute-start = (bf16[128,2048]{1,0:T(8,128)(2,1)S(1)}, bf16[128,2048]{1,0:T(8,128)(2,1)}, u32[]{:S(2)}, u32[]{:S(2)}) collective-permute-start(bf16[128,2048]{1,0:T(8,128)(2,1)S(1)} %fusion.3.refs_0_), channel_id=1, source_target_pairs={{0,8},{8,16},{16,24},{24,0},{1,9},{9,17},{17,25},{25,1},{2,10},{10... | collective-permute-start | bytes 1572872 | tf_op jit(solution)/shard_map/ppermute | solution.py:1075
  49.8 175.2 %all-gather.9.cloned.1.call-start = ((), (), s32[]{:S(2)}) async-start(), calls=%async_computation.9 | async-start | bytes 10485760 | tf_op jit(solution)/shard_map/all_gather | solution.py:1276
  51.4 17.7 %collective-permute-start.2 = (bf16[128,2048]{1,0:T(8,128)(2,1)}, bf16[128,2048]{1,0:T(8,128)(2,1)S(1)}, u32[]{:S(2)}, u32[]{:S(2)}) collective-permute-start(bf16[128,2048]{1,0:T(8,128)(2,1)} %collective-permute-done.refs_1_), channel_id=1, source_target_pairs={{0,8},{8,16},{16,24},{24,0},{1,9},{9,17},{17,25},{25,1},{2,10},{10... | collective-permute-start | bytes 1572872 | tf_op jit(solution)/shard_map/ppermute | solution.py:1075
  51.4 17.7 %collective-permute-start.5 = (bf16[8,64,768]{2,1,0:T(8,128)(2,1)S(1)}, bf16[8,64,768]{2,1,0:T(8,128)(2,1)S(1)}, u32[]{:S(2)}, u32[]{:S(2)}) collective-permute-start(bf16[8,64,768]{2,1,0:T(8,128)(2,1)S(1)} %all-to-all-done.refs_8_), channel_id=1, source_target_pairs={{0,1},{1,0},{2,3},{3,2},{4,5},{5,4},{6,7},{7,6},{8,9},{9,8},{10,11... | collective-permute-start | bytes 2359304 | tf_op jit(solution)/shard_map/ppermute | solution.py:1070
  83.9 18.5 %collective-permute-start.13 = (bf16[8,64,768]{2,1,0:T(8,128)(2,1)}, bf16[8,64,768]{2,1,0:T(8,128)(2,1)}, u32[]{:S(2)}, u32[]{:S(2)}) collective-permute-start(bf16[8,64,768]{2,1,0:T(8,128)(2,1)} %constant_dynamic-update-slice_fusion.refs_10_), channel_id=1, source_target_pairs={{0,1},{1,0},{2,3},{3,2},{4,5},{5,4},{6,7},{7,6},{8,9},{9,8},{10,11... | collective-permute-start | bytes 2359304 | tf_op jit(solution)/shard_map/ppermute | solution.py:1070
  84.0 18.5 %collective-permute-start.12 = (bf16[128,2048]{1,0:T(8,128)(2,1)}, bf16[128,2048]{1,0:T(8,128)(2,1)}, u32[]{:S(2)}, u32[]{:S(2)}) collective-permute-start(bf16[128,2048]{1,0:T(8,128)(2,1)} %collective-permute-done.6.refs_3_), channel_id=1, source_target_pairs={{0,4},{4,0},{1,5},{5,1},{2,6},{6,2},{3,7},{7,3},{8,12},{12,8},{9,1... | collective-permute-start | bytes 1572872 | tf_op jit(solution)/shard_map/ppermute | solution.py:1070
  102.6 21.0 %collective-permute-start.9 = (bf16[128,2048]{1,0:T(8,128)(2,1)S(1)}, bf16[128,2048]{1,0:T(8,128)(2,1)S(1)}, u32[]{:S(2)}, u32[]{:S(2)}) collective-permute-start(bf16[128,2048]{1,0:T(8,128)(2,1)S(1)} %copy-done.25), channel_id=1, source_target_pairs={{0,8},{8,16},{16,24},{24,0},{1,9},{9,17},{17,25},{25,1},{2,10},{10... | collective-permute-start | bytes 1572872 | tf_op jit(solution)/shard_map/ppermute | solution.py:1075
  112.0 38.1 %all-to-all-start.1 = ((bf16[4,192,1024]{2,1,0:T(8,128)(2,1)}), bf16[4,192,1024]{2,1,0:T(8,128)(2,1)S(1)}, u32[]{:S(2)}, u32[]{:S(2)}) async-start(bf16[4,192,1024]{2,1,0:T(8,128)(2,1)} %get-tuple-element.294), calls=%async_computation.1 | async-start | bytes 3145728 | tf_op jit(solution)/shard_map/all_to_all | solution.py:1288
  116.8 21.3 %collective-permute-start.11 = (bf16[128,2048]{1,0:T(8,128)(2,1)S(1)}, bf16[128,2048]{1,0:T(8,128)(2,1)S(1)}, u32[]{:S(2)}, u32[]{:S(2)}) collective-permute-start(bf16[128,2048]{1,0:T(8,128)(2,1)S(1)} %copy-done.25), channel_id=1, source_target_pairs={{0,4},{4,0},{1,5},{5,1},{2,6},{6,2},{3,7},{7,3},{8,12},{12,8},{9,1... | collective-permute-start | bytes 1572872 | tf_op jit(solution)/shard_map/ppermute | solution.py:1070
  123.6 26.5 %collective-permute-start.10 = (bf16[128,2048]{1,0:T(8,128)(2,1)S(1)}, bf16[128,2048]{1,0:T(8,128)(2,1)}, u32[]{:S(2)}, u32[]{:S(2)}) collective-permute-start(bf16[128,2048]{1,0:T(8,128)(2,1)S(1)} %collective-permute-done.9.refs_2_.refs_7_), channel_id=1, source_target_pairs={{0,8},{8,16},{16,24},{24,0},{1,9},{9,17},{17,25},{25,1},{2,10},{10... | collective-permute-start | bytes 1572872 | tf_op jit(solution)/shard_map/ppermute | solution.py:1075
  126.4 44.6 %collective-permute-start.15 = (bf16[128,2048]{1,0:T(8,128)(2,1)S(1)}, bf16[128,2048]{1,0:T(8,128)(2,1)}, u32[]{:S(2)}, u32[]{:S(2)}) collective-permute-start(bf16[128,2048]{1,0:T(8,128)(2,1)S(1)} %collective-permute-done.9.refs_2_.refs_7_), channel_id=1, source_target_pairs={{0,4},{4,0},{1,5},{5,1},{2,6},{6,2},{3,7},{7,3},{8,12},{12,8},{9,1... | collective-permute-start | bytes 1572872 | tf_op jit(solution)/shard_map/ppermute | solution.py:1070
  150.1 20.9 %collective-permute-start.16 = (bf16[128,2048]{1,0:T(8,128)(2,1)}, bf16[128,2048]{1,0:T(8,128)(2,1)}, u32[]{:S(2)}, u32[]{:S(2)}) collective-permute-start(bf16[128,2048]{1,0:T(8,128)(2,1)} %collective-permute-done.10.refs_2_.refs_9_), channel_id=1, source_target_pairs={{0,4},{4,0},{1,5},{5,1},{2,6},{6,2},{3,7},{7,3},{8,12},{12,8},{9,1... | collective-permute-start | bytes 1572872 | tf_op jit(solution)/shard_map/ppermute | solution.py:1070
  151.6 19.4 %collective-permute-start.14 = (bf16[128,2048]{1,0:T(8,128)(2,1)}, bf16[128,2048]{1,0:T(8,128)(2,1)S(1)}, u32[]{:S(2)}, u32[]{:S(2)}) collective-permute-start(bf16[128,2048]{1,0:T(8,128)(2,1)} %collective-permute-done.10.refs_2_.refs_9_), channel_id=1, source_target_pairs={{0,8},{8,16},{16,24},{24,0},{1,9},{9,17},{17,25},{25,1},{2,10},{10... | collective-permute-start | bytes 1572872 | tf_op jit(solution)/shard_map/ppermute | solution.py:1075
  171.1 27.2 %all-to-all-start.2 = ((bf16[32,80,128]{2,1,0:T(8,128)(2,1)}), bf16[32,80,128]{2,1,0:T(8,128)(2,1)S(1)}, u32[]{:S(2)}, u32[]{:S(2)}) async-start(bf16[32,80,128]{2,1,0:T(8,128)(2,1)} %get-tuple-element.303), calls=%async_computation.2 | async-start | bytes 1310720 | tf_op jit(solution)/shard_map/all_to_all | solution.py:1298
  176.4 188.0 %all-gather.11.cloned.1.call-start = ((), (), s32[]{:S(2)}) async-start(), calls=%async_computation.10 | async-start | bytes 2621440 | tf_op jit(solution)/shard_map/all_gather | solution.py:1347
  176.4 21.1 %collective-permute-start.17 = (bf16[128,2048]{1,0:T(8,128)(2,1)S(1)}, bf16[128,2048]{1,0:T(8,128)(2,1)S(1)}, u32[]{:S(2)}, u32[]{:S(2)}) collective-permute-start(bf16[128,2048]{1,0:T(8,128)(2,1)S(1)} %collective-permute-done.14.refs_2_.refs_11_), channel_id=1, source_target_pairs={{0,4},{4,0},{1,5},{5,1},{2,6},{6,2},{3,7},{7,3},{8,12},{12,8},{9,1... | collective-permute-start | bytes 1572872 | tf_op jit(solution)/shard_map/ppermute | solution.py:1070
  206.9 62.6 %collective-permute-start.26 = (bf16[2,8,64,128]{3,2,0,1:T(8,128)(2,1)}, bf16[2,8,64,128]{3,2,0,1:T(8,128)(2,1)S(1)}, u32[]{:S(2)}, u32[]{:S(2)}) collective-permute-start(bf16[2,8,64,128]{3,2,0,1:T(8,128)(2,1)} %fusion.22), channel_id=1, source_target_pairs={{0,2},{2,0},{1,3},{3,1},{4,6},{6,4},{5,7},{7,5},{8,10},{10,8},{9,1... | collective-permute-start | bytes 786440 | tf_op jit(solution)/shard_map/ppermute | solution.py:1070
  220.3 17.2 %collective-permute-start.21 = (bf16[128,2048]{1,0:T(8,128)(2,1)}, bf16[128,2048]{1,0:T(8,128)(2,1)}, u32[]{:S(2)}, u32[]{:S(2)}) collective-permute-start(bf16[128,2048]{1,0:T(8,128)(2,1)} %collective-permute-done.18.refs_0_.refs_7_), channel_id=1, source_target_pairs={{0,4},{4,0},{1,5},{5,1},{2,6},{6,2},{3,7},{7,3},{8,12},{12,8},{9,1... | collective-permute-start | bytes 1572872 | tf_op jit(solution)/shard_map/ppermute | solution.py:1070
  221.2 16.2 %collective-permute-start.20 = (bf16[128,2048]{1,0:T(8,128)(2,1)}, bf16[128,2048]{1,0:T(8,128)(2,1)}, u32[]{:S(2)}, u32[]{:S(2)}) collective-permute-start(bf16[128,2048]{1,0:T(8,128)(2,1)} %collective-permute-done.18.refs_0_.refs_7_), channel_id=1, source_target_pairs={{0,8},{8,16},{16,24},{24,0},{1,9},{9,17},{17,25},{25,1},{2,10},{10... | collective-permute-start | bytes 1572872 | tf_op jit(solution)/shard_map/ppermute | solution.py:1075
  239.0 16.0 %collective-permute-start.22 = (bf16[128,2048]{1,0:T(8,128)(2,1)}, bf16[128,2048]{1,0:T(8,128)(2,1)S(1)}, u32[]{:S(2)}, u32[]{:S(2)}) collective-permute-start(bf16[128,2048]{1,0:T(8,128)(2,1)} %collective-permute-done.20.refs_0_.refs_9_), channel_id=1, source_target_pairs={{0,8},{8,16},{16,24},{24,0},{1,9},{9,17},{17,25},{25,1},{2,10},{10... | collective-permute-start | bytes 1572872 | tf_op jit(solution)/shard_map/ppermute | solution.py:1075
  255.5 23.9 %collective-permute-start.24 = (bf16[128,2048]{1,0:T(8,128)(2,1)S(1)}, bf16[128,2048]{1,0:T(8,128)(2,1)}, u32[]{:S(2)}, u32[]{:S(2)}) collective-permute-start(bf16[128,2048]{1,0:T(8,128)(2,1)S(1)} %collective-permute-done.22.refs_0_.refs_11_), channel_id=1, source_target_pairs={{0,4},{4,0},{1,5},{5,1},{2,6},{6,2},{3,7},{7,3},{8,12},{12,8},{9,1... | collective-permute-start | bytes 1572872 | tf_op jit(solution)/shard_map/ppermute | solution.py:1070
  279.7 15.6 %collective-permute-start.27 = (bf16[128,2048]{1,0:T(8,128)(2,1)S(1)}, bf16[128,2048]{1,0:T(8,128)(2,1)S(1)}, u32[]{:S(2)}, u32[]{:S(2)}) collective-permute-start(bf16[128,2048]{1,0:T(8,128)(2,1)S(1)} %add_convert_fusion.14), channel_id=1, source_target_pairs={{0,8},{8,16},{16,24},{24,0},{1,9},{9,17},{17,25},{25,1},{2,10},{10... | collective-permute-start | bytes 1572872 | tf_op jit(solution)/shard_map/ppermute | solution.py:1075
  296.3 15.6 %collective-permute-start.30 = (bf16[128,2048]{1,0:T(8,128)(2,1)}, bf16[128,2048]{1,0:T(8,128)(2,1)S(1)}, u32[]{:S(2)}, u32[]{:S(2)}) collective-permute-start(bf16[128,2048]{1,0:T(8,128)(2,1)} %add_convert_fusion.13), channel_id=1, source_target_pairs={{0,8},{8,16},{16,24},{24,0},{1,9},{9,17},{17,25},{25,1},{2,10},{10... | collective-permute-start | bytes 1572872 | tf_op jit(solution)/shard_map/ppermute | solution.py:1075
  311.9 16.8 %collective-permute-start.34 = (bf16[2,256,2048]{2,1,0:T(8,128)(2,1)}, bf16[2,256,2048]{2,1,0:T(8,128)(2,1)}, u32[]{:S(2)}, u32[]{:S(2)}) collective-permute-start(bf16[2,256,2048]{2,1,0:T(8,128)(2,1)} %get-tuple-element.389), channel_id=1, source_target_pairs={{0,1},{1,0},{2,3},{3,2},{4,5},{5,4},{6,7},{7,6},{8,9},{9,8},{10,11... | collective-permute-start | bytes 6291464 | tf_op jit(solution)/shard_map/ppermute | solution.py:1070
  312.2 16.6 %collective-permute-start.32 = (bf16[128,2048]{1,0:T(8,128)(2,1)S(1)}, bf16[128,2048]{1,0:T(8,128)(2,1)S(1)}, u32[]{:S(2)}, u32[]{:S(2)}) collective-permute-start(bf16[128,2048]{1,0:T(8,128)(2,1)S(1)} %add_convert_fusion.12), channel_id=1, source_target_pairs={{0,8},{8,16},{16,24},{24,0},{1,9},{9,17},{17,25},{25,1},{2,10},{10... | collective-permute-start | bytes 1572872 | tf_op jit(solution)/shard_map/ppermute | solution.py:1075
  338.9 29.7 %collective-permute-start.36 = (bf16[2,256,2048]{2,1,0:T(8,128)(2,1)}, bf16[2,256,2048]{2,1,0:T(8,128)(2,1)}, u32[]{:S(2)}, u32[]{:S(2)}) collective-permute-start(bf16[2,256,2048]{2,1,0:T(8,128)(2,1)} %get-tuple-element.446), channel_id=1, source_target_pairs={{0,1},{1,0},{2,3},{3,2},{4,5},{5,4},{6,7},{7,6},{8,9},{9,8},{10,11... | collective-permute-start | bytes 6291464 | tf_op jit(solution)/shard_map/ppermute | solution.py:1070
  339.1 29.4 %all-to-all-start.3 = ((bf16[32,80,128]{2,1,0:T(8,128)(2,1)}), bf16[32,80,128]{2,1,0:T(8,128)(2,1)S(1)}, u32[]{:S(2)}, u32[]{:S(2)}) async-start(bf16[32,80,128]{2,1,0:T(8,128)(2,1)} %get-tuple-element.422), calls=%async_computation.3 | async-start | bytes 1310720 | tf_op jit(solution)/shard_map/all_to_all | solution.py:1357
  341.7 126.1 %reduce-scatter.2.cloned.1.call-start = ((), (), s32[]{:S(2)}) async-start(), calls=%async_computation.11 | async-start | bytes 2359296 | tf_op jit(solution)/shard_map/reduce_scatter | solution.py:1363
  341.8 26.7 %collective-permute-start.35 = (bf16[128,2048]{1,0:T(8,128)(2,1)S(1)}, bf16[128,2048]{1,0:T(8,128)(2,1)S(1)}, u32[]{:S(2)}, u32[]{:S(2)}) collective-permute-start(bf16[128,2048]{1,0:T(8,128)(2,1)S(1)} %copy-done.57), channel_id=1, source_target_pairs={{0,4},{4,0},{1,5},{5,1},{2,6},{6,2},{3,7},{7,3},{8,12},{12,8},{9,1... | collective-permute-start | bytes 1572872 | tf_op jit(solution)/shard_map/ppermute | solution.py:1070
  369.3 39.3 %collective-permute-start.41 = (bf16[2,256,2048]{2,1,0:T(8,128)(2,1)}, bf16[2,256,2048]{2,1,0:T(8,128)(2,1)S(1)}, u32[]{:S(2)}, u32[]{:S(2)}) collective-permute-start(bf16[2,256,2048]{2,1,0:T(8,128)(2,1)} %get-tuple-element.460), channel_id=1, source_target_pairs={{0,1},{1,0},{2,3},{3,2},{4,5},{5,4},{6,7},{7,6},{8,9},{9,8},{10,11... | collective-permute-start | bytes 6291464 | tf_op jit(solution)/shard_map/ppermute | solution.py:1070
  371.7 36.2 %collective-permute-start.38 = (bf16[128,2048]{1,0:T(8,128)(2,1)}, bf16[128,2048]{1,0:T(8,128)(2,1)}, u32[]{:S(2)}, u32[]{:S(2)}) collective-permute-start(bf16[128,2048]{1,0:T(8,128)(2,1)} %add_convert_fusion.11), channel_id=1, source_target_pairs={{0,8},{8,16},{16,24},{24,0},{1,9},{9,17},{17,25},{25,1},{2,10},{10... | collective-permute-start | bytes 1572872 | tf_op jit(solution)/shard_map/ppermute | solution.py:1075
  373.3 34.5 %collective-permute-start.39 = (bf16[128,2048]{1,0:T(8,128)(2,1)}, bf16[128,2048]{1,0:T(8,128)(2,1)}, u32[]{:S(2)}, u32[]{:S(2)}) collective-permute-start(bf16[128,2048]{1,0:T(8,128)(2,1)} %get-tuple-element.451), channel_id=1, source_target_pairs={{0,4},{4,0},{1,5},{5,1},{2,6},{6,2},{3,7},{7,3},{8,12},{12,8},{9,1... | collective-permute-start | bytes 1572872 | tf_op jit(solution)/shard_map/ppermute | solution.py:1070
  374.8 33.0 %collective-permute-start.40 = (bf16[128,2048]{1,0:T(8,128)(2,1)}, bf16[128,2048]{1,0:T(8,128)(2,1)S(1)}, u32[]{:S(2)}, u32[]{:S(2)}) collective-permute-start(bf16[128,2048]{1,0:T(8,128)(2,1)} %get-tuple-element.453), channel_id=1, source_target_pairs={{0,4},{4,0},{1,5},{5,1},{2,6},{6,2},{3,7},{7,3},{8,12},{12,8},{9,1... | collective-permute-start | bytes 1572872 | tf_op jit(solution)/shard_map/ppermute | solution.py:1070
  375.4 33.3 %collective-permute-start.37 = (bf16[256,2048]{1,0:T(8,128)(2,1)}, bf16[256,2048]{1,0:T(8,128)(2,1)}, u32[]{:S(2)}, u32[]{:S(2)}) collective-permute-start(bf16[256,2048]{1,0:T(8,128)(2,1)} %fusion.7), channel_id=1, source_target_pairs={{0,2},{2,0},{1,3},{3,1},{4,6},{6,4},{5,7},{7,5},{8,10},{10,8},{9,1... | collective-permute-start | bytes 3145736 | tf_op jit(solution)/shard_map/ppermute | solution.py:1070
  410.0 23.6 %all-to-all-start.4 = ((bf16[4,192,1024]{2,1,0:T(8,128)(2,1)}), bf16[4,192,1024]{2,1,0:T(8,128)(2,1)S(1)}, u32[]{:S(2)}, u32[]{:S(2)}) async-start(bf16[4,192,1024]{2,1,0:T(8,128)(2,1)} %attn_bwd.1), calls=%async_computation.4 | async-start | bytes 3145728 | tf_op jit(solution)/shard_map/all_to_all | solution.py:1375
  415.2 17.6 %collective-permute-start.42 = (bf16[128,2048]{1,0:T(8,128)(2,1)S(1)}, bf16[128,2048]{1,0:T(8,128)(2,1)}, u32[]{:S(2)}, u32[]{:S(2)}) collective-permute-start(bf16[128,2048]{1,0:T(8,128)(2,1)S(1)} %add_convert_fusion.10), channel_id=1, source_target_pairs={{0,8},{8,16},{16,24},{24,0},{1,9},{9,17},{17,25},{25,1},{2,10},{10... | collective-permute-start | bytes 1572872 | tf_op jit(solution)/shard_map/ppermute | solution.py:1075
  438.8 17.5 %collective-permute-start.44 = (bf16[128,2048]{1,0:T(8,128)(2,1)}, bf16[128,2048]{1,0:T(8,128)(2,1)S(1)}, u32[]{:S(2)}, u32[]{:S(2)}) collective-permute-start(bf16[128,2048]{1,0:T(8,128)(2,1)} %input_rows.1), channel_id=1, source_target_pairs={{0,4},{4,0},{1,5},{5,1},{2,6},{6,2},{3,7},{7,3},{8,12},{12,8},{9,1... | collective-permute-start | bytes 1572872 | tf_op jit(solution)/shard_map/ppermute | solution.py:1070
  464.0 19.8 %collective-permute-start.50 = (bf16[8,64,768]{2,1,0:T(8,128)(2,1)}, bf16[8,64,768]{2,1,0:T(8,128)(2,1)S(1)}, u32[]{:S(2)}, u32[]{:S(2)}) collective-permute-start(bf16[8,64,768]{2,1,0:T(8,128)(2,1)} %fusion.9), channel_id=1, source_target_pairs={{0,2},{2,0},{1,3},{3,1},{4,6},{6,4},{5,7},{7,5},{8,10},{10,8},{9,1... | collective-permute-start | bytes 2359304 | tf_op jit(solution)/shard_map/ppermute | solution.py:1070
  486.0 17.0 %collective-permute-start.51 = (bf16[128,2048]{1,0:T(8,128)(2,1)}, bf16[128,2048]{1,0:T(8,128)(2,1)}, u32[]{:S(2)}, u32[]{:S(2)}) collective-permute-start(bf16[128,2048]{1,0:T(8,128)(2,1)} %add_convert_fusion.5), channel_id=1, source_target_pairs={{0,8},{8,16},{16,24},{24,0},{1,9},{9,17},{17,25},{25,1},{2,10},{10... | collective-permute-start | bytes 1572872 | tf_op jit(solution)/shard_map/ppermute | solution.py:1075
  487.3 15.7 %collective-permute-start.53 = (bf16[128,2048]{1,0:T(8,128)(2,1)}, bf16[128,2048]{1,0:T(8,128)(2,1)}, u32[]{:S(2)}, u32[]{:S(2)}) collective-permute-start(bf16[128,2048]{1,0:T(8,128)(2,1)} %get-tuple-element.509), channel_id=1, source_target_pairs={{0,2},{2,0},{1,3},{3,1},{4,6},{6,4},{5,7},{7,5},{8,10},{10,8},{9,1... | collective-permute-start | bytes 1572872 | tf_op jit(solution)/shard_map/ppermute | solution.py:1070
  491.7 40.2 %all-to-all-start.5 = ((bf16[8,64,768]{2,1,0:T(8,128)(2,1)}), bf16[8,64,768]{2,1,0:T(8,128)(2,1)S(1)}, u32[]{:S(2)}, u32[]{:S(2)}) async-start(bf16[8,64,768]{2,1,0:T(8,128)(2,1)} %fusion.1), calls=%async_computation.6 | async-start | bytes 1572864 | tf_op jit(solution)/shard_map/all_to_all | solution.py:1399
  504.6 20.5 %collective-permute-start.54 = (bf16[128,2048]{1,0:T(8,128)(2,1)S(1)}, bf16[128,2048]{1,0:T(8,128)(2,1)S(1)}, u32[]{:S(2)}, u32[]{:S(2)}) collective-permute-start(bf16[128,2048]{1,0:T(8,128)(2,1)S(1)} %add_convert_fusion.4), channel_id=1, source_target_pairs={{0,8},{8,16},{16,24},{24,0},{1,9},{9,17},{17,25},{25,1},{2,10},{10... | collective-permute-start | bytes 1572872 | tf_op jit(solution)/shard_map/ppermute | solution.py:1075
  504.9 15.7 %collective-permute-start.55 = (bf16[128,2048]{1,0:T(8,128)(2,1)S(1)}, bf16[128,2048]{1,0:T(8,128)(2,1)S(1)}, u32[]{:S(2)}, u32[]{:S(2)}) collective-permute-start(bf16[128,2048]{1,0:T(8,128)(2,1)S(1)} %copy-done.61), channel_id=1, source_target_pairs={{0,4},{4,0},{1,5},{5,1},{2,6},{6,2},{3,7},{7,3},{8,12},{12,8},{9,1... | collective-permute-start | bytes 1572872 | tf_op jit(solution)/shard_map/ppermute | solution.py:1070
  505.9 21.0 %collective-permute-start.56 = (bf16[256,2048]{1,0:T(8,128)(2,1)S(1)}, bf16[256,2048]{1,0:T(8,128)(2,1)S(1)}, u32[]{:S(2)}, u32[]{:S(2)}) collective-permute-start(bf16[256,2048]{1,0:T(8,128)(2,1)S(1)} %copy-done.18), channel_id=1, source_target_pairs={{0,2},{2,0},{1,3},{3,1},{4,6},{6,4},{5,7},{7,5},{8,10},{10,8},{9,1... | collective-permute-start | bytes 3145736 | tf_op jit(solution)/shard_map/ppermute | solution.py:1070
  (86 other events, 1039.5 us)
Sparse Core Ops, SparseCore 0:
  9.6 37.1 all-gather.4
  49.9 104.2 all-gather.6
  156.3 68.6 all-gather.8
  339.0 25.3 all-gather.10
  373.4 70.9 reduce-scatter.1

commit v7 on v6

--- a/solution.py
+++ b/solution.py
@@ -842,25 +842,28 @@
     ]
     for c in w_in + x_in:
         c.start()
-    for c in w_in + x_in:
+    for c in w_in:
         c.wait()
-    out = [
-        pltpu.make_async_copy(x_scr, rows_ref, out_sem.at[0]),
-        pltpu.make_async_copy(w_scr, w_ref, out_sem.at[1]),
-    ]
-    for c in out:
-        c.start()
+    leaving = [pltpu.make_async_copy(w_scr, w_ref, out_sem.at[0])]
+    leaving[0].start()
     group = heads * HD
-    for i in range(3):
-        y = mxu(x_scr[...], w_scr[:, i * group : (i + 1) * group]).T
-        for h in range(heads):
-            at = slice(i * HD, (i + 1) * HD)
-            a, b = y[h * HD : h * HD + half], y[h * HD + half : (h + 1) * HD]
-            if i < 2:
-                c, s = cos_ref[...], sin_ref[...]
-                a, b = a * c - b * s, b * c + a * s
-            out_ref[h, at] = jnp.concatenate([a, b], axis=0).astype(BF16)
-    for c in out:
+    some = count * tok // 2
+    for t in range(2):
+        rows = slice(t * some, (t + 1) * some)
+        for c in x_in[t * count // 2 : (t + 1) * count // 2]:
+            c.wait()
+        leaving.append(pltpu.make_async_copy(x_scr.at[rows], rows_ref.at[rows], out_sem.at[1 + t]))
+        leaving[-1].start()
+        for i in range(3):
+            y = mxu(x_scr[rows, :], w_scr[:, i * group : (i + 1) * group]).T
+            for h in range(heads):
+                at = slice(i * HD, (i + 1) * HD)
+                a, b = y[h * HD : h * HD + half], y[h * HD + half : (h + 1) * HD]
+                if i < 2:
+                    c, s = cos_ref[:, rows], sin_ref[:, rows]
+                    a, b = a * c - b * s, b * c + a * s
+                out_ref[h, at, rows] = jnp.concatenate([a, b], axis=0).astype(BF16)
+    for c in leaving:
         c.wait()
 
 
@@ -882,7 +885,7 @@
             pltpu.VMEM((width, cols), BF16),
             pltpu.SemaphoreType.DMA((count,)),
             pltpu.SemaphoreType.DMA((4, groups)),
-            pltpu.SemaphoreType.DMA((2,)),
+            pltpu.SemaphoreType.DMA((3,)),
         ],
         compiler_params=pltpu.CompilerParams(vmem_limit_bytes=60 << 20),
         cost_estimate=pl.CostEstimate(

time: 549 us -> 549 us (level)
  transfers between devices with their start and end apart: 68 -> 68, of which waited for: 37 -> 37; matrix products, arithmetic and copies ran while one was open for 11% -> 11% of each run, Pallas kernels for 29% -> 30%
where the time goes in v7:
time: 549 us; the launch traced here: 542 us
  waiting for transfers between devices  198 us (36%)
  Pallas kernels  169 us (31%)
  starting transfers between devices  80.4 us (15%)
  other arithmetic  53 us (10%)
  local copies, waits for them, and re-layouts  16.9 us (3%)
  between operations  15 us (3%)
  matrix products  8.91 us (2%)
    ppermute x39, waiting for transfers between devices, swap(): return lax.ppermute(v, axis, [(0, 1), (1, 0)])  138 us
    pallas_call x4, Pallas kernels, ffn(): pl.pallas_call(functools.partial(ffn_kernel, count=count, step=step), in_...  49.8 us
    ppermute x18, waiting for transfers between devices, shift(): return lax.ppermute(v, 'ctx', [(i, (i + 1) % n) for i in range(n)])  45.2 us
    ppermute x39, starting transfers between devices, swap(): return lax.ppermute(v, axis, [(0, 1), (1, 0)])  38.6 us
    pallas_call x3, Pallas kernels, outer(): pl.pallas_call(functools.partial(outer_kernel, lefts=len(left), rights=le...  32.2 us
    pallas_call x1, Pallas kernels, attn_bwd(): pl.pallas_call(functools.partial(attn_bwd_kernel, blocks=blocks, width=wi...  31.9 us
    pallas_call x1, Pallas kernels, attn_fwd(): pl.pallas_call(functools.partial(attn_fwd_kernel, blocks=blocks, width=co...  19.2 us
    ppermute x18, starting transfers between devices, shift(): return lax.ppermute(v, 'ctx', [(i, (i + 1) % n) for i in range(n)])  14.4 us
  transfers between devices with their start and end apart: 68, of which 37 were waited for; matrix products, arithmetic and copies ran while one was open for 11% of the time, Pallas kernels for 30%

profile of v7, /device:TPU:0, one launch (start us, length us, event | category | flops | bytes accessed | tf_op | source)
XLA Modules:
  0.0 541.8 jit_solution(14848007523824883027)
XLA Ops:
  10.9 7.4 %all-to-all-start = ((bf16[8,64,768]{2,1,0:T(8,128)(2,1)}), bf16[8,64,768]{2,1,0:T(8,128)(2,1)S(1)}, u32[]{:S(2)}, u32[]{:S(2)}) async-start(bf16[8,64,768]{2,1,0:T(8,128)(2,1)} %maximum_bitcast_fusion), calls=%async_computation | async-start | bytes 1572864 | tf_op jit(solution)/shard_map/all_to_all | solution.py:1201
  22.8 17.5 %collective-permute-done.1.refs_4_ = bf16[128,2048]{1,0:T(8,128)(2,1)S(1)} collective-permute-done((bf16[128,2048]{1,0:T(8,128)(2,1)S(1)}, bf16[128,2048]{1,0:T(8,128)(2,1)S(1)}, u32[]{:S(2)}, u32[]{:S(2)}) %collective-permute-start.1) | collective-permute-done | bytes 524320 | tf_op jit(solution)/shard_map/ppermute | solution.py:1073
  41.2 5.4 collective-permute-done.refs_1_
  46.6 3.2 all-to-all-done.refs_8_
  54.4 10.6 %collective-permute-done.4 = bf16[4,64,768]{2,1,0:T(8,128)(2,1)S(1)} collective-permute-done((bf16[4,64,768]{2,1,0:T(8,128)(2,1)S(1)}, bf16[4,64,768]{2,1,0:T(8,128)(2,1)S(1)}, u32[]{:S(2)}, u32[]{:S(2)}) %collective-permute-start.4) | collective-permute-done | bytes 393248 | tf_op jit(solution)/shard_map/ppermute | solution.py:1073
  65.0 4.2 collective-permute-done.2.refs_2_
  69.3 3.2 collective-permute-start.8
  73.2 5.0 collective-permute-done.8
  78.6 4.6 collective-permute-done.6.refs_3_
  86.8 15.6 %collective-permute-done.12.refs_7_ = bf16[128,2048]{1,0:T(8,128)(2,1)} collective-permute-done((bf16[128,2048]{1,0:T(8,128)(2,1)}, bf16[128,2048]{1,0:T(8,128)(2,1)}, u32[]{:S(2)}, u32[]{:S(2)}) %collective-permute-start.12) | collective-permute-done | bytes 524320 | tf_op jit(solution)/shard_map/ppermute | solution.py:1073
  102.6 10.5 %qkv.1 = (bf16[4,192,1024]{2,1,0:T(8,128)(2,1)}, bf16[1024,2048]{1,0:T(8,128)(2,1)}, bf16[2048,768]{1,0:T(8,128)(2,1)}) custom-call(s32[1]{0:T(128)} %bitcast.2.near_ref, bf16[128,2048]{1,0:T(8,128)(2,1)} %copy-done.34, bf16[128,2048]{1,0:T(8,128)(2,1)} %collective-permute-done.refs_1_, bf16[128,2048]{1,0:T(8,128)(2,1)} %copy-done.63, ...), custom_call_target="tpu_custom_call" | custom-call | flops 3221225472 | bytes 14680064 | tf_op jit(solution)/shard_map/qkv/pallas_call | solution.py:874
  113.2 3.6 all-to-all-start.1
  119.3 4.3 collective-permute-done.9.refs_2_.refs_7_
  123.6 2.8 multiply_sine_fusion
  127.6 10.5 %collective-permute-done.11.refs_3_.refs_6_ = bf16[128,2048]{1,0:T(8,128)(2,1)S(1)} collective-permute-done((bf16[128,2048]{1,0:T(8,128)(2,1)S(1)}, bf16[128,2048]{1,0:T(8,128)(2,1)S(1)}, u32[]{:S(2)}, u32[]{:S(2)}) %collective-permute-start.11) | collective-permute-done | bytes 524320 | tf_op jit(solution)/shard_map/ppermute | solution.py:1073
  139.0 11.0 %collective-permute-done.10.refs_2_.refs_9_ = bf16[128,2048]{1,0:T(8,128)(2,1)} collective-permute-done((bf16[128,2048]{1,0:T(8,128)(2,1)S(1)}, bf16[128,2048]{1,0:T(8,128)(2,1)}, u32[]{:S(2)}, u32[]{:S(2)}) %collective-permute-start.10) | collective-permute-done | bytes 524320 | tf_op jit(solution)/shard_map/ppermute | solution.py:1078
  151.8 19.2 %attn_fwd.1 = (bf16[32,80,128]{2,1,0:T(8,128)(2,1)}, f32[64,4096]{1,0:T(8,128)}, f32[1,4096]{1,0:T(1,128)}, bf16[192,4096]{1,0:T(8,128)(2,1)}) custom-call(s32[2,8]{1,0:T(2,128)} %pad_add_fusion.place_ref, bf16[4,192,1024]{2,1,0:T(8,128)(2,1)} %copy-done.13, bf16[16,128]{1,0:T(8,128)(2,1)} %pad.4.extra_ref), custom_call_target="tpu_custom_call" | custom-call | flops 8589934592 | bytes 8388608 | tf_op jit(solution)/shard_map/attn_fwd/pallas_call | solution.py:464
  171.1 5.2 all-to-all-start.2
  178.2 19.2 %collective-permute-done.17.refs_3_.refs_12_ = bf16[128,2048]{1,0:T(8,128)(2,1)S(1)} collective-permute-done((bf16[128,2048]{1,0:T(8,128)(2,1)S(1)}, bf16[128,2048]{1,0:T(8,128)(2,1)S(1)}, u32[]{:S(2)}, u32[]{:S(2)}) %collective-permute-start.17) | collective-permute-done | bytes 524320 | tf_op jit(solution)/shard_map/ppermute | solution.py:1073
  198.4 4.7 multiply_reduce_fusion
  208.2 9.5 %collective-permute-done.19.refs_1_.refs_6_ = bf16[128,2048]{1,0:T(8,128)(2,1)} collective-permute-done((bf16[128,2048]{1,0:T(8,128)(2,1)S(1)}, bf16[128,2048]{1,0:T(8,128)(2,1)}, u32[]{:S(2)}, u32[]{:S(2)}) %collective-permute-start.19) | collective-permute-done | bytes 524320 | tf_op jit(solution)/shard_map/ppermute | solution.py:1073
  221.2 3.6 all-gather.9.cloned.1.call-done.refs_5_
  224.8 12.4 %ffn.4 = (bf16[128,2048]{1,0:T(8,128)(2,1)}, bf16[128,2048]{1,0:T(8,128)(2,1)}, bf16[128,2048]{1,0:T(8,128)(2,1)}, bf16[128,2048]{1,0:T(8,128)(2,1)}, bf16[256,1...) custom-call(bf16[128,2048]{1,0:T(8,128)(2,1)} %copy-done.33, ...), custom_call_target="tpu_custom_call" | custom-call | flops 6442450944 | bytes 20971520 | tf_op jit(solution)/shard_map/ffn/pallas_call | solution.py:734
  240.4 12.4 %ffn.5 = (bf16[128,2048]{1,0:T(8,128)(2,1)}, bf16[128,2048]{1,0:T(8,128)(2,1)}, bf16[128,2048]{1,0:T(8,128)(2,1)}, bf16[128,2048]{1,0:T(8,128)(2,1)}, bf16[256,1...) custom-call(bf16[128,2048]{1,0:T(8,128)(2,1)} %collective-permute-done.18.refs_0_.refs_7_, ...), custom_call_target="tpu_custom_call" | custom-call | flops 6442450944 | bytes 20971520 | tf_op jit(solution)/shard_map/ffn/pallas_call | solution.py:734
  256.8 12.5 %ffn.6 = (bf16[128,2048]{1,0:T(8,128)(2,1)}, bf16[128,2048]{1,0:T(8,128)(2,1)}, bf16[128,2048]{1,0:T(8,128)(2,1)}, bf16[128,2048]{1,0:T(8,128)(2,1)}, bf16[256,1...) custom-call(bf16[128,2048]{1,0:T(8,128)(2,1)} %collective-permute-done.20.refs_0_.refs_9_, ...), custom_call_target="tpu_custom_call" | custom-call | flops 6442450944 | bytes 20971520 | tf_op jit(solution)/shard_map/ffn/pallas_call | solution.py:734
  269.8 9.4 %collective-permute-done.24.refs_1_.refs_12_ = bf16[128,2048]{1,0:T(8,128)(2,1)} collective-permute-done((bf16[128,2048]{1,0:T(8,128)(2,1)S(1)}, bf16[128,2048]{1,0:T(8,128)(2,1)}, u32[]{:S(2)}, u32[]{:S(2)}) %collective-permute-start.24) | collective-permute-done | bytes 524320 | tf_op jit(solution)/shard_map/ppermute | solution.py:1073
  281.1 12.4 %ffn.7 = (bf16[128,2048]{1,0:T(8,128)(2,1)}, bf16[128,2048]{1,0:T(8,128)(2,1)}, bf16[128,2048]{1,0:T(8,128)(2,1)}, bf16[128,2048]{1,0:T(8,128)(2,1)}, bf16[256,1...) custom-call(bf16[128,2048]{1,0:T(8,128)(2,1)} %copy-done.60, ...), custom_call_target="tpu_custom_call" | custom-call | flops 6442450944 | bytes 20971520 | tf_op jit(solution)/shard_map/ffn/pallas_call | solution.py:734
  298.8 10.8 %outer.3 = (bf16[2,256,2048]{2,1,0:T(8,128)(2,1)}, bf16[2,256,2048]{2,1,0:T(8,128)(2,1)}) custom-call(s32[4]{0:T(128)} %broadcast_xor_fusion.refs_0_, bf16[256,1024]{1,0:T(8,128)(2,1)} %get-tuple-element.371.refs_1_, bf16[256,1024]{1,0:T(8,128)(2,1)} %get-tuple-element.372.refs_2_, bf16[256,1024]{1,0:T(8,128)(2,1)} %get-tuple-element.373.refs_3_, ...), custom_call_target="tpu_custom_call" | custom-call | flops 4294967296 | bytes 10485760 | tf_op jit(solution)/shard_map/outer/pallas_call | solution.py:801
  315.3 10.7 %outer.4 = (bf16[2,256,2048]{2,1,0:T(8,128)(2,1)}, bf16[2,256,2048]{2,1,0:T(8,128)(2,1)}) custom-call(s32[4]{0:T(128)} %broadcast_xor_fusion.refs_0_, bf16[256,1024]{1,0:T(8,128)(2,1)} %get-tuple-element.394.refs_1_, bf16[256,1024]{1,0:T(8,128)(2,1)} %get-tuple-element.395.refs_2_, bf16[256,1024]{1,0:T(8,128)(2,1)} %get-tuple-element.396.refs_3_, ...), custom_call_target="tpu_custom_call" | custom-call | flops 4294967296 | bytes 10485760 | tf_op jit(solution)/shard_map/outer/pallas_call | solution.py:801
  329.3 9.3 %mid_grad.1 = (f32[128,2048]{1,0:T(8,128)}, bf16[128,2048]{1,0:T(8,128)(2,1)}, bf16[32,80,128]{2,1,0:T(8,128)(2,1)}) custom-call(bf16[128,2048]{1,0:T(8,128)(2,1)} %get-tuple-element.419.own_ref, bf16[128,2048]{1,0:T(8,128)(2,1)} %copy-done.31, bf16[128,2048]{1,0:T(8,128)(2,1)} %copy-done.30, f32[128,2048]{1,0:T(8,128)} %copy-done, bf16[128,2048]{1,0:T(8,128)(2,1)} %refs_5_, ...), custom_call_target="tpu_custom_call" | custom-call | flops 1073741824 | bytes 8388608 | tf_op jit(solution)/shard_map/mid_grad/pallas_call | solution.py:1050
  338.9 2.6 all-to-all-start.3
  343.4 3.1 fusion.7
  346.4 10.7 %outer.5 = (bf16[2,256,2048]{2,1,0:T(8,128)(2,1)}, bf16[2,256,2048]{2,1,0:T(8,128)(2,1)}) custom-call(s32[4]{0:T(128)} %broadcast_xor_fusion.refs_0_, bf16[256,1024]{1,0:T(8,128)(2,1)} %get-tuple-element.429.refs_1_, bf16[256,1024]{1,0:T(8,128)(2,1)} %get-tuple-element.430.refs_2_, bf16[256,1024]{1,0:T(8,128)(2,1)} %get-tuple-element.431.refs_3_, ...), custom_call_target="tpu_custom_call" | custom-call | flops 4294967296 | bytes 10485760 | tf_op jit(solution)/shard_map/outer/pallas_call | solution.py:801
  357.9 6.2 %all-gather.11.cloned.1.call-done = bf16[512,2048]{1,0:T(8,128)(2,1)} async-done(((bf16[128,2048]{1,0:T(8,128)(2,1)}), bf16[512,2048]{1,0:T(8,128)(2,1)}) %all-gather.11.cloned.1.call-update) | async-done | bytes 2097168 | tf_op jit(solution)/shard_map/all_gather | solution.py:1350
  364.1 4.2 convolution_convert_fusion
  375.7 31.9 %attn_bwd.1 = bf16[4,192,1024]{2,1,0:T(8,128)(2,1)} custom-call(s32[2,8]{1,0:T(2,128)} %pad_add_fusion.place_ref, bf16[192,4096]{1,0:T(8,128)(2,1)} %get-tuple-element.454.seq_hbm, f32[64,4096]{1,0:T(8,128)} %get-tuple-element.455.o32_hbm, f32[1,4096]{1,0:T(1,128)} %get-tuple-element.456.lse_ref, bf16[32,80,128]{2,1,0:T(8,128)(2,1)} %copy-done.24, ...), custom_call_target="tpu_custom_call" | custom-call | flops 21474836480 | bytes 8388608 | tf_op jit(solution)/shard_map/attn_bwd/pallas_call | solution.py:598
  409.8 3.6 all-to-all-start.4
  423.0 8.8 %collective-permute-done.43 = bf16[128,2048]{1,0:T(8,128)(2,1)S(1)} collective-permute-done((bf16[128,2048]{1,0:T(8,128)(2,1)}, bf16[128,2048]{1,0:T(8,128)(2,1)S(1)}, u32[]{:S(2)}, u32[]{:S(2)}) %collective-permute-start.43) | collective-permute-done | bytes 524320 | tf_op jit(solution)/shard_map/ppermute | solution.py:1073
  434.6 4.0 input_rows.1
  443.5 12.6 %heads_back.1 = (bf16[2,8,64,768]{3,2,1,0:T(8,128)(2,1)}, bf16[2,8,64,768]{3,2,1,0:T(8,128)(2,1)}, bf16[128,2048]{1,0:T(8,128)(2,1)}, bf16[128,2048]{1,0:T(8,128...) custom-call(s32[1]{0:T(128)} %bitcast.2.near_ref, ...), custom_call_target="tpu_custom_call" | custom-call | flops 6442450944 | bytes 16252928 | tf_op jit(solution)/shard_map/heads_back/pallas_call | solution.py:987
  456.8 3.6 collective-permute-done.49
  467.6 12.0 %collective-permute-done.48 = bf16[128,2048]{1,0:T(8,128)(2,1)S(1)} collective-permute-done((bf16[128,2048]{1,0:T(8,128)(2,1)}, bf16[128,2048]{1,0:T(8,128)(2,1)S(1)}, u32[]{:S(2)}, u32[]{:S(2)}) %collective-permute-start.48) | collective-permute-done | bytes 524320 | tf_op jit(solution)/shard_map/ppermute | solution.py:1073
  491.4 4.8 all-to-all-start.5
  498.2 2.8 collective-permute-done.52
  507.4 3.4 bitcast_add_fusion.1
  510.8 3.4 bitcast_add_fusion
  515.3 5.0 collective-permute-done.55
  520.3 4.5 collective-permute-done.54
  (312 shorter events, 128.9 us)
Async XLA Ops:
  7.2 142.8 %all-gather.5.cloned.1.call-start = ((), (), s32[]{:S(2)}) async-start(), calls=%async_computation.7 | async-start | bytes 5242880 | tf_op jit(solution)/shard_map/all_gather | solution.py:1266
  10.9 38.8 %all-to-all-start = ((bf16[8,64,768]{2,1,0:T(8,128)(2,1)}), bf16[8,64,768]{2,1,0:T(8,128)(2,1)S(1)}, u32[]{:S(2)}, u32[]{:S(2)}) async-start(bf16[8,64,768]{2,1,0:T(8,128)(2,1)} %maximum_bitcast_fusion), calls=%async_computation | async-start | bytes 1572864 | tf_op jit(solution)/shard_map/all_to_all | solution.py:1201
  18.4 152.7 %all-gather.7.cloned.1.call-start = ((), (), s32[]{:S(2)}) async-start(), calls=%async_computation.8 | async-start | bytes 8650752 | tf_op jit(solution)/shard_map/all_gather | solution.py:1271
  19.3 21.0 %collective-permute-start.1 = (bf16[128,2048]{1,0:T(8,128)(2,1)S(1)}, bf16[128,2048]{1,0:T(8,128)(2,1)S(1)}, u32[]{:S(2)}, u32[]{:S(2)}) collective-permute-start(bf16[128,2048]{1,0:T(8,128)(2,1)S(1)} %fusion.3.refs_0_), channel_id=1, source_target_pairs={{0,4},{4,0},{1,5},{5,1},{2,6},{6,2},{3,7},{7,3},{8,12},{12,8},{9,1... | collective-permute-start | bytes 1572872 | tf_op jit(solution)/shard_map/ppermute | solution.py:1073
  21.4 25.2 %collective-permute-start = (bf16[128,2048]{1,0:T(8,128)(2,1)S(1)}, bf16[128,2048]{1,0:T(8,128)(2,1)}, u32[]{:S(2)}, u32[]{:S(2)}) collective-permute-start(bf16[128,2048]{1,0:T(8,128)(2,1)S(1)} %fusion.3.refs_0_), channel_id=1, source_target_pairs={{0,8},{8,16},{16,24},{24,0},{1,9},{9,17},{17,25},{25,1},{2,10},{10... | collective-permute-start | bytes 1572872 | tf_op jit(solution)/shard_map/ppermute | solution.py:1078
  49.8 175.0 %all-gather.9.cloned.1.call-start = ((), (), s32[]{:S(2)}) async-start(), calls=%async_computation.9 | async-start | bytes 10485760 | tf_op jit(solution)/shard_map/all_gather | solution.py:1279
  51.4 17.7 %collective-permute-start.2 = (bf16[128,2048]{1,0:T(8,128)(2,1)}, bf16[128,2048]{1,0:T(8,128)(2,1)S(1)}, u32[]{:S(2)}, u32[]{:S(2)}) collective-permute-start(bf16[128,2048]{1,0:T(8,128)(2,1)} %collective-permute-done.refs_1_), channel_id=1, source_target_pairs={{0,8},{8,16},{16,24},{24,0},{1,9},{9,17},{17,25},{25,1},{2,10},{10... | collective-permute-start | bytes 1572872 | tf_op jit(solution)/shard_map/ppermute | solution.py:1078
  51.4 17.7 %collective-permute-start.5 = (bf16[8,64,768]{2,1,0:T(8,128)(2,1)S(1)}, bf16[8,64,768]{2,1,0:T(8,128)(2,1)S(1)}, u32[]{:S(2)}, u32[]{:S(2)}) collective-permute-start(bf16[8,64,768]{2,1,0:T(8,128)(2,1)S(1)} %all-to-all-done.refs_8_), channel_id=1, source_target_pairs={{0,1},{1,0},{2,3},{3,2},{4,5},{5,4},{6,7},{7,6},{8,9},{9,8},{10,11... | collective-permute-start | bytes 2359304 | tf_op jit(solution)/shard_map/ppermute | solution.py:1073
  83.9 18.5 %collective-permute-start.13 = (bf16[8,64,768]{2,1,0:T(8,128)(2,1)}, bf16[8,64,768]{2,1,0:T(8,128)(2,1)}, u32[]{:S(2)}, u32[]{:S(2)}) collective-permute-start(bf16[8,64,768]{2,1,0:T(8,128)(2,1)} %constant_dynamic-update-slice_fusion.refs_10_), channel_id=1, source_target_pairs={{0,1},{1,0},{2,3},{3,2},{4,5},{5,4},{6,7},{7,6},{8,9},{9,8},{10,11... | collective-permute-start | bytes 2359304 | tf_op jit(solution)/shard_map/ppermute | solution.py:1073
  84.0 18.5 %collective-permute-start.12 = (bf16[128,2048]{1,0:T(8,128)(2,1)}, bf16[128,2048]{1,0:T(8,128)(2,1)}, u32[]{:S(2)}, u32[]{:S(2)}) collective-permute-start(bf16[128,2048]{1,0:T(8,128)(2,1)} %collective-permute-done.6.refs_3_), channel_id=1, source_target_pairs={{0,4},{4,0},{1,5},{5,1},{2,6},{6,2},{3,7},{7,3},{8,12},{12,8},{9,1... | collective-permute-start | bytes 1572872 | tf_op jit(solution)/shard_map/ppermute | solution.py:1073
  102.6 21.0 %collective-permute-start.9 = (bf16[128,2048]{1,0:T(8,128)(2,1)S(1)}, bf16[128,2048]{1,0:T(8,128)(2,1)S(1)}, u32[]{:S(2)}, u32[]{:S(2)}) collective-permute-start(bf16[128,2048]{1,0:T(8,128)(2,1)S(1)} %copy-done.25), channel_id=1, source_target_pairs={{0,8},{8,16},{16,24},{24,0},{1,9},{9,17},{17,25},{25,1},{2,10},{10... | collective-permute-start | bytes 1572872 | tf_op jit(solution)/shard_map/ppermute | solution.py:1078
  113.2 36.8 %all-to-all-start.1 = ((bf16[4,192,1024]{2,1,0:T(8,128)(2,1)}), bf16[4,192,1024]{2,1,0:T(8,128)(2,1)S(1)}, u32[]{:S(2)}, u32[]{:S(2)}) async-start(bf16[4,192,1024]{2,1,0:T(8,128)(2,1)} %get-tuple-element.294), calls=%async_computation.1 | async-start | bytes 3145728 | tf_op jit(solution)/shard_map/all_to_all | solution.py:1291
  118.0 20.1 %collective-permute-start.11 = (bf16[128,2048]{1,0:T(8,128)(2,1)S(1)}, bf16[128,2048]{1,0:T(8,128)(2,1)S(1)}, u32[]{:S(2)}, u32[]{:S(2)}) collective-permute-start(bf16[128,2048]{1,0:T(8,128)(2,1)S(1)} %copy-done.25), channel_id=1, source_target_pairs={{0,4},{4,0},{1,5},{5,1},{2,6},{6,2},{3,7},{7,3},{8,12},{12,8},{9,1... | collective-permute-start | bytes 1572872 | tf_op jit(solution)/shard_map/ppermute | solution.py:1073
  123.6 26.3 %collective-permute-start.10 = (bf16[128,2048]{1,0:T(8,128)(2,1)S(1)}, bf16[128,2048]{1,0:T(8,128)(2,1)}, u32[]{:S(2)}, u32[]{:S(2)}) collective-permute-start(bf16[128,2048]{1,0:T(8,128)(2,1)S(1)} %collective-permute-done.9.refs_2_.refs_7_), channel_id=1, source_target_pairs={{0,8},{8,16},{16,24},{24,0},{1,9},{9,17},{17,25},{25,1},{2,10},{10... | collective-permute-start | bytes 1572872 | tf_op jit(solution)/shard_map/ppermute | solution.py:1078
  126.4 44.6 %collective-permute-start.15 = (bf16[128,2048]{1,0:T(8,128)(2,1)S(1)}, bf16[128,2048]{1,0:T(8,128)(2,1)}, u32[]{:S(2)}, u32[]{:S(2)}) collective-permute-start(bf16[128,2048]{1,0:T(8,128)(2,1)S(1)} %collective-permute-done.9.refs_2_.refs_7_), channel_id=1, source_target_pairs={{0,4},{4,0},{1,5},{5,1},{2,6},{6,2},{3,7},{7,3},{8,12},{12,8},{9,1... | collective-permute-start | bytes 1572872 | tf_op jit(solution)/shard_map/ppermute | solution.py:1073
  150.0 21.1 %collective-permute-start.16 = (bf16[128,2048]{1,0:T(8,128)(2,1)}, bf16[128,2048]{1,0:T(8,128)(2,1)}, u32[]{:S(2)}, u32[]{:S(2)}) collective-permute-start(bf16[128,2048]{1,0:T(8,128)(2,1)} %collective-permute-done.10.refs_2_.refs_9_), channel_id=1, source_target_pairs={{0,4},{4,0},{1,5},{5,1},{2,6},{6,2},{3,7},{7,3},{8,12},{12,8},{9,1... | collective-permute-start | bytes 1572872 | tf_op jit(solution)/shard_map/ppermute | solution.py:1073
  151.5 19.5 %collective-permute-start.14 = (bf16[128,2048]{1,0:T(8,128)(2,1)}, bf16[128,2048]{1,0:T(8,128)(2,1)S(1)}, u32[]{:S(2)}, u32[]{:S(2)}) collective-permute-start(bf16[128,2048]{1,0:T(8,128)(2,1)} %collective-permute-done.10.refs_2_.refs_9_), channel_id=1, source_target_pairs={{0,8},{8,16},{16,24},{24,0},{1,9},{9,17},{17,25},{25,1},{2,10},{10... | collective-permute-start | bytes 1572872 | tf_op jit(solution)/shard_map/ppermute | solution.py:1078
  171.1 27.1 %all-to-all-start.2 = ((bf16[32,80,128]{2,1,0:T(8,128)(2,1)}), bf16[32,80,128]{2,1,0:T(8,128)(2,1)S(1)}, u32[]{:S(2)}, u32[]{:S(2)}) async-start(bf16[32,80,128]{2,1,0:T(8,128)(2,1)} %get-tuple-element.303), calls=%async_computation.2 | async-start | bytes 1310720 | tf_op jit(solution)/shard_map/all_to_all | solution.py:1301
  176.3 187.9 %all-gather.11.cloned.1.call-start = ((), (), s32[]{:S(2)}) async-start(), calls=%async_computation.10 | async-start | bytes 2621440 | tf_op jit(solution)/shard_map/all_gather | solution.py:1350
  176.3 21.1 %collective-permute-start.17 = (bf16[128,2048]{1,0:T(8,128)(2,1)S(1)}, bf16[128,2048]{1,0:T(8,128)(2,1)S(1)}, u32[]{:S(2)}, u32[]{:S(2)}) collective-permute-start(bf16[128,2048]{1,0:T(8,128)(2,1)S(1)} %collective-permute-done.14.refs_2_.refs_11_), channel_id=1, source_target_pairs={{0,4},{4,0},{1,5},{5,1},{2,6},{6,2},{3,7},{7,3},{8,12},{12,8},{9,1... | collective-permute-start | bytes 1572872 | tf_op jit(solution)/shard_map/ppermute | solution.py:1073
  206.8 62.5 %collective-permute-start.26 = (bf16[2,8,64,128]{3,2,0,1:T(8,128)(2,1)}, bf16[2,8,64,128]{3,2,0,1:T(8,128)(2,1)S(1)}, u32[]{:S(2)}, u32[]{:S(2)}) collective-permute-start(bf16[2,8,64,128]{3,2,0,1:T(8,128)(2,1)} %fusion.22), channel_id=1, source_target_pairs={{0,2},{2,0},{1,3},{3,1},{4,6},{6,4},{5,7},{7,5},{8,10},{10,8},{9,1... | collective-permute-start | bytes 786440 | tf_op jit(solution)/shard_map/ppermute | solution.py:1073
  220.2 17.0 %collective-permute-start.21 = (bf16[128,2048]{1,0:T(8,128)(2,1)}, bf16[128,2048]{1,0:T(8,128)(2,1)}, u32[]{:S(2)}, u32[]{:S(2)}) collective-permute-start(bf16[128,2048]{1,0:T(8,128)(2,1)} %collective-permute-done.18.refs_0_.refs_7_), channel_id=1, source_target_pairs={{0,4},{4,0},{1,5},{5,1},{2,6},{6,2},{3,7},{7,3},{8,12},{12,8},{9,1... | collective-permute-start | bytes 1572872 | tf_op jit(solution)/shard_map/ppermute | solution.py:1073
  221.2 16.1 %collective-permute-start.20 = (bf16[128,2048]{1,0:T(8,128)(2,1)}, bf16[128,2048]{1,0:T(8,128)(2,1)}, u32[]{:S(2)}, u32[]{:S(2)}) collective-permute-start(bf16[128,2048]{1,0:T(8,128)(2,1)} %collective-permute-done.18.refs_0_.refs_7_), channel_id=1, source_target_pairs={{0,8},{8,16},{16,24},{24,0},{1,9},{9,17},{17,25},{25,1},{2,10},{10... | collective-permute-start | bytes 1572872 | tf_op jit(solution)/shard_map/ppermute | solution.py:1078
  237.2 15.6 %collective-permute-start.23 = (bf16[128,2048]{1,0:T(8,128)(2,1)}, bf16[128,2048]{1,0:T(8,128)(2,1)S(1)}, u32[]{:S(2)}, u32[]{:S(2)}) collective-permute-start(bf16[128,2048]{1,0:T(8,128)(2,1)} %collective-permute-done.20.refs_0_.refs_9_), channel_id=1, source_target_pairs={{0,4},{4,0},{1,5},{5,1},{2,6},{6,2},{3,7},{7,3},{8,12},{12,8},{9,1... | collective-permute-start | bytes 1572872 | tf_op jit(solution)/shard_map/ppermute | solution.py:1073
  238.8 16.0 %collective-permute-start.22 = (bf16[128,2048]{1,0:T(8,128)(2,1)}, bf16[128,2048]{1,0:T(8,128)(2,1)S(1)}, u32[]{:S(2)}, u32[]{:S(2)}) collective-permute-start(bf16[128,2048]{1,0:T(8,128)(2,1)} %collective-permute-done.20.refs_0_.refs_9_), channel_id=1, source_target_pairs={{0,8},{8,16},{16,24},{24,0},{1,9},{9,17},{17,25},{25,1},{2,10},{10... | collective-permute-start | bytes 1572872 | tf_op jit(solution)/shard_map/ppermute | solution.py:1078
  255.3 24.0 %collective-permute-start.24 = (bf16[128,2048]{1,0:T(8,128)(2,1)S(1)}, bf16[128,2048]{1,0:T(8,128)(2,1)}, u32[]{:S(2)}, u32[]{:S(2)}) collective-permute-start(bf16[128,2048]{1,0:T(8,128)(2,1)S(1)} %collective-permute-done.22.refs_0_.refs_11_), channel_id=1, source_target_pairs={{0,4},{4,0},{1,5},{5,1},{2,6},{6,2},{3,7},{7,3},{8,12},{12,8},{9,1... | collective-permute-start | bytes 1572872 | tf_op jit(solution)/shard_map/ppermute | solution.py:1073
  279.4 15.6 %collective-permute-start.27 = (bf16[128,2048]{1,0:T(8,128)(2,1)S(1)}, bf16[128,2048]{1,0:T(8,128)(2,1)S(1)}, u32[]{:S(2)}, u32[]{:S(2)}) collective-permute-start(bf16[128,2048]{1,0:T(8,128)(2,1)S(1)} %add_convert_fusion.14), channel_id=1, source_target_pairs={{0,8},{8,16},{16,24},{24,0},{1,9},{9,17},{17,25},{25,1},{2,10},{10... | collective-permute-start | bytes 1572872 | tf_op jit(solution)/shard_map/ppermute | solution.py:1078
  311.7 16.8 %collective-permute-start.34 = (bf16[2,256,2048]{2,1,0:T(8,128)(2,1)}, bf16[2,256,2048]{2,1,0:T(8,128)(2,1)}, u32[]{:S(2)}, u32[]{:S(2)}) collective-permute-start(bf16[2,256,2048]{2,1,0:T(8,128)(2,1)} %get-tuple-element.389), channel_id=1, source_target_pairs={{0,1},{1,0},{2,3},{3,2},{4,5},{5,4},{6,7},{7,6},{8,9},{9,8},{10,11... | collective-permute-start | bytes 6291464 | tf_op jit(solution)/shard_map/ppermute | solution.py:1073
  312.0 16.6 %collective-permute-start.32 = (bf16[128,2048]{1,0:T(8,128)(2,1)S(1)}, bf16[128,2048]{1,0:T(8,128)(2,1)S(1)}, u32[]{:S(2)}, u32[]{:S(2)}) collective-permute-start(bf16[128,2048]{1,0:T(8,128)(2,1)S(1)} %add_convert_fusion.12), channel_id=1, source_target_pairs={{0,8},{8,16},{16,24},{24,0},{1,9},{9,17},{17,25},{25,1},{2,10},{10... | collective-permute-start | bytes 1572872 | tf_op jit(solution)/shard_map/ppermute | solution.py:1078
  338.7 29.7 %collective-permute-start.36 = (bf16[2,256,2048]{2,1,0:T(8,128)(2,1)}, bf16[2,256,2048]{2,1,0:T(8,128)(2,1)}, u32[]{:S(2)}, u32[]{:S(2)}) collective-permute-start(bf16[2,256,2048]{2,1,0:T(8,128)(2,1)} %get-tuple-element.446), channel_id=1, source_target_pairs={{0,1},{1,0},{2,3},{3,2},{4,5},{5,4},{6,7},{7,6},{8,9},{9,8},{10,11... | collective-permute-start | bytes 6291464 | tf_op jit(solution)/shard_map/ppermute | solution.py:1073
  338.9 29.4 %all-to-all-start.3 = ((bf16[32,80,128]{2,1,0:T(8,128)(2,1)}), bf16[32,80,128]{2,1,0:T(8,128)(2,1)S(1)}, u32[]{:S(2)}, u32[]{:S(2)}) async-start(bf16[32,80,128]{2,1,0:T(8,128)(2,1)} %get-tuple-element.422), calls=%async_computation.3 | async-start | bytes 1310720 | tf_op jit(solution)/shard_map/all_to_all | solution.py:1360
  341.5 126.1 %reduce-scatter.2.cloned.1.call-start = ((), (), s32[]{:S(2)}) async-start(), calls=%async_computation.11 | async-start | bytes 2359296 | tf_op jit(solution)/shard_map/reduce_scatter | solution.py:1366
  341.6 26.7 %collective-permute-start.35 = (bf16[128,2048]{1,0:T(8,128)(2,1)S(1)}, bf16[128,2048]{1,0:T(8,128)(2,1)S(1)}, u32[]{:S(2)}, u32[]{:S(2)}) collective-permute-start(bf16[128,2048]{1,0:T(8,128)(2,1)S(1)} %copy-done.57), channel_id=1, source_target_pairs={{0,4},{4,0},{1,5},{5,1},{2,6},{6,2},{3,7},{7,3},{8,12},{12,8},{9,1... | collective-permute-start | bytes 1572872 | tf_op jit(solution)/shard_map/ppermute | solution.py:1073
  369.1 39.3 %collective-permute-start.41 = (bf16[2,256,2048]{2,1,0:T(8,128)(2,1)}, bf16[2,256,2048]{2,1,0:T(8,128)(2,1)S(1)}, u32[]{:S(2)}, u32[]{:S(2)}) collective-permute-start(bf16[2,256,2048]{2,1,0:T(8,128)(2,1)} %get-tuple-element.460), channel_id=1, source_target_pairs={{0,1},{1,0},{2,3},{3,2},{4,5},{5,4},{6,7},{7,6},{8,9},{9,8},{10,11... | collective-permute-start | bytes 6291464 | tf_op jit(solution)/shard_map/ppermute | solution.py:1073
  371.5 36.2 %collective-permute-start.38 = (bf16[128,2048]{1,0:T(8,128)(2,1)}, bf16[128,2048]{1,0:T(8,128)(2,1)}, u32[]{:S(2)}, u32[]{:S(2)}) collective-permute-start(bf16[128,2048]{1,0:T(8,128)(2,1)} %add_convert_fusion.11), channel_id=1, source_target_pairs={{0,8},{8,16},{16,24},{24,0},{1,9},{9,17},{17,25},{25,1},{2,10},{10... | collective-permute-start | bytes 1572872 | tf_op jit(solution)/shard_map/ppermute | solution.py:1078
  373.1 34.5 %collective-permute-start.39 = (bf16[128,2048]{1,0:T(8,128)(2,1)}, bf16[128,2048]{1,0:T(8,128)(2,1)}, u32[]{:S(2)}, u32[]{:S(2)}) collective-permute-start(bf16[128,2048]{1,0:T(8,128)(2,1)} %get-tuple-element.451), channel_id=1, source_target_pairs={{0,4},{4,0},{1,5},{5,1},{2,6},{6,2},{3,7},{7,3},{8,12},{12,8},{9,1... | collective-permute-start | bytes 1572872 | tf_op jit(solution)/shard_map/ppermute | solution.py:1073
  374.6 33.0 %collective-permute-start.40 = (bf16[128,2048]{1,0:T(8,128)(2,1)}, bf16[128,2048]{1,0:T(8,128)(2,1)S(1)}, u32[]{:S(2)}, u32[]{:S(2)}) collective-permute-start(bf16[128,2048]{1,0:T(8,128)(2,1)} %get-tuple-element.453), channel_id=1, source_target_pairs={{0,4},{4,0},{1,5},{5,1},{2,6},{6,2},{3,7},{7,3},{8,12},{12,8},{9,1... | collective-permute-start | bytes 1572872 | tf_op jit(solution)/shard_map/ppermute | solution.py:1073
  375.2 33.3 %collective-permute-start.37 = (bf16[256,2048]{1,0:T(8,128)(2,1)}, bf16[256,2048]{1,0:T(8,128)(2,1)}, u32[]{:S(2)}, u32[]{:S(2)}) collective-permute-start(bf16[256,2048]{1,0:T(8,128)(2,1)} %fusion.7), channel_id=1, source_target_pairs={{0,2},{2,0},{1,3},{3,1},{4,6},{6,4},{5,7},{7,5},{8,10},{10,8},{9,1... | collective-permute-start | bytes 3145736 | tf_op jit(solution)/shard_map/ppermute | solution.py:1073
  409.8 23.6 %all-to-all-start.4 = ((bf16[4,192,1024]{2,1,0:T(8,128)(2,1)}), bf16[4,192,1024]{2,1,0:T(8,128)(2,1)S(1)}, u32[]{:S(2)}, u32[]{:S(2)}) async-start(bf16[4,192,1024]{2,1,0:T(8,128)(2,1)} %attn_bwd.1), calls=%async_computation.4 | async-start | bytes 3145728 | tf_op jit(solution)/shard_map/all_to_all | solution.py:1378
  415.0 17.6 %collective-permute-start.42 = (bf16[128,2048]{1,0:T(8,128)(2,1)S(1)}, bf16[128,2048]{1,0:T(8,128)(2,1)}, u32[]{:S(2)}, u32[]{:S(2)}) collective-permute-start(bf16[128,2048]{1,0:T(8,128)(2,1)S(1)} %add_convert_fusion.10), channel_id=1, source_target_pairs={{0,8},{8,16},{16,24},{24,0},{1,9},{9,17},{17,25},{25,1},{2,10},{10... | collective-permute-start | bytes 1572872 | tf_op jit(solution)/shard_map/ppermute | solution.py:1078
  438.6 17.5 %collective-permute-start.44 = (bf16[128,2048]{1,0:T(8,128)(2,1)}, bf16[128,2048]{1,0:T(8,128)(2,1)S(1)}, u32[]{:S(2)}, u32[]{:S(2)}) collective-permute-start(bf16[128,2048]{1,0:T(8,128)(2,1)} %input_rows.1), channel_id=1, source_target_pairs={{0,4},{4,0},{1,5},{5,1},{2,6},{6,2},{3,7},{7,3},{8,12},{12,8},{9,1... | collective-permute-start | bytes 1572872 | tf_op jit(solution)/shard_map/ppermute | solution.py:1073
  463.8 19.8 %collective-permute-start.50 = (bf16[8,64,768]{2,1,0:T(8,128)(2,1)}, bf16[8,64,768]{2,1,0:T(8,128)(2,1)S(1)}, u32[]{:S(2)}, u32[]{:S(2)}) collective-permute-start(bf16[8,64,768]{2,1,0:T(8,128)(2,1)} %fusion.9), channel_id=1, source_target_pairs={{0,2},{2,0},{1,3},{3,1},{4,6},{6,4},{5,7},{7,5},{8,10},{10,8},{9,1... | collective-permute-start | bytes 2359304 | tf_op jit(solution)/shard_map/ppermute | solution.py:1073
  485.8 17.0 %collective-permute-start.51 = (bf16[128,2048]{1,0:T(8,128)(2,1)}, bf16[128,2048]{1,0:T(8,128)(2,1)}, u32[]{:S(2)}, u32[]{:S(2)}) collective-permute-start(bf16[128,2048]{1,0:T(8,128)(2,1)} %add_convert_fusion.5), channel_id=1, source_target_pairs={{0,8},{8,16},{16,24},{24,0},{1,9},{9,17},{17,25},{25,1},{2,10},{10... | collective-permute-start | bytes 1572872 | tf_op jit(solution)/shard_map/ppermute | solution.py:1078
  487.1 15.7 %collective-permute-start.53 = (bf16[128,2048]{1,0:T(8,128)(2,1)}, bf16[128,2048]{1,0:T(8,128)(2,1)}, u32[]{:S(2)}, u32[]{:S(2)}) collective-permute-start(bf16[128,2048]{1,0:T(8,128)(2,1)} %get-tuple-element.509), channel_id=1, source_target_pairs={{0,2},{2,0},{1,3},{3,1},{4,6},{6,4},{5,7},{7,5},{8,10},{10,8},{9,1... | collective-permute-start | bytes 1572872 | tf_op jit(solution)/shard_map/ppermute | solution.py:1073
  491.4 40.3 %all-to-all-start.5 = ((bf16[8,64,768]{2,1,0:T(8,128)(2,1)}), bf16[8,64,768]{2,1,0:T(8,128)(2,1)S(1)}, u32[]{:S(2)}, u32[]{:S(2)}) async-start(bf16[8,64,768]{2,1,0:T(8,128)(2,1)} %fusion.1), calls=%async_computation.6 | async-start | bytes 1572864 | tf_op jit(solution)/shard_map/all_to_all | solution.py:1402
  504.4 20.5 %collective-permute-start.54 = (bf16[128,2048]{1,0:T(8,128)(2,1)S(1)}, bf16[128,2048]{1,0:T(8,128)(2,1)S(1)}, u32[]{:S(2)}, u32[]{:S(2)}) collective-permute-start(bf16[128,2048]{1,0:T(8,128)(2,1)S(1)} %add_convert_fusion.4), channel_id=1, source_target_pairs={{0,8},{8,16},{16,24},{24,0},{1,9},{9,17},{17,25},{25,1},{2,10},{10... | collective-permute-start | bytes 1572872 | tf_op jit(solution)/shard_map/ppermute | solution.py:1078
  504.7 15.7 %collective-permute-start.55 = (bf16[128,2048]{1,0:T(8,128)(2,1)S(1)}, bf16[128,2048]{1,0:T(8,128)(2,1)S(1)}, u32[]{:S(2)}, u32[]{:S(2)}) collective-permute-start(bf16[128,2048]{1,0:T(8,128)(2,1)S(1)} %copy-done.61), channel_id=1, source_target_pairs={{0,4},{4,0},{1,5},{5,1},{2,6},{6,2},{3,7},{7,3},{8,12},{12,8},{9,1... | collective-permute-start | bytes 1572872 | tf_op jit(solution)/shard_map/ppermute | solution.py:1073
  505.7 21.0 %collective-permute-start.56 = (bf16[256,2048]{1,0:T(8,128)(2,1)S(1)}, bf16[256,2048]{1,0:T(8,128)(2,1)S(1)}, u32[]{:S(2)}, u32[]{:S(2)}) collective-permute-start(bf16[256,2048]{1,0:T(8,128)(2,1)S(1)} %copy-done.18), channel_id=1, source_target_pairs={{0,2},{2,0},{1,3},{3,1},{4,6},{6,4},{5,7},{7,5},{8,10},{10,8},{9,1... | collective-permute-start | bytes 3145736 | tf_op jit(solution)/shard_map/ppermute | solution.py:1073
  (86 other events, 1039.2 us)
Sparse Core Ops, SparseCore 0:
  9.6 37.1 all-gather.4
  49.9 103.9 all-gather.6
  156.1 68.6 all-gather.8
  338.8 25.3 all-gather.10
  373.2 70.9 reduce-scatter.1
